TPU v7x, 32 devices: a whole 2x2x4 slice. The times are simulated.
32 devices in a mesh: dp: 8 (over z, x), mp: 4 (over y, core).
Axes of the slice: x: 2, y: 2, z: 4, core: 2. Of those that a mesh axis runs over, the one named last changes fastest.
Arguments:
- token_ids: int32 [32, 512], P('dp'), may hold values from 0 to 50303
- mlm_targets: int32 [32, 32], P('dp'), may hold values from 0 to 50303
- page_lengths: int32 [32], P(('dp', 'mp')), may hold values from 1 to 512, as said below
- box_coords: int32 [4, 32, 512], P(None, ('dp', 'mp')), may hold values from 0 to 1023
- mlm_positions: int32 [32, 32], P(('dp', 'mp')), may hold values from 0 to 511, as said below
- align_pairs: int32 [32, 32, 2], P(('dp', 'mp')), may hold values from 0 to 511, as said below
- align_labels: int32 [32, 32], P(('dp', 'mp')), may hold values 0 or 1
- table: float32 [50304, 768], P(('mp', 'dp'))
- text_mats: float32 [2, 768, 3072], P(None, 'dp')
- layout_mats: float32 [2, 192, 768], P(None, 'dp')
- text_ffn: float32 [2, 3072, 1536], P(None, ('mp', 'dp')), may hold values from -0.21875 to 0.21875
- layout_ffn: float32 [2, 768, 384], P(None, ('mp', 'dp')), may hold values from -0.4375 to 0.4375
- small_params: float32 [762240], P('dp')
- table_momentum: float32 [50304, 768], P(('mp', 'dp')), may hold values from -1.9073486e-05 to 1.9073486e-05
- text_mats_momentum: float32 [2, 768, 3072], P(None, 'dp'), may hold values from -1.9073486e-05 to 1.9073486e-05
- layout_mats_momentum: float32 [2, 192, 768], P(None, 'dp'), may hold values from -1.9073486e-05 to 1.9073486e-05
- text_ffn_momentum: float32 [2, 3072, 1536], P(None, ('mp', 'dp')), may hold values from -1.9073486e-05 to 1.9073486e-05
- layout_ffn_momentum: float32 [2, 768, 384], P(None, ('mp', 'dp')), may hold values from -1.9073486e-05 to 1.9073486e-05
- small_momentum: float32 [762240], P('dp'), may hold values from -6.1035156e-05 to 6.1035156e-05
- table_average: float32 [50304, 768], P(('mp', 'dp')), may hold values from -0.21875 to 0.21875
- text_mats_average: float32 [2, 768, 3072], P(None, 'dp'), may hold values from -0.21875 to 0.21875
- layout_mats_average: float32 [2, 192, 768], P(None, 'dp'), may hold values from -0.4375 to 0.4375
- text_ffn_average: float32 [2, 3072, 1536], P(None, ('mp', 'dp')), may hold values from -0.21875 to 0.21875
- layout_ffn_average: float32 [2, 768, 384], P(None, ('mp', 'dp')), may hold values from -0.4375 to 0.4375
- small_average: float32 [762240], P('dp'), may hold values from -6 to 6
Outputs:
- loss_sum: float32 [], replicated
- loss_count: float32 [], replicated
- grad_norm: float32 [], replicated
- new_table: float32 [50304, 768], P(('mp', 'dp'))
- new_text_mats: float32 [2, 768, 3072], P(None, 'dp')
- new_layout_mats: float32 [2, 192, 768], P(None, 'dp')
- new_text_ffn: float32 [2, 3072, 1536], P(None, ('mp', 'dp'))
- new_layout_ffn: float32 [2, 768, 384], P(None, ('mp', 'dp'))
- new_small: float32 [762240], P('dp')
- table_copy: bfloat16 [50304, 768], P(('mp', 'dp'))
- text_mats_copy: bfloat16 [2, 768, 3072], P(None, 'dp')
- layout_mats_copy: bfloat16 [2, 192, 768], P(None, 'dp')
- text_ffn_copy: bfloat16 [2, 3072, 1536], P(None, ('mp', 'dp'))
- layout_ffn_copy: bfloat16 [2, 768, 384], P(None, ('mp', 'dp'))
- table_momentum_new: float32 [50304, 768], P(('mp', 'dp'))
- text_mats_momentum_new: float32 [2, 768, 3072], P(None, 'dp')
- layout_mats_momentum_new: float32 [2, 192, 768], P(None, 'dp')
- text_ffn_momentum_new: float32 [2, 3072, 1536], P(None, ('mp', 'dp'))
- layout_ffn_momentum_new: float32 [2, 768, 384], P(None, ('mp', 'dp'))
- small_momentum_new: float32 [762240], P('dp')
- table_average_new: float32 [50304, 768], P(('mp', 'dp'))
- text_mats_average_new: float32 [2, 768, 3072], P(None, 'dp')
- layout_mats_average_new: float32 [2, 192, 768], P(None, 'dp')
- text_ffn_average_new: float32 [2, 3072, 1536], P(None, ('mp', 'dp'))
- layout_ffn_average_new: float32 [2, 768, 384], P(None, ('mp', 'dp'))
- small_average_new: float32 [762240], P('dp')
Inputs may be any that keep to these rules, and one draw needn't show every extreme that they name: `page_lengths`: the live tokens of each page; slots beyond are padding. Some page has 512. `mlm_positions`: every slot lies below its page's length. `align_pairs`: both slots of a pair lie below their page's length.
All inputs are finite; a program needn't handle non-finite values. No bound on the sum of `align_labels` on one device may be relied on, other than what follows from the above.
Results may differ from a plain program's by a relative error of at most 0.011.
Values may be sent and summed in bfloat16 or wider, within the bound.
No kernel may reach another device: no remote copies, remote signals or barrier semaphores. Data moves between devices by JAX's collectives and lax.ppermute only.
A program may use at most 320 MiB of HBM per device.

v0:
```python
import math

import jax
import jax.numpy as jnp
from jax import lax
from jax.sharding import PartitionSpec as P

WIDTH = 768
HEADS = 12
FFN_UNITS = 3072
LAYOUT_WIDTH = 192
LAYOUT_UNITS = 768
BOXES = 1024
PAGE_SLOTS = 512
PAIRS = 32
LAYERS = 2


EPSILON = 1e-05
CLIP_NORM = 0.01
LEARN_RATE = 10000.0
MOMENTUM = 0.5
AVERAGE_DECAY = 0.5
MASK_FILL = -1e30
PRECISE = lax.Precision.HIGHEST


def merged(x, axis, combine):
    everything = jax.tree.map(lambda part: lax.all_gather(part, axis), x)
    initial = jax.tree.map(lambda part: part[0], everything)

    def lap(k, so_far):
        return combine(so_far, jax.tree.map(lambda part: part[k], everything))

    return lax.fori_loop(1, lax.axis_size(axis), lap, initial)


def small_shapes():
    return [
        (LAYERS, 8, WIDTH),
        (LAYERS, 8, LAYOUT_WIDTH),
        (LAYERS, FFN_UNITS),
        (LAYERS, LAYOUT_UNITS),
        (2, WIDTH),
        (2, LAYOUT_WIDTH),
        (PAGE_SLOTS, WIDTH),
        (PAGE_SLOTS, LAYOUT_WIDTH),
        (2, BOXES, LAYOUT_WIDTH // 4),
        (LAYOUT_WIDTH, WIDTH),
    ]


def unpack_small(flat_vec):
    pieces = []
    offset = 0
    for piece_dims in small_shapes():
        amount = math.prod(piece_dims)
        pieces.append(flat_vec[offset : offset + amount].reshape(piece_dims))
        offset = offset + amount
    return pieces


def norm_apply(values, gain_row, bias_row):
    centre = values - jnp.mean(values, axis=-1, keepdims=True)
    spread = jnp.mean(centre * centre, axis=-1, keepdims=True)
    return centre * lax.rsqrt(spread + EPSILON) * gain_row + bias_row


def norm_back(values, gain_row, bias_row, grad_out):
    unused, pullback = jax.vjp(norm_apply, values, gain_row, bias_row)
    return pullback(grad_out)


def gelu_exact(values):
    return jax.nn.gelu(values, approximate=False)


def contract_rows(left, right):
    return lax.dot_general(
        left, right, (((0,), (0,)), ((), ())), preferred_element_type=jnp.float32
    )


def contract_cols(left, right):
    return lax.dot_general(
        left, right, (((1,), (1,)), ((), ())), preferred_element_type=jnp.float32
    )


def heads_view(values, pages):
    return values.reshape(pages, PAGE_SLOTS, HEADS, values.shape[-1] // HEADS)


def lane_pair(first, second):
    return (
        lax.all_gather(first, "mp", axis=0, tiled=True),
        lax.all_gather(second, "mp", axis=0, tiled=True),
    )


def lane_sum(first, second):
    return (
        lax.psum_scatter(first.astype(jnp.bfloat16), "mp", scatter_dimension=0, tiled=True).astype(
            jnp.float32
        ),
        lax.psum_scatter(second.astype(jnp.bfloat16), "mp", scatter_dimension=0, tiled=True).astype(
            jnp.float32
        ),
    )


def project_qkv(rows_low, mats, vectors, width):
    joined = jnp.dot(rows_low, mats[:, : 3 * width], preferred_element_type=jnp.float32)
    query = (joined[:, :width] + vectors[0]).astype(jnp.bfloat16)
    keys = joined[:, width : 2 * width].astype(jnp.bfloat16)
    values = (joined[:, 2 * width :] + vectors[1]).astype(jnp.bfloat16)
    return (query, keys, values)


def scale_pair():
    return (1.0 / math.sqrt(WIDTH // HEADS), 1.0 / math.sqrt(LAYOUT_WIDTH // HEADS))


def scores_of(text_views, layout_views, key_live):
    text_scale, layout_scale = scale_pair()
    scores = (
        jnp.einsum(
            "pqhd,pkhd->phqk", text_views[0], text_views[1], preferred_element_type=jnp.float32
        )
        * text_scale
    )
    scores = (
        scores
        + jnp.einsum(
            "pqhd,pkhd->phqk", layout_views[0], layout_views[1], preferred_element_type=jnp.float32
        )
        * layout_scale
    )
    return jnp.where(key_live[:, None, None, :], scores, MASK_FILL)


def attend(text_qkv, layout_qkv, key_live, pages):
    text_views = [heads_view(item, pages) for item in text_qkv]
    layout_views = [heads_view(item, pages) for item in layout_qkv]
    scores = scores_of(text_views, layout_views, key_live)
    peak = jnp.max(scores, axis=-1, keepdims=True)
    expo = jnp.exp(scores - peak)
    total = jnp.sum(expo, axis=-1, keepdims=True)
    probs = (expo / total).astype(jnp.bfloat16)
    text_out = jnp.einsum(
        "phqk,pkhd->pqhd", probs, text_views[2], preferred_element_type=jnp.float32
    )
    layout_out = jnp.einsum(
        "phqk,pkhd->pqhd", probs, layout_views[2], preferred_element_type=jnp.float32
    )
    return (
        text_out.reshape(-1, WIDTH).astype(jnp.bfloat16),
        layout_out.reshape(-1, LAYOUT_WIDTH).astype(jnp.bfloat16),
        peak + jnp.log(total),
    )


def attend_back(text_qkv, layout_qkv, key_live, pages, log_total, text_grad, layout_grad):
    text_scale, layout_scale = scale_pair()
    text_views = [heads_view(item, pages) for item in text_qkv]
    layout_views = [heads_view(item, pages) for item in layout_qkv]
    probs = jnp.exp(scores_of(text_views, layout_views, key_live) - log_total)
    probs_low = probs.astype(jnp.bfloat16)
    text_go = heads_view(text_grad, pages)
    layout_go = heads_view(layout_grad, pages)
    grad_probs = jnp.einsum(
        "pqhd,pkhd->phqk", text_go, text_views[2], preferred_element_type=jnp.float32
    )
    grad_probs = grad_probs + jnp.einsum(
        "pqhd,pkhd->phqk", layout_go, layout_views[2], preferred_element_type=jnp.float32
    )
    grad_scores = (
        probs * (grad_probs - jnp.sum(grad_probs * probs, axis=-1, keepdims=True))
    ).astype(jnp.bfloat16)
    results = []
    for views, grad_out, scale_of, width in (
        (text_views, text_go, text_scale, WIDTH),
        (layout_views, layout_go, layout_scale, LAYOUT_WIDTH),
    ):
        grad_q = (
            jnp.einsum("phqk,pkhd->pqhd", grad_scores, views[1], preferred_element_type=jnp.float32)
            * scale_of
        )
        grad_k = (
            jnp.einsum("phqk,pqhd->pkhd", grad_scores, views[0], preferred_element_type=jnp.float32)
            * scale_of
        )
        grad_v = jnp.einsum(
            "phqk,pqhd->pkhd", probs_low, grad_out, preferred_element_type=jnp.float32
        )
        results.append([item.reshape(-1, width) for item in (grad_q, grad_k, grad_v)])
    return results


def project_back(rows_low, mats, grads, width):
    lows = [item.astype(jnp.bfloat16) for item in grads]
    joined = jnp.concatenate(lows, 1)
    rows_grad = contract_cols(joined, mats[:, : 3 * width])
    mats_grad = contract_rows(rows_low, joined)
    return (
        rows_grad,
        mats_grad,
        jnp.sum(lows[0], 0, dtype=jnp.float32),
        jnp.sum(lows[2], 0, dtype=jnp.float32),
    )


def ffn_front(rows_in, unit_mats, bias_in):
    width = rows_in.shape[1]
    pre_act = contract_cols(rows_in, unit_mats[:, :width]) + bias_in
    hidden = gelu_exact(pre_act).astype(jnp.bfloat16)
    return (
        pre_act,
        hidden,
        jnp.dot(hidden, unit_mats[:, width:], preferred_element_type=jnp.float32),
    )


def ffn_back(rows_in, unit_mats, pre_act, hidden, grad_rows):
    width = rows_in.shape[1]
    grad_hidden = contract_cols(grad_rows, unit_mats[:, width:])
    grad_pre = jax.vjp(gelu_exact, pre_act)[1](grad_hidden)[0].astype(jnp.bfloat16)
    grad_in = jnp.dot(grad_pre, unit_mats[:, :width], preferred_element_type=jnp.float32)
    unit_grad = jnp.concatenate(
        [contract_rows(grad_pre, rows_in), contract_rows(hidden, grad_rows)], 1
    )
    return (grad_in, unit_grad, jnp.sum(grad_pre, 0, dtype=jnp.float32))


def layer_forward(text, layout, weights, key_live, pages, lane):
    (
        text_mats,
        layout_mats,
        text_units,
        layout_units,
        text_bias,
        layout_bias,
        text_vec,
        layout_vec,
    ) = weights
    text_low = text.astype(jnp.bfloat16)
    layout_low = layout.astype(jnp.bfloat16)
    text_qkv = project_qkv(text_low, text_mats, text_vec, WIDTH)
    layout_qkv = project_qkv(layout_low, layout_mats, layout_vec, LAYOUT_WIDTH)
    text_att, layout_att, log_total = attend(text_qkv, layout_qkv, key_live, pages)
    text_first = (
        text
        + jnp.dot(text_att, text_mats[:, 3 * WIDTH :], preferred_element_type=jnp.float32)
        + text_vec[2]
    )
    layout_first = (
        layout
        + jnp.dot(
            layout_att, layout_mats[:, 3 * LAYOUT_WIDTH :], preferred_element_type=jnp.float32
        )
        + layout_vec[2]
    )
    text_mid = norm_apply(text_first, text_vec[3], text_vec[4])
    layout_mid = norm_apply(layout_first, layout_vec[3], layout_vec[4])
    text_rows, layout_rows = lane_pair(
        text_mid.astype(jnp.bfloat16), layout_mid.astype(jnp.bfloat16)
    )
    text_full, layout_full = (text_units, layout_units)
    text_in_bias = lax.dynamic_slice_in_dim(
        text_bias, lane * text_units.shape[0], text_units.shape[0]
    )
    layout_in_bias = lax.dynamic_slice_in_dim(
        layout_bias, lane * layout_units.shape[0], layout_units.shape[0]
    )
    text_pre, text_hidden, text_part = ffn_front(text_rows, text_full, text_in_bias)
    layout_pre, layout_hidden, layout_part = ffn_front(layout_rows, layout_full, layout_in_bias)
    text_ffn_out, layout_ffn_out = lane_sum(text_part, layout_part)
    text_last = text_mid + text_ffn_out + text_vec[5]
    layout_last = layout_mid + layout_ffn_out + layout_vec[5]
    cache = (
        text_low,
        layout_low,
        text_qkv,
        layout_qkv,
        log_total,
        text_att,
        layout_att,
        text_first,
        layout_first,
        text_rows,
        layout_rows,
        text_full,
        layout_full,
        text_pre,
        layout_pre,
        text_hidden,
        layout_hidden,
        text_last,
        layout_last,
    )
    return (
        norm_apply(text_last, text_vec[6], text_vec[7]),
        norm_apply(layout_last, layout_vec[6], layout_vec[7]),
        cache,
    )


def layer_backward(cache, grad_text, grad_layout, weights, key_live, pages, lane):
    (
        text_low,
        layout_low,
        text_qkv,
        layout_qkv,
        log_total,
        text_att,
        layout_att,
        text_first,
        layout_first,
        text_rows,
        layout_rows,
        text_full,
        layout_full,
        text_pre,
        layout_pre,
        text_hidden,
        layout_hidden,
        text_last,
        layout_last,
    ) = cache
    (
        text_mats,
        layout_mats,
        text_units,
        layout_units,
        text_bias,
        layout_bias,
        text_vec,
        layout_vec,
    ) = weights
    last_t, gain2_t, bias2_t = norm_back(text_last, text_vec[6], text_vec[7], grad_text)
    last_l, gain2_l, bias2_l = norm_back(layout_last, layout_vec[6], layout_vec[7], grad_layout)
    rows_grad_t, rows_grad_l = lane_pair(last_t.astype(jnp.bfloat16), last_l.astype(jnp.bfloat16))
    in_part_t, unit_grad_t, in_bias_t = ffn_back(
        text_rows, text_full, text_pre, text_hidden, rows_grad_t
    )
    in_part_l, unit_grad_l, in_bias_l = ffn_back(
        layout_rows, layout_full, layout_pre, layout_hidden, rows_grad_l
    )
    in_grad_t, in_grad_l = lane_sum(in_part_t, in_part_l)
    in_bias_t = lax.dynamic_update_slice_in_dim(
        jnp.zeros((FFN_UNITS,), jnp.float32), in_bias_t, lane * text_units.shape[0], 0
    )
    in_bias_l = lax.dynamic_update_slice_in_dim(
        jnp.zeros((LAYOUT_UNITS,), jnp.float32), in_bias_l, lane * layout_units.shape[0], 0
    )
    first_t, gain1_t, bias1_t = norm_back(text_first, text_vec[3], text_vec[4], last_t + in_grad_t)
    first_l, gain1_l, bias1_l = norm_back(
        layout_first, layout_vec[3], layout_vec[4], last_l + in_grad_l
    )
    first_low_t = first_t.astype(jnp.bfloat16)
    first_low_l = first_l.astype(jnp.bfloat16)
    out_proj_t = contract_rows(text_att, first_low_t)
    out_proj_l = contract_rows(layout_att, first_low_l)
    att_grad_t = contract_cols(first_low_t, text_mats[:, 3 * WIDTH :]).astype(jnp.bfloat16)
    att_grad_l = contract_cols(first_low_l, layout_mats[:, 3 * LAYOUT_WIDTH :]).astype(jnp.bfloat16)
    text_dqkv, layout_dqkv = attend_back(
        text_qkv, layout_qkv, key_live, pages, log_total, att_grad_t, att_grad_l
    )
    rows_t, qkv_grad_t, q_bias_t, v_bias_t = project_back(text_low, text_mats, text_dqkv, WIDTH)
    rows_l, qkv_grad_l, q_bias_l, v_bias_l = project_back(
        layout_low, layout_mats, layout_dqkv, LAYOUT_WIDTH
    )
    vec_grad_t = jnp.stack(
        [
            q_bias_t,
            v_bias_t,
            jnp.sum(first_t, 0),
            gain1_t,
            bias1_t,
            jnp.sum(last_t, 0),
            gain2_t,
            bias2_t,
        ]
    )
    vec_grad_l = jnp.stack(
        [
            q_bias_l,
            v_bias_l,
            jnp.sum(first_l, 0),
            gain1_l,
            bias1_l,
            jnp.sum(last_l, 0),
            gain2_l,
            bias2_l,
        ]
    )
    grads = (
        jnp.concatenate([qkv_grad_t, out_proj_t], 1),
        jnp.concatenate([qkv_grad_l, out_proj_l], 1),
        unit_grad_t,
        unit_grad_l,
        in_bias_t,
        in_bias_l,
        vec_grad_t,
        vec_grad_l,
    )
    return (first_t + rows_t, first_l + rows_l, grads)


def apply_update(master, grad, moment, average, loss_count, factor):
    clipped = grad / loss_count * factor
    moment_new = MOMENTUM * moment + clipped
    master_new = master - LEARN_RATE * (clipped + MOMENTUM * moment_new)
    return (master_new, moment_new, AVERAGE_DECAY * average + (1.0 - AVERAGE_DECAY) * master_new)


def on_device(
    token_ids,
    mlm_targets,
    page_lengths,
    box_coords,
    mlm_positions,
    align_pairs,
    align_labels,
    table,
    text_mats,
    layout_mats,
    text_ffn,
    layout_ffn,
    small_params,
    table_momentum,
    text_mats_momentum,
    layout_mats_momentum,
    text_ffn_momentum,
    layout_ffn_momentum,
    small_momentum,
    table_average,
    text_mats_average,
    layout_mats_average,
    text_ffn_average,
    layout_ffn_average,
    small_average,
):
    lane = lax.axis_index("mp")
    pages = page_lengths.shape[0]
    mask_slots = mlm_positions.shape[1]
    table_all, tmats_all, lmats_all, tffn_lane, lffn_lane, small_all = (
        lax.all_gather(table.astype(jnp.bfloat16), "dp", axis=0, tiled=True),
        lax.all_gather(text_mats.astype(jnp.bfloat16), "dp", axis=1, tiled=True),
        lax.all_gather(layout_mats.astype(jnp.bfloat16), "dp", axis=1, tiled=True),
        lax.all_gather(text_ffn.astype(jnp.bfloat16), "dp", axis=1, tiled=True),
        lax.all_gather(layout_ffn.astype(jnp.bfloat16), "dp", axis=1, tiled=True),
        lax.all_gather(small_params.astype(jnp.bfloat16), "dp", axis=0, tiled=True),
    )
    (
        text_vec,
        layout_vec,
        text_bias,
        layout_bias,
        text_emb,
        layout_emb,
        text_pos,
        layout_pos,
        box_table,
        align_mat,
    ) = unpack_small(small_all.astype(jnp.float32))
    key_live = jnp.arange(PAGE_SLOTS)[None, :] < page_lengths[:, None]
    vocab_rows = table_all.shape[0]
    vocab_start = lane * vocab_rows
    local_ids = token_ids.reshape(-1) - vocab_start
    inside = (local_ids >= 0) & (local_ids < vocab_rows)
    safe_ids = jnp.where(inside, local_ids, 0)
    embedded = lax.psum_scatter(
        jnp.where(
            inside[:, None], jnp.take(table_all, safe_ids, axis=0).astype(jnp.float32), 0.0
        ).astype(jnp.bfloat16),
        "mp",
        scatter_dimension=0,
        tiled=True,
    ).astype(jnp.float32)

    def text_embed_fn(embed_vals, pos_table, emb_rows):
        return norm_apply(embed_vals + jnp.tile(pos_table, (pages, 1)), emb_rows[0], emb_rows[1])

    def layout_embed_fn(box_rows, pos_table, emb_rows):
        looked = [jnp.take(box_rows[number % 2], box_coords[number], axis=0) for number in range(4)]
        layout_pre = jnp.concatenate(looked, -1).reshape(-1, LAYOUT_WIDTH) + jnp.tile(
            pos_table, (pages, 1)
        )
        return norm_apply(layout_pre, emb_rows[0], emb_rows[1])

    text, text_pull = jax.vjp(text_embed_fn, embedded, text_pos, text_emb)
    layout, layout_pull = jax.vjp(layout_embed_fn, box_table, layout_pos, layout_emb)
    caches = []
    layer_weights = []
    for layer_no in range(LAYERS):
        weights = (
            tmats_all[layer_no],
            lmats_all[layer_no],
            tffn_lane[layer_no],
            lffn_lane[layer_no],
            text_bias[layer_no],
            layout_bias[layer_no],
            text_vec[layer_no],
            layout_vec[layer_no],
        )
        text, layout, cache = layer_forward(text, layout, weights, key_live, pages, lane)
        caches.append(cache)
        layer_weights.append(weights)
    page_base = jnp.arange(pages)[:, None] * PAGE_SLOTS
    row_index = (page_base + mlm_positions).reshape(-1)
    live_own = (
        (jnp.arange(mask_slots)[None, :] * PAGE_SLOTS < mask_slots * page_lengths[:, None])
        .astype(jnp.float32)
        .reshape(-1)
    )
    chosen_all, live_all = (
        lax.all_gather(text[row_index].astype(jnp.bfloat16), "mp", axis=0, tiled=True),
        lax.all_gather(live_own.astype(jnp.bfloat16), "mp", axis=0, tiled=True),
    )
    logits = contract_cols(chosen_all, table_all)
    target_local = mlm_targets.reshape(-1) - vocab_start
    target_in = (target_local >= 0) & (target_local < vocab_rows)
    target_logit = jnp.where(
        target_in,
        jnp.take_along_axis(logits, jnp.where(target_in, target_local, 0)[:, None], axis=1)[:, 0],
        0.0,
    )
    row_peak = jnp.max(logits, axis=1)
    row_total = jnp.sum(jnp.exp(logits - row_peak[:, None]), axis=1)

    def combine(first, second):
        peak = jnp.maximum(first[0], second[0])
        return (
            peak,
            first[1] * jnp.exp(first[0] - peak) + second[1] * jnp.exp(second[0] - peak),
            first[2] + second[2],
        )

    all_peak, all_total, all_target = merged((row_peak, row_total, target_logit), "mp", combine)
    log_total = all_peak + jnp.log(all_total)
    live_rows = live_all.astype(jnp.float32)
    own_rows = pages * mask_slots
    own_loss = jnp.sum(
        lax.dynamic_slice_in_dim((log_total - all_target) * live_rows, lane * own_rows, own_rows)
    )
    one_hot = (jnp.arange(vocab_rows)[None, :] == target_local[:, None]).astype(jnp.float32)
    grad_low = ((jnp.exp(logits - log_total[:, None]) - one_hot) * live_rows[:, None]).astype(
        jnp.bfloat16
    )
    table_grad = contract_rows(grad_low, chosen_all)
    chosen_grad = lax.psum_scatter(
        jnp.dot(grad_low, table_all, preferred_element_type=jnp.float32).astype(jnp.bfloat16),
        "mp",
        scatter_dimension=0,
        tiled=True,
    ).astype(jnp.float32)
    first_rows = (page_base + align_pairs[:, :, 0]).reshape(-1)
    second_rows = (page_base + align_pairs[:, :, 1]).reshape(-1)
    answer = align_labels.reshape(-1).astype(jnp.float32)

    def pair_loss(text_rows, layout_rows, align_weight):
        right = jnp.dot(layout_rows[second_rows], align_weight, precision=PRECISE)
        logit = jnp.sum(text_rows[first_rows] * right, axis=-1) / math.sqrt(WIDTH)
        return jnp.sum(jax.nn.softplus(logit) - answer * logit)

    align_part, align_pull = jax.vjp(pair_loss, text, layout, align_mat)
    grad_text, grad_layout, align_grad = align_pull(jnp.ones((), jnp.float32))
    grad_text = grad_text.at[row_index].add(chosen_grad)
    layer_grads = [None] * LAYERS
    for layer_no in reversed(range(LAYERS)):
        grad_text, grad_layout, layer_grads[layer_no] = layer_backward(
            caches[layer_no], grad_text, grad_layout, layer_weights[layer_no], key_live, pages, lane
        )
    embed_grad, text_pos_grad, text_emb_grad = text_pull(grad_text)
    box_grad, layout_pos_grad, layout_emb_grad = layout_pull(grad_layout)
    grad_sent = lax.all_gather(embed_grad.astype(jnp.bfloat16), "mp", axis=0, tiled=True)
    table_grad = (
        table_grad
        + jax.ops.segment_sum(
            grad_sent.astype(jnp.float32),
            jnp.where(inside, local_ids, vocab_rows),
            num_segments=vocab_rows + 1,
        )[:vocab_rows]
    )

    def stacked(member):
        return jnp.stack([layer_grads[layer_no][member] for layer_no in range(LAYERS)])

    small_grad = jnp.concatenate(
        [
            item.reshape(-1)
            for item in (
                stacked(6),
                stacked(7),
                stacked(4),
                stacked(5),
                text_emb_grad,
                layout_emb_grad,
                text_pos_grad,
                layout_pos_grad,
                box_grad,
                align_grad,
            )
        ]
    )
    reduced = (
        lax.psum_scatter(
            table_grad.astype(jnp.bfloat16), "dp", scatter_dimension=0, tiled=True
        ).astype(jnp.float32),
        lax.psum_scatter(
            stacked(0).astype(jnp.bfloat16), "dp", scatter_dimension=1, tiled=True
        ).astype(jnp.float32),
        lax.psum_scatter(
            stacked(1).astype(jnp.bfloat16), "dp", scatter_dimension=1, tiled=True
        ).astype(jnp.float32),
        lax.psum_scatter(
            stacked(2).astype(jnp.bfloat16), "dp", scatter_dimension=1, tiled=True
        ).astype(jnp.float32),
        lax.psum_scatter(
            stacked(3).astype(jnp.bfloat16), "dp", scatter_dimension=1, tiled=True
        ).astype(jnp.float32),
        lax.psum_scatter(
            small_grad.astype(jnp.bfloat16), "dp", scatter_dimension=0, tiled=True
        ).astype(jnp.float32),
    )
    tmats_grad, lmats_grad, small_sum = (
        lax.psum(reduced[1].astype(jnp.bfloat16), "mp").astype(jnp.float32),
        lax.psum(reduced[2].astype(jnp.bfloat16), "mp").astype(jnp.float32),
        lax.psum(reduced[5].astype(jnp.bfloat16), "mp").astype(jnp.float32),
    )
    final_grads = (reduced[0], tmats_grad, lmats_grad, reduced[3], reduced[4], small_sum)
    lane_first = (lane == 0).astype(jnp.float32)
    squares = (
        jnp.sum(reduced[0] * reduced[0])
        + jnp.sum(reduced[3] * reduced[3])
        + jnp.sum(reduced[4] * reduced[4])
    )
    squares = squares + lane_first * (
        jnp.sum(tmats_grad * tmats_grad)
        + jnp.sum(lmats_grad * lmats_grad)
        + jnp.sum(small_sum * small_sum)
    )
    count_part = jnp.sum(live_own) + jnp.float32(pages * PAIRS)
    total_squares, loss_sum, loss_count = lax.psum(
        (squares, own_loss + align_part, count_part), ("dp", "mp")
    )
    grad_norm = jnp.sqrt(total_squares) / loss_count
    factor = jnp.minimum(1.0, CLIP_NORM / grad_norm)
    masters = (table, text_mats, layout_mats, text_ffn, layout_ffn, small_params)
    moments = (
        table_momentum,
        text_mats_momentum,
        layout_mats_momentum,
        text_ffn_momentum,
        layout_ffn_momentum,
        small_momentum,
    )
    averages = (
        table_average,
        text_mats_average,
        layout_mats_average,
        text_ffn_average,
        layout_ffn_average,
        small_average,
    )
    updated = [
        apply_update(
            masters[number],
            final_grads[number],
            moments[number],
            averages[number],
            loss_count,
            factor,
        )
        for number in range(6)
    ]
    new_masters = [item[0] for item in updated]
    new_moments = [item[1] for item in updated]
    new_averages = [item[2] for item in updated]
    copies = [item.astype(jnp.bfloat16) for item in new_masters[:5]]
    return (
        loss_sum,
        loss_count,
        grad_norm,
        new_masters[0],
        new_masters[1],
        new_masters[2],
        new_masters[3],
        new_masters[4],
        new_masters[5],
        copies[0],
        copies[1],
        copies[2],
        copies[3],
        copies[4],
        new_moments[0],
        new_moments[1],
        new_moments[2],
        new_moments[3],
        new_moments[4],
        new_moments[5],
        new_averages[0],
        new_averages[1],
        new_averages[2],
        new_averages[3],
        new_averages[4],
        new_averages[5],
    )


def solution(mesh):
    return jax.shard_map(
        on_device,
        mesh=mesh,
        in_specs=(
            P("dp", None),
            P("dp", None),
            P(("dp", "mp")),
            P(None, ("dp", "mp"), None),
            P(("dp", "mp"), None),
            P(("dp", "mp"), None, None),
            P(("dp", "mp"), None),
            P(("mp", "dp"), None),
            P(None, "dp", None),
            P(None, "dp", None),
            P(None, ("mp", "dp"), None),
            P(None, ("mp", "dp"), None),
            P("dp"),
            P(("mp", "dp"), None),
            P(None, "dp", None),
            P(None, "dp", None),
            P(None, ("mp", "dp"), None),
            P(None, ("mp", "dp"), None),
            P("dp"),
            P(("mp", "dp"), None),
            P(None, "dp", None),
            P(None, "dp", None),
            P(None, ("mp", "dp"), None),
            P(None, ("mp", "dp"), None),
            P("dp"),
        ),
        out_specs=(
            P(),
            P(),
            P(),
            P(("mp", "dp"), None),
            P(None, "dp", None),
            P(None, "dp", None),
            P(None, ("mp", "dp"), None),
            P(None, ("mp", "dp"), None),
            P("dp"),
            P(("mp", "dp"), None),
            P(None, "dp", None),
            P(None, "dp", None),
            P(None, ("mp", "dp"), None),
            P(None, ("mp", "dp"), None),
            P(("mp", "dp"), None),
            P(None, "dp", None),
            P(None, "dp", None),
            P(None, ("mp", "dp"), None),
            P(None, ("mp", "dp"), None),
            P("dp"),
            P(("mp", "dp"), None),
            P(None, "dp", None),
            P(None, "dp", None),
            P(None, ("mp", "dp"), None),
            P(None, ("mp", "dp"), None),
            P("dp"),
        ),
        check_vma=False,
    )
```

profile of v0, /device:TPU:0, one launch (start us, length us, event | category | flops | bytes accessed | tf_op | source)
XLA Modules:
  0.0 2375.0 jit_solution(4147110681546713516)
XLA Ops:
  20.6 365.2 %all-gather.29.cloned.1.call-done = bf16[8,1572,768]{2,1,0:T(8,128)(2,1)} async-done(((bf16[1,1572,768]{2,1,0:T(8,128)(2,1)}), bf16[8,1572,768]{2,1,0:T(8,128)(2,1)}) %all-gather.29.cloned.1.call-update) | async-done | bytes 19316752 | tf_op jit(solution)/shard_map/all_gather | solution.py:448
  385.8 21.9 reshape.1493
  407.7 17.6 gather_fusion
  431.5 32.6 %all_gather.70 = bf16[2,192,768]{2,1,0:T(8,128)(2,1)S(1)} all-gather(bf16[2,24,768]{2,1,0:T(8,128)(2,1)S(1)} %convert_element_type.588), channel_id=1, replica_groups=mesh['dp'=8,'mp'=4] {'dp'}, dimensions={1}, use_global_device_ids=true | all-gather | bytes 663552 | tf_op jit(solution)/shard_map/all_gather | solution.py:450
  465.0 14.9 all-reduce.21.cloned.1.call-done
  493.2 126.9 %all-gather.15.cloned.1.call-done = bf16[2,768,3072]{2,1,0:T(8,128)(2,1)} async-done(((bf16[2,96,3072]{2,1,0:T(8,128)(2,1)}), bf16[2,768,3072]{2,1,0:T(8,128)(2,1)}) %all-gather.15.cloned.1.call-update) | async-done | bytes 9437200 | tf_op jit(solution)/shard_map/all_gather | solution.py:449
  620.1 8.4 slice_bitcast_fusion.1
  628.5 30.7 %reduce-scatter.20.cloned.1.call-done = bf16[512,768]{1,0:T(8,128)(2,1)} async-done(((bf16[2048,768]{1,0:T(8,128)(2,1)}), bf16[512,768]{1,0:T(8,128)(2,1)}) %reduce-scatter.20.cloned.1.call-update) | async-done | bytes 786448 | tf_op jit(solution)/shard_map/reduce_scatter | solution.py:473
  670.8 7.8 fusion.260
  678.6 6.6 fusion.245
  699.5 32.0 %all_gather.74 = bf16[2,192,384]{2,1,0:T(8,128)(2,1)S(1)} all-gather(bf16[2,24,384]{2,1,0:T(8,128)(2,1)S(1)} %convert_element_type.609), channel_id=1, replica_groups=mesh['dp'=8,'mp'=4] {'dp'}, dimensions={1}, use_global_device_ids=true | all-gather | bytes 331776 | tf_op jit(solution)/shard_map/all_gather | solution.py:452
  734.5 13.0 all-gather.19.cloned.1.call-done
  758.3 13.2 all_gather.73
  780.5 19.0 multiply_convert_fusion.4
  810.3 37.9 %reduce-scatter.22.cloned.1.call-done = bf16[512,768]{1,0:T(8,128)(2,1)} async-done(((bf16[2048,768]{1,0:T(8,128)(2,1)}), bf16[512,768]{1,0:T(8,128)(2,1)}) %reduce-scatter.22.cloned.1.call-update) | async-done | bytes 786448 | tf_op jit(solution)/shard_map/reduce_scatter | solution.py:103
  861.6 7.9 fusion.261
  869.5 6.8 fusion.248
  898.4 13.1 all_gather.83
  911.5 4.9 multiply_convert_fusion.9
  917.9 5.3 all-gather.21.cloned.1.call-done
  923.2 19.4 multiply_convert_fusion.3
  951.7 5.9 all-reduce.9
  966.1 24.6 %reduce-scatter.26.cloned.1.call-done = bf16[512,768]{1,0:T(8,128)(2,1)} async-done(((bf16[2048,768]{1,0:T(8,128)(2,1)}), bf16[512,768]{1,0:T(8,128)(2,1)}) %reduce-scatter.26.cloned.1.call-update) | async-done | bytes 786448 | tf_op jit(solution)/shard_map/reduce_scatter | solution.py:103
  1001.0 5.8 all_gather.76
  1006.8 11.5 fusion.250
  1018.3 5.6 gather_fusion.4
  1027.9 5.0 all-gather.4
  1033.0 5.0 all-gather.5
  1038.6 5.0 all-gather.3
  1049.9 12.5 convolution_convert_fusion.23
  1068.8 13.6 reduce-scatter.30.cloned.1.call-done
  1095.6 8.7 all_gather.85
  1107.3 14.4 all-gather.23.cloned.1.call-done
  1121.8 11.2 convert_reduce_fusion
  1140.2 8.5 reduce-scatter.34.cloned.1.call-done
  1154.4 35.2 %reduce-scatter.32.cloned.1.call-done = bf16[512,768]{1,0:T(8,128)(2,1)} async-done(((bf16[2048,768]{1,0:T(8,128)(2,1)}), bf16[512,768]{1,0:T(8,128)(2,1)}) %reduce-scatter.32.cloned.1.call-update) | async-done | bytes 786448 | tf_op jit(solution)/shard_map/reduce_scatter | solution.py:103
  1196.9 6.7 fusion.262
  1203.6 6.9 fusion.253
  1210.5 9.4 multiply_reduce_fusion.1
  1219.9 6.9 multiply_convert_fusion.1
  1238.4 6.5 fusion.257
  1244.8 5.3 fusion.85
  1255.5 13.4 all_gather.87
  1272.8 11.2 convert_reduce_fusion.1
  1304.9 6.2 convolution_convert_fusion.12
  1338.7 7.7 fusion.259
  1357.7 6.4 fusion.263
  1364.1 15.1 multiply_reduce_fusion
  1379.3 6.9 multiply_convert_fusion
  1400.9 6.4 multiply_reduce_fusion.2
  1409.6 5.7 convolution_convert_fusion.14
  1422.2 12.6 copy.219
  1466.7 13.2 dynamic-update-slice.8
  1488.7 5.7 dynamic-update-slice.11
  1509.8 8.1 pad_maximum_fusion
  1525.8 30.3 %scatter_custom_fusion.3 = f32[12577,768]{1,0:T(8,128)} fusion(s32[2048]{0:T(1024)} %bitcast.475, f32[]{:T(128)} %constant.111.clone.1, bf16[2048,768]{1,0:T(8,128)(2,1)} %all-gather.27.cloned.1.call-done), kind=kCustom, calls=%fused_computation.29 | custom fusion | flops 3145728 | bytes 41782784 | tf_op jit(solution)/shard_map/scatter-add | solution.py:580
  1556.1 24.5 %fusion.8 = bf16[12576,768]{1,0:T(8,128)(2,1)} fusion(f32[12577,768]{1,0:T(8,128)} %scatter_custom_fusion.3, bf16[128,768]{1,0:T(8,128)(2,1)S(1)} %copy-done.96, f32[128,12576]{0,1:T(8,128)} %get-tuple-element.523, f32[128]{0:T(128)S(1)} %copy-done.269, s32[128]{0:T(128)S(1)} %copy-done.243, f32[128]{0:T(128)S(1)} %copy-done.245), kind=kOutput, calls=%fused_computation.28 | convolution fusion | flops 2501517312 | bytes 64587264 | tf_op jit(solution)/shard_map/dot_general | solution.py:79
  1580.6 132.6 %all-reduce.23.cloned.1.call-done = (bf16[2,768,1536]{2,0,1:T(2,128)(2,1)}, bf16[762240]{0:T(1024)(128)(2,1)}) async-done(((bf16[2,768,1536]{2,0,1:T(2,128)(2,1)}, bf16[762240]{0:T(1024)(128)(2,1)}), (bf16[2,768,1536]{2,0,1:T(2,128)(2,1)}, bf16[762240]{0:T(1024)(128)(2,1)})) %all-reduce.23.cloned.1.call-update) | async-done | bytes 6243088
  1714.9 164.2 %reduce-scatter.40.cloned.1.call-done = bf16[2,96,3072]{2,1,0:T(8,128)(2,1)} async-done(((bf16[2,768,3072]{2,1,0:T(8,128)(2,1)}), bf16[2,96,3072]{2,1,0:T(8,128)(2,1)}) %reduce-scatter.40.cloned.1.call-update) | async-done | bytes 1179664 | tf_op jit(solution)/shard_map/reduce_scatter | solution.py:611
  1879.2 379.4 %fusion = bf16[1576,768]{1,0:T(8,128)(2,1)S(1)} fusion(bf16[12576,768]{1,0:T(8,128)(2,1)} %fusion.8), kind=kCustom, calls=%all-reduce-scatter | all-reduce-scatter fusion | flops 9682945 | bytes 21737984
  2261.6 10.6 concatenate.68
  2286.1 46.3 %all-reduce.14 = (f32[]{:T(128)}, f32[]{:T(128)}, f32[]{:T(128)}) all-reduce(f32[]{:T(128)S(6)} %add.853, f32[]{:T(128)S(6)} %add.854, f32[]{:T(128)S(6)} %add.872), channel_id=1, replica_groups=mesh['dp'=8,'mp'=4] {'dp','mp'}, use_global_device_ids=true, to_apply=%region_36.38 | all-reduce | flops 3 | bytes 24 | tf_op jit(solution)/shard_map/psum | solution.py:645
  2346.7 8.0 add_multiply_fusion.1
  2356.2 5.6 add_multiply_fusion
  (1190 shorter events, 407.1 us)
Async XLA Ops:
  7.2 378.6 %all-gather.29.cloned.1.call-start = ((), (), s32[]{:S(2)}) async-start(), calls=%async_computation.32 | async-start | bytes 21786624 | tf_op jit(solution)/shard_map/all_gather | solution.py:448
  11.3 468.5 %all-reduce.21.cloned.1.call-start = ((), (), s32[]{:S(2)}) async-start(), calls=%async_computation.31 | async-start | bytes 3051520
  18.6 601.4 %all-gather.15.cloned.1.call-start = ((), (), s32[]{:S(2)}) async-start(), calls=%async_computation.14 | async-start | bytes 10616832 | tf_op jit(solution)/shard_map/all_gather | solution.py:449
  19.9 639.3 %reduce-scatter.20.cloned.1.call-start = ((), (), s32[]{:S(2)}) async-start(), calls=%async_computation.13 | async-start | bytes 3932160 | tf_op jit(solution)/shard_map/reduce_scatter | solution.py:473
  427.5 320.0 %all-gather.19.cloned.1.call-start = ((), (), s32[]{:S(2)}) async-start(), calls=%async_computation.16 | async-start | bytes 5308416 | tf_op jit(solution)/shard_map/all_gather | solution.py:451
  429.7 350.8 %all-gather.17.cloned.1.call-start = ((), (), s32[]{:S(2)}) async-start(), calls=%async_computation.15 | async-start | bytes 3932160 | tf_op jit(solution)/shard_map/all_gather | solution.py:96
  430.9 50.1 %copy-start.288 = (s32[1,512]{1,0:T(1,128)}, s32[1,512]{1,0:T(1,128)S(1)}, u32[]{:S(2)}) copy-start(s32[1,512]{1,0:T(1,128)S(1)} %get-tuple-element.417) | copy-start | bytes 6148
  430.9 51.1 %copy-start.286 = (s32[1,512]{1,0:T(1,128)}, s32[1,512]{1,0:T(1,128)S(1)}, u32[]{:S(2)}) copy-start(s32[1,512]{1,0:T(1,128)S(1)} %get-tuple-element.497) | copy-start | bytes 6148
  430.9 51.1 %copy-start.289 = (s32[1,512]{1,0:T(1,128)}, s32[1,512]{1,0:T(1,128)S(1)}, u32[]{:S(2)}) copy-start(s32[1,512]{1,0:T(1,128)S(1)} %get-tuple-element.495) | copy-start | bytes 6148
  489.1 267.5 %copy-start.27 = (f32[512,192]{0,1:T(8,128)}, f32[512,192]{0,1:T(8,128)S(1)}, u32[]{:S(2)}) copy-start(f32[512,192]{0,1:T(8,128)S(1)} %get-tuple-element.415) | copy-start | bytes 1179652
  489.1 139.4 %copy-start.165 = (f32[512]{0:T(512)}, f32[512]{0:T(512)S(1)}, u32[]{:S(2)}) copy-start(f32[512]{0:T(512)S(1)} %broadcast_multiply_fusion.4) | copy-start | bytes 6148
  489.2 139.3 %copy-start.201 = (f32[512]{0:T(512)}, f32[512]{0:T(512)S(1)}, u32[]{:S(2)}) copy-start(f32[512]{0:T(512)S(1)} %multiply_reduce_fusion.31) | copy-start | bytes 6148
  489.2 139.3 %copy-start.184 = (f32[512]{0:T(512)}, f32[512]{0:T(512)S(1)}, u32[]{:S(2)}) copy-start(f32[512]{0:T(512)S(1)} %fusion.177) | copy-start | bytes 6148
  489.9 138.6 %copy-start.224 = (f32[192]{0:T(256)}, f32[192]{0:T(256)S(1)}, u32[]{:S(2)}) copy-start(f32[192]{0:T(256)S(1)} %get-tuple-element.451) | copy-start | bytes 2308
  489.9 138.6 %copy-start.255 = (f32[192]{0:T(256)}, f32[192]{0:T(256)S(1)}, u32[]{:S(2)}) copy-start(f32[192]{0:T(256)S(1)} %get-tuple-element.452) | copy-start | bytes 2308
  493.2 355.0 %copy-start.145 = (f32[768]{0:T(1024)}, f32[768]{0:T(1024)S(1)}, u32[]{:S(2)}) copy-start(f32[768]{0:T(1024)S(1)} %get-tuple-element.466) | copy-start | bytes 9220
  493.2 166.0 %copy-start.41 = (f32[512,768]{1,0:T(8,128)S(1)}, f32[512,768]{1,0:T(8,128)}, u32[]{:S(2)}) copy-start(f32[512,768]{1,0:T(8,128)} %tile_reshape.4) | copy-start | bytes 4718596
  660.7 34.5 %copy-start.10 = (f32[512,768]{1,0:T(8,128)}, f32[512,768]{1,0:T(8,128)S(1)}, u32[]{:S(2)}) copy-start(f32[512,768]{1,0:T(8,128)S(1)} %get-tuple-element.425) | copy-start | bytes 4718596
  660.7 34.5 %copy-start.196 = (f32[512]{0:T(512)}, f32[512]{0:T(512)S(1)}, u32[]{:S(2)}) copy-start(f32[512]{0:T(512)S(1)} %broadcast_multiply_fusion.9) | copy-start | bytes 6148
  697.9 150.4 %copy-start.5 = (f32[512,768]{1,0:T(8,128)}, f32[512,768]{1,0:T(8,128)S(1)}, u32[]{:S(2)}) copy-start(f32[512,768]{1,0:T(8,128)S(1)} %get-tuple-element.512) | copy-start | bytes 4718596
  697.9 150.3 %copy-start.148 = (f32[512]{0:T(512)}, f32[512]{0:T(512)S(1)}, u32[]{:S(2)}) copy-start(f32[512]{0:T(512)S(1)} %broadcast_multiply_fusion.8) | copy-start | bytes 6148
  698.2 150.0 %copy-start.155 = (f32[512]{0:T(512)}, f32[512]{0:T(512)S(1)}, u32[]{:S(2)}) copy-start(f32[512]{0:T(512)S(1)} %fusion.178) | copy-start | bytes 6148
  699.5 107.7 %reduce-scatter.24.cloned.1.call-start = ((), (), s32[]{:S(2)}) async-start(), calls=%async_computation.18 | async-start | bytes 983040 | tf_op jit(solution)/shard_map/reduce_scatter | solution.py:106
  732.3 44.1 %copy-start.112 = (bf16[192,384]{1,0:T(8,128)(2,1)}, bf16[192,384]{1,0:T(8,128)(2,1)S(1)}, u32[]{:S(2)}) copy-start(bf16[192,384]{1,0:T(8,128)(2,1)S(1)} %get-tuple-element.489) | copy-start | bytes 442372
  733.7 46.8 %copy-start.315 = (f32[768]{0:T(1024)}, f32[768]{0:T(1024)S(1)}, u32[]{:S(2)}) copy-start(f32[768]{0:T(1024)S(1)} %dynamic_slice.45) | copy-start | bytes 9220
  758.0 49.1 %copy-start.15 = (f32[512,192]{0,1:T(8,128)}, f32[512,192]{0,1:T(8,128)S(1)}, u32[]{:S(2)}) copy-start(f32[512,192]{0,1:T(8,128)S(1)} %get-tuple-element.515) | copy-start | bytes 1179652
  758.0 49.1 %copy-start.150 = (f32[512]{0:T(512)}, f32[512]{0:T(512)S(1)}, u32[]{:S(2)}) copy-start(f32[512]{0:T(512)S(1)} %broadcast_multiply_fusion.3) | copy-start | bytes 6148
  758.1 49.0 %copy-start.159 = (f32[512]{0:T(512)}, f32[512]{0:T(512)S(1)}, u32[]{:S(2)}) copy-start(f32[512]{0:T(512)S(1)} %fusion.180) | copy-start | bytes 6148
  778.7 69.5 %reduce-scatter.22.cloned.1.call-start = ((), (), s32[]{:S(2)}) async-start(), calls=%async_computation.17 | async-start | bytes 3932160 | tf_op jit(solution)/shard_map/reduce_scatter | solution.py:103
  805.2 118.0 %all-gather.21.cloned.1.call-start = ((), (), s32[]{:S(2)}) async-start(), calls=%async_computation.19 | async-start | bytes 3932160 | tf_op jit(solution)/shard_map/all_gather | solution.py:96
  808.3 39.9 %copy-start.168 = (f32[512]{0:T(512)}, f32[512]{0:T(512)S(1)}, u32[]{:S(2)}) copy-start(f32[512]{0:T(512)S(1)} %broadcast_multiply_fusion.2) | copy-start | bytes 6148
  808.4 39.9 %copy-start.208 = (f32[512]{0:T(512)}, f32[512]{0:T(512)S(1)}, u32[]{:S(2)}) copy-start(f32[512]{0:T(512)S(1)} %multiply_reduce_fusion.29) | copy-start | bytes 6148
  808.4 39.8 %copy-start.187 = (f32[512]{0:T(512)}, f32[512]{0:T(512)S(1)}, u32[]{:S(2)}) copy-start(f32[512]{0:T(512)S(1)} %fusion.181) | copy-start | bytes 6148
  809.5 60.0 %copy-start.72 = (bf16[512,192]{0,1:T(8,128)(2,1)}, bf16[512,192]{0,1:T(8,128)(2,1)S(1)}, u32[]{:S(2)}) copy-start(bf16[512,192]{0,1:T(8,128)(2,1)S(1)} %slice.767) | copy-start | bytes 589828
  810.3 82.1 %copy-start.74 = (bf16[512,192]{0,1:T(8,128)(2,1)}, bf16[512,192]{0,1:T(8,128)(2,1)S(1)}, u32[]{:S(2)}) copy-start(bf16[512,192]{0,1:T(8,128)(2,1)S(1)} %get-tuple-element.476) | copy-start | bytes 589828
  850.0 36.1 %copy-start.12 = (f32[512,768]{1,0:T(8,128)}, f32[512,768]{1,0:T(8,128)S(1)}, u32[]{:S(2)}) copy-start(f32[512,768]{1,0:T(8,128)S(1)} %get-tuple-element.411) | copy-start | bytes 4718596
  850.0 36.1 %copy-start.198 = (f32[512]{0:T(512)}, f32[512]{0:T(512)S(1)}, u32[]{:S(2)}) copy-start(f32[512]{0:T(512)S(1)} %broadcast_multiply_fusion.7) | copy-start | bytes 6148
  850.3 35.7 %copy-start.276 = (f32[512]{0:T(512)}, f32[512]{0:T(512)S(1)}, u32[]{:S(2)}) copy-start(f32[512]{0:T(512)S(1)} %fusion.179) | copy-start | bytes 6148
  890.2 72.4 %reduce-scatter.28.cloned.1.call-start = ((), (), s32[]{:S(2)}) async-start(), calls=%async_computation.21 | async-start | bytes 983040 | tf_op jit(solution)/shard_map/reduce_scatter | solution.py:106
  917.8 72.9 %reduce-scatter.26.cloned.1.call-start = ((), (), s32[]{:S(2)}) async-start(), calls=%async_computation.20 | async-start | bytes 3932160 | tf_op jit(solution)/shard_map/reduce_scatter | solution.py:103
  948.2 134.1 %reduce-scatter.30.cloned.1.call-start = ((), (), s32[]{:S(2)}) async-start(), calls=%async_computation.22 | async-start | bytes 245760 | tf_op jit(solution)/shard_map/reduce_scatter | solution.py:552
  959.3 31.3 %copy-start.324 = (s32[32]{0:T(128)}, s32[32]{0:T(128)S(1)}, u32[]{:S(2)}) copy-start(s32[32]{0:T(128)S(1)} %get-tuple-element.505) | copy-start | bytes 388
  1062.4 59.3 %all-gather.23.cloned.1.call-start = ((), (), s32[]{:S(2)}) async-start(), calls=%async_computation.23 | async-start | bytes 3932160 | tf_op jit(solution)/shard_map/all_gather | solution.py:96
  1092.9 55.8 %reduce-scatter.34.cloned.1.call-start = ((), (), s32[]{:S(2)}) async-start(), calls=%async_computation.25 | async-start | bytes 983040 | tf_op jit(solution)/shard_map/reduce_scatter | solution.py:106
  1107.3 82.3 %reduce-scatter.32.cloned.1.call-start = ((), (), s32[]{:S(2)}) async-start(), calls=%async_computation.24 | async-start | bytes 3932160 | tf_op jit(solution)/shard_map/reduce_scatter | solution.py:103
  1138.6 51.0 %copy-start.8 = (f32[512,768]{1,0:T(8,128)S(1)}, f32[512,768]{1,0:T(8,128)}, u32[]{:S(2)}) copy-start(f32[512,768]{1,0:T(8,128)} %copy-done.7) | copy-start | bytes 4718596
  1138.6 51.0 %copy-start.158 = (f32[512]{0:T(512)S(1)}, f32[512]{0:T(512)}, u32[]{:S(2)}) copy-start(f32[512]{0:T(512)} %copy-done.157) | copy-start | bytes 6148
  1138.6 134.2 %all-gather.25.cloned.1.call-start = ((), (), s32[]{:S(2)}) async-start(), calls=%async_computation.26 | async-start | bytes 3932160 | tf_op jit(solution)/shard_map/all_gather | solution.py:96
  1152.5 39.8 %copy-start.213 = (f32[512]{0:T(512)S(1)}, f32[512]{0:T(512)}, u32[]{:S(2)}) copy-start(f32[512]{0:T(512)} %copy-done.212) | copy-start | bytes 6148
  1152.5 39.8 %copy-start.178 = (f32[512]{0:T(512)S(1)}, f32[512]{0:T(512)}, u32[]{:S(2)}) copy-start(f32[512]{0:T(512)} %copy-done.177) | copy-start | bytes 6148
  1193.2 122.2 %copy-start.279 = (f32[512]{0:T(512)}, f32[512]{0:T(512)S(1)}, u32[]{:S(2)}) copy-start(f32[512]{0:T(512)S(1)} %negate_multiply_fusion.12) | copy-start | bytes 6148
  1238.3 93.5 %reduce-scatter.38.cloned.1.call-start = ((), (), s32[]{:S(2)}) async-start(), calls=%async_computation.28 | async-start | bytes 983040 | tf_op jit(solution)/shard_map/reduce_scatter | solution.py:106
  1272.7 77.1 %reduce-scatter.36.cloned.1.call-start = ((), (), s32[]{:S(2)}) async-start(), calls=%async_computation.27 | async-start | bytes 3932160 | tf_op jit(solution)/shard_map/reduce_scatter | solution.py:103
  1289.7 233.7 %reduce-scatter.42.cloned.1.call-start = ((), (), s32[]{:S(2)}) async-start(), calls=%async_computation.33 | async-start | bytes 331776
  1330.2 194.0 %reduce-scatter.44.cloned.1.call-start = ((), (), s32[]{:S(2)}) async-start(), calls=%async_computation.34 | async-start | bytes 663552
  1400.8 125.0 %all-gather.27.cloned.1.call-start = ((), (), s32[]{:S(2)}) async-start(), calls=%async_computation.29 | async-start | bytes 3932160 | tf_op jit(solution)/shard_map/all_gather | solution.py:577
  1409.1 304.1 %all-reduce.23.cloned.1.call-start = ((), (), s32[]{:S(2)}) async-start(), calls=%async_computation.35 | async-start | bytes 12488704
  1494.5 384.7 %reduce-scatter.40.cloned.1.call-start = ((), (), s32[]{:S(2)}) async-start(), calls=%async_computation.30 | async-start | bytes 10616832 | tf_op jit(solution)/shard_map/reduce_scatter | solution.py:611
  1517.9 760.5 %all-reduce.25.cloned.1.call-start = ((), (), s32[]{:S(2)}) async-start(), calls=%async_computation.36 | async-start | bytes 2891776 | tf_op jit(solution)/shard_map/psum | solution.py:628
  2258.6 3.0 collective-permute-start
  2272.2 62.3 %copy-start.138 = (f32[2,24,384]{2,1,0:T(8,128)S(1)}, f32[2,24,384]{2,1,0:T(8,128)}, u32[]{:S(2)}) copy-start(f32[2,24,384]{2,1,0:T(8,128)} %param.40) | copy-start | bytes 221188
  2272.2 62.3 %copy-start.152 = (f32[2,24,384]{2,1,0:T(8,128)S(1)}, f32[2,24,384]{2,1,0:T(8,128)}, u32[]{:S(2)}) copy-start(f32[2,24,384]{2,1,0:T(8,128)} %param.52) | copy-start | bytes 221188
  2274.1 63.4 %copy-start.125 = (f32[2,24,768]{2,1,0:T(8,128)S(1)}, f32[2,24,768]{2,1,0:T(8,128)}, u32[]{:S(2)}) copy-start(f32[2,24,768]{2,1,0:T(8,128)} %param.38) | copy-start | bytes 442372
  2274.1 63.4 %copy-start.144 = (f32[2,24,768]{2,1,0:T(8,128)S(1)}, f32[2,24,768]{2,1,0:T(8,128)}, u32[]{:S(2)}) copy-start(f32[2,24,768]{2,1,0:T(8,128)} %param.50) | copy-start | bytes 442372
  (336 other events, 2064.1 us)
Sparse Core Ops, SparseCore 0:
  11.4 374.3 all-gather.28
  389.9 89.8 all-reduce.20
  482.6 137.4 all-gather.14
  623.1 36.0 reduce-scatter.19
  662.0 85.4 all-gather.18
  749.6 30.8 all-gather.16
  783.8 23.3 reduce-scatter.23
  810.2 37.9 reduce-scatter.21
  890.4 32.7 all-gather.20
  926.3 23.2 reduce-scatter.27
  952.7 37.9 reduce-scatter.25
  1062.5 19.7 reduce-scatter.29
  1093.0 28.6 all-gather.22
  1124.9 23.7 reduce-scatter.33
  1151.6 37.9 reduce-scatter.31
  1238.4 32.7 all-gather.24
  1274.3 23.2 reduce-scatter.37
  1300.6 37.9 reduce-scatter.35
  1342.8 58.6 reduce-scatter.41
  1405.6 61.1 reduce-scatter.43
  1468.9 27.5 all-gather.26
  1501.6 211.5 all-reduce.22
  1717.2 161.9 reduce-scatter.39
  1882.9 40.5 all-reduce.24
where the time goes:
time: 2390 us; the launch traced here: 2370 us
  waiting for transfers between devices  992 us (42%)
  blocking collectives  565 us (24%)
  matrix products  338 us (14%)
  local copies, waits for them, and re-layouts  239 us (10%)
  other arithmetic  204 us (9%)
  between operations  32.4 us (1%)
    unnamed x2, blocking collectives  385 us
    all_gather x1, waiting for transfers between devices, on_device(): lax.all_gather(table.astype(jnp.bfloat16), 'dp', axis=0, tiled=True)  365 us
    reduce_scatter x1, waiting for transfers between devices, on_device(): lax.psum_scatter(stacked(0).astype(jnp.bfloat16), 'dp', scatter_dimension...  164 us
    unnamed x29, waiting for transfers between devices  149 us
    all_gather x1, waiting for transfers between devices, on_device(): lax.all_gather(text_mats.astype(jnp.bfloat16), 'dp', axis=1, tiled=True)  127 us
    unnamed x781, local copies, waits for them, and re-layouts  117 us
    dot_general x17, matrix products, contract_cols(): lax.dot_general(left, right, (((1,), (1,)), ((), ())), preferred_element_...  104 us
    reduce_scatter x4, waiting for transfers between devices, lane_sum(): lax.psum_scatter(first.astype(jnp.bfloat16), 'mp', scatter_dimension=0, t...  97.7 us
  transfers between devices with their start and end apart: 25, of which 17 were waited for; matrix products, arithmetic and copies ran while one was open for 40% of the time, Pallas kernels for 0%

commit v1 on v0

v1 whole, which is shorter than its diff:
```python
import math

import jax
import jax.numpy as jnp
from jax import lax
from jax.experimental import pallas as pl
from jax.experimental.pallas import tpu as pltpu
from jax.sharding import PartitionSpec as P

WIDTH = 768
HEADS = 12
FFN_UNITS = 3072
LAYOUT_WIDTH = 192
LAYOUT_UNITS = 768
BOXES = 1024
PAGE_SLOTS = 512
PAIRS = 32
LAYERS = 2


EPSILON = 1e-05
CLIP_NORM = 0.01
LEARN_RATE = 10000.0
MOMENTUM = 0.5
AVERAGE_DECAY = 0.5
MASK_FILL = -1e30
PRECISE = lax.Precision.HIGHEST


def small_shapes():
    return [
        (LAYERS, 8, WIDTH),
        (LAYERS, 8, LAYOUT_WIDTH),
        (LAYERS, FFN_UNITS),
        (LAYERS, LAYOUT_UNITS),
        (2, WIDTH),
        (2, LAYOUT_WIDTH),
        (PAGE_SLOTS, WIDTH),
        (PAGE_SLOTS, LAYOUT_WIDTH),
        (2, BOXES, LAYOUT_WIDTH // 4),
        (LAYOUT_WIDTH, WIDTH),
    ]


def unpack_small(flat_vec):
    pieces = []
    offset = 0
    for piece_dims in small_shapes():
        amount = math.prod(piece_dims)
        pieces.append(flat_vec[offset : offset + amount].reshape(piece_dims))
        offset = offset + amount
    return pieces


def norm_apply(values, gain_row, bias_row):
    centre = values - jnp.mean(values, axis=-1, keepdims=True)
    spread = jnp.mean(centre * centre, axis=-1, keepdims=True)
    return centre * lax.rsqrt(spread + EPSILON) * gain_row + bias_row


def norm_back(values, gain_row, bias_row, grad_out):
    unused, pullback = jax.vjp(norm_apply, values, gain_row, bias_row)
    return pullback(grad_out)


def gelu_exact(values):
    return jax.nn.gelu(values, approximate=False)


def contract_rows(left, right):
    return lax.dot_general(
        left, right, (((0,), (0,)), ((), ())), preferred_element_type=jnp.float32
    )


def contract_cols(left, right):
    return lax.dot_general(
        left, right, (((1,), (1,)), ((), ())), preferred_element_type=jnp.float32
    )


def heads_view(values, pages):
    return values.reshape(pages, PAGE_SLOTS, HEADS, values.shape[-1] // HEADS)


ROUND_ROWS = 32


def bits_of(size):
    return list(reversed(range(size.bit_length() - 1)))


def hop(values, axis, bit):
    pairs = [(spot, spot ^ (1 << bit)) for spot in range(lax.axis_size(axis))]
    return lax.ppermute(values, axis, pairs)


def own_bit(axis, bit):
    return (lax.axis_index(axis) >> bit) & 1


def routes():
    far = [("dp", bit) for bit in bits_of(lax.axis_size("dp"))]
    high = [("mp", bit) for bit in bits_of(lax.axis_size("mp"))[:-1]]
    core = ("mp", 0)
    return (far[:-1], far[-1], high, core)


def add_low(kept, came):
    return (kept.astype(jnp.float32) + came.astype(jnp.float32)).astype(jnp.bfloat16)


def tie(value, *waits):
    def kernel(*refs):
        pass

    spec = pl.BlockSpec(memory_space=pl.ANY)
    return pl.pallas_call(
        kernel,
        out_shape=jax.ShapeDtypeStruct(value.shape, value.dtype),
        in_specs=[spec] * (1 + len(waits)),
        out_specs=spec,
        input_output_aliases={0: 0},
        cost_estimate=pl.CostEstimate(flops=0, bytes_accessed=0, transcendentals=0),
    )(value, *waits)


def put_in_order(own, came, places):
    slots, rows, width = own.shape

    def kernel(place_ref, own_ref, came_ref, out_ref):
        mine = place_ref[slots] == pl.program_id(0)

        @pl.when(mine)
        def _():
            out_ref[...] = own_ref[...]

        @pl.when(jnp.logical_not(mine))
        def _():
            out_ref[...] = came_ref[...]

    piece = pl.BlockSpec((1, rows, width), lambda half, spot, place: (place[spot], 0, 0))
    return pl.pallas_call(
        kernel,
        out_shape=jax.ShapeDtypeStruct((2, slots * rows, width), own.dtype),
        grid_spec=pltpu.PrefetchScalarGridSpec(
            num_scalar_prefetch=1,
            grid=(2, slots),
            in_specs=[piece, piece],
            out_specs=pl.BlockSpec((1, rows, width), lambda half, spot, place: (half, spot, 0)),
        ),
        cost_estimate=pl.CostEstimate(
            flops=0, bytes_accessed=12 * slots * rows * width, transcendentals=0
        ),
    )(places, own, came)


HEAD_PAIRS = HEADS // 2
TEXT_HEAD = WIDTH // HEADS
LAYOUT_HEAD = LAYOUT_WIDTH // HEADS


def pair_split(values):
    return values.reshape(PAGE_SLOTS, HEAD_PAIRS, 2 * LAYOUT_HEAD).transpose(1, 0, 2)


def pair_join(values):
    return values.transpose(1, 0, 2).reshape(PAGE_SLOTS, LAYOUT_WIDTH)


def head_of(text_ref, layout_ref, head, scaled=False):
    text = text_ref[:, head * TEXT_HEAD : (head + 1) * TEXT_HEAD]
    layout = layout_ref[0, :, head * LAYOUT_HEAD : (head + 1) * LAYOUT_HEAD]
    if scaled:
        text_scale, layout_scale = scale_pair()
        text = (text.astype(jnp.float32) * text_scale).astype(text.dtype)
        layout = (layout.astype(jnp.float32) * layout_scale).astype(layout.dtype)
    return jnp.concatenate([text, layout], 1)


def store_heads(text_ref, layout_ref, both):
    text_ref[...] = jnp.concatenate([item[:, :TEXT_HEAD] for item in both], 1).astype(
        text_ref.dtype
    )
    layout_ref[0] = jnp.concatenate([item[:, TEXT_HEAD:] for item in both], 1).astype(
        layout_ref.dtype
    )


def attend_kernel(length, qt, kt, vt, ql, kl, vl, out_t, out_l, lse):
    live = lax.broadcasted_iota(jnp.int32, (PAGE_SLOTS, PAGE_SLOTS), 1) < length[0]
    outs = []
    for head in range(2):
        query, keys = head_of(qt, ql, head, True), head_of(kt, kl, head)
        scores = jnp.where(live, contract_cols(query, keys), MASK_FILL)
        peak = jnp.max(scores, 1, keepdims=True)
        expo = jnp.exp(scores - peak)
        total = jnp.sum(expo, 1, keepdims=True)
        probs = (expo * (1.0 / total)).astype(jnp.bfloat16)
        outs.append(
            jnp.dot(probs, head_of(vt, vl, head), preferred_element_type=jnp.float32)
        )
        lse[0, :, head : head + 1] = peak + jnp.log(total)
    store_heads(out_t, out_l, outs)


def attend_back_kernel(length, qt, kt, vt, ql, kl, vl, got, gol, lse, *outs):
    dqt, dkt, dvt, dql, dkl, dvl = outs
    text_scale, layout_scale = scale_pair()
    live = lax.broadcasted_iota(jnp.int32, (PAGE_SLOTS, PAGE_SLOTS), 0) < length[0]
    column = lax.broadcasted_iota(jnp.int32, (1, TEXT_HEAD + LAYOUT_HEAD), 1)
    scales = jnp.where(column < TEXT_HEAD, text_scale, layout_scale)
    grads_q, grads_k, grads_v = [], [], []
    for head in range(2):
        query, keys = head_of(qt, ql, head, True), head_of(kt, kl, head)
        values, grad = head_of(vt, vl, head), head_of(got, gol, head)
        scores = jnp.where(live, contract_cols(keys, query), MASK_FILL)
        probs = jnp.exp(scores - lse[0, head : head + 1, :])
        grad_probs = contract_cols(values, grad)
        shift = jnp.sum(probs * grad_probs, 0, keepdims=True)
        grad_scores = (probs * (grad_probs - shift)).astype(jnp.bfloat16)
        grads_v.append(
            jnp.dot(probs.astype(jnp.bfloat16), grad, preferred_element_type=jnp.float32)
        )
        grads_k.append(jnp.dot(grad_scores, query, preferred_element_type=jnp.float32))
        grads_q.append(contract_rows(grad_scores, keys) * scales)
    store_heads(dqt, dql, grads_q)
    store_heads(dkt, dkl, grads_k)
    store_heads(dvt, dvl, grads_v)


def pair_specs():
    text = pl.BlockSpec((PAGE_SLOTS, 2 * TEXT_HEAD), lambda step: (0, step))
    layout = pl.BlockSpec((1, PAGE_SLOTS, 2 * LAYOUT_HEAD), lambda step: (step, 0, 0))
    return text, layout


def attend(text_qkv, layout_qkv, lengths):
    text, layout = pair_specs()
    low = jnp.bfloat16
    out_t, out_l, lse = pl.pallas_call(
        attend_kernel,
        grid=(HEAD_PAIRS,),
        in_specs=[pl.BlockSpec(memory_space=pltpu.SMEM)] + [text] * 3 + [layout] * 3,
        out_specs=[text, layout, pl.BlockSpec((1, PAGE_SLOTS, 2), lambda step: (step, 0, 0))],
        out_shape=[
            jax.ShapeDtypeStruct((PAGE_SLOTS, WIDTH), low),
            jax.ShapeDtypeStruct((HEAD_PAIRS, PAGE_SLOTS, 2 * LAYOUT_HEAD), low),
            jax.ShapeDtypeStruct((HEAD_PAIRS, PAGE_SLOTS, 2), jnp.float32),
        ],
        cost_estimate=pl.CostEstimate(
            flops=12000000000, bytes_accessed=8000000, transcendentals=3200000
        ),
        compiler_params=pltpu.CompilerParams(vmem_limit_bytes=24 * 1024 * 1024),
    )(lengths, *text_qkv, *[pair_split(item) for item in layout_qkv])
    return (out_t, pair_join(out_l), lse.transpose(0, 2, 1))


def attend_back(text_qkv, layout_qkv, lengths, lse, text_grad, layout_grad):
    text, layout = pair_specs()
    low = jnp.bfloat16
    text_out = jax.ShapeDtypeStruct((PAGE_SLOTS, WIDTH), low)
    layout_out = jax.ShapeDtypeStruct((HEAD_PAIRS, PAGE_SLOTS, 2 * LAYOUT_HEAD), low)
    outs = pl.pallas_call(
        attend_back_kernel,
        grid=(HEAD_PAIRS,),
        in_specs=[pl.BlockSpec(memory_space=pltpu.SMEM)]
        + [text] * 3
        + [layout] * 3
        + [text, layout, pl.BlockSpec((1, 2, PAGE_SLOTS), lambda step: (step, 0, 0))],
        out_specs=[text] * 3 + [layout] * 3,
        out_shape=[text_out] * 3 + [layout_out] * 3,
        cost_estimate=pl.CostEstimate(
            flops=20000000000, bytes_accessed=14000000, transcendentals=3200000
        ),
        compiler_params=pltpu.CompilerParams(vmem_limit_bytes=32 * 1024 * 1024),
    )(
        lengths,
        *text_qkv,
        *[pair_split(item) for item in layout_qkv],
        text_grad,
        pair_split(layout_grad),
        lse,
    )
    return (list(outs[:3]), [pair_join(item) for item in outs[3:]])


ERF_TERMS = (0.254829592, -0.284496736, 1.421413741, -1.453152027, 1.061405429)


def gelu_pair(values):
    size = jnp.abs(values)
    base = 1.0 / (1.0 + (0.3275911 / math.sqrt(2.0)) * size)
    series = ERF_TERMS[4]
    for term in reversed(ERF_TERMS[:4]):
        series = series * base + term
    bell = jnp.exp(values * values * -0.5)
    tail = 0.5 * series * base * bell
    share = jnp.where(values < 0.0, tail, 1.0 - tail)
    return (values * share, share + values * bell * (1.0 / math.sqrt(2.0 * math.pi)))


def ffn_kernel(rows_ref, in_ref, out_ref, bias_ref, hidden_ref, slope_ref, part_ref):
    width = rows_ref.shape[1]
    units_in, units_out = in_ref[...], out_ref[...]

    @pl.when(pl.program_id(0) == 0)
    def _():
        part_ref[...] = jnp.zeros_like(part_ref)

    step = PAGE_SLOTS // 2
    for number in range(2):
        rows = pl.ds(number * step, step)
        pre_act = contract_cols(rows_ref[rows, :], units_in) + bias_ref[...]
        hidden, slope = gelu_pair(pre_act)
        hidden = hidden.astype(jnp.bfloat16)
        hidden_ref[rows, :] = hidden
        slope_ref[rows, :] = slope.astype(jnp.bfloat16)
        part_ref[rows, :] += jnp.dot(hidden, units_out, preferred_element_type=jnp.float32)


def ffn_front(rows_in, units, bias_in, chunks):
    slots, width = rows_in.shape
    total = bias_in.shape[0]
    chunk = total // chunks
    whole = pl.BlockSpec((slots, width), lambda step: (0, 0))
    piece = pl.BlockSpec((slots, chunk), lambda step: (0, step))
    unit = pl.BlockSpec((chunk, width), lambda step: (step, 0))
    return pl.pallas_call(
        ffn_kernel,
        grid=(chunks,),
        in_specs=[whole, unit, unit, pl.BlockSpec((1, chunk), lambda step: (0, step))],
        out_specs=[piece, piece, whole],
        out_shape=[
            jax.ShapeDtypeStruct((slots, total), jnp.bfloat16),
            jax.ShapeDtypeStruct((slots, total), jnp.bfloat16),
            jax.ShapeDtypeStruct((slots, width), jnp.float32),
        ],
        cost_estimate=pl.CostEstimate(
            flops=4 * slots * width * total,
            bytes_accessed=4 * total * (width + slots),
            transcendentals=2 * slots * total,
        ),
        compiler_params=pltpu.CompilerParams(vmem_limit_bytes=40 * 1024 * 1024),
    )(rows_in, *units, bias_in[None])


def tail_route(flip):
    far, near, high, core = routes()
    return (high + [near] if flip else [near] + high) + [core]


def key_mask(key, axis):
    return sum(1 << bit for name, bit in key if name == axis)


class Spread:
    def __init__(self, block, joined, apart):
        self.joined, self.apart = list(joined), list(apart)
        self.masks = [frozenset()]
        self.pieces = {frozenset(): block[None]}

    def advance(self, wait=None):
        if self.joined:
            step = self.joined.pop(0)
            (held,) = self.pieces.values()
            came = hop(held if wait is None else tie(held, wait), *step)
            self.pieces = {frozenset(): jnp.concatenate([held, came], 0)}
            self.masks = self.masks + [mask | {step} for mask in self.masks]
            return came
        step = self.apart.pop(0)
        for key, piece in list(self.pieces.items()):
            came = hop(piece if wait is None else tie(piece, wait), *step)
            self.pieces[key | {step}] = came
        return came


def half_spread(own, near_first=False):
    far, near, high, core = routes()
    return Spread(own, [near] + far if near_first else far + [near], [core])


def half_result(chain):
    core = routes()[3]
    spot = lax.axis_index("dp")
    masks = [key_mask(mask, "dp") for mask in chain.masks]
    slot_of = {mask: number for number, mask in enumerate(masks)}
    table = jnp.array([slot_of[number] for number in range(len(masks))], jnp.int32)
    numbers = jnp.arange(len(masks))
    marks = (spot ^ numbers)[:, None] == numbers[None, :]
    places = jnp.sum(jnp.where(marks, table[None, :], 0), 1, dtype=jnp.int32)
    places = jnp.concatenate([places, own_bit(*core).astype(jnp.int32)[None]])
    own, came = chain.pieces[frozenset()], chain.pieces[frozenset([core])]
    return put_in_order(own, came, places)


def unit_spread(block, flip):
    return Spread(block, routes()[0], tail_route(flip))


def unit_keys():
    far, near, high, core = routes()
    keys = [frozenset()]
    for step in [near] + list(reversed(high)) + [core]:
        keys = keys + [key | {step} for key in keys]
    return keys


def unit_result(chain, rows):
    pieces = [chain.pieces[key] for key in unit_keys()]
    main = jnp.concatenate([piece[:, :rows] for piece in pieces], 0)
    extra = jnp.concatenate([piece[:, rows:] for piece in pieces], 0)
    return (main.reshape(-1, main.shape[-1]), extra)


def unit_blocks():
    far = [frozenset()]
    for step in routes()[0]:
        far = far + [mask | {step} for mask in far]
    masks = [key | mask for key in unit_keys() for mask in far]
    spots = jnp.array([key_mask(mask, "dp") for mask in masks], jnp.int32)
    lanes = jnp.array([key_mask(mask, "mp") for mask in masks], jnp.int32)
    lanes, spots = lanes ^ lax.axis_index("mp"), spots ^ lax.axis_index("dp")
    return lanes * lax.axis_size("dp") + spots


class UnitSum:
    def __init__(self, kept, sent, flip):
        far, near, high, core = routes()
        self.order = high + [near]
        self.left = list(reversed(tail_route(flip)[:-1])) + list(reversed(far))
        shape = (2,) * len(self.order) + (lax.axis_size("dp") // 2,) + kept.shape[1:]
        self.kept, self.came = kept.reshape(shape), hop(sent, *core).reshape(shape)

    def half(self, values, side, where):
        if where is not None:
            return lax.index_in_dim(values, side, where, keepdims=False)
        size = values.shape[0] // 2
        return values[side * size : (side + 1) * size]

    def advance(self):
        step = self.left.pop(0)
        where = self.order.index(step) if step in self.order else None
        if where is not None:
            self.order.remove(step)
        sent, kept = [
            add_low(self.half(self.kept, side, where), self.half(self.came, side, where))
            for side in (1, 0)
        ]
        self.kept, self.came = kept, hop(sent, *step)
        return self.came

    def finish(self):
        while self.left:
            self.advance()
        return (self.kept.astype(jnp.float32) + self.came.astype(jnp.float32))[0]


def to_rows(values):
    flat = values.reshape(values.shape[0], -1)
    flat = jnp.pad(flat, ((0, 0), (0, -flat.shape[1] % WIDTH)))
    return flat.reshape(values.shape[0], -1, WIDTH)


def from_rows(values, rows):
    flat = values.reshape(values.shape[0], -1)[:, : rows * LAYOUT_WIDTH]
    return flat.reshape(-1, LAYOUT_WIDTH)


class HalfSum:
    def __init__(self, halves):
        far, near, high, core = routes()
        self.order = far + [near]
        self.left = [near] + list(reversed(far))
        first = own_bit(*core) == 0
        shape = (2,) * len(self.order) + halves[0].shape[1:]
        sent = jnp.where(first, halves[1], halves[0]).reshape(shape)
        self.kept = jnp.where(first, halves[0], halves[1]).reshape(shape)
        self.came = hop(sent, *core)

    def advance(self):
        step = self.left.pop(0)
        where = self.order.index(step)
        self.order.remove(step)
        mine = own_bit(*step)

        def side(values, number):
            return lax.dynamic_index_in_dim(values, number, where, keepdims=False)

        sent = add_low(side(self.kept, 1 - mine), side(self.came, 1 - mine))
        kept = add_low(side(self.kept, mine), side(self.came, mine))
        self.kept, self.came = kept, hop(sent, *step)
        return self.came

    def finish(self):
        while self.left:
            self.advance()
        far, near, high, core = routes()
        held = add_low(self.kept, self.came)
        for step in high:
            held = add_low(held, hop(held, *step))
        other = hop(held, *core)
        first = own_bit(*core) == 0
        return jnp.stack([jnp.where(first, held, other), jnp.where(first, other, held)]).astype(
            jnp.float32
        )


def own_half(values):
    half = values.shape[-1] // 2
    return jnp.where(own_bit("mp", 0) == 0, values[..., :half], values[..., half:])


def sum_everywhere(values):
    far, near, high, core = routes()
    for step in [core] + high + [near] + far:
        values = values + hop(values, *step)
    return values


def show_all(values):
    everywhere = ("dp", "mp")
    count = lax.axis_size("dp") * lax.axis_size("mp")
    return lax.all_to_all(
        jnp.broadcast_to(values[None], (count,) + values.shape), everywhere, 0, 0, tiled=True
    )


def trade(values):
    return lax.all_to_all(values, ("dp", "mp"), 0, 0, tiled=True)


def project_qkv(rows_low, mats, vectors, width):
    joined = jnp.dot(rows_low, mats[0], preferred_element_type=jnp.float32)
    query = (joined[:, :width] + vectors[0]).astype(jnp.bfloat16)
    keys = joined[:, width:].astype(jnp.bfloat16)
    values = jnp.dot(rows_low, mats[1][:, :width], preferred_element_type=jnp.float32)
    return (query, keys, (values + vectors[1]).astype(jnp.bfloat16))


def scale_pair():
    return (1.0 / math.sqrt(WIDTH // HEADS), 1.0 / math.sqrt(LAYOUT_WIDTH // HEADS))


def project_back(rows_low, mats, grads, width):
    first = jnp.concatenate(grads[:2], 1)
    rows_grad = contract_cols(first, mats[0]) + contract_cols(grads[2], mats[1][:, :width])
    return (
        rows_grad,
        contract_rows(rows_low, first).astype(jnp.bfloat16),
        contract_rows(rows_low, grads[2]).astype(jnp.bfloat16),
        jnp.sum(grads[0], 0, dtype=jnp.float32),
        jnp.sum(grads[2], 0, dtype=jnp.float32),
    )


def ffn_back_kernel(
    rows_ref, grad_ref, in_ref, out_ref, hidden_ref, slope_ref, part_ref, bias_ref, *sums
):
    step, last = pl.program_id(0), pl.num_programs(0) // 2
    rows, grad = rows_ref[...], grad_ref[...]
    grad_hidden = contract_cols(grad, out_ref[...])
    grad_pre = grad_hidden * slope_ref[...].astype(jnp.float32)
    grad_low = grad_pre.astype(jnp.bfloat16)
    bias_ref[...] = jnp.sum(grad_low.astype(jnp.float32), 0, keepdims=True)

    @pl.when(step == 0)
    def _():
        part_ref[...] = jnp.zeros_like(part_ref)

    part_ref[...] += jnp.dot(grad_low, in_ref[...], preferred_element_type=jnp.float32)
    results = [contract_rows(grad_low, rows), contract_rows(hidden_ref[...], grad)]

    def store(targets):
        for target, result in zip(targets, results):
            if len(target.shape) == 2:
                target[...] = result.astype(target.dtype)
            else:
                blocks = result.astype(target.dtype).reshape(target.shape[0], -1, rows.shape[1])
                target[:, : blocks.shape[1], :] = blocks

    @pl.when(step < last)
    def _():
        store(sums[:2])

    @pl.when(step >= last)
    def _():
        store(sums[2:])


def ffn_back(rows_in, units, slope, hidden, grad_rows, chunks, slot_rows):
    slots, width = rows_in.shape
    total = hidden.shape[1]
    chunk, half = total // chunks, chunks // 2
    whole = pl.BlockSpec((slots, width), lambda step: (0, 0))
    piece = pl.BlockSpec((slots, chunk), lambda step: (0, step))
    unit = pl.BlockSpec((chunk, width), lambda step: (step, 0))

    def first(step):
        return jnp.minimum(step, half - 1)

    def second(step):
        return jnp.maximum(step - half, 0)

    if slot_rows is None:
        shape = (total // 2, width)
        sum_specs = [
            pl.BlockSpec((chunk, width), lambda step, turn=turn: (turn(step), 0))
            for turn in (first, first, second, second)
        ]
    else:
        rows, padded = slot_rows
        shape = (total // (2 * rows), padded, width)
        sum_specs = [
            pl.BlockSpec((chunk // rows, padded, width), lambda step, turn=turn: (turn(step), 0, 0))
            for turn in (first, first, second, second)
        ]
    return pl.pallas_call(
        ffn_back_kernel,
        grid=(chunks,),
        in_specs=[whole, whole, unit, unit, piece, piece],
        out_specs=[whole, pl.BlockSpec((1, chunk), lambda step: (0, step))] + sum_specs,
        out_shape=[
            jax.ShapeDtypeStruct((slots, width), jnp.float32),
            jax.ShapeDtypeStruct((1, total), jnp.float32),
        ]
        + [jax.ShapeDtypeStruct(shape, jnp.bfloat16)] * 4,
        cost_estimate=pl.CostEstimate(
            flops=8 * slots * width * total,
            bytes_accessed=8 * total * (width + slots),
            transcendentals=0,
        ),
        compiler_params=pltpu.CompilerParams(vmem_limit_bytes=48 * 1024 * 1024),
    )(rows_in, grad_rows, *units, hidden, slope)


def stream_forward(rows, att, mats, units, bias_in, vec):
    width = rows.shape[1]
    first = (
        rows + jnp.dot(att, mats[1][:, width:], preferred_element_type=jnp.float32) + vec[2]
    )
    mid = norm_apply(first, vec[3], vec[4])
    mid_low = mid.astype(jnp.bfloat16)
    hidden, slope, part = ffn_front(mid_low, units, bias_in, 4 if width == WIDTH else 1)
    last = mid + part + vec[5]
    return (norm_apply(last, vec[6], vec[7]), (first, mid_low, slope, hidden, last))


def layer_forward(text, layout, weights, lengths):
    (tm, lm, tu, lu, tb, lb, tv, lv) = weights[:8]
    text_low = text.astype(jnp.bfloat16)
    layout_low = layout.astype(jnp.bfloat16)
    text_qkv = project_qkv(text_low, tm, tv, WIDTH)
    layout_qkv = project_qkv(layout_low, lm, lv, LAYOUT_WIDTH)
    text_att, layout_att, log_total = attend(text_qkv, layout_qkv, lengths)
    text_new, text_kept = stream_forward(text, text_att, tm, tu, tb, tv)
    layout_new, layout_kept = stream_forward(layout, layout_att, lm, lu, lb, lv)
    cache = (
        text_low,
        layout_low,
        text_qkv,
        layout_qkv,
        log_total,
        text_att,
        layout_att,
        text_kept,
        layout_kept,
    )
    return (text_new, layout_new, cache)


def stream_back(kept, att, mats, units, vec, grad, slot_rows):
    first, mid_low, slope, hidden, last = kept
    width = first.shape[1]
    last_g, gain2, bias2 = norm_back(last, vec[6], vec[7], grad)
    in_grad, bias_in_g, *unit_grads = ffn_back(
        mid_low,
        units,
        slope,
        hidden,
        last_g.astype(jnp.bfloat16),
        4 if width == WIDTH else 2,
        slot_rows,
    )
    first_g, gain1, bias1 = norm_back(first, vec[3], vec[4], last_g + in_grad)
    first_low = first_g.astype(jnp.bfloat16)
    out_proj = contract_rows(att, first_low).astype(jnp.bfloat16)
    att_grad = contract_cols(first_low, mats[1][:, width:]).astype(jnp.bfloat16)
    vec_tail = [jnp.sum(first_g, 0), gain1, bias1, jnp.sum(last_g, 0), gain2, bias2]
    return (first_g, att_grad, out_proj, unit_grads, bias_in_g[0], vec_tail)


def layer_backward(cache, grad_text, grad_layout, weights, lengths, plan):
    (
        text_low,
        layout_low,
        text_qkv,
        layout_qkv,
        log_total,
        text_att,
        layout_att,
        text_kept,
        layout_kept,
    ) = cache
    (tm, lm, tu, lu, tb, lb, tv, lv) = weights
    count = lax.axis_size("dp") * lax.axis_size("mp")
    rows = FFN_UNITS // count
    layout_rows = -(-(LAYOUT_UNITS // count * LAYOUT_WIDTH) // WIDTH)
    padded = -(-(rows + layout_rows) // 8) * 8
    first_l, att_l, out_l, lu_g, lb_g, tail_l = stream_back(
        layout_kept, layout_att, lm, lu, lv, grad_layout, None
    )
    first_t, att_t, out_t, tu_g, tb_g, tail_t = stream_back(
        text_kept, text_att, tm, tu, tv, grad_text, (rows, padded)
    )
    joined = []
    for text_g, layout_g in zip(tu_g, lu_g):
        extra = jnp.pad(
            to_rows(layout_g.reshape(count // 2, -1, LAYOUT_WIDTH)),
            ((0, 0), (0, padded - rows - layout_rows), (0, 0)),
        )
        joined.append(lax.dynamic_update_slice(text_g, extra, (0, rows, 0)))
    att_t = plan.after_units(att_t, joined)
    text_dqkv, layout_dqkv = attend_back(
        text_qkv, layout_qkv, lengths, log_total, att_t, att_l
    )
    text_dqkv[0] = plan.after_attend(text_dqkv[0])
    rows_t, qk_t, v_t, q_bias_t, v_bias_t = project_back(text_low, tm, text_dqkv, WIDTH)
    rows_l, qk_l, v_l, q_bias_l, v_bias_l = project_back(
        layout_low, lm, layout_dqkv, LAYOUT_WIDTH
    )
    grads = (
        tb_g,
        lb_g,
        jnp.stack([q_bias_t, v_bias_t] + tail_t),
        jnp.stack([q_bias_l, v_bias_l] + tail_l),
    )
    plan.after_mats(
        (qk_t, jnp.concatenate([v_t, out_t], 1)), (qk_l, jnp.concatenate([v_l, out_l], 1))
    )
    return (first_t + rows_t, first_l + rows_l, grads)


class Plan:
    def __init__(self):
        self.units = []
        self.mats = []

    def step(self, value, items):
        return tie(value, *[item.advance() for item in items]) if items else value

    def after_units(self, value, grads):
        keep_in, keep_out, send_in, send_out = grads
        self.units.append([UnitSum(keep_in, send_in, False), UnitSum(keep_out, send_out, True)])
        if self.mats:
            return self.step(value, self.units[0] + self.mats[0][:1])
        return tie(value, *[item.came for item in self.units[0]])

    def after_attend(self, value):
        if self.mats:
            return self.step(value, self.units[0] + self.mats[0][:1] + self.units[1])
        return value

    def after_mats(self, text_halves, layout_halves):
        dp = lax.axis_size("dp")

        def blocks(halves):
            return [item.reshape(dp, -1, item.shape[-1]) for item in halves]

        self.mats.append([HalfSum(blocks(text_halves)), HalfSum(blocks(layout_halves))])

    def between(self, value):
        return self.step(value, self.units[0])


def split_high(values):
    high = values.astype(jnp.bfloat16)
    return (high, (values - high.astype(jnp.float32)).astype(jnp.bfloat16))


def add_rows(marks, values):
    high, low = split_high(values)
    return contract_rows(marks, high) + contract_rows(marks, low)


def apply_update(master, grad, moment, average, loss_count, factor):
    clipped = grad / loss_count * factor
    moment_new = MOMENTUM * moment + clipped
    master_new = master - LEARN_RATE * (clipped + MOMENTUM * moment_new)
    return (master_new, moment_new, AVERAGE_DECAY * average + (1.0 - AVERAGE_DECAY) * master_new)


def on_device(
    token_ids,
    mlm_targets,
    page_lengths,
    box_coords,
    mlm_positions,
    align_pairs,
    align_labels,
    table,
    text_mats,
    layout_mats,
    text_ffn,
    layout_ffn,
    small_params,
    table_momentum,
    text_mats_momentum,
    layout_mats_momentum,
    text_ffn_momentum,
    layout_ffn_momentum,
    small_momentum,
    table_average,
    text_mats_average,
    layout_mats_average,
    text_ffn_average,
    layout_ffn_average,
    small_average,
):
    lane, spot = lax.axis_index("mp"), lax.axis_index("dp")
    dp, mp = lax.axis_size("dp"), lax.axis_size("mp")
    count = dp * mp
    slots = PAGE_SLOTS
    mask_slots = mlm_positions.shape[1]
    pages = 1
    vocab_rows = table.shape[0]
    low = jnp.bfloat16

    own_ids = lax.dynamic_index_in_dim(token_ids, lane, 0, keepdims=False)
    own_targets = lax.dynamic_index_in_dim(mlm_targets, lane, 0, keepdims=False)
    shown = show_all(
        jnp.concatenate([own_ids, own_targets, jnp.broadcast_to(page_lengths, (mask_slots,))])
    )
    all_ids = shown[:, :slots]
    all_targets = shown[:, slots : slots + mask_slots].reshape(-1)
    all_lengths = shown[:, slots + mask_slots]
    table_low = table.astype(low)
    share = small_params.shape[0]
    line = 2 * WIDTH
    layout_rows = layout_mats.shape[1] * LAYOUT_WIDTH * 2 * LAYERS // line
    small_rows = -(-share // (16 * line)) * 8
    pad_rows = -(layout_rows + small_rows) % 16
    small_pad = jnp.pad(small_params.astype(low), (0, 2 * small_rows * line - share))
    small_half = lax.dynamic_slice_in_dim(
        small_pad, (lane & 1) * small_rows * line, small_rows * line
    ).reshape(small_rows, line)
    tmats_half = own_half(text_mats.astype(low))
    extra = jnp.concatenate(
        [
            small_half,
            own_half(layout_mats.astype(low)).reshape(layout_rows, line),
            jnp.zeros((pad_rows, line), low),
        ],
        0,
    )
    unit_rows = text_ffn.shape[1]
    layout_units = layout_ffn.shape[1]
    layout_unit_rows = -(-(layout_units * LAYOUT_WIDTH) // WIDTH)
    unit_pad = -(unit_rows + layout_unit_rows) % 8

    def unit_block(layer_no, part):
        return jnp.concatenate(
            [
                text_ffn[layer_no, :, part * WIDTH : (part + 1) * WIDTH].astype(low),
                to_rows(
                    layout_ffn[
                        layer_no : layer_no + 1, :, part * LAYOUT_WIDTH : (part + 1) * LAYOUT_WIDTH
                    ].astype(low)
                )[0],
                jnp.zeros((unit_pad, WIDTH), low),
            ],
            0,
        )

    mats_chains = [half_spread(tmats_half[layer_no]) for layer_no in range(LAYERS)]
    extra_chain = half_spread(extra, True)
    unit_chains = [
        [unit_spread(unit_block(layer_no, part), part == 1) for part in range(2)]
        for layer_no in range(LAYERS)
    ]
    far_steps = len(routes()[0])
    extra_chain.advance()
    wait = None
    for number in range(far_steps):
        wait = mats_chains[0].advance(wait)
    for number in range(far_steps):
        wait = extra_chain.advance(wait)
    for layer_no in range(LAYERS):
        if layer_no:
            for number in range(far_steps):
                wait = mats_chains[layer_no].advance(wait)
        for number in range(far_steps):
            waits = [chain.advance(wait) for chain in unit_chains[layer_no]]
            wait = waits[1]
    while extra_chain.apart:
        extra_chain.advance()
    for layer_no in range(LAYERS):
        for chain in [mats_chains[layer_no]] + unit_chains[layer_no]:
            while chain.joined or chain.apart:
                chain.advance()
    tmats_all = [half_result(chain) for chain in mats_chains]
    extra_all = half_result(extra_chain).reshape(2, dp, extra.shape[0], line)
    small_all = (
        extra_all[:, :, :small_rows]
        .transpose(1, 0, 2, 3)
        .reshape(dp, 2 * small_rows * line)[:, :share]
        .reshape(-1)
    )
    lmats_all = extra_all[:, :, small_rows : small_rows + layout_rows].reshape(
        2, dp, LAYERS, -1, 2 * LAYOUT_WIDTH
    )
    (
        text_vec,
        layout_vec,
        text_bias,
        layout_bias,
        text_emb,
        layout_emb,
        text_pos,
        layout_pos,
        box_table,
        align_mat,
    ) = unpack_small(small_all.astype(jnp.float32))

    own_block = lane * dp + spot
    steps = jnp.arange(slots)
    earlier = steps[None, :] < steps[:, None]
    all_first = ~jnp.any((all_ids[:, :, None] == all_ids[:, None, :]) & earlier[None], -1)
    all_blocks = all_ids // vocab_rows
    counts = jnp.sum(
        (all_blocks[:, None, :] == jnp.arange(count)[None, :, None]) & all_first[:, None, :],
        -1,
        dtype=jnp.int32,
    )
    rounds = (jnp.max(counts) + ROUND_ROWS - 1) // ROUND_ROWS
    mine = all_first & (all_blocks == own_block)
    order = contract_cols(mine.astype(low), earlier.astype(low)).astype(jnp.int32)
    local = all_ids - own_block * vocab_rows
    page_first = lax.dynamic_index_in_dim(all_first, spot * mp + lane, 0, keepdims=False)
    same = own_ids[:, None] == own_ids[None, :]
    first_at = jnp.min(jnp.where(same, steps[None, :], slots), 1)
    block_own = own_ids // vocab_rows
    rank = jnp.sum(
        page_first[None, :]
        & (block_own[:, None] == block_own[None, :])
        & (steps[None, :] < first_at[:, None]),
        1,
        dtype=jnp.int32,
    )
    source = (block_own % dp) * mp + block_own // dp

    def asked_marks(turn):
        turn_rank = order - turn * ROUND_ROWS
        chosen = mine[:, None, :] & (turn_rank[:, None, :] == jnp.arange(ROUND_ROWS)[None, :, None])
        rows = jnp.sum(jnp.where(chosen, local[:, None, :] + 1, 0), -1).reshape(-1) - 1
        return (rows[:, None] == jnp.arange(vocab_rows)[None, :]).astype(low)

    def held_marks(turn):
        turn_rank = rank - turn * ROUND_ROWS
        inside = (turn_rank >= 0) & (turn_rank < ROUND_ROWS)
        place = jnp.where(inside, source * ROUND_ROWS + turn_rank, -1)
        return (place[:, None] == jnp.arange(count * ROUND_ROWS)[None, :]).astype(low)

    def fetch(turn, so_far):
        rows = jnp.dot(asked_marks(turn), table_low, preferred_element_type=jnp.float32)
        came = trade(rows.astype(low))
        return so_far + jnp.dot(held_marks(turn), came, preferred_element_type=jnp.float32)

    embedded = lax.fori_loop(
        1, rounds, fetch, fetch(0, jnp.zeros((slots, WIDTH), jnp.float32))
    )

    def text_embed_fn(embed_vals, pos_table, emb_rows):
        return norm_apply(embed_vals + pos_table, emb_rows[0], emb_rows[1])

    box_marks = [
        (box_coords[number, 0][:, None] == jnp.arange(BOXES)[None, :]).astype(low)
        for number in range(4)
    ]
    box_low = box_table.astype(low)
    looked = jnp.concatenate(
        [
            jnp.dot(box_marks[number], box_low[number % 2], preferred_element_type=jnp.float32)
            for number in range(4)
        ],
        1,
    )

    text, text_pull = jax.vjp(text_embed_fn, embedded, text_pos, text_emb)
    layout, layout_pull = jax.vjp(text_embed_fn, looked, layout_pos, layout_emb)
    caches = []
    layer_weights = []
    slot_marks = (unit_blocks()[:, None] == jnp.arange(count)[None, :]).astype(jnp.float32)
    for layer_no in range(LAYERS):
        results = [unit_result(chain, unit_rows) for chain in unit_chains[layer_no]]
        weights = (
            tmats_all[layer_no],
            lmats_all[:, :, layer_no].reshape(2, LAYOUT_WIDTH, -1),
            [item[0] for item in results],
            [
                from_rows(item[1][:, :layout_unit_rows], layout_units)
                for item in results
            ],
            jnp.dot(
                slot_marks, text_bias[layer_no].reshape(count, -1), precision=PRECISE
            ).reshape(-1),
            jnp.dot(
                slot_marks, layout_bias[layer_no].reshape(count, -1), precision=PRECISE
            ).reshape(-1),
            text_vec[layer_no],
            layout_vec[layer_no],
        )
        text, layout, cache = layer_forward(text, layout, weights, page_lengths)
        caches.append(cache)
        layer_weights.append(weights)

    row_index = mlm_positions.reshape(-1)
    live_all = (
        (jnp.arange(mask_slots)[None, :] * slots < mask_slots * all_lengths[:, None])
        .astype(jnp.float32)
        .reshape(-1)
    )
    chosen_marks = (row_index[:, None] == steps[None, :]).astype(low)
    chosen_own = jnp.dot(
        chosen_marks, text.astype(low), preferred_element_type=jnp.float32
    ).astype(low)
    chosen_all = show_all(chosen_own).reshape(count * mask_slots, WIDTH)
    logits = contract_cols(chosen_all, table_low)
    target_local = all_targets - own_block * vocab_rows
    target_in = target_local[:, None] == jnp.arange(vocab_rows)[None, :]
    target_logit = jnp.sum(jnp.where(target_in, logits, 0.0), 1)
    row_peak = jnp.max(logits, axis=1)
    row_total = jnp.sum(jnp.exp(logits - row_peak[:, None]), axis=1)
    stats = show_all(jnp.stack([row_peak, row_total, target_logit]))
    all_peak = jnp.max(stats[:, 0], 0)
    all_total = jnp.sum(stats[:, 1] * jnp.exp(stats[:, 0] - all_peak[None]), 0)
    all_target = jnp.sum(stats[:, 2], 0)
    log_total = all_peak + jnp.log(all_total)
    own_start = (spot * mp + lane) * mask_slots
    live_own = lax.dynamic_slice_in_dim(live_all, own_start, mask_slots)
    own_loss = jnp.sum(
        lax.dynamic_slice_in_dim((log_total - all_target) * live_all, own_start, mask_slots)
    )
    grad_low = (
        (jnp.exp(logits - log_total[:, None]) - target_in.astype(jnp.float32)) * live_all[:, None]
    ).astype(low)
    table_grad = contract_rows(grad_low, chosen_all)
    chosen_parts = trade(jnp.dot(grad_low, table_low, preferred_element_type=jnp.float32).astype(low))
    chosen_grad = jnp.sum(
        chosen_parts.reshape(count, mask_slots, WIDTH).astype(jnp.float32), 0
    )

    first_marks = (align_pairs[0, :, 0][:, None] == steps[None, :]).astype(jnp.float32)
    second_marks = (align_pairs[0, :, 1][:, None] == steps[None, :]).astype(jnp.float32)
    answer = align_labels.reshape(-1).astype(jnp.float32)
    first_rows = jnp.dot(first_marks, text, precision=PRECISE)
    second_rows = jnp.dot(second_marks, layout, precision=PRECISE)

    def pair_loss(text_rows, layout_rows, align_weight):
        right = jnp.dot(layout_rows, align_weight, precision=PRECISE)
        logit = jnp.sum(text_rows * right, axis=-1) / math.sqrt(WIDTH)
        return jnp.sum(jax.nn.softplus(logit) - answer * logit)

    align_part, align_pull = jax.vjp(pair_loss, first_rows, second_rows, align_mat)
    first_back, second_back, align_grad = align_pull(jnp.ones((), jnp.float32))
    grad_text = add_rows(
        jnp.concatenate([first_marks.astype(low), chosen_marks], 0),
        jnp.concatenate([first_back, chosen_grad], 0),
    )
    grad_layout = add_rows(second_marks.astype(low), second_back)

    plan = Plan()
    layer_grads = [None] * LAYERS
    for layer_no in reversed(range(LAYERS)):
        grad_text, grad_layout, layer_grads[layer_no] = layer_backward(
            caches[layer_no], grad_text, grad_layout, layer_weights[layer_no], page_lengths, plan
        )
        if layer_no:
            grad_text = plan.between(grad_text)

    embed_grad, text_pos_grad, text_emb_grad = text_pull(grad_text)
    looked_grad, layout_pos_grad, layout_emb_grad = layout_pull(grad_layout)
    quarter = LAYOUT_WIDTH // 4
    box_parts = [
        add_rows(box_marks[number], looked_grad[:, number * quarter : (number + 1) * quarter])
        for number in range(4)
    ]
    box_grad = jnp.stack([box_parts[0] + box_parts[2], box_parts[1] + box_parts[3]])
    embed_low = embed_grad.astype(low)

    def give(turn, so_far):
        came = trade(contract_rows(held_marks(turn), embed_low).astype(low))
        return so_far + contract_rows(asked_marks(turn), came)

    table_sum = lax.fori_loop(1, rounds, give, give(0, table_grad))

    def stacked(member):
        return jnp.stack([layer_grads[layer_no][member] for layer_no in range(LAYERS)])

    def in_order(member):
        return jnp.stack(
            [
                lax.dot_general(
                    slot_marks,
                    layer_grads[layer_no][member].reshape(count, -1),
                    (((0,), (0,)), ((), ())),
                    precision=PRECISE,
                )
                for layer_no in range(LAYERS)
            ]
        )

    small_grad = jnp.concatenate(
        [
            item.reshape(-1)
            for item in (
                stacked(2),
                stacked(3),
                in_order(0),
                in_order(1),
                text_emb_grad,
                layout_emb_grad,
                text_pos_grad,
                layout_pos_grad,
                box_grad,
                align_grad,
            )
        ]
    )
    small_blocks = jnp.pad(
        small_grad.astype(low).reshape(dp, share), ((0, 0), (0, 2 * small_rows * line - share))
    ).reshape(dp, 2, small_rows, line)
    small_total = HalfSum([small_blocks[:, 0], small_blocks[:, 1]])
    small_sum = small_total.finish().reshape(-1)[:share]
    plan.units.reverse()
    plan.mats.reverse()

    def whole_mats(number):
        halves = [plan.mats[layer_no][number].finish() for layer_no in range(LAYERS)]
        return jnp.stack([jnp.concatenate([item[0], item[1]], 1) for item in halves])

    tmats_sum = whole_mats(0)
    lmats_sum = whole_mats(1)
    unit_sums = [
        [item.finish() for item in plan.units[layer_no]] for layer_no in range(LAYERS)
    ]
    tffn_sum = jnp.stack(
        [jnp.concatenate([item[:unit_rows] for item in pair], 1) for pair in unit_sums]
    )
    lffn_sum = jnp.stack(
        [
            jnp.concatenate(
                [
                    from_rows(item[None, unit_rows : unit_rows + layout_unit_rows], layout_units)
                    for item in pair
                ],
                1,
            )
            for pair in unit_sums
        ]
    )
    final_grads = (table_sum, tmats_sum, lmats_sum, tffn_sum, lffn_sum, small_sum)
    lane_first = (lane == 0).astype(jnp.float32)
    squares = (
        jnp.sum(table_sum * table_sum) + jnp.sum(tffn_sum * tffn_sum) + jnp.sum(lffn_sum * lffn_sum)
    )
    squares = squares + lane_first * (
        jnp.sum(tmats_sum * tmats_sum)
        + jnp.sum(lmats_sum * lmats_sum)
        + jnp.sum(small_sum * small_sum)
    )
    count_part = jnp.sum(live_own) + jnp.float32(pages * PAIRS)
    sums = sum_everywhere(
        jnp.broadcast_to(
            jnp.stack([squares, own_loss + align_part, count_part, squares])[:, None], (4, 128)
        )
    )
    total_squares, loss_sum, loss_count = sums[0, 0], sums[1, 0], sums[2, 0]
    grad_norm = jnp.sqrt(total_squares) / loss_count
    factor = jnp.minimum(1.0, CLIP_NORM / grad_norm)
    masters = (table, text_mats, layout_mats, text_ffn, layout_ffn, small_params)
    moments = (
        table_momentum,
        text_mats_momentum,
        layout_mats_momentum,
        text_ffn_momentum,
        layout_ffn_momentum,
        small_momentum,
    )
    averages = (
        table_average,
        text_mats_average,
        layout_mats_average,
        text_ffn_average,
        layout_ffn_average,
        small_average,
    )
    updated = [
        apply_update(
            masters[number],
            final_grads[number],
            moments[number],
            averages[number],
            loss_count,
            factor,
        )
        for number in range(6)
    ]
    new_masters = [item[0] for item in updated]
    new_moments = [item[1] for item in updated]
    new_averages = [item[2] for item in updated]
    copies = [item.astype(jnp.bfloat16) for item in new_masters[:5]]
    return (
        loss_sum,
        loss_count,
        grad_norm,
        new_masters[0],
        new_masters[1],
        new_masters[2],
        new_masters[3],
        new_masters[4],
        new_masters[5],
        copies[0],
        copies[1],
        copies[2],
        copies[3],
        copies[4],
        new_moments[0],
        new_moments[1],
        new_moments[2],
        new_moments[3],
        new_moments[4],
        new_moments[5],
        new_averages[0],
        new_averages[1],
        new_averages[2],
        new_averages[3],
        new_averages[4],
        new_averages[5],
    )


def solution(mesh):
    return jax.shard_map(
        on_device,
        mesh=mesh,
        in_specs=(
            P("dp", None),
            P("dp", None),
            P(("dp", "mp")),
            P(None, ("dp", "mp"), None),
            P(("dp", "mp"), None),
            P(("dp", "mp"), None, None),
            P(("dp", "mp"), None),
            P(("mp", "dp"), None),
            P(None, "dp", None),
            P(None, "dp", None),
            P(None, ("mp", "dp"), None),
            P(None, ("mp", "dp"), None),
            P("dp"),
            P(("mp", "dp"), None),
            P(None, "dp", None),
            P(None, "dp", None),
            P(None, ("mp", "dp"), None),
            P(None, ("mp", "dp"), None),
            P("dp"),
            P(("mp", "dp"), None),
            P(None, "dp", None),
            P(None, "dp", None),
            P(None, ("mp", "dp"), None),
            P(None, ("mp", "dp"), None),
            P("dp"),
        ),
        out_specs=(
            P(),
            P(),
            P(),
            P(("mp", "dp"), None),
            P(None, "dp", None),
            P(None, "dp", None),
            P(None, ("mp", "dp"), None),
            P(None, ("mp", "dp"), None),
            P("dp"),
            P(("mp", "dp"), None),
            P(None, "dp", None),
            P(None, "dp", None),
            P(None, ("mp", "dp"), None),
            P(None, ("mp", "dp"), None),
            P(("mp", "dp"), None),
            P(None, "dp", None),
            P(None, "dp", None),
            P(None, ("mp", "dp"), None),
            P(None, ("mp", "dp"), None),
            P("dp"),
            P(("mp", "dp"), None),
            P(None, "dp", None),
            P(None, "dp", None),
            P(None, ("mp", "dp"), None),
            P(None, ("mp", "dp"), None),
            P("dp"),
        ),
        check_vma=False,
    )
```

time: 2390 us -> 1310 us (0.55)
  waiting for transfers between devices: 992 us -> 340 us
  blocking collectives: 565 us -> 0 us
  matrix products: 338 us -> 126 us
  Pallas kernels: 0 us -> 162 us
  starting transfers between devices: 4.03 us -> 111 us
  local copies, waits for them, and re-layouts: 239 us -> 328 us
    all_gather x8 -> x0, waiting for transfers between devices: 527 us -> none  [the longest x1 365 us: on_device(): lax.all_gather(table.astype(jnp.bfloat16), 'dp', axis=0, tiled=True)]
    unnamed x2 -> x0, blocking collectives: 385 us -> none
    reduce_scatter x11 -> x0, waiting for transfers between devices: 317 us -> none  [the longest x1 164 us: on_device(): lax.psum_scatter(stacked(0).astype(jnp.bfloat16), 'dp', scatter_dimension...]
    ppermute x0 -> x103, waiting for transfers between devices: none -> 300 us  [hop(): return lax.ppermute(values, axis, pairs)]
    pallas_call x0 -> x32, Pallas kernels: none -> 162 us  [the longest x4 41.8 us: ffn_back(): pl.pallas_call(ffn_back_kernel, grid=(chunks,), in_specs=[whole, whole, u...]
    unnamed x29 -> x0, waiting for transfers between devices: 149 us -> none
    all_gather x10 -> x0, blocking collectives: 134 us -> none  [the longest x4 48.4 us: lane_pair(): lax.all_gather(second, 'mp', axis=0, tiled=True)]
    dot_general x44 -> x33, matrix products: 174 us -> 47.7 us  [the longest x1 8.4 us: on_device(): jnp.dot(grad_low, table_low, preferred_element_type=jnp.float32).astype(low)]
  transfers between devices with their start and end apart: 25 -> 109, of which waited for: 17 -> 48; matrix products, arithmetic and copies ran while one was open for 40% -> 40% of each run, Pallas kernels for 0% -> 7%
where the time goes in v1:
time: 1310 us; the launch traced here: 1290 us
  waiting for transfers between devices  340 us (26%)
  local copies, waits for them, and re-layouts  328 us (25%)
  other arithmetic  203 us (15%)
  Pallas kernels  162 us (12%)
  matrix products  126 us (10%)
  starting transfers between devices  111 us (8%)
  between operations  16.7 us (1%)
    ppermute x103, waiting for transfers between devices, hop(): return lax.ppermute(values, axis, pairs)  300 us
    unnamed x933, local copies, waits for them, and re-layouts  169 us
    ppermute x103, starting transfers between devices, hop(): return lax.ppermute(values, axis, pairs)  87.9 us
    convert_element_type x42, other arithmetic, add_low(): (kept.astype(jnp.float32) + came.astype(jnp.float32)).astype(jnp.bfloat16)  48.5 us
    dot_general x27, matrix products, contract_rows(): lax.dot_general(left, right, (((0,), (0,)), ((), ())), preferred_element_...  46.2 us
    pallas_call x4, Pallas kernels, ffn_back(): pl.pallas_call(ffn_back_kernel, grid=(chunks,), in_specs=[whole, whole, u...  41.8 us
    pallas_call x3, Pallas kernels, put_in_order(): pl.pallas_call(kernel, out_shape=jax.ShapeDtypeStruct((2, slots * rows, w...  35.1 us
    dot_general x14, matrix products, contract_cols(): lax.dot_general(left, right, (((1,), (1,)), ((), ())), preferred_element_...  31.6 us
  transfers between devices with their start and end apart: 109, of which 48 were waited for; matrix products, arithmetic and copies ran while one was open for 40% of the time, Pallas kernels for 7%

profile of v1, /device:TPU:0, one launch (start us, length us, event | category | flops | bytes accessed | tf_op | source)
XLA Modules:
  0.0 1286.5 jit_solution(87014540984592799)
XLA Ops:
  26.0 4.0 convert_element_type.1371
  30.4 9.4 and_reduce_fusion
  46.2 11.8 collective-permute-done.2.refs_1_
  68.7 6.0 collective-permute-done.3.refs_1_
  76.3 6.1 fusion.39
  82.3 7.7 collective-permute-done.4.refs_1_
  95.4 13.0 %collective-permute-done.9.refs_1_ = bf16[1,104,768]{2,1,0:T(8,128)(2,1)S(1)} collective-permute-done((bf16[1,104,768]{2,1,0:T(8,128)(2,1)}, bf16[1,104,768]{2,1,0:T(8,128)(2,1)S(1)}, u32[]{:S(2)}, u32[]{:S(2)}) %collective-permute-start.9) | collective-permute-done | bytes 159776 | tf_op jit(solution)/shard_map/ppermute | solution.py:95
  117.4 4.2 collective-permute-done.18.refs_1_
  145.9 7.4 collective-permute-done.20
  157.0 7.1 collective-permute-done.12
  172.8 10.9 shard_map.488
  200.9 4.2 all-to-all-start.3
  209.3 14.2 %slice.1083 = bf16[31760,24]{1,0:T(8,128)(2,1)} reshape(bf16[762240]{0:T(1024)(128)(2,1)S(1)} %reshape.1375) | data formatting | bytes 3048960 | tf_op jit(solution)/shard_map/slice | solution.py:50
  252.2 4.8 collective-permute-done.31.refs_1_
  269.0 11.0 collective-permute-done.13
  298.1 4.0 collective-permute-done.40
  321.7 8.3 collective-permute-done.41
  333.4 9.5 collective-permute-done.33
  355.0 12.2 shard_map.489
  373.6 14.4 %shard_map.490 = (bf16[512,768]{1,0:T(8,128)(2,1)S(1)}, bf16[6,512,32]{2,1,0:T(8,128)(2,1)S(1)}, f32[6,512,2]{2,1,0:T(8,128)S(1)}) custom-call(s32[1]{0:T(128)} %copy.598.length, bf16[512,768]{1,0:T(8,128)(2,1)S(1)} %fusion.41.qt, bf16[512,768]{1,0:T(8,128)(2,1)S(1)} %slice.1806.kt, bf16[512,768]{1,0:T(8,128)(2,1)S(1)} %add_convert_fusion.14.vt, ...), custom_call_target="tpu_custom_call" | custom-call | flops 12000000000 | bytes 8000000 | tf_op jit(solution)/shard_map/pallas_call | solution.py:241
  410.2 13.0 %shard_map.495 = (bf16[512,3072]{1,0:T(8,128)(2,1)S(1)}, bf16[512,3072]{1,0:T(8,128)(2,1)S(1)}, f32[512,768]{1,0:T(8,128)S(1)}) custom-call(bf16[512,768]{1,0:T(8,128)(2,1)S(1)} %fusion.43.rows_ref, bf16[3072,768]{1,0:T(8,128)(2,1)S(1)} %bitcast.573, bf16[3072,768]{1,0:T(8,128)(2,1)} %bitcast.652, f32[1,3072]{1,0:T(1,128)S(1)} %broadcast_in_dim_reshape.14.bias_ref), custom_call_target="tpu_custom_call" | custom-call | flops 4831838208 | bytes 15728640 | tf_op jit(solution)/shard_map/pallas_call | solution.py:329
  442.7 8.1 collective-permute-done.35
  460.7 12.0 shard_map.498
  479.3 14.4 %shard_map.500 = (bf16[512,768]{1,0:T(8,128)(2,1)S(1)}, bf16[6,512,32]{2,1,0:T(8,128)(2,1)S(1)}, f32[6,512,2]{2,1,0:T(8,128)S(1)}) custom-call(s32[1]{0:T(128)} %copy.598.length, bf16[512,768]{1,0:T(8,128)(2,1)S(1)} %fusion.40.qt, bf16[512,768]{1,0:T(8,128)(2,1)S(1)} %slice.1805.kt, bf16[512,768]{1,0:T(8,128)(2,1)S(1)} %add_convert_fusion.13.vt, ...), custom_call_target="tpu_custom_call" | custom-call | flops 12000000000 | bytes 8000000 | tf_op jit(solution)/shard_map/pallas_call | solution.py:241
  495.5 13.4 %shard_map.505 = (bf16[512,3072]{1,0:T(8,128)(2,1)S(1)}, bf16[512,3072]{1,0:T(8,128)(2,1)S(1)}, f32[512,768]{1,0:T(8,128)S(1)}) custom-call(bf16[512,768]{1,0:T(8,128)(2,1)S(1)} %fusion.45.rows_ref, bf16[3072,768]{1,0:T(8,128)(2,1)} %bitcast.52.in_ref, bf16[3072,768]{1,0:T(8,128)(2,1)} %bitcast.650, f32[1,3072]{1,0:T(1,128)S(1)} %broadcast_in_dim_reshape.16.bias_ref), custom_call_target="tpu_custom_call" | custom-call | flops 4831838208 | bytes 15728640 | tf_op jit(solution)/shard_map/pallas_call | solution.py:329
  515.4 4.7 all-to-all-start.4
  536.4 21.2 %all-to-all-done.4 = bf16[32,32,768]{2,1,0:T(8,128)(2,1)} async-done(((bf16[32,32,768]{2,1,0:T(8,128)(2,1)}), bf16[32,32,768]{2,1,0:T(8,128)(2,1)}, u32[]{:S(2)}, u32[]{:S(2)}) %all-to-all-start.4) | async-done | bytes 1572896 | tf_op jit(solution)/shard_map/all_to_all | solution.py:524
  557.7 4.9 fusion.299
  566.2 4.0 all-to-all-start.5
  576.2 9.5 all-to-all-done.5
  588.4 8.4 convolution_convert_fusion.2
  629.0 9.0 all-to-all-done.6
  643.4 18.8 %shard_map.507 = (f32[512,768]{1,0:T(8,128)S(1)}, f32[1,3072]{1,0:T(1,128)S(1)}, bf16[16,104,768]{2,1,0:T(8,128)(2,1)S(1)}, bf16[16,104,768]{2,1,0:T(8,128)(2,1)...) custom-call(bf16[512,768]{1,0:T(8,128)(2,1)S(1)} %copy-done.45, ...), custom_call_target="tpu_custom_call" | custom-call | flops 9663676416 | bytes 31457280 | tf_op jit(solution)/shard_map/pallas_call | solution.py:618
  695.7 13.0 %shard_map.510 = (bf16[512,768]{1,0:T(8,128)(2,1)S(1)}, bf16[512,768]{1,0:T(8,128)(2,1)S(1)}, bf16[512,768]{1,0:T(8,128)(2,1)S(1)}, bf16[6,512,32]{2,1,0:T(8,128...) custom-call(s32[1]{0:T(128)} %copy.598.length, bf16[512,768]{1,0:T(8,128)(2,1)S(1)} %copy-done.42, ...), custom_call_target="tpu_custom_call" | custom-call | flops 20000000000 | bytes 14000000 | tf_op jit(solution)/shard_map/pallas_call | solution.py:264
  734.1 4.4 add_add_fusion.6.refs_0_
  757.6 4.4 collective-permute-done.89
  785.2 10.0 collective-permute-done.50.refs_1_
  803.3 18.7 %shard_map.512 = (f32[512,768]{1,0:T(8,128)S(1)}, f32[1,3072]{1,0:T(1,128)S(1)}, bf16[16,104,768]{2,1,0:T(8,128)(2,1)S(1)}, bf16[16,104,768]{2,1,0:T(8,128)(2,1)...) custom-call(bf16[512,768]{1,0:T(8,128)(2,1)S(1)} %copy-done.30, ...), custom_call_target="tpu_custom_call" | custom-call | flops 9663676416 | bytes 31457280 | tf_op jit(solution)/shard_map/pallas_call | solution.py:618
  841.0 6.2 collective-permute-done.57.refs_2_
  847.3 8.8 collective-permute-done.56.refs_1_
  867.8 21.0 %collective-permute-done.55.refs_3_ = bf16[2,2,96,1536]{3,2,1,0:T(8,128)(2,1)S(1)} collective-permute-done((bf16[2,2,96,1536]{3,2,1,0:T(8,128)(2,1)}, bf16[2,2,96,1536]{3,2,1,0:T(8,128)(2,1)S(1)}, u32[]{:S(2)}, u32[]{:S(2)}) %collective-permute-start.55) | collective-permute-done | bytes 1179680 | tf_op jit(solution)/shard_map/ppermute | solution.py:95
  897.7 13.4 %shard_map.515 = (bf16[512,768]{1,0:T(8,128)(2,1)S(1)}, bf16[512,768]{1,0:T(8,128)(2,1)S(1)}, bf16[512,768]{1,0:T(8,128)(2,1)S(1)}, bf16[6,512,32]{2,1,0:T(8,128...) custom-call(s32[1]{0:T(128)} %copy.598.length, bf16[512,768]{1,0:T(8,128)(2,1)S(1)} %copy-done.28, ...), custom_call_target="tpu_custom_call" | custom-call | flops 20000000000 | bytes 14000000 | tf_op jit(solution)/shard_map/pallas_call | solution.py:264
  976.7 8.6 collective-permute-done.77
  988.6 22.6 %collective-permute-done.78 = bf16[96,1536]{1,0:T(8,128)(2,1)S(1)} collective-permute-done((bf16[96,1536]{1,0:T(8,128)(2,1)S(1)}, bf16[96,1536]{1,0:T(8,128)(2,1)S(1)}, u32[]{:S(2)}, u32[]{:S(2)}) %collective-permute-start.78) | collective-permute-done | bytes 294944 | tf_op jit(solution)/shard_map/ppermute | solution.py:95
  1019.5 5.3 multiply_reduce_fusion.2
  1045.0 13.2 %dynamic-update-slice.6 = bf16[762240]{0:T(1024)(128)(2,1)} dynamic-update-slice(bf16[762240]{0:T(1024)(128)(2,1)} %dynamic-update-slice.5, bf16[393216]{0:T(1024)(128)(2,1)S(1)} %reshape.1439, s32[]{} %constant.493) | dynamic-update-slice | bytes 1572868
  1058.2 4.4 dynamic-update-slice.7
  1062.6 4.4 dynamic-update-slice.8
  1067.0 5.7 dynamic-update-slice.9
  1072.7 4.4 convert_element_type.1725
  1095.2 5.7 collective-permute-done.67
  1101.5 8.6 collective-permute-done.64
  1111.4 7.7 collective-permute-done.65
  1120.1 6.1 collective-permute-done.94
  1152.4 23.7 %collective-permute-done.72 = bf16[2,2,96,1536]{3,2,1,0:T(8,128)(2,1)} collective-permute-done((bf16[2,2,96,1536]{3,2,1,0:T(8,128)(2,1)}, bf16[2,2,96,1536]{3,2,1,0:T(8,128)(2,1)}, u32[]{:S(2)}, u32[]{:S(2)}) %collective-permute-start.72) | collective-permute-done | bytes 1179680 | tf_op jit(solution)/shard_map/ppermute | solution.py:95
  1181.0 12.6 collective-permute-done.73
  1196.4 4.9 fusion.14
  1201.3 7.7 collective-permute-done.74
  1211.3 9.2 convolution_add_fusion
  1221.0 4.2 multiply_reduce_fusion
  1240.3 4.5 collective-permute-done.101
  1257.3 4.7 add_multiply_fusion.2
  1263.9 6.1 add_multiply_fusion.1
  1272.6 7.6 add_multiply_fusion
  (1650 shorter events, 676.6 us)
Async XLA Ops:
  3.1 42.4 %collective-permute-start = (bf16[1,48,1536]{2,1,0:T(8,128)(2,1)S(1)}, bf16[1,48,1536]{2,1,0:T(8,128)(2,1)S(1)}, u32[]{:S(2)}, u32[]{:S(2)}) collective-permute-start(bf16[1,48,1536]{2,1,0:T(8,128)(2,1)S(1)} %maximum_bitcast_fusion.8), channel_id=1, source_target_pairs={{0,4},{4,0},{8,12},{12,8},{16,20},{20,16},{24,28},{28,24},{1,5},{5... | collective-permute-start | bytes 442376 | tf_op jit(solution)/shard_map/ppermute | solution.py:95
  8.1 33.2 %collective-permute-start.1 = (bf16[1,96,1536]{2,1,0:T(8,128)(2,1)S(1)}, bf16[1,96,1536]{2,1,0:T(8,128)(2,1)S(1)}, u32[]{:S(2)}, u32[]{:S(2)}) collective-permute-start(bf16[1,96,1536]{2,1,0:T(8,128)(2,1)S(1)} %get-tuple-element.615), channel_id=1, source_target_pairs={{0,16},{4,20},{8,24},{12,28},{16,0},{20,4},{24,8},{28,12},{1,17},{... | collective-permute-start | bytes 884744 | tf_op jit(solution)/shard_map/ppermute | solution.py:95
  67.2 47.3 %collective-permute-start.6 = (bf16[4,96,1536]{2,1,0:T(8,128)(2,1)}, bf16[4,96,1536]{2,1,0:T(8,128)(2,1)}, u32[]{:S(2)}, u32[]{:S(2)}) collective-permute-start(bf16[4,96,1536]{2,1,0:T(8,128)(2,1)} %pad_maximum_fusion.7), channel_id=1, source_target_pairs={{0,4},{4,0},{8,12},{12,8},{16,20},{20,16},{24,28},{28,24},{1,5},{5... | collective-permute-start | bytes 3538952 | tf_op jit(solution)/shard_map/ppermute | solution.py:95
  90.9 20.7 %collective-permute-start.8 = (bf16[1,104,768]{2,1,0:T(8,128)(2,1)}, bf16[1,104,768]{2,1,0:T(8,128)(2,1)}, u32[]{:S(2)}, u32[]{:S(2)}) collective-permute-start(bf16[1,104,768]{2,1,0:T(8,128)(2,1)} %shard_map.491), channel_id=1, source_target_pairs={{0,16},{4,20},{8,24},{12,28},{16,0},{20,4},{24,8},{28,12},{1,17},{... | collective-permute-start | bytes 479240 | tf_op jit(solution)/shard_map/ppermute | solution.py:95
  95.4 77.4 %collective-permute-start.5 = (bf16[8,48,1536]{2,1,0:T(8,128)(2,1)S(1)}, bf16[8,48,1536]{2,1,0:T(8,128)(2,1)}, u32[]{:S(2)}, u32[]{:S(2)}) collective-permute-start(bf16[8,48,1536]{2,1,0:T(8,128)(2,1)S(1)} %pad_maximum_fusion.6.own_ref), channel_id=1, source_target_pairs={{0,1},{1,0},{2,3},{3,2},{4,5},{5,4},{6,7},{7,6},{8,9},{9,8},{10,11... | collective-permute-start | bytes 3538952 | tf_op jit(solution)/shard_map/ppermute | solution.py:95
  113.2 19.0 %collective-permute-start.10 = (bf16[2,104,768]{2,1,0:T(8,128)(2,1)}, bf16[2,104,768]{2,1,0:T(8,128)(2,1)}, u32[]{:S(2)}, u32[]{:S(2)}) collective-permute-start(bf16[2,104,768]{2,1,0:T(8,128)(2,1)} %shard_map.493), channel_id=1, source_target_pairs={{0,8},{4,12},{8,0},{12,4},{16,24},{20,28},{24,16},{28,20},{1,9},{5... | collective-permute-start | bytes 958472 | tf_op jit(solution)/shard_map/ppermute | solution.py:95
  117.4 237.6 %collective-permute-start.7 = (bf16[8,96,1536]{2,1,0:T(8,128)(2,1)}, bf16[8,96,1536]{2,1,0:T(8,128)(2,1)}, u32[]{:S(2)}, u32[]{:S(2)}) collective-permute-start(bf16[8,96,1536]{2,1,0:T(8,128)(2,1)} %pad_maximum_fusion.own_ref), channel_id=1, source_target_pairs={{0,1},{1,0},{2,3},{3,2},{4,5},{5,4},{6,7},{7,6},{8,9},{9,8},{10,11... | collective-permute-start | bytes 7077896 | tf_op jit(solution)/shard_map/ppermute | solution.py:95
  121.6 16.2 %collective-permute-start.26 = (bf16[1,96,1536]{2,1,0:T(8,128)(2,1)}, bf16[1,96,1536]{2,1,0:T(8,128)(2,1)S(1)}, u32[]{:S(2)}, u32[]{:S(2)}) collective-permute-start(bf16[1,96,1536]{2,1,0:T(8,128)(2,1)} %shard_map.496), channel_id=1, source_target_pairs={{0,16},{4,20},{8,24},{12,28},{16,0},{20,4},{24,8},{28,12},{1,17},{... | collective-permute-start | bytes 884744 | tf_op jit(solution)/shard_map/ppermute | solution.py:95
  125.4 17.0 %collective-permute-start.19 = (bf16[4,104,768]{2,1,0:T(8,128)(2,1)}, bf16[4,104,768]{2,1,0:T(8,128)(2,1)}, u32[]{:S(2)}, u32[]{:S(2)}) collective-permute-start(bf16[4,104,768]{2,1,0:T(8,128)(2,1)} %pad_maximum_fusion.13), channel_id=1, source_target_pairs={{0,4},{4,0},{8,12},{12,8},{16,20},{20,16},{24,28},{28,24},{1,5},{5... | collective-permute-start | bytes 1916936 | tf_op jit(solution)/shard_map/ppermute | solution.py:95
  135.7 17.6 %collective-permute-start.20 = (bf16[4,104,768]{2,1,0:T(8,128)(2,1)}, bf16[4,104,768]{2,1,0:T(8,128)(2,1)}, u32[]{:S(2)}, u32[]{:S(2)}) collective-permute-start(bf16[4,104,768]{2,1,0:T(8,128)(2,1)} %pad_maximum_fusion.13), channel_id=1, source_target_pairs={{0,2},{1,3},{2,0},{3,1},{4,6},{5,7},{6,4},{7,5},{8,10},{9,11},{10,... | collective-permute-start | bytes 1916936 | tf_op jit(solution)/shard_map/ppermute | solution.py:95
  137.8 17.0 %collective-permute-start.11 = (bf16[4,104,768]{2,1,0:T(8,128)(2,1)S(1)}, bf16[4,104,768]{2,1,0:T(8,128)(2,1)}, u32[]{:S(2)}, u32[]{:S(2)}) collective-permute-start(bf16[4,104,768]{2,1,0:T(8,128)(2,1)S(1)} %pad_maximum_fusion.12), channel_id=1, source_target_pairs={{0,4},{4,0},{8,12},{12,8},{16,20},{20,16},{24,28},{28,24},{1,5},{5... | collective-permute-start | bytes 1916936 | tf_op jit(solution)/shard_map/ppermute | solution.py:95
  142.4 21.7 %collective-permute-start.12 = (bf16[4,104,768]{2,1,0:T(8,128)(2,1)S(1)}, bf16[4,104,768]{2,1,0:T(8,128)(2,1)S(1)}, u32[]{:S(2)}, u32[]{:S(2)}) collective-permute-start(bf16[4,104,768]{2,1,0:T(8,128)(2,1)S(1)} %pad_maximum_fusion.12), channel_id=1, source_target_pairs={{0,2},{1,3},{2,0},{3,1},{4,6},{5,7},{6,4},{7,5},{8,10},{9,11},{10,... | collective-permute-start | bytes 1916936 | tf_op jit(solution)/shard_map/ppermute | solution.py:95
  153.3 108.1 %collective-permute-start.22 = (bf16[4,104,768]{2,1,0:T(8,128)(2,1)}, bf16[4,104,768]{2,1,0:T(8,128)(2,1)}, u32[]{:S(2)}, u32[]{:S(2)}) collective-permute-start(bf16[4,104,768]{2,1,0:T(8,128)(2,1)} %pad_maximum_fusion.13), channel_id=1, source_target_pairs={{0,1},{1,0},{2,3},{3,2},{4,5},{5,4},{6,7},{7,6},{8,9},{9,8},{10,11... | collective-permute-start | bytes 1916936 | tf_op jit(solution)/shard_map/ppermute | solution.py:95
  154.8 84.4 %collective-permute-start.27 = (bf16[2,96,1536]{2,1,0:T(8,128)(2,1)}, bf16[2,96,1536]{2,1,0:T(8,128)(2,1)}, u32[]{:S(2)}, u32[]{:S(2)}) collective-permute-start(bf16[2,96,1536]{2,1,0:T(8,128)(2,1)} %shard_map.497), channel_id=1, source_target_pairs={{0,8},{4,12},{8,0},{12,4},{16,24},{20,28},{24,16},{28,20},{1,9},{5... | collective-permute-start | bytes 1769480 | tf_op jit(solution)/shard_map/ppermute | solution.py:95
  164.1 95.9 %collective-permute-start.21 = (bf16[4,104,768]{2,1,0:T(8,128)(2,1)}, bf16[4,104,768]{2,1,0:T(8,128)(2,1)}, u32[]{:S(2)}, u32[]{:S(2)}) collective-permute-start(bf16[4,104,768]{2,1,0:T(8,128)(2,1)} %collective-permute-done.20), channel_id=1, source_target_pairs={{0,4},{4,0},{8,12},{12,8},{16,20},{20,16},{24,28},{28,24},{1,5},{5... | collective-permute-start | bytes 1916936 | tf_op jit(solution)/shard_map/ppermute | solution.py:95
  200.9 43.5 %all-to-all-start.3 = ((bf16[32,32,768]{2,1,0:T(8,128)(2,1)}), bf16[32,32,768]{2,1,0:T(8,128)(2,1)}, u32[]{:S(2)}, u32[]{:S(2)}) async-start(bf16[32,32,768]{2,1,0:T(8,128)(2,1)} %bitcast.601), calls=%async_computation.3 | async-start | bytes 3145728 | tf_op jit(solution)/shard_map/all_to_all | solution.py:530
  239.2 18.6 %collective-permute-start.30 = (bf16[1,104,768]{2,1,0:T(8,128)(2,1)}, bf16[1,104,768]{2,1,0:T(8,128)(2,1)}, u32[]{:S(2)}, u32[]{:S(2)}) collective-permute-start(bf16[1,104,768]{2,1,0:T(8,128)(2,1)} %shard_map.501), channel_id=1, source_target_pairs={{0,16},{4,20},{8,24},{12,28},{16,0},{20,4},{24,8},{28,12},{1,17},{... | collective-permute-start | bytes 479240 | tf_op jit(solution)/shard_map/ppermute | solution.py:95
  257.8 29.2 %collective-permute-start.14 = (bf16[4,104,768]{2,1,0:T(8,128)(2,1)}, bf16[4,104,768]{2,1,0:T(8,128)(2,1)}, u32[]{:S(2)}, u32[]{:S(2)}) collective-permute-start(bf16[4,104,768]{2,1,0:T(8,128)(2,1)} %copy-done.172), channel_id=1, source_target_pairs={{0,1},{1,0},{2,3},{3,2},{4,5},{5,4},{6,7},{7,6},{8,9},{9,8},{10,11... | collective-permute-start | bytes 1916936 | tf_op jit(solution)/shard_map/ppermute | solution.py:95
  261.5 35.2 %collective-permute-start.16 = (bf16[4,104,768]{2,1,0:T(8,128)(2,1)S(1)}, bf16[4,104,768]{2,1,0:T(8,128)(2,1)S(1)}, u32[]{:S(2)}, u32[]{:S(2)}) collective-permute-start(bf16[4,104,768]{2,1,0:T(8,128)(2,1)S(1)} %copy-done.241), channel_id=1, source_target_pairs={{0,1},{1,0},{2,3},{3,2},{4,5},{5,4},{6,7},{7,6},{8,9},{9,8},{10,11... | collective-permute-start | bytes 1916936 | tf_op jit(solution)/shard_map/ppermute | solution.py:95
  263.4 16.6 %collective-permute-start.13 = (bf16[4,104,768]{2,1,0:T(8,128)(2,1)}, bf16[4,104,768]{2,1,0:T(8,128)(2,1)}, u32[]{:S(2)}, u32[]{:S(2)}) collective-permute-start(bf16[4,104,768]{2,1,0:T(8,128)(2,1)} %collective-permute-done.11), channel_id=1, source_target_pairs={{0,2},{1,3},{2,0},{3,1},{4,6},{5,7},{6,4},{7,5},{8,10},{9,11},{10,... | collective-permute-start | bytes 1916936 | tf_op jit(solution)/shard_map/ppermute | solution.py:95
  266.5 25.3 %collective-permute-start.15 = (bf16[4,104,768]{2,1,0:T(8,128)(2,1)}, bf16[4,104,768]{2,1,0:T(8,128)(2,1)S(1)}, u32[]{:S(2)}, u32[]{:S(2)}) collective-permute-start(bf16[4,104,768]{2,1,0:T(8,128)(2,1)} %collective-permute-done.11), channel_id=1, source_target_pairs={{0,1},{1,0},{2,3},{3,2},{4,5},{5,4},{6,7},{7,6},{8,9},{9,8},{10,11... | collective-permute-start | bytes 1916936 | tf_op jit(solution)/shard_map/ppermute | solution.py:95
  280.0 71.4 %collective-permute-start.28 = (bf16[4,96,1536]{2,1,0:T(8,128)(2,1)}, bf16[4,96,1536]{2,1,0:T(8,128)(2,1)}, u32[]{:S(2)}, u32[]{:S(2)}) collective-permute-start(bf16[4,96,1536]{2,1,0:T(8,128)(2,1)} %pad_maximum_fusion.8), channel_id=1, source_target_pairs={{0,4},{4,0},{8,12},{12,8},{16,20},{20,16},{24,28},{28,24},{1,5},{5... | collective-permute-start | bytes 3538952 | tf_op jit(solution)/shard_map/ppermute | solution.py:95
  287.0 19.5 %collective-permute-start.32 = (bf16[2,104,768]{2,1,0:T(8,128)(2,1)S(1)}, bf16[2,104,768]{2,1,0:T(8,128)(2,1)S(1)}, u32[]{:S(2)}, u32[]{:S(2)}) collective-permute-start(bf16[2,104,768]{2,1,0:T(8,128)(2,1)S(1)} %copy-done.204), channel_id=1, source_target_pairs={{0,8},{4,12},{8,0},{12,4},{16,24},{20,28},{24,16},{28,20},{1,9},{5... | collective-permute-start | bytes 958472 | tf_op jit(solution)/shard_map/ppermute | solution.py:95
  306.5 25.5 %collective-permute-start.42 = (bf16[4,104,768]{2,1,0:T(8,128)(2,1)}, bf16[4,104,768]{2,1,0:T(8,128)(2,1)}, u32[]{:S(2)}, u32[]{:S(2)}) collective-permute-start(bf16[4,104,768]{2,1,0:T(8,128)(2,1)} %pad_maximum_fusion.15), channel_id=1, source_target_pairs={{0,2},{1,3},{2,0},{3,1},{4,6},{5,7},{6,4},{7,5},{8,10},{9,11},{10,... | collective-permute-start | bytes 1916936 | tf_op jit(solution)/shard_map/ppermute | solution.py:95
  312.5 17.5 %collective-permute-start.41 = (bf16[4,104,768]{2,1,0:T(8,128)(2,1)}, bf16[4,104,768]{2,1,0:T(8,128)(2,1)}, u32[]{:S(2)}, u32[]{:S(2)}) collective-permute-start(bf16[4,104,768]{2,1,0:T(8,128)(2,1)} %pad_maximum_fusion.15), channel_id=1, source_target_pairs={{0,4},{4,0},{8,12},{12,8},{16,20},{20,16},{24,28},{28,24},{1,5},{5... | collective-permute-start | bytes 1916936 | tf_op jit(solution)/shard_map/ppermute | solution.py:95
  313.5 29.4 %collective-permute-start.33 = (bf16[4,104,768]{2,1,0:T(8,128)(2,1)}, bf16[4,104,768]{2,1,0:T(8,128)(2,1)S(1)}, u32[]{:S(2)}, u32[]{:S(2)}) collective-permute-start(bf16[4,104,768]{2,1,0:T(8,128)(2,1)} %pad_maximum_fusion.14), channel_id=1, source_target_pairs={{0,4},{4,0},{8,12},{12,8},{16,20},{20,16},{24,28},{28,24},{1,5},{5... | collective-permute-start | bytes 1916936 | tf_op jit(solution)/shard_map/ppermute | solution.py:95
  332.0 100.1 %collective-permute-start.44 = (bf16[4,104,768]{2,1,0:T(8,128)(2,1)}, bf16[4,104,768]{2,1,0:T(8,128)(2,1)}, u32[]{:S(2)}, u32[]{:S(2)}) collective-permute-start(bf16[4,104,768]{2,1,0:T(8,128)(2,1)} %pad_maximum_fusion.15), channel_id=1, source_target_pairs={{0,1},{1,0},{2,3},{3,2},{4,5},{5,4},{6,7},{7,6},{8,9},{9,8},{10,11... | collective-permute-start | bytes 1916936 | tf_op jit(solution)/shard_map/ppermute | solution.py:95
  342.9 108.8 %collective-permute-start.36 = (bf16[4,104,768]{2,1,0:T(8,128)(2,1)}, bf16[4,104,768]{2,1,0:T(8,128)(2,1)}, u32[]{:S(2)}, u32[]{:S(2)}) collective-permute-start(bf16[4,104,768]{2,1,0:T(8,128)(2,1)} %pad_maximum_fusion.14), channel_id=1, source_target_pairs={{0,1},{1,0},{2,3},{3,2},{4,5},{5,4},{6,7},{7,6},{8,9},{9,8},{10,11... | collective-permute-start | bytes 1916936 | tf_op jit(solution)/shard_map/ppermute | solution.py:95
  345.2 91.3 %collective-permute-start.46 = (bf16[4,104,768]{2,1,0:T(8,128)(2,1)}, bf16[4,104,768]{2,1,0:T(8,128)(2,1)}, u32[]{:S(2)}, u32[]{:S(2)}) collective-permute-start(bf16[4,104,768]{2,1,0:T(8,128)(2,1)} %collective-permute-done.42), channel_id=1, source_target_pairs={{0,1},{1,0},{2,3},{3,2},{4,5},{5,4},{6,7},{7,6},{8,9},{9,8},{10,11... | collective-permute-start | bytes 1916936 | tf_op jit(solution)/shard_map/ppermute | solution.py:95
  351.4 76.7 %collective-permute-start.43 = (bf16[4,104,768]{2,1,0:T(8,128)(2,1)}, bf16[4,104,768]{2,1,0:T(8,128)(2,1)}, u32[]{:S(2)}, u32[]{:S(2)}) collective-permute-start(bf16[4,104,768]{2,1,0:T(8,128)(2,1)} %collective-permute-done.42), channel_id=1, source_target_pairs={{0,4},{4,0},{8,12},{12,8},{16,20},{20,16},{24,28},{28,24},{1,5},{5... | collective-permute-start | bytes 1916936 | tf_op jit(solution)/shard_map/ppermute | solution.py:95
  355.0 79.2 %collective-permute-start.45 = (bf16[4,104,768]{2,1,0:T(8,128)(2,1)}, bf16[4,104,768]{2,1,0:T(8,128)(2,1)}, u32[]{:S(2)}, u32[]{:S(2)}) collective-permute-start(bf16[4,104,768]{2,1,0:T(8,128)(2,1)} %collective-permute-done.41), channel_id=1, source_target_pairs={{0,1},{1,0},{2,3},{3,2},{4,5},{5,4},{6,7},{7,6},{8,9},{9,8},{10,11... | collective-permute-start | bytes 1916936 | tf_op jit(solution)/shard_map/ppermute | solution.py:95
  428.3 29.4 %collective-permute-start.38 = (bf16[4,104,768]{2,1,0:T(8,128)(2,1)S(1)}, bf16[4,104,768]{2,1,0:T(8,128)(2,1)S(1)}, u32[]{:S(2)}, u32[]{:S(2)}) collective-permute-start(bf16[4,104,768]{2,1,0:T(8,128)(2,1)S(1)} %copy-done.245), channel_id=1, source_target_pairs={{0,1},{1,0},{2,3},{3,2},{4,5},{5,4},{6,7},{7,6},{8,9},{9,8},{10,11... | collective-permute-start | bytes 1916936 | tf_op jit(solution)/shard_map/ppermute | solution.py:95
  432.1 22.0 %collective-permute-start.37 = (bf16[4,104,768]{2,1,0:T(8,128)(2,1)S(1)}, bf16[4,104,768]{2,1,0:T(8,128)(2,1)S(1)}, u32[]{:S(2)}, u32[]{:S(2)}) collective-permute-start(bf16[4,104,768]{2,1,0:T(8,128)(2,1)S(1)} %copy-done.243), channel_id=1, source_target_pairs={{0,1},{1,0},{2,3},{3,2},{4,5},{5,4},{6,7},{7,6},{8,9},{9,8},{10,11... | collective-permute-start | bytes 1916936 | tf_op jit(solution)/shard_map/ppermute | solution.py:95
  434.2 16.7 %collective-permute-start.35 = (bf16[4,104,768]{2,1,0:T(8,128)(2,1)S(1)}, bf16[4,104,768]{2,1,0:T(8,128)(2,1)S(1)}, u32[]{:S(2)}, u32[]{:S(2)}) collective-permute-start(bf16[4,104,768]{2,1,0:T(8,128)(2,1)S(1)} %copy-done.243), channel_id=1, source_target_pairs={{0,2},{1,3},{2,0},{3,1},{4,6},{5,7},{6,4},{7,5},{8,10},{9,11},{10,... | collective-permute-start | bytes 1916936 | tf_op jit(solution)/shard_map/ppermute | solution.py:95
  436.5 24.2 %collective-permute-start.29 = (bf16[8,96,1536]{2,1,0:T(8,128)(2,1)S(1)}, bf16[8,96,1536]{2,1,0:T(8,128)(2,1)}, u32[]{:S(2)}, u32[]{:S(2)}) collective-permute-start(bf16[8,96,1536]{2,1,0:T(8,128)(2,1)S(1)} %copy-done.111), channel_id=1, source_target_pairs={{0,1},{1,0},{2,3},{3,2},{4,5},{5,4},{6,7},{7,6},{8,9},{9,8},{10,11... | collective-permute-start | bytes 7077896 | tf_op jit(solution)/shard_map/ppermute | solution.py:95
  515.4 42.2 %all-to-all-start.4 = ((bf16[32,32,768]{2,1,0:T(8,128)(2,1)}), bf16[32,32,768]{2,1,0:T(8,128)(2,1)}, u32[]{:S(2)}, u32[]{:S(2)}) async-start(bf16[32,32,768]{2,1,0:T(8,128)(2,1)} %broadcast_in_dim.191), calls=%async_computation.4 | async-start | bytes 3145728 | tf_op jit(solution)/shard_map/all_to_all | solution.py:524
  566.2 19.5 %all-to-all-start.5 = ((f32[32,3,1024]{2,1,0:T(4,128)}), f32[32,3,1024]{2,1,0:T(4,128)}, u32[]{:S(2)}, u32[]{:S(2)}) async-start(f32[32,3,1024]{2,1,0:T(4,128)} %broadcast_in_dim.193), calls=%async_computation.5 | async-start | bytes 1048576 | tf_op jit(solution)/shard_map/all_to_all | solution.py:524
  596.8 41.2 %all-to-all-start.6 = ((bf16[32,32,768]{2,1,0:T(8,128)(2,1)}), bf16[32,32,768]{2,1,0:T(8,128)(2,1)}, u32[]{:S(2)}, u32[]{:S(2)}) async-start(bf16[32,32,768]{2,1,0:T(8,128)(2,1)} %bitcast.603), calls=%async_computation.6 | async-start | bytes 3145728 | tf_op jit(solution)/shard_map/all_to_all | solution.py:530
  664.4 22.2 %collective-permute-start.49 = (bf16[16,104,768]{2,1,0:T(8,128)(2,1)}, bf16[16,104,768]{2,1,0:T(8,128)(2,1)}, u32[]{:S(2)}, u32[]{:S(2)}) collective-permute-start(bf16[16,104,768]{2,1,0:T(8,128)(2,1)} %pad_dynamic-update-slice_fusion.6), channel_id=1, source_target_pairs={{0,1},{1,0},{2,3},{3,2},{4,5},{5,4},{6,7},{7,6},{8,9},{9,8},{10,11... | collective-permute-start | bytes 7667720 | tf_op jit(solution)/shard_map/ppermute | solution.py:95
  665.2 21.4 %collective-permute-start.48 = (bf16[16,104,768]{2,1,0:T(8,128)(2,1)}, bf16[16,104,768]{2,1,0:T(8,128)(2,1)}, u32[]{:S(2)}, u32[]{:S(2)}) collective-permute-start(bf16[16,104,768]{2,1,0:T(8,128)(2,1)} %pad_dynamic-update-slice_fusion.7), channel_id=1, source_target_pairs={{0,1},{1,0},{2,3},{3,2},{4,5},{5,4},{6,7},{7,6},{8,9},{9,8},{10,11... | collective-permute-start | bytes 7667720 | tf_op jit(solution)/shard_map/ppermute | solution.py:95
  716.6 64.4 %collective-permute-start.51 = (bf16[2,4,104,768]{3,2,1,0:T(8,128)(2,1)}, bf16[2,4,104,768]{3,2,1,0:T(8,128)(2,1)}, u32[]{:S(2)}, u32[]{:S(2)}) collective-permute-start(bf16[2,4,104,768]{3,2,1,0:T(8,128)(2,1)} %get-tuple-element.515), channel_id=1, source_target_pairs={{0,4},{4,0},{8,12},{12,8},{16,20},{20,16},{24,28},{28,24},{1,5},{5... | collective-permute-start | bytes 3833864 | tf_op jit(solution)/shard_map/ppermute | solution.py:95
  727.5 20.9 %collective-permute-start.86 = (bf16[2,2,2,24,384]{4,3,0,2,1:T(8,128)(2,1)S(1)}, bf16[2,2,2,24,384]{4,3,0,2,1:T(8,128)(2,1)S(1)}, u32[]{:S(2)}, u32[]{:S(2)}) collective-permute-start(bf16[2,2,2,24,384]{4,3,0,2,1:T(8,128)(2,1)S(1)} %copy.418), channel_id=1, source_target_pairs={{0,1},{1,0},{2,3},{3,2},{4,5},{5,4},{6,7},{7,6},{8,9},{9,8},{10,11... | collective-permute-start | bytes 442376 | tf_op jit(solution)/shard_map/ppermute | solution.py:95
  763.8 31.4 %collective-permute-start.50 = (bf16[2,4,104,768]{3,2,1,0:T(8,128)(2,1)}, bf16[2,4,104,768]{3,2,1,0:T(8,128)(2,1)}, u32[]{:S(2)}, u32[]{:S(2)}) collective-permute-start(bf16[2,4,104,768]{3,2,1,0:T(8,128)(2,1)} %bitcast.616), channel_id=1, source_target_pairs={{0,2},{1,3},{2,0},{3,1},{4,6},{5,7},{6,4},{7,5},{8,10},{9,11},{10,... | collective-permute-start | bytes 3833864 | tf_op jit(solution)/shard_map/ppermute | solution.py:95
  778.5 78.4 %collective-permute-start.54 = (bf16[2,2,2,96,1536]{4,3,0,2,1:T(8,128)(2,1)}, bf16[2,2,2,96,1536]{4,3,0,2,1:T(8,128)(2,1)}, u32[]{:S(2)}, u32[]{:S(2)}) collective-permute-start(bf16[2,2,2,96,1536]{4,3,0,2,1:T(8,128)(2,1)} %copy.391), channel_id=1, source_target_pairs={{0,1},{1,0},{2,3},{3,2},{4,5},{5,4},{6,7},{7,6},{8,9},{9,8},{10,11... | collective-permute-start | bytes 7077896 | tf_op jit(solution)/shard_map/ppermute | solution.py:95
  783.6 51.8 %collective-permute-start.53 = (bf16[4,104,768]{2,1,0:T(8,128)(2,1)}, bf16[4,104,768]{2,1,0:T(8,128)(2,1)}, u32[]{:S(2)}, u32[]{:S(2)}) collective-permute-start(bf16[4,104,768]{2,1,0:T(8,128)(2,1)} %get-tuple-element.527), channel_id=1, source_target_pairs={{0,2},{1,3},{2,0},{3,1},{4,6},{5,7},{6,4},{7,5},{8,10},{9,11},{10,... | collective-permute-start | bytes 1916936 | tf_op jit(solution)/shard_map/ppermute | solution.py:95
  802.1 34.6 %collective-permute-start.52 = (bf16[4,104,768]{2,1,0:T(8,128)(2,1)}, bf16[4,104,768]{2,1,0:T(8,128)(2,1)}, u32[]{:S(2)}, u32[]{:S(2)}) collective-permute-start(bf16[4,104,768]{2,1,0:T(8,128)(2,1)} %get-tuple-element.529), channel_id=1, source_target_pairs={{0,4},{4,0},{8,12},{12,8},{16,20},{20,16},{24,28},{28,24},{1,5},{5... | collective-permute-start | bytes 1916936 | tf_op jit(solution)/shard_map/ppermute | solution.py:95
  828.6 135.8 %collective-permute-start.61 = (bf16[16,104,768]{2,1,0:T(8,128)(2,1)}, bf16[16,104,768]{2,1,0:T(8,128)(2,1)}, u32[]{:S(2)}, u32[]{:S(2)}) collective-permute-start(bf16[16,104,768]{2,1,0:T(8,128)(2,1)} %pad_dynamic-update-slice_fusion), channel_id=1, source_target_pairs={{0,1},{1,0},{2,3},{3,2},{4,5},{5,4},{6,7},{7,6},{8,9},{9,8},{10,11... | collective-permute-start | bytes 7667720 | tf_op jit(solution)/shard_map/ppermute | solution.py:95
  829.3 142.3 %collective-permute-start.59 = (bf16[16,104,768]{2,1,0:T(8,128)(2,1)}, bf16[16,104,768]{2,1,0:T(8,128)(2,1)}, u32[]{:S(2)}, u32[]{:S(2)}) collective-permute-start(bf16[16,104,768]{2,1,0:T(8,128)(2,1)} %pad_dynamic-update-slice_fusion.2), channel_id=1, source_target_pairs={{0,1},{1,0},{2,3},{3,2},{4,5},{5,4},{6,7},{7,6},{8,9},{9,8},{10,11... | collective-permute-start | bytes 7667720 | tf_op jit(solution)/shard_map/ppermute | solution.py:95
  838.2 17.9 %collective-permute-start.56 = (bf16[2,104,768]{2,1,0:T(8,128)(2,1)S(1)}, bf16[2,104,768]{2,1,0:T(8,128)(2,1)S(1)}, u32[]{:S(2)}, u32[]{:S(2)}) collective-permute-start(bf16[2,104,768]{2,1,0:T(8,128)(2,1)S(1)} %get-tuple-element.591), channel_id=1, source_target_pairs={{0,8},{4,12},{8,0},{12,4},{16,24},{20,28},{24,16},{28,20},{1,9},{5... | collective-permute-start | bytes 958472 | tf_op jit(solution)/shard_map/ppermute | solution.py:95
  861.5 27.3 %collective-permute-start.55 = (bf16[2,2,96,1536]{3,2,1,0:T(8,128)(2,1)}, bf16[2,2,96,1536]{3,2,1,0:T(8,128)(2,1)S(1)}, u32[]{:S(2)}, u32[]{:S(2)}) collective-permute-start(bf16[2,2,96,1536]{3,2,1,0:T(8,128)(2,1)} %copy.392), channel_id=1, source_target_pairs={{0,4},{4,0},{8,12},{12,8},{16,20},{20,16},{24,28},{28,24},{1,5},{5... | collective-permute-start | bytes 3538952 | tf_op jit(solution)/shard_map/ppermute | solution.py:95
  930.7 37.2 %collective-permute-start.58 = (bf16[2,96,1536]{2,1,0:T(8,128)(2,1)}, bf16[2,96,1536]{2,1,0:T(8,128)(2,1)}, u32[]{:S(2)}, u32[]{:S(2)}) collective-permute-start(bf16[2,96,1536]{2,1,0:T(8,128)(2,1)} %get-tuple-element.537), channel_id=1, source_target_pairs={{0,8},{4,12},{8,0},{12,4},{16,24},{20,28},{24,16},{28,20},{1,9},{5... | collective-permute-start | bytes 1769480 | tf_op jit(solution)/shard_map/ppermute | solution.py:95
  964.3 24.1 %collective-permute-start.85 = (bf16[24,384]{1,0:T(8,128)(2,1)S(1)}, bf16[24,384]{1,0:T(8,128)(2,1)S(1)}, u32[]{:S(2)}, u32[]{:S(2)}) collective-permute-start(bf16[24,384]{1,0:T(8,128)(2,1)S(1)} %add_convert_fusion.40), channel_id=1, source_target_pairs={{0,1},{1,0},{2,3},{3,2},{4,5},{5,4},{6,7},{7,6},{8,9},{9,8},{10,11... | collective-permute-start | bytes 55304 | tf_op jit(solution)/shard_map/ppermute | solution.py:95
  966.9 46.4 %collective-permute-start.62 = (bf16[2,4,104,768]{3,2,1,0:T(8,128)(2,1)S(1)}, bf16[2,4,104,768]{3,2,1,0:T(8,128)(2,1)S(1)}, u32[]{:S(2)}, u32[]{:S(2)}) collective-permute-start(bf16[2,4,104,768]{3,2,1,0:T(8,128)(2,1)S(1)} %get-tuple-element.513), channel_id=1, source_target_pairs={{0,4},{4,0},{8,12},{12,8},{16,20},{20,16},{24,28},{28,24},{1,5},{5... | collective-permute-start | bytes 3833864 | tf_op jit(solution)/shard_map/ppermute | solution.py:95
  968.9 16.4 %collective-permute-start.77 = (bf16[96,1536]{1,0:T(8,128)(2,1)S(1)}, bf16[96,1536]{1,0:T(8,128)(2,1)S(1)}, u32[]{:S(2)}, u32[]{:S(2)}) collective-permute-start(bf16[96,1536]{1,0:T(8,128)(2,1)S(1)} %fusion.159), channel_id=1, source_target_pairs={{0,16},{4,20},{8,24},{12,28},{16,0},{20,4},{24,8},{28,12},{1,17},{... | collective-permute-start | bytes 884744 | tf_op jit(solution)/shard_map/ppermute | solution.py:95
  975.0 41.4 %collective-permute-start.60 = (bf16[2,4,104,768]{3,2,1,0:T(8,128)(2,1)S(1)}, bf16[2,4,104,768]{3,2,1,0:T(8,128)(2,1)S(1)}, u32[]{:S(2)}, u32[]{:S(2)}) collective-permute-start(bf16[2,4,104,768]{3,2,1,0:T(8,128)(2,1)S(1)} %bitcast.617), channel_id=1, source_target_pairs={{0,2},{1,3},{2,0},{3,1},{4,6},{5,7},{6,4},{7,5},{8,10},{9,11},{10,... | collective-permute-start | bytes 3833864 | tf_op jit(solution)/shard_map/ppermute | solution.py:95
  986.4 24.8 %collective-permute-start.78 = (bf16[96,1536]{1,0:T(8,128)(2,1)S(1)}, bf16[96,1536]{1,0:T(8,128)(2,1)S(1)}, u32[]{:S(2)}, u32[]{:S(2)}) collective-permute-start(bf16[96,1536]{1,0:T(8,128)(2,1)S(1)} %fusion.135), channel_id=1, source_target_pairs={{0,2},{1,3},{2,0},{3,1},{4,6},{5,7},{6,4},{7,5},{8,10},{9,11},{10,... | collective-permute-start | bytes 884744 | tf_op jit(solution)/shard_map/ppermute | solution.py:95
  1014.8 74.3 %collective-permute-start.66 = (bf16[4,104,768]{2,1,0:T(8,128)(2,1)}, bf16[4,104,768]{2,1,0:T(8,128)(2,1)}, u32[]{:S(2)}, u32[]{:S(2)}) collective-permute-start(bf16[4,104,768]{2,1,0:T(8,128)(2,1)} %get-tuple-element.525), channel_id=1, source_target_pairs={{0,2},{1,3},{2,0},{3,1},{4,6},{5,7},{6,4},{7,5},{8,10},{9,11},{10,... | collective-permute-start | bytes 1916936 | tf_op jit(solution)/shard_map/ppermute | solution.py:95
  1035.0 55.5 %collective-permute-start.63 = (bf16[4,104,768]{2,1,0:T(8,128)(2,1)}, bf16[4,104,768]{2,1,0:T(8,128)(2,1)}, u32[]{:S(2)}, u32[]{:S(2)}) collective-permute-start(bf16[4,104,768]{2,1,0:T(8,128)(2,1)} %get-tuple-element.523), channel_id=1, source_target_pairs={{0,4},{4,0},{8,12},{12,8},{16,20},{20,16},{24,28},{28,24},{1,5},{5... | collective-permute-start | bytes 1916936 | tf_op jit(solution)/shard_map/ppermute | solution.py:95
  1085.2 46.0 %collective-permute-start.71 = (bf16[2,2,2,96,1536]{4,3,0,2,1:T(8,128)(2,1)}, bf16[2,2,2,96,1536]{4,3,0,2,1:T(8,128)(2,1)}, u32[]{:S(2)}, u32[]{:S(2)}) collective-permute-start(bf16[2,2,2,96,1536]{4,3,0,2,1:T(8,128)(2,1)} %copy.404), channel_id=1, source_target_pairs={{0,1},{1,0},{2,3},{3,2},{4,5},{5,4},{6,7},{7,6},{8,9},{9,8},{10,11... | collective-permute-start | bytes 7077896 | tf_op jit(solution)/shard_map/ppermute | solution.py:95
  1091.7 18.3 %collective-permute-start.64 = (bf16[2,104,768]{2,1,0:T(8,128)(2,1)S(1)}, bf16[2,104,768]{2,1,0:T(8,128)(2,1)S(1)}, u32[]{:S(2)}, u32[]{:S(2)}) collective-permute-start(bf16[2,104,768]{2,1,0:T(8,128)(2,1)S(1)} %get-tuple-element.587), channel_id=1, source_target_pairs={{0,8},{4,12},{8,0},{12,4},{16,24},{20,28},{24,16},{28,20},{1,9},{5... | collective-permute-start | bytes 958472 | tf_op jit(solution)/shard_map/ppermute | solution.py:95
  1093.9 25.3 %collective-permute-start.93 = (bf16[2,2,32,1536]{3,2,1,0:T(8,128)(2,1)S(1)}, bf16[2,2,32,1536]{3,2,1,0:T(8,128)(2,1)S(1)}, u32[]{:S(2)}, u32[]{:S(2)}) collective-permute-start(bf16[2,2,32,1536]{3,2,1,0:T(8,128)(2,1)S(1)} %fusion.149), channel_id=1, source_target_pairs={{0,4},{4,0},{8,12},{12,8},{16,20},{20,16},{24,28},{28,24},{1,5},{5... | collective-permute-start | bytes 1179656 | tf_op jit(solution)/shard_map/ppermute | solution.py:95
  1127.6 68.8 %all-to-all-start.7 = ((bf16[32,32,768]{2,1,0:T(8,128)(2,1)}), bf16[32,32,768]{2,1,0:T(8,128)(2,1)}, u32[]{:S(2)}, u32[]{:S(2)}) async-start(bf16[32,32,768]{2,1,0:T(8,128)(2,1)} %bitcast.602), calls=%async_computation.7 | async-start | bytes 3145728 | tf_op jit(solution)/shard_map/all_to_all | solution.py:530
  1135.8 40.3 %collective-permute-start.72 = (bf16[2,2,96,1536]{3,2,1,0:T(8,128)(2,1)}, bf16[2,2,96,1536]{3,2,1,0:T(8,128)(2,1)}, u32[]{:S(2)}, u32[]{:S(2)}) collective-permute-start(bf16[2,2,96,1536]{3,2,1,0:T(8,128)(2,1)} %copy.406), channel_id=1, source_target_pairs={{0,4},{4,0},{8,12},{12,8},{16,20},{20,16},{24,28},{28,24},{1,5},{5... | collective-permute-start | bytes 3538952 | tf_op jit(solution)/shard_map/ppermute | solution.py:95
  1152.3 27.7 %collective-permute-start.97 = (bf16[32,1536]{1,0:T(8,128)(2,1)S(1)}, bf16[32,1536]{1,0:T(8,128)(2,1)S(1)}, u32[]{:S(2)}, u32[]{:S(2)}) collective-permute-start(bf16[32,1536]{1,0:T(8,128)(2,1)S(1)} %add_convert_fusion.34), channel_id=1, source_target_pairs={{0,1},{1,0},{2,3},{3,2},{4,5},{5,4},{6,7},{7,6},{8,9},{9,8},{10,11... | collective-permute-start | bytes 294920 | tf_op jit(solution)/shard_map/ppermute | solution.py:95
  (475 other events, 5356.9 us)

commit v2 on v1

--- a/solution.py
+++ b/solution.py
@@ -1,3 +1,4 @@
+import functools
 import math
 
 import jax
@@ -37,19 +38,116 @@
         (2, LAYOUT_WIDTH),
         (PAGE_SLOTS, WIDTH),
         (PAGE_SLOTS, LAYOUT_WIDTH),
-        (2, BOXES, LAYOUT_WIDTH // 4),
+        (2, BOXES // 8, 2 * LAYOUT_WIDTH),
         (LAYOUT_WIDTH, WIDTH),
     ]
 
 
-def unpack_small(flat_vec):
-    pieces = []
+def small_views():
+    views = []
     offset = 0
     for piece_dims in small_shapes():
         amount = math.prod(piece_dims)
-        pieces.append(flat_vec[offset : offset + amount].reshape(piece_dims))
+        width = piece_dims[-1] if piece_dims[-1] % 128 == 0 else 2 * piece_dims[-1]
+        views.append((offset // 128, amount // width, width))
         offset = offset + amount
-    return pieces
+    return views, offset // 128
+
+
+def small_half_rows(share):
+    return -(-share // (128 * 32)) * 16
+
+
+def pack_small(items, dp):
+    views, total = small_views()
+    share = total * 128 // dp
+    rows = 2 * small_half_rows(share)
+
+    def kernel(*refs):
+        sources, out_ref, flat = refs[: len(items)], refs[len(items)], refs[len(items) + 1]
+        flat[total:, :] = jnp.zeros((flat.shape[0] - total, 128), jnp.float32)
+        for source, (start, count, width) in zip(sources, views):
+            per = width // 128
+            for part in range(per):
+                flat[pl.ds(start + part, count, stride=per), :] = source[
+                    :, part * 128 : (part + 1) * 128
+                ]
+        column = lax.broadcasted_iota(jnp.int32, (rows, 128), 1)
+        for number in range(dp):
+            start, shift = number * share // 128, number * share % 128
+            block = flat[pl.ds(start, rows), :]
+            if shift:
+                after = flat[pl.ds(start + 1, rows), :]
+                block = jnp.where(
+                    column < 128 - shift,
+                    pltpu.roll(block, 128 - shift, 1),
+                    pltpu.roll(after, 128 - shift, 1),
+                )
+            out_ref[number] = block.astype(out_ref.dtype)
+
+    whole = pl.BlockSpec(memory_space=pltpu.VMEM)
+    return pl.pallas_call(
+        kernel,
+        out_shape=jax.ShapeDtypeStruct((dp, rows, 128), jnp.bfloat16),
+        in_specs=[whole] * len(items),
+        out_specs=whole,
+        scratch_shapes=[pltpu.VMEM((total + rows + 8, 128), jnp.float32)],
+        cost_estimate=pl.CostEstimate(flops=0, bytes_accessed=2000000, transcendentals=0),
+        compiler_params=pltpu.CompilerParams(vmem_limit_bytes=32 * 1024 * 1024),
+    )(*[item.reshape(count, width) for item, (start, count, width) in zip(items, views)])
+
+
+def unpack_small(own, came, places, extra_rows):
+    views, total = small_views()
+    dp = own.shape[0]
+    share = total * 128 // dp
+    half = small_half_rows(share)
+
+    def kernel(place_ref, own_ref, came_ref, *refs):
+        targets, extra_ref, flat, turned = refs[:-3], refs[-3], refs[-2], refs[-1]
+        mine = [(place_ref[dp] == side).astype(jnp.float32) for side in range(2)]
+        for number in range(dp):
+            start, shift = number * share // 128, number * share % 128
+            rows = -(-(share + shift) // 128)
+            slot = place_ref[number]
+            for side in range(2):
+                both = own_ref[slot].astype(jnp.float32), came_ref[slot].astype(jnp.float32)
+                whole = jnp.where(mine[side] > 0.5, *both)
+                extra_ref[side, number] = whole[half : half + extra_rows].astype(extra_ref.dtype)
+                part = whole[:half]
+                turned[pl.ds(8 + side * half, half), :] = (
+                    pltpu.roll(part, shift, 1) if shift else part
+                )
+            block = turned[pl.ds(8, rows), :]
+            if shift:
+                turned[7:8, :] = flat[pl.ds(start, 1), :]
+                column = lax.broadcasted_iota(jnp.int32, (rows, 128), 1)
+                block = jnp.where(column >= shift, block, turned[pl.ds(7, rows), :])
+            flat[pl.ds(start, rows), :] = block
+        for target, (start, count, width) in zip(targets, views):
+            per = width // 128
+            for part in range(per):
+                target[:, part * 128 : (part + 1) * 128] = flat[
+                    pl.ds(start + part, count, stride=per), :
+                ]
+
+    whole = pl.BlockSpec(memory_space=pltpu.VMEM)
+    *outs, extra = pl.pallas_call(
+        kernel,
+        out_shape=[
+            jax.ShapeDtypeStruct((count, width), jnp.float32) for start, count, width in views
+        ]
+        + [jax.ShapeDtypeStruct((2, dp, extra_rows, 128), jnp.bfloat16)],
+        in_specs=[pl.BlockSpec(memory_space=pltpu.SMEM), whole, whole],
+        out_specs=[whole] * (len(views) + 1),
+        scratch_shapes=[
+            pltpu.VMEM((total + 8, 128), jnp.float32),
+            pltpu.VMEM((2 * half + 16, 128), jnp.float32),
+        ],
+        cost_estimate=pl.CostEstimate(flops=0, bytes_accessed=2000000, transcendentals=0),
+        compiler_params=pltpu.CompilerParams(vmem_limit_bytes=32 * 1024 * 1024),
+    )(places, own, came)
+    return [item.reshape(piece_dims) for item, piece_dims in zip(outs, small_shapes())], extra
 
 
 def norm_apply(values, gain_row, bias_row):
@@ -128,31 +226,156 @@
 def put_in_order(own, came, places):
     slots, rows, width = own.shape
 
-    def kernel(place_ref, own_ref, came_ref, out_ref):
-        mine = place_ref[slots] == pl.program_id(0)
-
-        @pl.when(mine)
-        def _():
-            out_ref[...] = own_ref[...]
-
-        @pl.when(jnp.logical_not(mine))
-        def _():
-            out_ref[...] = came_ref[...]
-
-    piece = pl.BlockSpec((1, rows, width), lambda half, spot, place: (place[spot], 0, 0))
+    def kernel(place_ref, own_ref, came_ref, out_ref, sems):
+        side = place_ref[slots]
+
+        def copies(half, source):
+            return [
+                pltpu.make_async_copy(
+                    source.at[place_ref[spot]],
+                    out_ref.at[half, pl.ds(spot * rows, rows)],
+                    sems.at[half, spot],
+                )
+                for spot in range(slots)
+            ]
+
+        for half in range(2):
+            for mine, source in ((True, own_ref), (False, came_ref)):
+
+                @pl.when((side == half) == mine)
+                def _(half=half, source=source):
+                    for copy in copies(half, source):
+                        copy.start()
+
+        for half in range(2):
+            for copy in copies(half, own_ref):
+                copy.wait()
+
+    anywhere = pl.BlockSpec(memory_space=pl.ANY)
     return pl.pallas_call(
         kernel,
         out_shape=jax.ShapeDtypeStruct((2, slots * rows, width), own.dtype),
-        grid_spec=pltpu.PrefetchScalarGridSpec(
-            num_scalar_prefetch=1,
-            grid=(2, slots),
-            in_specs=[piece, piece],
-            out_specs=pl.BlockSpec((1, rows, width), lambda half, spot, place: (half, spot, 0)),
+        in_specs=[pl.BlockSpec(memory_space=pltpu.SMEM), anywhere, anywhere],
+        out_specs=pl.BlockSpec(memory_space=pltpu.VMEM),
+        scratch_shapes=[pltpu.SemaphoreType.DMA((2, slots))],
+        cost_estimate=pl.CostEstimate(
+            flops=0, bytes_accessed=2 * slots * rows * width, transcendentals=0
         ),
+        compiler_params=pltpu.CompilerParams(vmem_limit_bytes=16 * 1024 * 1024),
+    )(places, own, came)
+
+
+def embed_kernel(
+    coords, embedded, text_pos, layout_pos, tables, text_emb, layout_emb, *outs
+):
+    text_pre, layout_pre, text, layout = outs
+    quarter = LAYOUT_WIDTH // 4
+    low = jnp.bfloat16
+    row = lax.broadcasted_iota(jnp.int32, (PAGE_SLOTS, BOXES // 8), 1)
+    lanes = lax.broadcasted_iota(jnp.int32, (PAGE_SLOTS, 8 * quarter), 1) // quarter
+    fold_in = lax.broadcasted_iota(jnp.int32, (8 * quarter, LAYOUT_WIDTH), 0) % quarter
+    fold_out = lax.broadcasted_iota(jnp.int32, (8 * quarter, LAYOUT_WIDTH), 1)
+    looked = jnp.zeros((PAGE_SLOTS, LAYOUT_WIDTH), jnp.float32)
+    for number in range(4):
+        spot = coords[:, number : number + 1]
+        marks = (spot // 8 == row).astype(jnp.float32).astype(low)
+        wide = jnp.dot(
+            marks, tables[number % 2].astype(low), preferred_element_type=jnp.float32
+        )
+        kept = jnp.where(spot % 8 == lanes, wide, 0.0).astype(low)
+        fold = (fold_in + number * quarter == fold_out).astype(jnp.float32).astype(low)
+        looked = looked + jnp.dot(kept, fold, preferred_element_type=jnp.float32)
+    layout_pre[...] = looked + layout_pos[...]
+    text_pre[...] = embedded[...] + text_pos[...]
+    text[...] = norm_apply(text_pre[...], text_emb[0:1, :], text_emb[1:2, :])
+    layout[...] = norm_apply(layout_pre[...], layout_emb[0:1, :], layout_emb[1:2, :])
+
+
+def embed_streams(*operands):
+    whole = pl.BlockSpec(memory_space=pltpu.VMEM)
+    return pl.pallas_call(
+        embed_kernel,
+        out_shape=[
+            jax.ShapeDtypeStruct((PAGE_SLOTS, width), jnp.float32)
+            for width in (WIDTH, LAYOUT_WIDTH) * 2
+        ],
+        in_specs=[whole] * len(operands),
+        out_specs=[whole] * 4,
+        cost_estimate=pl.CostEstimate(flops=0, bytes_accessed=2000000, transcendentals=0),
+        compiler_params=pltpu.CompilerParams(vmem_limit_bytes=24 * 1024 * 1024),
+    )(*operands)
+
+
+def mats_kernel(side, rows, query, keys, values, att, first, sent_ref, kept_ref, result):
+    step = pl.program_id(0)
+    half = jnp.where(step < 2, 1 - side[0], side[0])
+    cases = ((rows, query), (rows, keys), (rows, values), (att, first))
+    for number, (left, right) in enumerate(cases):
+
+        @pl.when(half * 2 + step % 2 == number)
+        def _(left=left, right=right):
+            result[...] = contract_rows(left[...], right[...])
+
+    def store(target):
+        blocks = result[...].astype(target.dtype).reshape(target.shape[0], -1, WIDTH)
+        target[:, : blocks.shape[1], :] = blocks
+
+    @pl.when(step < 2)
+    def _():
+        store(sent_ref)
+
+    @pl.when(step >= 2)
+    def _():
+        store(kept_ref)
+
+
+def mats_sums(side, operands, padded):
+    dp = lax.axis_size("dp")
+    whole = pl.BlockSpec((PAGE_SLOTS, WIDTH), lambda step: (0, 0))
+    shape = jax.ShapeDtypeStruct((dp, padded, 2 * WIDTH), jnp.bfloat16)
+    return pl.pallas_call(
+        mats_kernel,
+        grid=(4,),
+        in_specs=[pl.BlockSpec(memory_space=pltpu.SMEM)] + [whole] * 6,
+        out_specs=[
+            pl.BlockSpec((dp, padded, WIDTH), lambda step: (0, 0, jnp.minimum(step, 1))),
+            pl.BlockSpec((dp, padded, WIDTH), lambda step: (0, 0, jnp.maximum(step - 2, 0))),
+        ],
+        out_shape=[shape, shape],
+        scratch_shapes=[pltpu.VMEM((WIDTH, WIDTH), jnp.float32)],
         cost_estimate=pl.CostEstimate(
-            flops=0, bytes_accessed=12 * slots * rows * width, transcendentals=0
+            flops=2 * PAGE_SLOTS * WIDTH * WIDTH, bytes_accessed=4000000, transcendentals=0
         ),
-    )(places, own, came)
+        compiler_params=pltpu.CompilerParams(vmem_limit_bytes=32 * 1024 * 1024),
+    )(side, *operands)
+
+
+def take_extra(pieces, rows):
+    slots, total, width = pieces[0].shape
+
+    def kernel(*refs):
+        out_ref, sems = refs[-2], refs[-1]
+        copies = [
+            pltpu.make_async_copy(
+                ref.at[:, pl.ds(rows, total - rows)],
+                out_ref.at[pl.ds(number * slots, slots)],
+                sems.at[number],
+            )
+            for number, ref in enumerate(refs[:-2])
+        ]
+        for copy in copies:
+            copy.start()
+        for copy in copies:
+            copy.wait()
+
+    return pl.pallas_call(
+        kernel,
+        out_shape=jax.ShapeDtypeStruct((slots * len(pieces), total - rows, width), pieces[0].dtype),
+        in_specs=[pl.BlockSpec(memory_space=pl.ANY)] * len(pieces),
+        out_specs=pl.BlockSpec(memory_space=pltpu.VMEM),
+        scratch_shapes=[pltpu.SemaphoreType.DMA((len(pieces),))],
+        cost_estimate=pl.CostEstimate(flops=0, bytes_accessed=500000, transcendentals=0),
+    )(*pieces)
 
 
 HEAD_PAIRS = HEADS // 2
@@ -160,17 +383,9 @@
 LAYOUT_HEAD = LAYOUT_WIDTH // HEADS
 
 
-def pair_split(values):
-    return values.reshape(PAGE_SLOTS, HEAD_PAIRS, 2 * LAYOUT_HEAD).transpose(1, 0, 2)
-
-
-def pair_join(values):
-    return values.transpose(1, 0, 2).reshape(PAGE_SLOTS, LAYOUT_WIDTH)
-
-
 def head_of(text_ref, layout_ref, head, scaled=False):
     text = text_ref[:, head * TEXT_HEAD : (head + 1) * TEXT_HEAD]
-    layout = layout_ref[0, :, head * LAYOUT_HEAD : (head + 1) * LAYOUT_HEAD]
+    layout = layout_ref[:, head * LAYOUT_HEAD : (head + 1) * LAYOUT_HEAD]
     if scaled:
         text_scale, layout_scale = scale_pair()
         text = (text.astype(jnp.float32) * text_scale).astype(text.dtype)
@@ -182,12 +397,28 @@
     text_ref[...] = jnp.concatenate([item[:, :TEXT_HEAD] for item in both], 1).astype(
         text_ref.dtype
     )
-    layout_ref[0] = jnp.concatenate([item[:, TEXT_HEAD:] for item in both], 1).astype(
-        layout_ref.dtype
-    )
-
-
-def attend_kernel(length, qt, kt, vt, ql, kl, vl, out_t, out_l, lse):
+    layout = jnp.concatenate([item[:, TEXT_HEAD:] for item in both], 1).astype(layout_ref.dtype)
+    width = layout.shape[1]
+    for pair in range(HEAD_PAIRS):
+
+        @pl.when(pl.program_id(0) == pair)
+        def _(pair=pair):
+            layout_ref[:, pair * width : (pair + 1) * width] = layout
+
+
+def own_pair(sources, targets):
+    width = targets[0].shape[1]
+    for pair in range(HEAD_PAIRS):
+
+        @pl.when(pl.program_id(0) == pair)
+        def _(pair=pair):
+            for source, target in zip(sources, targets):
+                target[...] = source[:, pair * width : (pair + 1) * width]
+
+
+def attend_kernel(length, qt, kt, vt, *refs):
+    out_t, out_l, lse, ql, kl, vl = refs[3:]
+    own_pair(refs[:3], (ql, kl, vl))
     live = lax.broadcasted_iota(jnp.int32, (PAGE_SLOTS, PAGE_SLOTS), 1) < length[0]
     outs = []
     for head in range(2):
@@ -204,8 +435,9 @@
     store_heads(out_t, out_l, outs)
 
 
-def attend_back_kernel(length, qt, kt, vt, ql, kl, vl, got, gol, lse, *outs):
-    dqt, dkt, dvt, dql, dkl, dvl = outs
+def attend_back_kernel(length, qt, kt, vt, got, *refs):
+    lse, dqt, dkt, dvt, dql, dkl, dvl, ql, kl, vl, gol = refs[4:]
+    own_pair(refs[:4], (ql, kl, vl, gol))
     text_scale, layout_scale = scale_pair()
     live = lax.broadcasted_iota(jnp.int32, (PAGE_SLOTS, PAGE_SLOTS), 0) < length[0]
     column = lax.broadcasted_iota(jnp.int32, (1, TEXT_HEAD + LAYOUT_HEAD), 1)
@@ -231,12 +463,12 @@
 
 def pair_specs():
     text = pl.BlockSpec((PAGE_SLOTS, 2 * TEXT_HEAD), lambda step: (0, step))
-    layout = pl.BlockSpec((1, PAGE_SLOTS, 2 * LAYOUT_HEAD), lambda step: (step, 0, 0))
-    return text, layout
+    layout = pl.BlockSpec((PAGE_SLOTS, LAYOUT_WIDTH), lambda step: (0, 0))
+    return text, layout, pltpu.VMEM((PAGE_SLOTS, 2 * LAYOUT_HEAD), jnp.bfloat16)
 
 
 def attend(text_qkv, layout_qkv, lengths):
-    text, layout = pair_specs()
+    text, layout, pair = pair_specs()
     low = jnp.bfloat16
     out_t, out_l, lse = pl.pallas_call(
         attend_kernel,
@@ -245,44 +477,39 @@
         out_specs=[text, layout, pl.BlockSpec((1, PAGE_SLOTS, 2), lambda step: (step, 0, 0))],
         out_shape=[
             jax.ShapeDtypeStruct((PAGE_SLOTS, WIDTH), low),
-            jax.ShapeDtypeStruct((HEAD_PAIRS, PAGE_SLOTS, 2 * LAYOUT_HEAD), low),
+            jax.ShapeDtypeStruct((PAGE_SLOTS, LAYOUT_WIDTH), low),
             jax.ShapeDtypeStruct((HEAD_PAIRS, PAGE_SLOTS, 2), jnp.float32),
         ],
+        scratch_shapes=[pair] * 3,
         cost_estimate=pl.CostEstimate(
-            flops=12000000000, bytes_accessed=8000000, transcendentals=3200000
+            flops=4000000000, bytes_accessed=2000000, transcendentals=100000
         ),
         compiler_params=pltpu.CompilerParams(vmem_limit_bytes=24 * 1024 * 1024),
-    )(lengths, *text_qkv, *[pair_split(item) for item in layout_qkv])
-    return (out_t, pair_join(out_l), lse.transpose(0, 2, 1))
+    )(lengths, *text_qkv, *layout_qkv)
+    return (out_t, out_l, lse.transpose(0, 2, 1))
 
 
 def attend_back(text_qkv, layout_qkv, lengths, lse, text_grad, layout_grad):
-    text, layout = pair_specs()
+    text, layout, pair = pair_specs()
     low = jnp.bfloat16
     text_out = jax.ShapeDtypeStruct((PAGE_SLOTS, WIDTH), low)
-    layout_out = jax.ShapeDtypeStruct((HEAD_PAIRS, PAGE_SLOTS, 2 * LAYOUT_HEAD), low)
+    layout_out = jax.ShapeDtypeStruct((PAGE_SLOTS, LAYOUT_WIDTH), low)
     outs = pl.pallas_call(
         attend_back_kernel,
         grid=(HEAD_PAIRS,),
         in_specs=[pl.BlockSpec(memory_space=pltpu.SMEM)]
-        + [text] * 3
-        + [layout] * 3
-        + [text, layout, pl.BlockSpec((1, 2, PAGE_SLOTS), lambda step: (step, 0, 0))],
+        + [text] * 4
+        + [layout] * 4
+        + [pl.BlockSpec((1, 2, PAGE_SLOTS), lambda step: (step, 0, 0))],
         out_specs=[text] * 3 + [layout] * 3,
         out_shape=[text_out] * 3 + [layout_out] * 3,
+        scratch_shapes=[pair] * 4,
         cost_estimate=pl.CostEstimate(
-            flops=20000000000, bytes_accessed=14000000, transcendentals=3200000
+            flops=5000000000, bytes_accessed=3000000, transcendentals=100000
         ),
         compiler_params=pltpu.CompilerParams(vmem_limit_bytes=32 * 1024 * 1024),
-    )(
-        lengths,
-        *text_qkv,
-        *[pair_split(item) for item in layout_qkv],
-        text_grad,
-        pair_split(layout_grad),
-        lse,
-    )
-    return (list(outs[:3]), [pair_join(item) for item in outs[3:]])
+    )(lengths, *text_qkv, text_grad, *layout_qkv, layout_grad, lse)
+    return (list(outs[:3]), list(outs[3:]))
 
 
 ERF_TERMS = (0.254829592, -0.284496736, 1.421413741, -1.453152027, 1.061405429)
@@ -300,9 +527,63 @@
     return (values * share, share + values * bell * (1.0 / math.sqrt(2.0 * math.pi)))
 
 
-def ffn_kernel(rows_ref, in_ref, out_ref, bias_ref, hidden_ref, slope_ref, part_ref):
-    width = rows_ref.shape[1]
-    units_in, units_out = in_ref[...], out_ref[...]
+def load_units(pieces_in, pieces_out, rows, buffers, sems, chunks):
+    per = len(pieces_in) // chunks
+    slots = pieces_in[0].shape[0]
+    step = pl.program_id(0)
+
+    def copies(turn):
+        made = []
+        for number in range(per):
+            for side, pieces in enumerate((pieces_in, pieces_out)):
+                made.append(
+                    pltpu.make_async_copy(
+                        pieces[turn * per + number].at[:, pl.ds(0, rows)],
+                        buffers[side].at[turn % 2, pl.ds(number * slots, slots)],
+                        sems.at[turn % 2, 2 * number + side],
+                    )
+                )
+        return made
+
+    for turn in range(chunks):
+
+        @pl.when(step == turn)
+        def _(turn=turn):
+            if turn == 0:
+                for copy in copies(0):
+                    copy.start()
+            if turn + 1 < chunks:
+                for copy in copies(turn + 1):
+                    copy.start()
+            for copy in copies(turn):
+                copy.wait()
+
+    slot = step % 2
+    return [buffer[slot].reshape(-1, buffer.shape[-1]) for buffer in buffers]
+
+
+def unit_plan(units, chunk, rows, chunks):
+    width = units[0][0].shape[-1] if rows else units[0].shape[-1]
+    if not rows:
+        unit = pl.BlockSpec((chunk, width), lambda step: (step, 0))
+        return list(units), [unit, unit], []
+    anywhere = pl.BlockSpec(memory_space=pl.ANY)
+    operands = list(units[0]) + list(units[1])
+    buffer = pltpu.VMEM((2, chunk // rows, rows, width), jnp.bfloat16)
+    sems = pltpu.SemaphoreType.DMA((2, len(operands) // chunks))
+    return operands, [anywhere] * len(operands), [buffer, buffer, sems]
+
+
+def take_units(refs, scratch, rows, chunks):
+    if not rows:
+        return [ref[...] for ref in refs]
+    half = len(refs) // 2
+    return load_units(refs[:half], refs[half:], rows, scratch[:2], scratch[2], chunks)
+
+
+def ffn_kernel(rows, chunks, count, rows_ref, bias_ref, *refs):
+    hidden_ref, slope_ref, part_ref = refs[count : count + 3]
+    units_in, units_out = take_units(refs[:count], refs[count + 3 :], rows, chunks)
 
     @pl.when(pl.program_id(0) == 0)
     def _():
@@ -310,39 +591,40 @@
 
     step = PAGE_SLOTS // 2
     for number in range(2):
-        rows = pl.ds(number * step, step)
-        pre_act = contract_cols(rows_ref[rows, :], units_in) + bias_ref[...]
+        span = pl.ds(number * step, step)
+        pre_act = contract_cols(rows_ref[span, :], units_in) + bias_ref[...]
         hidden, slope = gelu_pair(pre_act)
         hidden = hidden.astype(jnp.bfloat16)
-        hidden_ref[rows, :] = hidden
-        slope_ref[rows, :] = slope.astype(jnp.bfloat16)
-        part_ref[rows, :] += jnp.dot(hidden, units_out, preferred_element_type=jnp.float32)
-
-
-def ffn_front(rows_in, units, bias_in, chunks):
+        hidden_ref[span, :] = hidden
+        slope_ref[span, :] = slope.astype(jnp.bfloat16)
+        part_ref[span, :] += jnp.dot(hidden, units_out, preferred_element_type=jnp.float32)
+
+
+def ffn_front(rows_in, units, bias_in, chunks, rows):
     slots, width = rows_in.shape
     total = bias_in.shape[0]
     chunk = total // chunks
     whole = pl.BlockSpec((slots, width), lambda step: (0, 0))
     piece = pl.BlockSpec((slots, chunk), lambda step: (0, step))
-    unit = pl.BlockSpec((chunk, width), lambda step: (step, 0))
+    operands, specs, scratch = unit_plan(units, chunk, rows, chunks)
     return pl.pallas_call(
-        ffn_kernel,
+        functools.partial(ffn_kernel, rows, chunks, len(operands)),
         grid=(chunks,),
-        in_specs=[whole, unit, unit, pl.BlockSpec((1, chunk), lambda step: (0, step))],
+        in_specs=[whole, pl.BlockSpec((1, chunk), lambda step: (0, step))] + specs,
         out_specs=[piece, piece, whole],
         out_shape=[
             jax.ShapeDtypeStruct((slots, total), jnp.bfloat16),
             jax.ShapeDtypeStruct((slots, total), jnp.bfloat16),
             jax.ShapeDtypeStruct((slots, width), jnp.float32),
         ],
+        scratch_shapes=scratch,
         cost_estimate=pl.CostEstimate(
-            flops=4 * slots * width * total,
-            bytes_accessed=4 * total * (width + slots),
-            transcendentals=2 * slots * total,
+            flops=slots * width * total,
+            bytes_accessed=total * (width + slots),
+            transcendentals=0,
         ),
         compiler_params=pltpu.CompilerParams(vmem_limit_bytes=40 * 1024 * 1024),
-    )(rows_in, *units, bias_in[None])
+    )(rows_in, bias_in[None], *operands)
 
 
 def tail_route(flip):
@@ -364,13 +646,19 @@
         if self.joined:
             step = self.joined.pop(0)
             (held,) = self.pieces.values()
-            came = hop(held if wait is None else tie(held, wait), *step)
+            held = held if wait is None else tie(held, wait)
+            self.sent = [held]
+            came = hop(held, *step)
             self.pieces = {frozenset(): jnp.concatenate([held, came], 0)}
             self.masks = self.masks + [mask | {step} for mask in self.masks]
             return came
         step = self.apart.pop(0)
+        self.sent = []
         for key, piece in list(self.pieces.items()):
-            came = hop(piece if wait is None else tie(piece, wait), *step)
+            piece = piece if wait is None else tie(piece, wait)
+            self.sent.append(piece)
+            came = hop(piece, *step)
+            self.pieces[key] = piece
             self.pieces[key | {step}] = came
         return came
 
@@ -380,7 +668,7 @@
     return Spread(own, [near] + far if near_first else far + [near], [core])
 
 
-def half_result(chain):
+def half_parts(chain):
     core = routes()[3]
     spot = lax.axis_index("dp")
     masks = [key_mask(mask, "dp") for mask in chain.masks]
@@ -390,8 +678,7 @@
     marks = (spot ^ numbers)[:, None] == numbers[None, :]
     places = jnp.sum(jnp.where(marks, table[None, :], 0), 1, dtype=jnp.int32)
     places = jnp.concatenate([places, own_bit(*core).astype(jnp.int32)[None]])
-    own, came = chain.pieces[frozenset()], chain.pieces[frozenset([core])]
-    return put_in_order(own, came, places)
+    return chain.pieces[frozenset()], chain.pieces[frozenset([core])], places
 
 
 def unit_spread(block, flip):
@@ -406,11 +693,8 @@
     return keys
 
 
-def unit_result(chain, rows):
-    pieces = [chain.pieces[key] for key in unit_keys()]
-    main = jnp.concatenate([piece[:, :rows] for piece in pieces], 0)
-    extra = jnp.concatenate([piece[:, rows:] for piece in pieces], 0)
-    return (main.reshape(-1, main.shape[-1]), extra)
+def unit_result(chain):
+    return [chain.pieces[key] for key in unit_keys()]
 
 
 def unit_blocks():
@@ -430,6 +714,7 @@
         self.order = high + [near]
         self.left = list(reversed(tail_route(flip)[:-1])) + list(reversed(far))
         shape = (2,) * len(self.order) + (lax.axis_size("dp") // 2,) + kept.shape[1:]
+        self.sent = sent
         self.kept, self.came = kept.reshape(shape), hop(sent, *core).reshape(shape)
 
     def half(self, values, side, where):
@@ -447,8 +732,9 @@
             add_low(self.half(self.kept, side, where), self.half(self.came, side, where))
             for side in (1, 0)
         ]
+        self.sent = sent
         self.kept, self.came = kept, hop(sent, *step)
-        return self.came
+        return self.sent
 
     def finish(self):
         while self.left:
@@ -462,46 +748,46 @@
     return flat.reshape(values.shape[0], -1, WIDTH)
 
 
-def from_rows(values, rows):
-    flat = values.reshape(values.shape[0], -1)[:, : rows * LAYOUT_WIDTH]
-    return flat.reshape(-1, LAYOUT_WIDTH)
+def from_rows(values, units):
+    flat = values.reshape(values.shape[0], -1)[:, : units * 2 * LAYOUT_WIDTH]
+    return flat.reshape(-1, 2 * LAYOUT_WIDTH)
 
 
 class HalfSum:
-    def __init__(self, halves):
+    def __init__(self, sent, kept):
         far, near, high, core = routes()
         self.order = far + [near]
-        self.left = [near] + list(reversed(far))
-        first = own_bit(*core) == 0
-        shape = (2,) * len(self.order) + halves[0].shape[1:]
-        sent = jnp.where(first, halves[1], halves[0]).reshape(shape)
-        self.kept = jnp.where(first, halves[0], halves[1]).reshape(shape)
-        self.came = hop(sent, *core)
+        self.left = [near] + list(reversed(far)) + high + [core]
+        shape = (2,) * len(self.order) + sent.shape[1:]
+        self.sent = sent
+        self.kept, self.came = kept.reshape(shape), hop(sent, *core).reshape(shape)
 
     def advance(self):
+        far, near, high, core = routes()
         step = self.left.pop(0)
-        where = self.order.index(step)
-        self.order.remove(step)
-        mine = own_bit(*step)
-
-        def side(values, number):
-            return lax.dynamic_index_in_dim(values, number, where, keepdims=False)
-
-        sent = add_low(side(self.kept, 1 - mine), side(self.came, 1 - mine))
-        kept = add_low(side(self.kept, mine), side(self.came, mine))
-        self.kept, self.came = kept, hop(sent, *step)
-        return self.came
+        if step == core or step in high:
+            self.kept = self.sent = add_low(self.kept, self.came)
+            self.came = hop(self.kept, *step)
+        else:
+            where = self.order.index(step)
+            self.order.remove(step)
+            mine = own_bit(*step)
+
+            def side(values, number):
+                return lax.dynamic_index_in_dim(values, number, where, keepdims=False)
+
+            sent = add_low(side(self.kept, 1 - mine), side(self.came, 1 - mine))
+            kept = add_low(side(self.kept, mine), side(self.came, mine))
+            self.sent = sent
+            self.kept, self.came = kept, hop(sent, *step)
+        return self.sent
 
     def finish(self):
         while self.left:
             self.advance()
-        far, near, high, core = routes()
-        held = add_low(self.kept, self.came)
-        for step in high:
-            held = add_low(held, hop(held, *step))
-        other = hop(held, *core)
-        first = own_bit(*core) == 0
-        return jnp.stack([jnp.where(first, held, other), jnp.where(first, other, held)]).astype(
+        first = own_bit(*routes()[3]) == 0
+        own, other = self.kept, self.came
+        return jnp.stack([jnp.where(first, own, other), jnp.where(first, other, own)]).astype(
             jnp.float32
         )
 
@@ -542,24 +828,24 @@
     return (1.0 / math.sqrt(WIDTH // HEADS), 1.0 / math.sqrt(LAYOUT_WIDTH // HEADS))
 
 
-def project_back(rows_low, mats, grads, width):
+def project_back(mats, grads, width):
     first = jnp.concatenate(grads[:2], 1)
     rows_grad = contract_cols(first, mats[0]) + contract_cols(grads[2], mats[1][:, :width])
     return (
         rows_grad,
-        contract_rows(rows_low, first).astype(jnp.bfloat16),
-        contract_rows(rows_low, grads[2]).astype(jnp.bfloat16),
         jnp.sum(grads[0], 0, dtype=jnp.float32),
         jnp.sum(grads[2], 0, dtype=jnp.float32),
     )
 
 
 def ffn_back_kernel(
-    rows_ref, grad_ref, in_ref, out_ref, hidden_ref, slope_ref, part_ref, bias_ref, *sums
+    rows_of, chunks, count, rows_ref, grad_ref, hidden_ref, slope_ref, extra_ref, *refs
 ):
-    step, last = pl.program_id(0), pl.num_programs(0) // 2
+    part_ref, bias_ref, *sums = refs[count : count + 6]
+    units_in, units_out = take_units(refs[:count], refs[count + 6 :], rows_of, chunks)
+    step, last = pl.program_id(0), chunks // 2
     rows, grad = rows_ref[...], grad_ref[...]
-    grad_hidden = contract_cols(grad, out_ref[...])
+    grad_hidden = contract_cols(grad, units_out)
     grad_pre = grad_hidden * slope_ref[...].astype(jnp.float32)
     grad_low = grad_pre.astype(jnp.bfloat16)
     bias_ref[...] = jnp.sum(grad_low.astype(jnp.float32), 0, keepdims=True)
@@ -568,7 +854,7 @@
     def _():
         part_ref[...] = jnp.zeros_like(part_ref)
 
-    part_ref[...] += jnp.dot(grad_low, in_ref[...], preferred_element_type=jnp.float32)
+    part_ref[...] += jnp.dot(grad_low, units_in, preferred_element_type=jnp.float32)
     results = [contract_rows(grad_low, rows), contract_rows(hidden_ref[...], grad)]
 
     def store(targets):
@@ -578,6 +864,8 @@
             else:
                 blocks = result.astype(target.dtype).reshape(target.shape[0], -1, rows.shape[1])
                 target[:, : blocks.shape[1], :] = blocks
+                if target.shape[1] > blocks.shape[1]:
+                    target[:, blocks.shape[1] :, :] = extra_ref[...]
 
     @pl.when(step < last)
     def _():
@@ -588,13 +876,15 @@
         store(sums[2:])
 
 
-def ffn_back(rows_in, units, slope, hidden, grad_rows, chunks, slot_rows):
+def ffn_back(rows_in, units, slope, hidden, grad_rows, chunks, slot_rows, extra):
     slots, width = rows_in.shape
     total = hidden.shape[1]
     chunk, half = total // chunks, chunks // 2
     whole = pl.BlockSpec((slots, width), lambda step: (0, 0))
     piece = pl.BlockSpec((slots, chunk), lambda step: (0, step))
-    unit = pl.BlockSpec((chunk, width), lambda step: (step, 0))
+    operands, specs, scratch = unit_plan(
+        units, chunk, slot_rows[0] if slot_rows else None, chunks
+    )
 
     def first(step):
         return jnp.minimum(step, half - 1)
@@ -602,59 +892,74 @@
     def second(step):
         return jnp.maximum(step - half, 0)
 
+    turns = (first, first, second, second)
     if slot_rows is None:
-        shape = (total // 2, width)
+        shapes = [(total // 2, width)] * 4
         sum_specs = [
-            pl.BlockSpec((chunk, width), lambda step, turn=turn: (turn(step), 0))
-            for turn in (first, first, second, second)
+            pl.BlockSpec((chunk, width), lambda step, turn=turn: (turn(step), 0)) for turn in turns
         ]
+        extra_spec = pl.BlockSpec(memory_space=pltpu.VMEM)
     else:
         rows, padded = slot_rows
-        shape = (total // (2 * rows), padded, width)
+        heights = [padded, rows] * 2
+        shapes = [(total // (2 * rows), height, width) for height in heights]
         sum_specs = [
-            pl.BlockSpec((chunk // rows, padded, width), lambda step, turn=turn: (turn(step), 0, 0))
-            for turn in (first, first, second, second)
+            pl.BlockSpec((chunk // rows, height, width), lambda step, turn=turn: (turn(step), 0, 0))
+            for height, turn in zip(heights, turns)
         ]
+        extra_spec = pl.BlockSpec((chunk // rows, padded - rows, width), lambda step: (step, 0, 0))
     return pl.pallas_call(
-        ffn_back_kernel,
+        functools.partial(
+            ffn_back_kernel, slot_rows[0] if slot_rows else None, chunks, len(operands)
+        ),
         grid=(chunks,),
-        in_specs=[whole, whole, unit, unit, piece, piece],
+        in_specs=[whole, whole, piece, piece, extra_spec] + specs,
         out_specs=[whole, pl.BlockSpec((1, chunk), lambda step: (0, step))] + sum_specs,
         out_shape=[
             jax.ShapeDtypeStruct((slots, width), jnp.float32),
             jax.ShapeDtypeStruct((1, total), jnp.float32),
         ]
-        + [jax.ShapeDtypeStruct(shape, jnp.bfloat16)] * 4,
+        + [jax.ShapeDtypeStruct(shape, jnp.bfloat16) for shape in shapes],
+        scratch_shapes=scratch,
         cost_estimate=pl.CostEstimate(
-            flops=8 * slots * width * total,
-            bytes_accessed=8 * total * (width + slots),
+            flops=2 * slots * width * total,
+            bytes_accessed=2 * total * (width + slots),
             transcendentals=0,
         ),
         compiler_params=pltpu.CompilerParams(vmem_limit_bytes=48 * 1024 * 1024),
-    )(rows_in, grad_rows, *units, hidden, slope)
-
-
-def stream_forward(rows, att, mats, units, bias_in, vec):
+    )(rows_in, grad_rows, hidden, slope, extra, *operands)
+
+
+def stream_forward(rows, att, mats, units, bias_in, vec, unit_rows, hook):
     width = rows.shape[1]
     first = (
         rows + jnp.dot(att, mats[1][:, width:], preferred_element_type=jnp.float32) + vec[2]
     )
     mid = norm_apply(first, vec[3], vec[4])
-    mid_low = mid.astype(jnp.bfloat16)
-    hidden, slope, part = ffn_front(mid_low, units, bias_in, 4 if width == WIDTH else 1)
+    mid_low = hook(mid.astype(jnp.bfloat16))
+    chunks = 4 if width == WIDTH else 1
+    hidden, slope, part = ffn_front(mid_low, units, bias_in, chunks, unit_rows)
     last = mid + part + vec[5]
     return (norm_apply(last, vec[6], vec[7]), (first, mid_low, slope, hidden, last))
 
 
-def layer_forward(text, layout, weights, lengths):
-    (tm, lm, tu, lu, tb, lb, tv, lv) = weights[:8]
-    text_low = text.astype(jnp.bfloat16)
+def layer_forward(text, layout, weights, lengths, hooks):
+    (tm, lm, tb, lb, tv, lv) = weights
+    text_low = hooks["low"](text.astype(jnp.bfloat16))
     layout_low = layout.astype(jnp.bfloat16)
-    text_qkv = project_qkv(text_low, tm, tv, WIDTH)
+    text_qkv = list(project_qkv(text_low, tm, tv, WIDTH))
     layout_qkv = project_qkv(layout_low, lm, lv, LAYOUT_WIDTH)
+    text_qkv[0] = hooks["query"](text_qkv[0])
     text_att, layout_att, log_total = attend(text_qkv, layout_qkv, lengths)
-    text_new, text_kept = stream_forward(text, text_att, tm, tu, tb, tv)
-    layout_new, layout_kept = stream_forward(layout, layout_att, lm, lu, lb, lv)
+    text_att = hooks["att"](text_att)
+    tu, lu = hooks["units"]()
+    count = lax.axis_size("dp") * lax.axis_size("mp")
+    text_new, text_kept = stream_forward(
+        text, text_att, tm, tu, tb, tv, FFN_UNITS // count, hooks["mid"]
+    )
+    layout_new, layout_kept = stream_forward(
+        layout, layout_att, lm, lu, lb, lv, None, lambda value: value
+    )
     cache = (
         text_low,
         layout_low,
@@ -666,10 +971,10 @@
         text_kept,
         layout_kept,
     )
-    return (text_new, layout_new, cache)
-
-
-def stream_back(kept, att, mats, units, vec, grad, slot_rows):
+    return (text_new, layout_new, cache, (tu, lu))
+
+
+def stream_back(kept, att, mats, units, vec, grad, slot_rows, hook, extra):
     first, mid_low, slope, hidden, last = kept
     width = first.shape[1]
     last_g, gain2, bias2 = norm_back(last, vec[6], vec[7], grad)
@@ -678,16 +983,16 @@
         units,
         slope,
         hidden,
-        last_g.astype(jnp.bfloat16),
+        hook(last_g.astype(jnp.bfloat16)),
         4 if width == WIDTH else 2,
         slot_rows,
+        extra,
     )
     first_g, gain1, bias1 = norm_back(first, vec[3], vec[4], last_g + in_grad)
     first_low = first_g.astype(jnp.bfloat16)
-    out_proj = contract_rows(att, first_low).astype(jnp.bfloat16)
     att_grad = contract_cols(first_low, mats[1][:, width:]).astype(jnp.bfloat16)
     vec_tail = [jnp.sum(first_g, 0), gain1, bias1, jnp.sum(last_g, 0), gain2, bias2]
-    return (first_g, att_grad, out_proj, unit_grads, bias_in_g[0], vec_tail)
+    return (first_g, att_grad, first_low, unit_grads, bias_in_g[0], vec_tail)
 
 
 def layer_backward(cache, grad_text, grad_layout, weights, lengths, plan):
@@ -705,39 +1010,33 @@
     (tm, lm, tu, lu, tb, lb, tv, lv) = weights
     count = lax.axis_size("dp") * lax.axis_size("mp")
     rows = FFN_UNITS // count
-    layout_rows = -(-(LAYOUT_UNITS // count * LAYOUT_WIDTH) // WIDTH)
-    padded = -(-(rows + layout_rows) // 8) * 8
+    none = jnp.zeros((8, 128), jnp.float32)
     first_l, att_l, out_l, lu_g, lb_g, tail_l = stream_back(
-        layout_kept, layout_att, lm, lu, lv, grad_layout, None
-    )
+        layout_kept, layout_att, lm, lu, lv, grad_layout, None, lambda value: value, none
+    )
+    halves = [jnp.concatenate(lu_g[2 * side : 2 * side + 2], 1) for side in range(2)]
+    extra = to_rows(jnp.concatenate(halves, 0).reshape(count, -1, 2 * LAYOUT_WIDTH))
+    extra = jnp.pad(extra, ((0, 0), (0, -extra.shape[1] % 16), (0, 0)))
+    slot_rows = (rows, rows + extra.shape[1])
     first_t, att_t, out_t, tu_g, tb_g, tail_t = stream_back(
-        text_kept, text_att, tm, tu, tv, grad_text, (rows, padded)
-    )
-    joined = []
-    for text_g, layout_g in zip(tu_g, lu_g):
-        extra = jnp.pad(
-            to_rows(layout_g.reshape(count // 2, -1, LAYOUT_WIDTH)),
-            ((0, 0), (0, padded - rows - layout_rows), (0, 0)),
-        )
-        joined.append(lax.dynamic_update_slice(text_g, extra, (0, rows, 0)))
-    att_t = plan.after_units(att_t, joined)
+        text_kept, text_att, tm, tu, tv, grad_text, slot_rows, plan.before_units, extra
+    )
+    att_t = plan.after_units(att_t, tu_g)
     text_dqkv, layout_dqkv = attend_back(
         text_qkv, layout_qkv, lengths, log_total, att_t, att_l
     )
     text_dqkv[0] = plan.after_attend(text_dqkv[0])
-    rows_t, qk_t, v_t, q_bias_t, v_bias_t = project_back(text_low, tm, text_dqkv, WIDTH)
-    rows_l, qk_l, v_l, q_bias_l, v_bias_l = project_back(
-        layout_low, lm, layout_dqkv, LAYOUT_WIDTH
-    )
+    plan.after_mats(
+        (text_low, *text_dqkv, text_att, out_t), (layout_low, *layout_dqkv, layout_att, out_l)
+    )
+    rows_t, q_bias_t, v_bias_t = project_back(tm, text_dqkv, WIDTH)
+    rows_l, q_bias_l, v_bias_l = project_back(lm, layout_dqkv, LAYOUT_WIDTH)
     grads = (
         tb_g,
         lb_g,
         jnp.stack([q_bias_t, v_bias_t] + tail_t),
         jnp.stack([q_bias_l, v_bias_l] + tail_l),
     )
-    plan.after_mats(
-        (qk_t, jnp.concatenate([v_t, out_t], 1)), (qk_l, jnp.concatenate([v_l, out_l], 1))
-    )
     return (first_t + rows_t, first_l + rows_l, grads)
 
 
@@ -747,30 +1046,50 @@
         self.mats = []
 
     def step(self, value, items):
-        return tie(value, *[item.advance() for item in items]) if items else value
+        return tie(value, *[item.advance() for item in items])
+
+    def before_units(self, value):
+        return self.step(value, self.mats[:1]) if self.mats else value
 
     def after_units(self, value, grads):
         keep_in, keep_out, send_in, send_out = grads
         self.units.append([UnitSum(keep_in, send_in, False), UnitSum(keep_out, send_out, True)])
         if self.mats:
-            return self.step(value, self.units[0] + self.mats[0][:1])
-        return tie(value, *[item.came for item in self.units[0]])
+            return self.step(value, self.units[0] + self.mats[:1])
+        return self.step(value, self.units[0])
 
     def after_attend(self, value):
         if self.mats:
-            return self.step(value, self.units[0] + self.mats[0][:1] + self.units[1])
+            return self.step(value, self.units[0] + self.mats[:1] + self.units[1])
         return value
 
-    def after_mats(self, text_halves, layout_halves):
+    def after_mats(self, text, layout):
         dp = lax.axis_size("dp")
-
-        def blocks(halves):
-            return [item.reshape(dp, -1, item.shape[-1]) for item in halves]
-
-        self.mats.append([HalfSum(blocks(text_halves)), HalfSum(blocks(layout_halves))])
+        low = jnp.bfloat16
+        side = own_bit("mp", 0).astype(jnp.int32)
+        rows, query, keys, values, att, first = layout
+        first_half = contract_rows(rows, jnp.concatenate([query, keys], 1)).astype(low)
+        second_half = jnp.concatenate(
+            [contract_rows(rows, values), contract_rows(att, first)], 1
+        ).astype(low)
+        text_rows = WIDTH // dp
+        extras = [
+            jnp.where(side == number, second_half, first_half).reshape(dp, -1, 2 * WIDTH)
+            for number in range(2)
+        ]
+        padded = -(-(text_rows + extras[0].shape[1]) // 8) * 8
+        pad = ((0, 0), (0, padded - text_rows - extras[0].shape[1]), (0, 0))
+        sums = mats_sums(side[None], text, padded)
+        sent, kept = [
+            lax.dynamic_update_slice(item, jnp.pad(extra, pad), (0, text_rows, 0))
+            for item, extra in zip(sums, extras)
+        ]
+        self.mats.append(HalfSum(sent, kept))
 
     def between(self, value):
-        return self.step(value, self.units[0])
+        if len(self.mats) == 1:
+            return self.step(tie(value, self.mats[0].sent), self.units[0])
+        return self.step(tie(value, self.mats[1].sent), self.mats[:1])
 
 
 def split_high(values):
@@ -835,93 +1154,6 @@
     all_targets = shown[:, slots : slots + mask_slots].reshape(-1)
     all_lengths = shown[:, slots + mask_slots]
     table_low = table.astype(low)
-    share = small_params.shape[0]
-    line = 2 * WIDTH
-    layout_rows = layout_mats.shape[1] * LAYOUT_WIDTH * 2 * LAYERS // line
-    small_rows = -(-share // (16 * line)) * 8
-    pad_rows = -(layout_rows + small_rows) % 16
-    small_pad = jnp.pad(small_params.astype(low), (0, 2 * small_rows * line - share))
-    small_half = lax.dynamic_slice_in_dim(
-        small_pad, (lane & 1) * small_rows * line, small_rows * line
-    ).reshape(small_rows, line)
-    tmats_half = own_half(text_mats.astype(low))
-    extra = jnp.concatenate(
-        [
-            small_half,
-            own_half(layout_mats.astype(low)).reshape(layout_rows, line),
-            jnp.zeros((pad_rows, line), low),
-        ],
-        0,
-    )
-    unit_rows = text_ffn.shape[1]
-    layout_units = layout_ffn.shape[1]
-    layout_unit_rows = -(-(layout_units * LAYOUT_WIDTH) // WIDTH)
-    unit_pad = -(unit_rows + layout_unit_rows) % 8
-
-    def unit_block(layer_no, part):
-        return jnp.concatenate(
-            [
-                text_ffn[layer_no, :, part * WIDTH : (part + 1) * WIDTH].astype(low),
-                to_rows(
-                    layout_ffn[
-                        layer_no : layer_no + 1, :, part * LAYOUT_WIDTH : (part + 1) * LAYOUT_WIDTH
-                    ].astype(low)
-                )[0],
-                jnp.zeros((unit_pad, WIDTH), low),
-            ],
-            0,
-        )
-
-    mats_chains = [half_spread(tmats_half[layer_no]) for layer_no in range(LAYERS)]
-    extra_chain = half_spread(extra, True)
-    unit_chains = [
-        [unit_spread(unit_block(layer_no, part), part == 1) for part in range(2)]
-        for layer_no in range(LAYERS)
-    ]
-    far_steps = len(routes()[0])
-    extra_chain.advance()
-    wait = None
-    for number in range(far_steps):
-        wait = mats_chains[0].advance(wait)
-    for number in range(far_steps):
-        wait = extra_chain.advance(wait)
-    for layer_no in range(LAYERS):
-        if layer_no:
-            for number in range(far_steps):
-                wait = mats_chains[layer_no].advance(wait)
-        for number in range(far_steps):
-            waits = [chain.advance(wait) for chain in unit_chains[layer_no]]
-            wait = waits[1]
-    while extra_chain.apart:
-        extra_chain.advance()
-    for layer_no in range(LAYERS):
-        for chain in [mats_chains[layer_no]] + unit_chains[layer_no]:
-            while chain.joined or chain.apart:
-                chain.advance()
-    tmats_all = [half_result(chain) for chain in mats_chains]
-    extra_all = half_result(extra_chain).reshape(2, dp, extra.shape[0], line)
-    small_all = (
-        extra_all[:, :, :small_rows]
-        .transpose(1, 0, 2, 3)
-        .reshape(dp, 2 * small_rows * line)[:, :share]
-        .reshape(-1)
-    )
-    lmats_all = extra_all[:, :, small_rows : small_rows + layout_rows].reshape(
-        2, dp, LAYERS, -1, 2 * LAYOUT_WIDTH
-    )
-    (
-        text_vec,
-        layout_vec,
-        text_bias,
-        layout_bias,
-        text_emb,
-        layout_emb,
-        text_pos,
-        layout_pos,
-        box_table,
-        align_mat,
-    ) = unpack_small(small_all.astype(jnp.float32))
-
     own_block = lane * dp + spot
     steps = jnp.arange(slots)
     earlier = steps[None, :] < steps[:, None]
@@ -963,44 +1195,169 @@
 
     def fetch(turn, so_far):
         rows = jnp.dot(asked_marks(turn), table_low, preferred_element_type=jnp.float32)
-        came = trade(rows.astype(low))
-        return so_far + jnp.dot(held_marks(turn), came, preferred_element_type=jnp.float32)
-
+        sent = rows.astype(low)
+        came = trade(sent)
+        return (
+            so_far + jnp.dot(held_marks(turn), came, preferred_element_type=jnp.float32),
+            came,
+            sent,
+        )
+
+    share = small_params.shape[0]
+    line = 2 * WIDTH
+    half_rows = small_half_rows(share)
+    small_pad = jnp.pad(small_params.astype(low), (0, 2 * half_rows * 128 - share))
+    small_half = lax.dynamic_slice_in_dim(
+        small_pad.reshape(2 * half_rows, 128), (lane & 1) * half_rows, half_rows
+    )
+    tmats_half = own_half(text_mats.astype(low))
+    lmats_half = own_half(layout_mats.astype(low)).reshape(-1, 128)
+    extra = jnp.concatenate(
+        [small_half, lmats_half, jnp.zeros((-lmats_half.shape[0] % 16, 128), low)], 0
+    )
+    unit_rows = text_ffn.shape[1]
+    layout_units = layout_ffn.shape[1]
+    layout_unit_rows = -(-(2 * layout_units * LAYOUT_WIDTH) // WIDTH)
+    unit_pad = -layout_unit_rows % 16
+
+    def unit_block(layer_no, part):
+        text_part = text_ffn[layer_no, :, part * WIDTH : (part + 1) * WIDTH].astype(low)
+        if part:
+            return text_part
+        return jnp.concatenate(
+            [
+                text_part,
+                to_rows(layout_ffn[layer_no : layer_no + 1].astype(low))[0],
+                jnp.zeros((unit_pad, WIDTH), low),
+            ],
+            0,
+        )
+
+    mats_chains = [half_spread(tmats_half[layer_no]) for layer_no in range(LAYERS)]
+    extra_chain = half_spread(extra, True)
+    unit_chains = [
+        [unit_spread(unit_block(layer_no, part), part == 1) for part in range(2)]
+        for layer_no in range(LAYERS)
+    ]
+    far_steps = len(routes()[0])
+    embedded, came_first, rows_first = fetch(0, jnp.zeros((slots, WIDTH), jnp.float32))
     embedded = lax.fori_loop(
-        1, rounds, fetch, fetch(0, jnp.zeros((slots, WIDTH), jnp.float32))
-    )
-
-    def text_embed_fn(embed_vals, pos_table, emb_rows):
-        return norm_apply(embed_vals + pos_table, emb_rows[0], emb_rows[1])
-
-    box_marks = [
-        (box_coords[number, 0][:, None] == jnp.arange(BOXES)[None, :]).astype(low)
-        for number in range(4)
-    ]
-    box_low = box_table.astype(low)
-    looked = jnp.concatenate(
-        [
-            jnp.dot(box_marks[number], box_low[number % 2], preferred_element_type=jnp.float32)
-            for number in range(4)
-        ],
-        1,
-    )
-
-    text, text_pull = jax.vjp(text_embed_fn, embedded, text_pos, text_emb)
-    layout, layout_pull = jax.vjp(text_embed_fn, looked, layout_pos, layout_emb)
+        1, rounds, lambda turn, so_far: fetch(turn, so_far)[0], embedded
+    )
+    for number in range(far_steps + 1):
+        extra_wait = extra_chain.advance()
+        if number < far_steps:
+            mats_chains[0].advance()
+    mats_chains[0].advance()
+    extra_chain.advance(rows_first)
+    mats_chains[0].advance()
+    for number in range(far_steps):
+        for chain in unit_chains[0]:
+            chain.advance(extra_wait)
+        extra_wait = unit_chains[0][1].sent[0]
+    core_key = frozenset([routes()[3]])
+    extra_chain.pieces[core_key] = tie(extra_chain.pieces[core_key], came_first)
+    small_parts, lmats_all = unpack_small(*half_parts(extra_chain), lmats_half.shape[0])
+    lmats_all = lmats_all.reshape(2, dp, LAYERS, -1, 2 * LAYOUT_WIDTH)
+    tmats_first = put_in_order(*half_parts(mats_chains[0]))
+    (
+        text_vec,
+        layout_vec,
+        text_bias,
+        layout_bias,
+        text_emb,
+        layout_emb,
+        text_pos,
+        layout_pos,
+        box_table,
+        align_mat,
+    ) = small_parts
+
+    quarter = LAYOUT_WIDTH // 4
+    lanes = jnp.arange(8 * quarter)
+    fold = (lanes[:, None] % quarter == jnp.arange(quarter)[None, :]).astype(low)
+    box_marks, box_masks = [], []
+    for number in range(4):
+        coords = box_coords[number, 0][:, None]
+        box_marks.append((coords // 8 == jnp.arange(BOXES // 8)[None, :]).astype(low))
+        box_masks.append(coords % 8 == lanes[None, :] // quarter)
+    text_pre, layout_pre, text, layout = embed_streams(
+        box_coords[:, 0].T, embedded, text_pos, layout_pos, box_table, text_emb, layout_emb
+    )
     caches = []
     layer_weights = []
+
+    def push(value, chains):
+        waits = []
+        for chain in chains:
+            chain.advance()
+            waits = waits + chain.sent
+        return tie(value, *waits)
+
+    def settle(chains, left):
+        for chain in chains:
+            while len(chain.joined) + len(chain.apart) > left:
+                chain.advance()
+
+    def after(chains, wait):
+        for chain in chains:
+            chain.advance(wait)
+
+    def hooks_of(layer_no):
+        units = unit_chains[layer_no]
+        later = layer_no + 1 < LAYERS
+        if later:
+            next_mats, next_units = mats_chains[layer_no + 1], unit_chains[layer_no + 1]
+
+        def at_low(value):
+            if layer_no == 0:
+                value = push(value, units)
+            if later:
+                value = push(value, [next_mats])
+            return value
+
+        def at_query(value):
+            if layer_no:
+                value = push(value, units)
+            if later:
+                value = push(value, [next_mats])
+            return value
+
+        def at_att(value):
+            settle(units, 2)
+            value = push(value, units + ([next_mats] if later else []))
+            after(units, value)
+            return value
+
+        def at_mid(value):
+            return push(value, next_units) if later else value
+
+        return {
+            "low": at_low,
+            "query": at_query,
+            "att": at_att,
+            "mid": at_mid,
+            "units": lambda: units_of(layer_no),
+        }
+
+    def units_of(layer_no):
+        results = [unit_result(chain) for chain in unit_chains[layer_no]]
+        layout_both = from_rows(
+            take_extra(results[0], unit_rows)[:, :layout_unit_rows], layout_units
+        )
+        return (results, [layout_both[:, :LAYOUT_WIDTH], layout_both[:, LAYOUT_WIDTH:]])
+
     slot_marks = (unit_blocks()[:, None] == jnp.arange(count)[None, :]).astype(jnp.float32)
     for layer_no in range(LAYERS):
-        results = [unit_result(chain, unit_rows) for chain in unit_chains[layer_no]]
-        weights = (
-            tmats_all[layer_no],
+        if layer_no:
+            settle([mats_chains[layer_no]], 1)
+            text = push(text, unit_chains[layer_no] + [mats_chains[layer_no]])
+            tmats = put_in_order(*half_parts(mats_chains[layer_no]))
+        else:
+            tmats = tmats_first
+        weights = [
+            tmats,
             lmats_all[:, :, layer_no].reshape(2, LAYOUT_WIDTH, -1),
-            [item[0] for item in results],
-            [
-                from_rows(item[1][:, :layout_unit_rows], layout_units)
-                for item in results
-            ],
             jnp.dot(
                 slot_marks, text_bias[layer_no].reshape(count, -1), precision=PRECISE
             ).reshape(-1),
@@ -1009,8 +1366,11 @@
             ).reshape(-1),
             text_vec[layer_no],
             layout_vec[layer_no],
+        ]
+        text, layout, cache, units = layer_forward(
+            text, layout, weights, page_lengths, hooks_of(layer_no)
         )
-        text, layout, cache = layer_forward(text, layout, weights, page_lengths)
+        weights = weights[:2] + list(units) + weights[2:]
         caches.append(cache)
         layer_weights.append(weights)
 
@@ -1075,24 +1435,38 @@
         grad_text, grad_layout, layer_grads[layer_no] = layer_backward(
             caches[layer_no], grad_text, grad_layout, layer_weights[layer_no], page_lengths, plan
         )
-        if layer_no:
-            grad_text = plan.between(grad_text)
-
-    embed_grad, text_pos_grad, text_emb_grad = text_pull(grad_text)
-    looked_grad, layout_pos_grad, layout_emb_grad = layout_pull(grad_layout)
-    quarter = LAYOUT_WIDTH // 4
-    box_parts = [
-        add_rows(box_marks[number], looked_grad[:, number * quarter : (number + 1) * quarter])
-        for number in range(4)
-    ]
-    box_grad = jnp.stack([box_parts[0] + box_parts[2], box_parts[1] + box_parts[3]])
+        grad_text = plan.between(grad_text)
+
+    embed_grad, *text_emb_grad = norm_back(text_pre, text_emb[0], text_emb[1], grad_text)
+    looked_grad, *layout_emb_grad = norm_back(
+        layout_pre,
+        layout_emb[0],
+        layout_emb[1],
+        tie(grad_layout, plan.mats[1].advance()),
+    )
+    text_emb_grad, layout_emb_grad = jnp.stack(text_emb_grad), jnp.stack(layout_emb_grad)
+    box_parts = []
+    for number in range(4):
+        high, rest = split_high(looked_grad[:, number * quarter : (number + 1) * quarter])
+        wide = contract_cols(high, fold) + contract_cols(rest, fold)
+        box_parts.append(jnp.where(box_masks[number], wide, 0.0))
+    box_grad = jnp.stack(
+        [
+            add_rows(
+                jnp.concatenate([box_marks[side], box_marks[side + 2]], 0),
+                jnp.concatenate([box_parts[side], box_parts[side + 2]], 0),
+            )
+            for side in range(2)
+        ]
+    )
     embed_low = embed_grad.astype(low)
 
     def give(turn, so_far):
-        came = trade(contract_rows(held_marks(turn), embed_low).astype(low))
-        return so_far + contract_rows(asked_marks(turn), came)
-
-    table_sum = lax.fori_loop(1, rounds, give, give(0, table_grad))
+        sent = contract_rows(held_marks(turn), embed_low).astype(low)
+        return (so_far + contract_rows(asked_marks(turn), trade(sent)), sent)
+
+    table_sum, gave_rows = give(0, table_grad)
+    table_sum = lax.fori_loop(1, rounds, lambda turn, so_far: give(turn, so_far)[0], table_sum)
 
     def stacked(member):
         return jnp.stack([layer_grads[layer_no][member] for layer_no in range(LAYERS)])
@@ -1110,37 +1484,53 @@
             ]
         )
 
-    small_grad = jnp.concatenate(
-        [
-            item.reshape(-1)
-            for item in (
-                stacked(2),
-                stacked(3),
-                in_order(0),
-                in_order(1),
-                text_emb_grad,
-                layout_emb_grad,
-                text_pos_grad,
-                layout_pos_grad,
-                box_grad,
-                align_grad,
-            )
-        ]
-    )
-    small_blocks = jnp.pad(
-        small_grad.astype(low).reshape(dp, share), ((0, 0), (0, 2 * small_rows * line - share))
-    ).reshape(dp, 2, small_rows, line)
-    small_total = HalfSum([small_blocks[:, 0], small_blocks[:, 1]])
+    small_items = [
+        stacked(2),
+        stacked(3),
+        in_order(0),
+        in_order(1),
+        text_emb_grad,
+        layout_emb_grad,
+        embed_grad,
+        looked_grad,
+        box_grad,
+        align_grad,
+    ]
+    small_items[6] = tie(
+        embed_grad, gave_rows, *[item.advance() for item in plan.units[1]]
+    )
+    small_blocks = pack_small(small_items, dp).reshape(dp, 2, half_rows, 128)
+    first = own_bit("mp", 0) == 0
+    small_total = HalfSum(
+        jnp.where(first, small_blocks[:, 1], small_blocks[:, 0]),
+        jnp.where(first, small_blocks[:, 0], small_blocks[:, 1]),
+    )
+    chains = [plan.mats[1], small_total] + plan.units[1] + plan.units[0] + plan.mats[:1]
+    while any(chain.left for chain in chains):
+        for chain in chains:
+            if chain.left:
+                chain.advance()
     small_sum = small_total.finish().reshape(-1)[:share]
     plan.units.reverse()
     plan.mats.reverse()
-
-    def whole_mats(number):
-        halves = [plan.mats[layer_no][number].finish() for layer_no in range(LAYERS)]
-        return jnp.stack([jnp.concatenate([item[0], item[1]], 1) for item in halves])
-
-    tmats_sum = whole_mats(0)
-    lmats_sum = whole_mats(1)
+    mats_sums = [item.finish() for item in plan.mats]
+    mats_rows = text_mats.shape[1]
+    extra_rows = layout_mats.shape[1] * LAYOUT_WIDTH * 2 // line
+    tmats_sum = jnp.stack(
+        [jnp.concatenate([item[0, :mats_rows], item[1, :mats_rows]], 1) for item in mats_sums]
+    )
+    lmats_sum = jnp.stack(
+        [
+            jnp.concatenate(
+                [
+                    item[side, mats_rows : mats_rows + extra_rows].reshape(-1, 2 * LAYOUT_WIDTH)
+                    for side in range(2)
+                ],
+                1,
+            )
+            for item in mats_sums
+        ]
+    )
     unit_sums = [
         [item.finish() for item in plan.units[layer_no]] for layer_no in range(LAYERS)
     ]
@@ -1149,13 +1539,7 @@
     )
     lffn_sum = jnp.stack(
         [
-            jnp.concatenate(
-                [
-                    from_rows(item[None, unit_rows : unit_rows + layout_unit_rows], layout_units)
-                    for item in pair
-                ],
-                1,
-            )
+            from_rows(pair[0][None, unit_rows : unit_rows + layout_unit_rows], layout_units)
             for pair in unit_sums
         ]
     )

time: 1310 us -> 1100 us (0.84)
  local copies, waits for them, and re-layouts: 328 us -> 153 us
  waiting for transfers between devices: 340 us -> 272 us
  other arithmetic: 203 us -> 240 us
  Pallas kernels: 162 us -> 176 us
    ppermute x103 -> x91, waiting for transfers between devices: 300 us -> 208 us  [hop(): return lax.ppermute(values, axis, pairs)]
    unnamed x933 -> x978, local copies, waits for them, and re-layouts: 169 us -> 91.1 us
    pallas_call x3 -> x2, Pallas kernels: 35.1 us -> 5.97 us  [put_in_order(): pl.pallas_call(kernel, out_shape=jax.ShapeDtypeStruct((2, slots * rows, w...]
    pallas_call x8 -> x15, Pallas kernels: 71.8 us -> 99.8 us  [the longest x4 48 us: ffn_back(): pl.pallas_call(functools.partial(ffn_back_kernel, slot_rows[0] if slot_ro...]
    reshape x24 -> x12, local copies, waits for them, and re-layouts: 29 us -> 7.29 us  [the longest x4 2.64 us: after_mats(): jnp.where(side == number, second_half, first_half)]
    slice x13 -> x12, local copies, waits for them, and re-layouts: 24.7 us -> 3.52 us  [the longest x2 1.53 us: units_of(): layout_both[:, LAYOUT_WIDTH:]]
    all_to_all x3, waiting for transfers between devices: 30.7 us -> 48.4 us  [show_all(): lax.all_to_all(jnp.broadcast_to(values[None], (count,) + values.shape), e...]
    dot_general x27 -> x17, matrix products: 46.2 us -> 28.7 us  [contract_rows(): lax.dot_general(left, right, (((0,), (0,)), ((), ())), preferred_element_...]
  transfers between devices with their start and end apart: 109 -> 97, of which waited for: 48 -> 36; matrix products, arithmetic and copies ran while one was open for 40% -> 33% of each run, Pallas kernels for 7% -> 13%
where the time goes in v2:
time: 1100 us; the launch traced here: 1090 us
  waiting for transfers between devices  272 us (25%)
  other arithmetic  240 us (22%)
  Pallas kernels  176 us (16%)
  local copies, waits for them, and re-layouts  153 us (14%)
  matrix products  116 us (11%)
  starting transfers between devices  114 us (10%)
  between operations  16.8 us (2%)
    ppermute x91, waiting for transfers between devices, hop(): return lax.ppermute(values, axis, pairs)  208 us
    unnamed x978, local copies, waits for them, and re-layouts  91.1 us
    ppermute x91, starting transfers between devices, hop(): return lax.ppermute(values, axis, pairs)  86.6 us
    convert_element_type x34, other arithmetic, add_low(): (kept.astype(jnp.float32) + came.astype(jnp.float32)).astype(jnp.bfloat16)  59.9 us
    all_to_all x3, waiting for transfers between devices, show_all(): lax.all_to_all(jnp.broadcast_to(values[None], (count,) + values.shape), e...  48.4 us
    pallas_call x4, Pallas kernels, ffn_back(): pl.pallas_call(functools.partial(ffn_back_kernel, slot_rows[0] if slot_ro...  48 us
    dot_general x22, matrix products, contract_cols(): lax.dot_general(left, right, (((1,), (1,)), ((), ())), preferred_element_...  38.7 us
    pallas_call x2, Pallas kernels, attend_back(): pl.pallas_call(attend_back_kernel, grid=(HEAD_PAIRS,), in_specs=[pl.Block...  37.3 us
  transfers between devices with their start and end apart: 97, of which 36 were waited for; matrix products, arithmetic and copies ran while one was open for 33% of the time, Pallas kernels for 13%

profile of v2, /device:TPU:0, one launch (start us, length us, event | category | flops | bytes accessed | tf_op | source)
XLA Modules:
  0.0 1088.5 jit_solution(8042047748944212558)
XLA Ops:
  24.7 4.9 all-to-all-start.2
  30.5 4.0 convert_element_type.1095
  38.9 20.0 %all-to-all-done.2 = s32[32,1,576]{2,1,0:T(1,128)S(1)} async-done(((s32[32,1,576]{2,1,0:T(1,128)}), s32[32,1,576]{2,1,0:T(1,128)S(1)}, u32[]{:S(2)}, u32[]{:S(2)}) %all-to-all-start.2) | async-done | bytes 73760 | tf_op jit(solution)/shard_map/all_to_all | solution.py:810
  59.8 9.3 and_reduce_fusion
  73.4 6.1 fusion.27.refs_1_
  83.5 4.3 all-to-all-start.3
  97.0 31.9 %collective-permute-done.9 = bf16[2,96,1536]{2,1,0:T(8,128)(2,1)S(1)} collective-permute-done((bf16[2,96,1536]{2,1,0:T(8,128)(2,1)S(1)}, bf16[2,96,1536]{2,1,0:T(8,128)(2,1)S(1)}, u32[]{:S(2)}, u32[]{:S(2)}) %collective-permute-start.9) | collective-permute-done | bytes 589856 | tf_op jit(solution)/shard_map/ppermute | solution.py:193
  131.6 21.5 %collective-permute-done.2.refs_1_ = bf16[4,528,128]{2,1,0:T(8,128)(2,1)S(1)} collective-permute-done((bf16[4,528,128]{2,1,0:T(8,128)(2,1)S(1)}, bf16[4,528,128]{2,1,0:T(8,128)(2,1)S(1)}, u32[]{:S(2)}, u32[]{:S(2)}) %collective-permute-start.2) | collective-permute-done | bytes 540704 | tf_op jit(solution)/shard_map/ppermute | solution.py:193
  160.3 3.3 collective-permute-start.4
  184.2 4.6 collective-permute-done.5
  201.0 3.6 fusion.19
  223.7 3.6 shard_map.488
  262.9 16.5 %shard_map.497 = (bf16[512,768]{1,0:T(8,128)(2,1)S(1)}, bf16[512,192]{1,0:T(8,128)(2,1)S(1)}, f32[6,512,2]{2,1,0:T(8,128)S(1)}) custom-call(s32[1]{0:T(128)} %copy.437.length, bf16[512,768]{1,0:T(8,128)(2,1)S(1)} %copy-done.57, bf16[512,768]{1,0:T(8,128)(2,1)S(1)} %copy-done.96, bf16[512,768]{1,0:T(8,128)(2,1)S(1)} %add_convert_fusion.13.vt, ...), custom_call_target="tpu_custom_call" | custom-call | flops 4000000000 | bytes 2000000 | tf_op jit(solution)/shard_map/pallas_call | solution.py:473
  282.1 4.0 fusion.290
  314.7 4.8 collective-permute-done.35.refs_4_.refs_0_
  320.7 3.4 collective-permute-done.34.refs_2_.refs_0_
  328.2 13.9 %shard_map.508 = (bf16[512,3072]{1,0:T(8,128)(2,1)}, bf16[512,3072]{1,0:T(8,128)(2,1)}, f32[512,768]{1,0:T(8,128)S(1)}) custom-call(bf16[512,768]{1,0:T(8,128)(2,1)S(1)} %copy-done.19, f32[1,3072]{1,0:T(1,128)S(1)} %broadcast_in_dim_reshape.14.bias_ref, bf16[4,112,768]{2,1,0:T(8,128)(2,1)S(1)} %copy-done.10, bf16[4,112,768]{2,1,0:T(8,128)(2,1)} %shard_map.501.refs_1_, ...), custom_call_target="tpu_custom_call" | custom-call | flops 1207959552 | bytes 3932160 | tf_op jit(solution)/shard_map/pallas_call | solution.py:610
  347.0 3.4 fusion.25
  362.4 16.9 %shard_map.514 = (bf16[512,768]{1,0:T(8,128)(2,1)S(1)}, bf16[512,192]{1,0:T(8,128)(2,1)S(1)}, f32[6,512,2]{2,1,0:T(8,128)S(1)}) custom-call(s32[1]{0:T(128)} %copy.437.length, bf16[512,768]{1,0:T(8,128)(2,1)S(1)} %copy-done.59, bf16[512,768]{1,0:T(8,128)(2,1)S(1)} %copy-done.98, bf16[512,768]{1,0:T(8,128)(2,1)S(1)} %copy-done.150, ...), custom_call_target="tpu_custom_call" | custom-call | flops 4000000000 | bytes 2000000 | tf_op jit(solution)/shard_map/pallas_call | solution.py:473
  392.7 13.7 %shard_map.524 = (bf16[512,3072]{1,0:T(8,128)(2,1)}, bf16[512,3072]{1,0:T(8,128)(2,1)}, f32[512,768]{1,0:T(8,128)S(1)}) custom-call(bf16[512,768]{1,0:T(8,128)(2,1)S(1)} %fusion.49.rows_ref, f32[1,3072]{1,0:T(1,128)S(1)} %broadcast_in_dim_reshape.16.bias_ref, bf16[4,112,768]{2,1,0:T(8,128)(2,1)S(1)} %copy-done.7, bf16[4,112,768]{2,1,0:T(8,128)(2,1)S(1)} %copy-done.16, ...), custom_call_target="tpu_custom_call" | custom-call | flops 1207959552 | bytes 3932160 | tf_op jit(solution)/shard_map/pallas_call | solution.py:610
  409.6 6.3 all-to-all-start.4
  435.4 18.0 %all-to-all-done.4 = bf16[32,32,768]{2,1,0:T(8,128)(2,1)} async-done(((bf16[32,32,768]{2,1,0:T(8,128)(2,1)}), bf16[32,32,768]{2,1,0:T(8,128)(2,1)}, u32[]{:S(2)}, u32[]{:S(2)}) %all-to-all-start.4) | async-done | bytes 1572896 | tf_op jit(solution)/shard_map/all_to_all | solution.py:810
  453.4 4.9 fusion.293
  462.0 4.0 all-to-all-start.5
  471.1 10.5 all-to-all-done.5
  484.7 8.4 convolution_convert_fusion
  493.1 3.7 all-to-all-start.6
  518.6 15.7 %all-to-all-done.6 = bf16[32,32,768]{2,1,0:T(8,128)(2,1)} async-done(((bf16[32,32,768]{2,1,0:T(8,128)(2,1)}), bf16[32,32,768]{2,1,0:T(8,128)(2,1)}, u32[]{:S(2)}, u32[]{:S(2)}) %all-to-all-start.6) | async-done | bytes 1572896 | tf_op jit(solution)/shard_map/all_to_all | solution.py:816
  541.5 21.8 %shard_map.528 = (f32[512,768]{1,0:T(8,128)}, f32[1,3072]{1,0:T(1,128)S(1)}, bf16[16,112,768]{2,1,0:T(8,128)(2,1)}, bf16[16,96,768]{2,1,0:T(8,128)(2,1)}, bf16[1...) custom-call(bf16[512,768]{1,0:T(8,128)(2,1)} %copy-done.31, bf16[512,768]{1,0:T(8,128)(2,1)} %get-tuple-element.589.grad_ref, ...), custom_call_target="tpu_custom_call" | custom-call | flops 2415919104 | bytes 7864320 | tf_op jit(solution)/shard_map/pallas_call | solution.py:911
  574.2 4.2 multiply_reduce_fusion.4
  587.9 3.9 add_convert_fusion.10
  593.3 4.0 add_convert_fusion.2
  605.0 18.5 %shard_map.530 = (bf16[512,768]{1,0:T(8,128)(2,1)S(1)}, bf16[512,768]{1,0:T(8,128)(2,1)S(1)}, bf16[512,768]{1,0:T(8,128)(2,1)S(1)}, bf16[512,192]{1,0:T(8,128)(2...) custom-call(s32[1]{0:T(128)} %copy.437.length, bf16[512,768]{1,0:T(8,128)(2,1)S(1)} %copy-done.60, ...), custom_call_target="tpu_custom_call" | custom-call | flops 5000000000 | bytes 3000000 | tf_op jit(solution)/shard_map/pallas_call | solution.py:497
  644.2 4.3 shard_map.531
  654.3 4.3 add_add_fusion.6.refs_0_
  673.1 10.0 collective-permute-done.54
  696.2 9.2 collective-permute-done.53
  720.6 22.0 %shard_map.536 = (f32[512,768]{1,0:T(8,128)}, f32[1,3072]{1,0:T(1,128)S(1)}, bf16[16,112,768]{2,1,0:T(8,128)(2,1)}, bf16[16,96,768]{2,1,0:T(8,128)(2,1)}, bf16[1...) custom-call(bf16[512,768]{1,0:T(8,128)(2,1)} %shard_map.499.rows_ref, bf16[512,768]{1,0:T(8,128)(2,1)} %shard_map.534.grad_ref, ...), custom_call_target="tpu_custom_call" | custom-call | flops 2415919104 | bytes 7864320 | tf_op jit(solution)/shard_map/pallas_call | solution.py:911
  765.3 18.9 %shard_map.538 = (bf16[512,768]{1,0:T(8,128)(2,1)S(1)}, bf16[512,768]{1,0:T(8,128)(2,1)S(1)}, bf16[512,768]{1,0:T(8,128)(2,1)S(1)}, bf16[512,192]{1,0:T(8,128)(2...) custom-call(s32[1]{0:T(128)} %copy.437.length, bf16[512,768]{1,0:T(8,128)(2,1)S(1)} %copy-done.58, ...), custom_call_target="tpu_custom_call" | custom-call | flops 5000000000 | bytes 3000000 | tf_op jit(solution)/shard_map/pallas_call | solution.py:497
  790.3 3.2 fusion.85
  793.5 11.8 %collective-permute-done.61 = bf16[104,1536]{1,0:T(8,128)(2,1)S(1)} collective-permute-done((bf16[104,1536]{1,0:T(8,128)(2,1)S(1)}, bf16[104,1536]{1,0:T(8,128)(2,1)S(1)}, u32[]{:S(2)}, u32[]{:S(2)}) %collective-permute-start.61) | collective-permute-done | bytes 319520 | tf_op jit(solution)/shard_map/ppermute | solution.py:193
  808.1 4.6 add_convert_fusion.8
  816.8 4.0 add_convert_fusion
  827.0 5.2 shard_map.540
  832.3 5.2 add_add_fusion.5.refs_0_
  844.4 3.5 fusion.26.refs_1_
  857.5 11.2 %collective-permute-done.67 = bf16[4,96,768]{2,1,0:T(8,128)(2,1)S(1)} collective-permute-done((bf16[4,96,768]{2,1,0:T(8,128)(2,1)S(1)}, bf16[4,96,768]{2,1,0:T(8,128)(2,1)S(1)}, u32[]{:S(2)}, u32[]{:S(2)}) %collective-permute-start.67) | collective-permute-done | bytes 589856 | tf_op jit(solution)/shard_map/ppermute | solution.py:193
  870.1 7.3 collective-permute-done.68
  882.0 4.0 collective-permute-done.69
  887.8 3.7 collective-permute-done.64
  913.0 4.2 all-to-all-start.7
  933.8 39.8 %collective-permute-done.81 = bf16[2,2,384,128]{3,2,1,0:T(8,128)(2,1)S(1)} collective-permute-done((bf16[2,2,384,128]{3,2,1,0:T(8,128)(2,1)S(1)}, bf16[2,2,384,128]{3,2,1,0:T(8,128)(2,1)S(1)}, u32[]{:S(2)}, u32[]{:S(2)}) %collective-permute-start.81) | collective-permute-done | bytes 393248 | tf_op jit(solution)/shard_map/ppermute | solution.py:193
  979.2 5.2 fusion.14
  987.9 9.5 collective-permute-done.74
  999.3 6.7 convolution_add_fusion
  1007.0 3.6 collective-permute-start.84
  1010.7 3.7 collective-permute-done.75
  1018.5 4.2 multiply_reduce_fusion
  1038.7 3.6 collective-permute-done.88
  1042.3 4.5 collective-permute-done.89
  1046.8 3.6 collective-permute-done.90
  1059.3 4.7 add_multiply_fusion.2
  1066.0 6.1 add_multiply_fusion.1
  1074.6 7.6 add_multiply_fusion
  (1624 shorter events, 514.9 us)
Async XLA Ops:
  3.5 31.0 %collective-permute-start = (bf16[1,528,128]{2,1,0:T(8,128)(2,1)}, bf16[1,528,128]{2,1,0:T(8,128)(2,1)}, u32[]{:S(2)}, u32[]{:S(2)}) collective-permute-start(bf16[1,528,128]{2,1,0:T(8,128)(2,1)} %maximum_bitcast_fusion.6), channel_id=1, source_target_pairs={{0,4},{4,0},{8,12},{12,8},{16,20},{20,16},{24,28},{28,24},{1,5},{5... | collective-permute-start | bytes 405512 | tf_op jit(solution)/shard_map/ppermute | solution.py:193
  7.3 87.8 %collective-permute-start.29 = (bf16[1,96,768]{2,1,0:T(8,128)(2,1)}, bf16[1,96,768]{2,1,0:T(8,128)(2,1)}, u32[]{:S(2)}, u32[]{:S(2)}) collective-permute-start(bf16[1,96,768]{2,1,0:T(8,128)(2,1)} %get-tuple-element.624.refs_2_), channel_id=1, source_target_pairs={{0,16},{4,20},{8,24},{12,28},{16,0},{20,4},{24,8},{28,12},{1,17},{... | collective-permute-start | bytes 442376 | tf_op jit(solution)/shard_map/ppermute | solution.py:193
  10.8 153.6 %collective-permute-start.28 = (bf16[1,112,768]{2,1,0:T(8,128)(2,1)S(1)}, bf16[1,112,768]{2,1,0:T(8,128)(2,1)}, u32[]{:S(2)}, u32[]{:S(2)}) collective-permute-start(bf16[1,112,768]{2,1,0:T(8,128)(2,1)S(1)} %get-tuple-element.683.refs_1_), channel_id=1, source_target_pairs={{0,16},{4,20},{8,24},{12,28},{16,0},{20,4},{24,8},{28,12},{1,17},{... | collective-permute-start | bytes 516104 | tf_op jit(solution)/shard_map/ppermute | solution.py:193
  11.5 76.2 %collective-permute-start.8 = (bf16[1,96,1536]{2,1,0:T(8,128)(2,1)S(1)}, bf16[1,96,1536]{2,1,0:T(8,128)(2,1)S(1)}, u32[]{:S(2)}, u32[]{:S(2)}) collective-permute-start(bf16[1,96,1536]{2,1,0:T(8,128)(2,1)S(1)} %get-tuple-element.628), channel_id=1, source_target_pairs={{0,16},{4,20},{8,24},{12,28},{16,0},{20,4},{24,8},{28,12},{1,17},{... | collective-permute-start | bytes 884744 | tf_op jit(solution)/shard_map/ppermute | solution.py:193
  14.2 75.6 %collective-permute-start.12 = (bf16[1,96,1536]{2,1,0:T(8,128)(2,1)S(1)}, bf16[1,96,1536]{2,1,0:T(8,128)(2,1)S(1)}, u32[]{:S(2)}, u32[]{:S(2)}) collective-permute-start(bf16[1,96,1536]{2,1,0:T(8,128)(2,1)S(1)} %get-tuple-element.629.refs_1_), channel_id=1, source_target_pairs={{0,16},{4,20},{8,24},{12,28},{16,0},{20,4},{24,8},{28,12},{1,17},{... | collective-permute-start | bytes 884744 | tf_op jit(solution)/shard_map/ppermute | solution.py:193
  24.7 34.3 %all-to-all-start.2 = ((s32[32,1,576]{2,1,0:T(1,128)}), s32[32,1,576]{2,1,0:T(1,128)S(1)}, u32[]{:S(2)}, u32[]{:S(2)}) async-start(s32[32,1,576]{2,1,0:T(1,128)} %broadcast_in_dim.176), calls=%async_computation.2 | async-start | bytes 163840 | tf_op jit(solution)/shard_map/all_to_all | solution.py:810
  36.3 54.6 %collective-permute-start.1 = (bf16[2,528,128]{2,1,0:T(8,128)(2,1)}, bf16[2,528,128]{2,1,0:T(8,128)(2,1)S(1)}, u32[]{:S(2)}, u32[]{:S(2)}) collective-permute-start(bf16[2,528,128]{2,1,0:T(8,128)(2,1)} %pad_maximum_fusion.23), channel_id=1, source_target_pairs={{0,16},{4,20},{8,24},{12,28},{16,0},{20,4},{24,8},{28,12},{1,17},{... | collective-permute-start | bytes 811016 | tf_op jit(solution)/shard_map/ppermute | solution.py:193
  83.5 117.5 %all-to-all-start.3 = ((bf16[32,32,768]{2,1,0:T(8,128)(2,1)}), bf16[32,32,768]{2,1,0:T(8,128)(2,1)}, u32[]{:S(2)}, u32[]{:S(2)}) async-start(bf16[32,32,768]{2,1,0:T(8,128)(2,1)} %bitcast.11), calls=%async_computation.3 | async-start | bytes 3145728 | tf_op jit(solution)/shard_map/all_to_all | solution.py:816
  87.9 41.0 %collective-permute-start.9 = (bf16[2,96,1536]{2,1,0:T(8,128)(2,1)S(1)}, bf16[2,96,1536]{2,1,0:T(8,128)(2,1)S(1)}, u32[]{:S(2)}, u32[]{:S(2)}) collective-permute-start(bf16[2,96,1536]{2,1,0:T(8,128)(2,1)S(1)} %pad_maximum_fusion.12), channel_id=1, source_target_pairs={{0,8},{4,12},{8,0},{12,4},{16,24},{20,28},{24,16},{28,20},{1,9},{5... | collective-permute-start | bytes 1769480 | tf_op jit(solution)/shard_map/ppermute | solution.py:193
  90.7 65.7 %collective-permute-start.15 = (bf16[2,96,1536]{2,1,0:T(8,128)(2,1)}, bf16[2,96,1536]{2,1,0:T(8,128)(2,1)S(1)}, u32[]{:S(2)}, u32[]{:S(2)}) collective-permute-start(bf16[2,96,1536]{2,1,0:T(8,128)(2,1)} %pad_maximum_fusion.13.refs_1_), channel_id=1, source_target_pairs={{0,8},{4,12},{8,0},{12,4},{16,24},{20,28},{24,16},{28,20},{1,9},{5... | collective-permute-start | bytes 1769480 | tf_op jit(solution)/shard_map/ppermute | solution.py:193
  92.6 60.6 %collective-permute-start.2 = (bf16[4,528,128]{2,1,0:T(8,128)(2,1)S(1)}, bf16[4,528,128]{2,1,0:T(8,128)(2,1)S(1)}, u32[]{:S(2)}, u32[]{:S(2)}) collective-permute-start(bf16[4,528,128]{2,1,0:T(8,128)(2,1)S(1)} %pad_maximum_fusion.15), channel_id=1, source_target_pairs={{0,8},{4,12},{8,0},{12,4},{16,24},{20,28},{24,16},{28,20},{1,9},{5... | collective-permute-start | bytes 1622024 | tf_op jit(solution)/shard_map/ppermute | solution.py:193
  96.9 71.3 %collective-permute-start.33 = (bf16[2,96,768]{2,1,0:T(8,128)(2,1)}, bf16[2,96,768]{2,1,0:T(8,128)(2,1)}, u32[]{:S(2)}, u32[]{:S(2)}) collective-permute-start(bf16[2,96,768]{2,1,0:T(8,128)(2,1)} %pad_maximum_fusion.22.refs_2_), channel_id=1, source_target_pairs={{0,8},{4,12},{8,0},{12,4},{16,24},{20,28},{24,16},{28,20},{1,9},{5... | collective-permute-start | bytes 884744 | tf_op jit(solution)/shard_map/ppermute | solution.py:193
  130.1 61.6 %collective-permute-start.10 = (bf16[4,96,1536]{2,1,0:T(8,128)(2,1)}, bf16[4,96,1536]{2,1,0:T(8,128)(2,1)}, u32[]{:S(2)}, u32[]{:S(2)}) collective-permute-start(bf16[4,96,1536]{2,1,0:T(8,128)(2,1)} %pad_maximum_fusion.5), channel_id=1, source_target_pairs={{0,4},{4,0},{8,12},{12,8},{16,20},{20,16},{24,28},{28,24},{1,5},{5... | collective-permute-start | bytes 3538952 | tf_op jit(solution)/shard_map/ppermute | solution.py:193
  157.6 39.2 %collective-permute-start.30 = (bf16[4,96,1536]{2,1,0:T(8,128)(2,1)}, bf16[4,96,1536]{2,1,0:T(8,128)(2,1)}, u32[]{:S(2)}, u32[]{:S(2)}) collective-permute-start(bf16[4,96,1536]{2,1,0:T(8,128)(2,1)} %pad_maximum_fusion.6.refs_5_), channel_id=1, source_target_pairs={{0,4},{4,0},{8,12},{12,8},{16,20},{20,16},{24,28},{28,24},{1,5},{5... | collective-permute-start | bytes 3538952 | tf_op jit(solution)/shard_map/ppermute | solution.py:193
  171.1 17.8 %collective-permute-start.5 = (bf16[2,112,768]{2,1,0:T(8,128)(2,1)}, bf16[2,112,768]{2,1,0:T(8,128)(2,1)}, u32[]{:S(2)}, u32[]{:S(2)}) collective-permute-start(bf16[2,112,768]{2,1,0:T(8,128)(2,1)} %shard_map.491), channel_id=1, source_target_pairs={{0,8},{4,12},{8,0},{12,4},{16,24},{20,28},{24,16},{28,20},{1,9},{5... | collective-permute-start | bytes 1032200 | tf_op jit(solution)/shard_map/ppermute | solution.py:193
  177.6 18.5 %collective-permute-start.14 = (bf16[4,96,768]{2,1,0:T(8,128)(2,1)}, bf16[4,96,768]{2,1,0:T(8,128)(2,1)}, u32[]{:S(2)}, u32[]{:S(2)}) collective-permute-start(bf16[4,96,768]{2,1,0:T(8,128)(2,1)} %pad_maximum_fusion.11.refs_2_.refs_3_.refs_0_), channel_id=1, source_target_pairs={{0,2},{1,3},{2,0},{3,1},{4,6},{5,7},{6,4},{7,5},{8,10},{9,11},{10,... | collective-permute-start | bytes 1769480 | tf_op jit(solution)/shard_map/ppermute | solution.py:193
  183.1 21.5 %collective-permute-start.3 = (bf16[8,528,128]{2,1,0:T(8,128)(2,1)}, bf16[8,528,128]{2,1,0:T(8,128)(2,1)}, u32[]{:S(2)}, u32[]{:S(2)}) collective-permute-start(bf16[8,528,128]{2,1,0:T(8,128)(2,1)} %shard_map.485.own_ref), channel_id=1, source_target_pairs={{0,1},{1,0},{2,3},{3,2},{4,5},{5,4},{6,7},{7,6},{8,9},{9,8},{10,11... | collective-permute-start | bytes 3244040 | tf_op jit(solution)/shard_map/ppermute | solution.py:193
  188.9 112.8 %collective-permute-start.22 = (bf16[4,96,768]{2,1,0:T(8,128)(2,1)}, bf16[4,96,768]{2,1,0:T(8,128)(2,1)}, u32[]{:S(2)}, u32[]{:S(2)}) collective-permute-start(bf16[4,96,768]{2,1,0:T(8,128)(2,1)} %pad_maximum_fusion.11.refs_2_.refs_3_.refs_0_), channel_id=1, source_target_pairs={{0,4},{4,0},{8,12},{12,8},{16,20},{20,16},{24,28},{28,24},{1,5},{5... | collective-permute-start | bytes 1769480 | tf_op jit(solution)/shard_map/ppermute | solution.py:193
  191.7 94.4 %collective-permute-start.16 = (bf16[4,112,768]{2,1,0:T(8,128)(2,1)S(1)}, bf16[4,112,768]{2,1,0:T(8,128)(2,1)}, u32[]{:S(2)}, u32[]{:S(2)}) collective-permute-start(bf16[4,112,768]{2,1,0:T(8,128)(2,1)S(1)} %pad_maximum_fusion.9.refs_1_.refs_0_), channel_id=1, source_target_pairs={{0,2},{1,3},{2,0},{3,1},{4,6},{5,7},{6,4},{7,5},{8,10},{9,11},{10,... | collective-permute-start | bytes 2064392 | tf_op jit(solution)/shard_map/ppermute | solution.py:193
  196.1 54.0 %collective-permute-start.13 = (bf16[4,112,768]{2,1,0:T(8,128)(2,1)S(1)}, bf16[4,112,768]{2,1,0:T(8,128)(2,1)}, u32[]{:S(2)}, u32[]{:S(2)}) collective-permute-start(bf16[4,112,768]{2,1,0:T(8,128)(2,1)S(1)} %pad_maximum_fusion.9.refs_1_.refs_0_), channel_id=1, source_target_pairs={{0,4},{4,0},{8,12},{12,8},{16,20},{20,16},{24,28},{28,24},{1,5},{5... | collective-permute-start | bytes 2064392 | tf_op jit(solution)/shard_map/ppermute | solution.py:193
  196.8 107.3 %collective-permute-start.23 = (bf16[4,96,768]{2,1,0:T(8,128)(2,1)}, bf16[4,96,768]{2,1,0:T(8,128)(2,1)}, u32[]{:S(2)}, u32[]{:S(2)}) collective-permute-start(bf16[4,96,768]{2,1,0:T(8,128)(2,1)} %collective-permute-done.14.refs_4_.refs_0_), channel_id=1, source_target_pairs={{0,4},{4,0},{8,12},{12,8},{16,20},{20,16},{24,28},{28,24},{1,5},{5... | collective-permute-start | bytes 1769480 | tf_op jit(solution)/shard_map/ppermute | solution.py:193
  204.6 45.5 %collective-permute-start.11 = (bf16[8,96,1536]{2,1,0:T(8,128)(2,1)}, bf16[8,96,1536]{2,1,0:T(8,128)(2,1)}, u32[]{:S(2)}, u32[]{:S(2)}) collective-permute-start(bf16[8,96,1536]{2,1,0:T(8,128)(2,1)} %pad_maximum_fusion.own_ref), channel_id=1, source_target_pairs={{0,1},{1,0},{2,3},{3,2},{4,5},{5,4},{6,7},{7,6},{8,9},{9,8},{10,11... | collective-permute-start | bytes 7077896 | tf_op jit(solution)/shard_map/ppermute | solution.py:193
  250.0 36.3 %collective-permute-start.31 = (bf16[8,96,1536]{2,1,0:T(8,128)(2,1)}, bf16[8,96,1536]{2,1,0:T(8,128)(2,1)}, u32[]{:S(2)}, u32[]{:S(2)}) collective-permute-start(bf16[8,96,1536]{2,1,0:T(8,128)(2,1)} %pad_maximum_fusion.1.refs_3_.own_ref), channel_id=1, source_target_pairs={{0,1},{1,0},{2,3},{3,2},{4,5},{5,4},{6,7},{7,6},{8,9},{9,8},{10,11... | collective-permute-start | bytes 7077896 | tf_op jit(solution)/shard_map/ppermute | solution.py:193
  250.1 42.1 %collective-permute-start.17 = (bf16[4,112,768]{2,1,0:T(8,128)(2,1)}, bf16[4,112,768]{2,1,0:T(8,128)(2,1)S(1)}, u32[]{:S(2)}, u32[]{:S(2)}) collective-permute-start(bf16[4,112,768]{2,1,0:T(8,128)(2,1)} %collective-permute-done.13.refs_2_.refs_0_), channel_id=1, source_target_pairs={{0,2},{1,3},{2,0},{3,1},{4,6},{5,7},{6,4},{7,5},{8,10},{9,11},{10,... | collective-permute-start | bytes 2064392 | tf_op jit(solution)/shard_map/ppermute | solution.py:193
  286.1 20.6 %collective-permute-start.18 = (bf16[4,112,768]{2,1,0:T(8,128)(2,1)}, bf16[4,112,768]{2,1,0:T(8,128)(2,1)S(1)}, u32[]{:S(2)}, u32[]{:S(2)}) collective-permute-start(bf16[4,112,768]{2,1,0:T(8,128)(2,1)} %shard_map.500.refs_0_), channel_id=1, source_target_pairs={{0,1},{1,0},{2,3},{3,2},{4,5},{5,4},{6,7},{7,6},{8,9},{9,8},{10,11... | collective-permute-start | bytes 2064392 | tf_op jit(solution)/shard_map/ppermute | solution.py:193
  306.8 17.3 %collective-permute-start.34 = (bf16[4,112,768]{2,1,0:T(8,128)(2,1)S(1)}, bf16[4,112,768]{2,1,0:T(8,128)(2,1)S(1)}, u32[]{:S(2)}, u32[]{:S(2)}) collective-permute-start(bf16[4,112,768]{2,1,0:T(8,128)(2,1)S(1)} %pad_maximum_fusion.10.refs_1_.refs_0_), channel_id=1, source_target_pairs={{0,4},{4,0},{8,12},{12,8},{16,20},{20,16},{24,28},{28,24},{1,5},{5... | collective-permute-start | bytes 2064392 | tf_op jit(solution)/shard_map/ppermute | solution.py:193
  307.5 17.2 %collective-permute-start.24 = (bf16[4,96,768]{2,1,0:T(8,128)(2,1)}, bf16[4,96,768]{2,1,0:T(8,128)(2,1)}, u32[]{:S(2)}, u32[]{:S(2)}) collective-permute-start(bf16[4,96,768]{2,1,0:T(8,128)(2,1)} %shard_map.504.refs_8_), channel_id=1, source_target_pairs={{0,1},{1,0},{2,3},{3,2},{4,5},{5,4},{6,7},{7,6},{8,9},{9,8},{10,11... | collective-permute-start | bytes 1769480 | tf_op jit(solution)/shard_map/ppermute | solution.py:193
  307.5 17.5 %collective-permute-start.25 = (bf16[4,96,768]{2,1,0:T(8,128)(2,1)}, bf16[4,96,768]{2,1,0:T(8,128)(2,1)}, u32[]{:S(2)}, u32[]{:S(2)}) collective-permute-start(bf16[4,96,768]{2,1,0:T(8,128)(2,1)} %shard_map.505.refs_9_), channel_id=1, source_target_pairs={{0,1},{1,0},{2,3},{3,2},{4,5},{5,4},{6,7},{7,6},{8,9},{9,8},{10,11... | collective-permute-start | bytes 1769480 | tf_op jit(solution)/shard_map/ppermute | solution.py:193
  308.1 18.6 %collective-permute-start.26 = (bf16[4,96,768]{2,1,0:T(8,128)(2,1)}, bf16[4,96,768]{2,1,0:T(8,128)(2,1)}, u32[]{:S(2)}, u32[]{:S(2)}) collective-permute-start(bf16[4,96,768]{2,1,0:T(8,128)(2,1)} %shard_map.506.refs_10_), channel_id=1, source_target_pairs={{0,1},{1,0},{2,3},{3,2},{4,5},{5,4},{6,7},{7,6},{8,9},{9,8},{10,11... | collective-permute-start | bytes 1769480 | tf_op jit(solution)/shard_map/ppermute | solution.py:193
  324.0 58.0 %collective-permute-start.42 = (bf16[4,96,768]{2,1,0:T(8,128)(2,1)S(1)}, bf16[4,96,768]{2,1,0:T(8,128)(2,1)}, u32[]{:S(2)}, u32[]{:S(2)}) collective-permute-start(bf16[4,96,768]{2,1,0:T(8,128)(2,1)S(1)} %pad_maximum_fusion.14.refs_2_.refs_3_.refs_0_), channel_id=1, source_target_pairs={{0,4},{4,0},{8,12},{12,8},{16,20},{20,16},{24,28},{28,24},{1,5},{5... | collective-permute-start | bytes 1769480 | tf_op jit(solution)/shard_map/ppermute | solution.py:193
  324.8 58.1 %collective-permute-start.36 = (bf16[4,112,768]{2,1,0:T(8,128)(2,1)S(1)}, bf16[4,112,768]{2,1,0:T(8,128)(2,1)}, u32[]{:S(2)}, u32[]{:S(2)}) collective-permute-start(bf16[4,112,768]{2,1,0:T(8,128)(2,1)S(1)} %pad_maximum_fusion.10.refs_1_.refs_0_), channel_id=1, source_target_pairs={{0,2},{1,3},{2,0},{3,1},{4,6},{5,7},{6,4},{7,5},{8,10},{9,11},{10,... | collective-permute-start | bytes 2064392 | tf_op jit(solution)/shard_map/ppermute | solution.py:193
  325.1 57.5 %collective-permute-start.43 = (bf16[4,96,768]{2,1,0:T(8,128)(2,1)S(1)}, bf16[4,96,768]{2,1,0:T(8,128)(2,1)}, u32[]{:S(2)}, u32[]{:S(2)}) collective-permute-start(bf16[4,96,768]{2,1,0:T(8,128)(2,1)S(1)} %collective-permute-done.35.refs_4_.refs_0_), channel_id=1, source_target_pairs={{0,4},{4,0},{8,12},{12,8},{16,20},{20,16},{24,28},{28,24},{1,5},{5... | collective-permute-start | bytes 1769480 | tf_op jit(solution)/shard_map/ppermute | solution.py:193
  326.7 56.6 %collective-permute-start.37 = (bf16[4,112,768]{2,1,0:T(8,128)(2,1)S(1)}, bf16[4,112,768]{2,1,0:T(8,128)(2,1)}, u32[]{:S(2)}, u32[]{:S(2)}) collective-permute-start(bf16[4,112,768]{2,1,0:T(8,128)(2,1)S(1)} %collective-permute-done.34.refs_2_.refs_0_), channel_id=1, source_target_pairs={{0,2},{1,3},{2,0},{3,1},{4,6},{5,7},{6,4},{7,5},{8,10},{9,11},{10,... | collective-permute-start | bytes 2064392 | tf_op jit(solution)/shard_map/ppermute | solution.py:193
  409.6 43.8 %all-to-all-start.4 = ((bf16[32,32,768]{2,1,0:T(8,128)(2,1)}), bf16[32,32,768]{2,1,0:T(8,128)(2,1)}, u32[]{:S(2)}, u32[]{:S(2)}) async-start(bf16[32,32,768]{2,1,0:T(8,128)(2,1)} %broadcast_in_dim.188), calls=%async_computation.4 | async-start | bytes 3145728 | tf_op jit(solution)/shard_map/all_to_all | solution.py:810
  462.0 19.6 %all-to-all-start.5 = ((f32[32,3,1024]{2,1,0:T(4,128)}), f32[32,3,1024]{2,1,0:T(4,128)}, u32[]{:S(2)}, u32[]{:S(2)}) async-start(f32[32,3,1024]{2,1,0:T(4,128)} %broadcast_in_dim.190), calls=%async_computation.5 | async-start | bytes 1048576 | tf_op jit(solution)/shard_map/all_to_all | solution.py:810
  493.1 41.2 %all-to-all-start.6 = ((bf16[32,32,768]{2,1,0:T(8,128)(2,1)}), bf16[32,32,768]{2,1,0:T(8,128)(2,1)}, u32[]{:S(2)}, u32[]{:S(2)}) async-start(bf16[32,32,768]{2,1,0:T(8,128)(2,1)} %bitcast.490), calls=%async_computation.6 | async-start | bytes 3145728 | tf_op jit(solution)/shard_map/all_to_all | solution.py:816
  563.3 24.6 %collective-permute-start.49 = (bf16[16,96,768]{2,1,0:T(8,128)(2,1)}, bf16[16,96,768]{2,1,0:T(8,128)(2,1)}, u32[]{:S(2)}, u32[]{:S(2)}) collective-permute-start(bf16[16,96,768]{2,1,0:T(8,128)(2,1)} %get-tuple-element.365), channel_id=1, source_target_pairs={{0,1},{1,0},{2,3},{3,2},{4,5},{5,4},{6,7},{7,6},{8,9},{9,8},{10,11... | collective-permute-start | bytes 7077896 | tf_op jit(solution)/shard_map/ppermute | solution.py:193
  563.4 29.9 %collective-permute-start.48 = (bf16[16,112,768]{2,1,0:T(8,128)(2,1)}, bf16[16,112,768]{2,1,0:T(8,128)(2,1)}, u32[]{:S(2)}, u32[]{:S(2)}) collective-permute-start(bf16[16,112,768]{2,1,0:T(8,128)(2,1)} %get-tuple-element.363), channel_id=1, source_target_pairs={{0,1},{1,0},{2,3},{3,2},{4,5},{5,4},{6,7},{7,6},{8,9},{9,8},{10,11... | collective-permute-start | bytes 8257544 | tf_op jit(solution)/shard_map/ppermute | solution.py:193
  591.8 73.0 %collective-permute-start.51 = (bf16[2,4,96,768]{3,2,1,0:T(8,128)(2,1)}, bf16[2,4,96,768]{3,2,1,0:T(8,128)(2,1)}, u32[]{:S(2)}, u32[]{:S(2)}) collective-permute-start(bf16[2,4,96,768]{3,2,1,0:T(8,128)(2,1)} %get-tuple-element.571.refs_2_), channel_id=1, source_target_pairs={{0,4},{4,0},{8,12},{12,8},{16,20},{20,16},{24,28},{28,24},{1,5},{5... | collective-permute-start | bytes 3538952 | tf_op jit(solution)/shard_map/ppermute | solution.py:193
  597.3 88.5 %collective-permute-start.50 = (bf16[2,4,112,768]{3,2,1,0:T(8,128)(2,1)}, bf16[2,4,112,768]{3,2,1,0:T(8,128)(2,1)}, u32[]{:S(2)}, u32[]{:S(2)}) collective-permute-start(bf16[2,4,112,768]{3,2,1,0:T(8,128)(2,1)} %bitcast.54.refs_1_), channel_id=1, source_target_pairs={{0,2},{1,3},{2,0},{3,1},{4,6},{5,7},{6,4},{7,5},{8,10},{9,11},{10,... | collective-permute-start | bytes 4128776 | tf_op jit(solution)/shard_map/ppermute | solution.py:193
  663.1 53.6 %collective-permute-start.52 = (bf16[8,104,1536]{2,1,0:T(8,128)(2,1)}, bf16[8,104,1536]{2,1,0:T(8,128)(2,1)}, u32[]{:S(2)}, u32[]{:S(2)}) collective-permute-start(bf16[8,104,1536]{2,1,0:T(8,128)(2,1)} %pad_dynamic-update-slice_fusion.3.refs_1_), channel_id=1, source_target_pairs={{0,1},{1,0},{2,3},{3,2},{4,5},{5,4},{6,7},{7,6},{8,9},{9,8},{10,11... | collective-permute-start | bytes 7667720 | tf_op jit(solution)/shard_map/ppermute | solution.py:193
  667.6 15.4 %collective-permute-start.54 = (bf16[4,96,768]{2,1,0:T(8,128)(2,1)}, bf16[4,96,768]{2,1,0:T(8,128)(2,1)S(1)}, u32[]{:S(2)}, u32[]{:S(2)}) collective-permute-start(bf16[4,96,768]{2,1,0:T(8,128)(2,1)} %get-tuple-element.583.refs_2_), channel_id=1, source_target_pairs={{0,2},{1,3},{2,0},{3,1},{4,6},{5,7},{6,4},{7,5},{8,10},{9,11},{10,... | collective-permute-start | bytes 1769480 | tf_op jit(solution)/shard_map/ppermute | solution.py:193
  688.6 16.9 %collective-permute-start.53 = (bf16[4,112,768]{2,1,0:T(8,128)(2,1)}, bf16[4,112,768]{2,1,0:T(8,128)(2,1)}, u32[]{:S(2)}, u32[]{:S(2)}) collective-permute-start(bf16[4,112,768]{2,1,0:T(8,128)(2,1)} %get-tuple-element.575.refs_1_), channel_id=1, source_target_pairs={{0,4},{4,0},{8,12},{12,8},{16,20},{20,16},{24,28},{28,24},{1,5},{5... | collective-permute-start | bytes 2064392 | tf_op jit(solution)/shard_map/ppermute | solution.py:193
  695.1 15.7 %collective-permute-start.71 = (bf16[1,96,768]{2,1,0:T(8,128)(2,1)S(1)}, bf16[1,96,768]{2,1,0:T(8,128)(2,1)S(1)}, u32[]{:S(2)}, u32[]{:S(2)}) collective-permute-start(bf16[1,96,768]{2,1,0:T(8,128)(2,1)S(1)} %add_convert_fusion.33.refs_2_), channel_id=1, source_target_pairs={{0,16},{4,20},{8,24},{12,28},{16,0},{20,4},{24,8},{28,12},{1,17},{... | collective-permute-start | bytes 442376 | tf_op jit(solution)/shard_map/ppermute | solution.py:193
  715.1 40.0 %collective-permute-start.70 = (bf16[1,112,768]{2,1,0:T(8,128)(2,1)S(1)}, bf16[1,112,768]{2,1,0:T(8,128)(2,1)S(1)}, u32[]{:S(2)}, u32[]{:S(2)}) collective-permute-start(bf16[1,112,768]{2,1,0:T(8,128)(2,1)S(1)} %add_convert_fusion.29.refs_1_), channel_id=1, source_target_pairs={{0,16},{4,20},{8,24},{12,28},{16,0},{20,4},{24,8},{28,12},{1,17},{... | collective-permute-start | bytes 516104 | tf_op jit(solution)/shard_map/ppermute | solution.py:193
  719.6 37.4 %collective-permute-start.55 = (bf16[2,2,104,1536]{3,2,1,0:T(8,128)(2,1)}, bf16[2,2,104,1536]{3,2,1,0:T(8,128)(2,1)}, u32[]{:S(2)}, u32[]{:S(2)}) collective-permute-start(bf16[2,2,104,1536]{3,2,1,0:T(8,128)(2,1)} %fusion.54.refs_1_), channel_id=1, source_target_pairs={{0,4},{4,0},{8,12},{12,8},{16,20},{20,16},{24,28},{28,24},{1,5},{5... | collective-permute-start | bytes 3833864 | tf_op jit(solution)/shard_map/ppermute | solution.py:193
  748.8 59.3 %collective-permute-start.60 = (bf16[16,96,768]{2,1,0:T(8,128)(2,1)}, bf16[16,96,768]{2,1,0:T(8,128)(2,1)}, u32[]{:S(2)}, u32[]{:S(2)}) collective-permute-start(bf16[16,96,768]{2,1,0:T(8,128)(2,1)} %get-tuple-element.391), channel_id=1, source_target_pairs={{0,1},{1,0},{2,3},{3,2},{4,5},{5,4},{6,7},{7,6},{8,9},{9,8},{10,11... | collective-permute-start | bytes 7077896 | tf_op jit(solution)/shard_map/ppermute | solution.py:193
  748.8 67.9 %collective-permute-start.59 = (bf16[16,112,768]{2,1,0:T(8,128)(2,1)}, bf16[16,112,768]{2,1,0:T(8,128)(2,1)}, u32[]{:S(2)}, u32[]{:S(2)}) collective-permute-start(bf16[16,112,768]{2,1,0:T(8,128)(2,1)} %get-tuple-element.389), channel_id=1, source_target_pairs={{0,1},{1,0},{2,3},{3,2},{4,5},{5,4},{6,7},{7,6},{8,9},{9,8},{10,11... | collective-permute-start | bytes 8257544 | tf_op jit(solution)/shard_map/ppermute | solution.py:193
  759.7 27.7 %collective-permute-start.58 = (bf16[2,104,1536]{2,1,0:T(8,128)(2,1)}, bf16[2,104,1536]{2,1,0:T(8,128)(2,1)}, u32[]{:S(2)}, u32[]{:S(2)}) collective-permute-start(bf16[2,104,1536]{2,1,0:T(8,128)(2,1)} %get-tuple-element.579.refs_3_), channel_id=1, source_target_pairs={{0,8},{4,12},{8,0},{12,4},{16,24},{20,28},{24,16},{28,20},{1,9},{5... | collective-permute-start | bytes 1916936 | tf_op jit(solution)/shard_map/ppermute | solution.py:193
  788.4 16.9 %collective-permute-start.61 = (bf16[104,1536]{1,0:T(8,128)(2,1)S(1)}, bf16[104,1536]{1,0:T(8,128)(2,1)S(1)}, u32[]{:S(2)}, u32[]{:S(2)}) collective-permute-start(bf16[104,1536]{1,0:T(8,128)(2,1)S(1)} %fusion.136.refs_3_), channel_id=1, source_target_pairs={{0,16},{4,20},{8,24},{12,28},{16,0},{20,4},{24,8},{28,12},{1,17},{... | collective-permute-start | bytes 958472 | tf_op jit(solution)/shard_map/ppermute | solution.py:193
  812.7 38.7 %collective-permute-start.66 = (bf16[2,4,96,768]{3,2,1,0:T(8,128)(2,1)}, bf16[2,4,96,768]{3,2,1,0:T(8,128)(2,1)}, u32[]{:S(2)}, u32[]{:S(2)}) collective-permute-start(bf16[2,4,96,768]{3,2,1,0:T(8,128)(2,1)} %get-tuple-element.569.refs_5_), channel_id=1, source_target_pairs={{0,4},{4,0},{8,12},{12,8},{16,20},{20,16},{24,28},{28,24},{1,5},{5... | collective-permute-start | bytes 3538952 | tf_op jit(solution)/shard_map/ppermute | solution.py:193
  816.8 31.4 %collective-permute-start.79 = (bf16[104,1536]{1,0:T(8,128)(2,1)}, bf16[104,1536]{1,0:T(8,128)(2,1)}, u32[]{:S(2)}, u32[]{:S(2)}) collective-permute-start(bf16[104,1536]{1,0:T(8,128)(2,1)} %add_convert_fusion.20), channel_id=1, source_target_pairs={{0,1},{1,0},{2,3},{3,2},{4,5},{5,4},{6,7},{7,6},{8,9},{9,8},{10,11... | collective-permute-start | bytes 958472 | tf_op jit(solution)/shard_map/ppermute | solution.py:193
  820.7 33.3 %collective-permute-start.62 = (bf16[2,4,112,768]{3,2,1,0:T(8,128)(2,1)}, bf16[2,4,112,768]{3,2,1,0:T(8,128)(2,1)}, u32[]{:S(2)}, u32[]{:S(2)}) collective-permute-start(bf16[2,4,112,768]{3,2,1,0:T(8,128)(2,1)} %bitcast.79.refs_4_), channel_id=1, source_target_pairs={{0,2},{1,3},{2,0},{3,1},{4,6},{5,7},{6,4},{7,5},{8,10},{9,11},{10,... | collective-permute-start | bytes 4128776 | tf_op jit(solution)/shard_map/ppermute | solution.py:193
  838.2 55.0 %collective-permute-start.72 = (bf16[8,104,1536]{2,1,0:T(8,128)(2,1)}, bf16[8,104,1536]{2,1,0:T(8,128)(2,1)}, u32[]{:S(2)}, u32[]{:S(2)}) collective-permute-start(bf16[8,104,1536]{2,1,0:T(8,128)(2,1)} %pad_dynamic-update-slice_fusion.1.refs_1_), channel_id=1, source_target_pairs={{0,1},{1,0},{2,3},{3,2},{4,5},{5,4},{6,7},{7,6},{8,9},{9,8},{10,11... | collective-permute-start | bytes 7667720 | tf_op jit(solution)/shard_map/ppermute | solution.py:193
  853.1 15.6 %collective-permute-start.67 = (bf16[4,96,768]{2,1,0:T(8,128)(2,1)S(1)}, bf16[4,96,768]{2,1,0:T(8,128)(2,1)S(1)}, u32[]{:S(2)}, u32[]{:S(2)}) collective-permute-start(bf16[4,96,768]{2,1,0:T(8,128)(2,1)S(1)} %get-tuple-element.581.refs_3_), channel_id=1, source_target_pairs={{0,2},{1,3},{2,0},{3,1},{4,6},{5,7},{6,4},{7,5},{8,10},{9,11},{10,... | collective-permute-start | bytes 1769480 | tf_op jit(solution)/shard_map/ppermute | solution.py:193
  856.4 22.2 %collective-permute-start.63 = (bf16[4,112,768]{2,1,0:T(8,128)(2,1)S(1)}, bf16[4,112,768]{2,1,0:T(8,128)(2,1)S(1)}, u32[]{:S(2)}, u32[]{:S(2)}) collective-permute-start(bf16[4,112,768]{2,1,0:T(8,128)(2,1)S(1)} %get-tuple-element.573.refs_2_), channel_id=1, source_target_pairs={{0,4},{4,0},{8,12},{12,8},{16,20},{20,16},{24,28},{28,24},{1,5},{5... | collective-permute-start | bytes 2064392 | tf_op jit(solution)/shard_map/ppermute | solution.py:193
  893.2 35.1 %collective-permute-start.65 = (bf16[1,112,768]{2,1,0:T(8,128)(2,1)}, bf16[1,112,768]{2,1,0:T(8,128)(2,1)}, u32[]{:S(2)}, u32[]{:S(2)}) collective-permute-start(bf16[1,112,768]{2,1,0:T(8,128)(2,1)} %add_convert_fusion.27), channel_id=1, source_target_pairs={{0,16},{4,20},{8,24},{12,28},{16,0},{20,4},{24,8},{28,12},{1,17},{... | collective-permute-start | bytes 516104 | tf_op jit(solution)/shard_map/ppermute | solution.py:193
  913.0 66.2 %all-to-all-start.7 = ((bf16[32,32,768]{2,1,0:T(8,128)(2,1)}), bf16[32,32,768]{2,1,0:T(8,128)(2,1)}, u32[]{:S(2)}, u32[]{:S(2)}) async-start(bf16[32,32,768]{2,1,0:T(8,128)(2,1)} %bitcast.473), calls=%async_computation.7 | async-start | bytes 3145728 | tf_op jit(solution)/shard_map/all_to_all | solution.py:816
  926.6 49.9 %collective-permute-start.73 = (bf16[2,2,104,1536]{3,2,1,0:T(8,128)(2,1)}, bf16[2,2,104,1536]{3,2,1,0:T(8,128)(2,1)}, u32[]{:S(2)}, u32[]{:S(2)}) collective-permute-start(bf16[2,2,104,1536]{3,2,1,0:T(8,128)(2,1)} %fusion.55.refs_1_), channel_id=1, source_target_pairs={{0,4},{4,0},{8,12},{12,8},{16,20},{20,16},{24,28},{28,24},{1,5},{5... | collective-permute-start | bytes 3833864 | tf_op jit(solution)/shard_map/ppermute | solution.py:193
  930.7 42.9 %collective-permute-start.81 = (bf16[2,2,384,128]{3,2,1,0:T(8,128)(2,1)S(1)}, bf16[2,2,384,128]{3,2,1,0:T(8,128)(2,1)S(1)}, u32[]{:S(2)}, u32[]{:S(2)}) collective-permute-start(bf16[2,2,384,128]{3,2,1,0:T(8,128)(2,1)S(1)} %fusion.131), channel_id=1, source_target_pairs={{0,4},{4,0},{8,12},{12,8},{16,20},{20,16},{24,28},{28,24},{1,5},{5... | collective-permute-start | bytes 1179656 | tf_op jit(solution)/shard_map/ppermute | solution.py:193
  979.2 18.3 %collective-permute-start.74 = (bf16[2,104,1536]{2,1,0:T(8,128)(2,1)}, bf16[2,104,1536]{2,1,0:T(8,128)(2,1)}, u32[]{:S(2)}, u32[]{:S(2)}) collective-permute-start(bf16[2,104,1536]{2,1,0:T(8,128)(2,1)} %get-tuple-element.577), channel_id=1, source_target_pairs={{0,8},{4,12},{8,0},{12,4},{16,24},{20,28},{24,16},{28,20},{1,9},{5... | collective-permute-start | bytes 1916936 | tf_op jit(solution)/shard_map/ppermute | solution.py:193
  985.4 20.6 %collective-permute-start.83 = (bf16[384,128]{1,0:T(8,128)(2,1)S(1)}, bf16[384,128]{1,0:T(8,128)(2,1)S(1)}, u32[]{:S(2)}, u32[]{:S(2)}) collective-permute-start(bf16[384,128]{1,0:T(8,128)(2,1)S(1)} %fusion.162), channel_id=1, source_target_pairs={{0,16},{4,20},{8,24},{12,28},{16,0},{20,4},{24,8},{28,12},{1,17},{... | collective-permute-start | bytes 294920 | tf_op jit(solution)/shard_map/ppermute | solution.py:193
  998.5 15.9 %collective-permute-start.75 = (bf16[104,1536]{1,0:T(8,128)(2,1)S(1)}, bf16[104,1536]{1,0:T(8,128)(2,1)S(1)}, u32[]{:S(2)}, u32[]{:S(2)}) collective-permute-start(bf16[104,1536]{1,0:T(8,128)(2,1)S(1)} %fusion.139), channel_id=1, source_target_pairs={{0,16},{4,20},{8,24},{12,28},{16,0},{20,4},{24,8},{28,12},{1,17},{... | collective-permute-start | bytes 958472 | tf_op jit(solution)/shard_map/ppermute | solution.py:193
  1007.0 17.6 %collective-permute-start.84 = (bf16[384,128]{1,0:T(8,128)(2,1)S(1)}, bf16[384,128]{1,0:T(8,128)(2,1)S(1)}, u32[]{:S(2)}, u32[]{:S(2)}) collective-permute-start(bf16[384,128]{1,0:T(8,128)(2,1)S(1)} %fusion.146), channel_id=1, source_target_pairs={{0,2},{1,3},{2,0},{3,1},{4,6},{5,7},{6,4},{7,5},{8,10},{9,11},{10,... | collective-permute-start | bytes 294920 | tf_op jit(solution)/shard_map/ppermute | solution.py:193
  (520 other events, 4104.5 us)

commit v3 on v2

--- a/solution.py
+++ b/solution.py
@@ -289,6 +289,60 @@
     text_pre[...] = embedded[...] + text_pos[...]
     text[...] = norm_apply(text_pre[...], text_emb[0:1, :], text_emb[1:2, :])
     layout[...] = norm_apply(layout_pre[...], layout_emb[0:1, :], layout_emb[1:2, :])
+
+
+def norm_grads(values, gain, grad):
+    centre = values - jnp.mean(values, axis=-1, keepdims=True)
+    scale = lax.rsqrt(jnp.mean(centre * centre, axis=-1, keepdims=True) + EPSILON)
+    unit = centre * scale
+    lifted = grad * gain
+    inner = jnp.mean(lifted * unit, axis=-1, keepdims=True)
+    back = scale * (lifted - jnp.mean(lifted, axis=-1, keepdims=True) - unit * inner)
+    sums = [jnp.sum(item, 0, keepdims=True) for item in (grad * unit, grad)]
+    return back, jnp.concatenate(sums, 0)
+
+
+def embed_back_kernel(coords, text_pre, layout_pre, text_emb, layout_emb, *refs):
+    grad_text, grad_layout, text_back, layout_back, text_sums, layout_sums, boxes = refs
+    low = jnp.bfloat16
+    quarter = LAYOUT_WIDTH // 4
+    text_back[...], text_sums[...] = norm_grads(text_pre[...], text_emb[0:1, :], grad_text[...])
+    looked, layout_sums[...] = norm_grads(
+        layout_pre[...], layout_emb[0:1, :], grad_layout[...]
+    )
+    layout_back[...] = looked
+    high, rest = split_high(looked)
+    row = lax.broadcasted_iota(jnp.int32, (PAGE_SLOTS, BOXES // 8), 1)
+    lanes = lax.broadcasted_iota(jnp.int32, (PAGE_SLOTS, 8 * quarter), 1) // quarter
+    fold_in = lax.broadcasted_iota(jnp.int32, (8 * quarter, LAYOUT_WIDTH), 0) % quarter
+    fold_out = lax.broadcasted_iota(jnp.int32, (8 * quarter, LAYOUT_WIDTH), 1)
+    boxes[...] = jnp.zeros_like(boxes)
+    for number in range(4):
+        spot = coords[:, number : number + 1]
+        marks = (spot // 8 == row).astype(jnp.float32).astype(low)
+        fold = (fold_in + number * quarter == fold_out).astype(jnp.float32).astype(low)
+        wide = contract_cols(high, fold) + contract_cols(rest, fold)
+        kept = jnp.where(spot % 8 == lanes, wide, 0.0)
+        boxes[number % 2] += add_rows(marks, kept)
+
+
+def embed_back(*operands):
+    whole = pl.BlockSpec(memory_space=pltpu.VMEM)
+    shapes = [
+        (PAGE_SLOTS, WIDTH),
+        (PAGE_SLOTS, LAYOUT_WIDTH),
+        (2, WIDTH),
+        (2, LAYOUT_WIDTH),
+        (2, BOXES // 8, 2 * LAYOUT_WIDTH),
+    ]
+    return pl.pallas_call(
+        embed_back_kernel,
+        out_shape=[jax.ShapeDtypeStruct(shape, jnp.float32) for shape in shapes],
+        in_specs=[whole] * len(operands),
+        out_specs=[whole] * len(shapes),
+        cost_estimate=pl.CostEstimate(flops=0, bytes_accessed=2000000, transcendentals=0),
+        compiler_params=pltpu.CompilerParams(vmem_limit_bytes=32 * 1024 * 1024),
+    )(*operands)
 
 
 def embed_streams(*operands):
@@ -1060,7 +1114,7 @@
 
     def after_attend(self, value):
         if self.mats:
-            return self.step(value, self.units[0] + self.mats[:1] + self.units[1])
+            return self.step(value, self.units[1])
         return value
 
     def after_mats(self, text, layout):
@@ -1089,7 +1143,7 @@
     def between(self, value):
         if len(self.mats) == 1:
             return self.step(tie(value, self.mats[0].sent), self.units[0])
-        return self.step(tie(value, self.mats[1].sent), self.mats[:1])
+        return self.step(tie(value, self.mats[1].sent), self.units[0] + self.mats[:1])
 
 
 def split_high(values):
@@ -1147,30 +1201,13 @@
 
     own_ids = lax.dynamic_index_in_dim(token_ids, lane, 0, keepdims=False)
     own_targets = lax.dynamic_index_in_dim(mlm_targets, lane, 0, keepdims=False)
-    shown = show_all(
-        jnp.concatenate([own_ids, own_targets, jnp.broadcast_to(page_lengths, (mask_slots,))])
-    )
-    all_ids = shown[:, :slots]
-    all_targets = shown[:, slots : slots + mask_slots].reshape(-1)
-    all_lengths = shown[:, slots + mask_slots]
     table_low = table.astype(low)
     own_block = lane * dp + spot
     steps = jnp.arange(slots)
-    earlier = steps[None, :] < steps[:, None]
-    all_first = ~jnp.any((all_ids[:, :, None] == all_ids[:, None, :]) & earlier[None], -1)
-    all_blocks = all_ids // vocab_rows
-    counts = jnp.sum(
-        (all_blocks[:, None, :] == jnp.arange(count)[None, :, None]) & all_first[:, None, :],
-        -1,
-        dtype=jnp.int32,
-    )
-    rounds = (jnp.max(counts) + ROUND_ROWS - 1) // ROUND_ROWS
-    mine = all_first & (all_blocks == own_block)
-    order = contract_cols(mine.astype(low), earlier.astype(low)).astype(jnp.int32)
-    local = all_ids - own_block * vocab_rows
-    page_first = lax.dynamic_index_in_dim(all_first, spot * mp + lane, 0, keepdims=False)
-    same = own_ids[:, None] == own_ids[None, :]
-    first_at = jnp.min(jnp.where(same, steps[None, :], slots), 1)
+    first_at = jnp.min(
+        jnp.where(own_ids[:, None] == own_ids[None, :], steps[None, :], slots), 1
+    )
+    page_first = first_at == steps
     block_own = own_ids // vocab_rows
     rank = jnp.sum(
         page_first[None, :]
@@ -1180,22 +1217,33 @@
         dtype=jnp.int32,
     )
     source = (block_own % dp) * mp + block_own // dp
-
-    def asked_marks(turn):
-        turn_rank = order - turn * ROUND_ROWS
-        chosen = mine[:, None, :] & (turn_rank[:, None, :] == jnp.arange(ROUND_ROWS)[None, :, None])
-        rows = jnp.sum(jnp.where(chosen, local[:, None, :] + 1, 0), -1).reshape(-1) - 1
-        return (rows[:, None] == jnp.arange(vocab_rows)[None, :]).astype(low)
-
-    def held_marks(turn):
+    local_own = own_ids - block_own * vocab_rows
+    places = jnp.arange(count * ROUND_ROWS)
+
+    def place_of(turn):
         turn_rank = rank - turn * ROUND_ROWS
         inside = (turn_rank >= 0) & (turn_rank < ROUND_ROWS)
-        place = jnp.where(inside, source * ROUND_ROWS + turn_rank, -1)
-        return (place[:, None] == jnp.arange(count * ROUND_ROWS)[None, :]).astype(low)
-
-    def fetch(turn, so_far):
-        rows = jnp.dot(asked_marks(turn), table_low, preferred_element_type=jnp.float32)
-        sent = rows.astype(low)
+        return jnp.where(inside, source * ROUND_ROWS + turn_rank, -1)
+
+    def requests(turn):
+        asked = (place_of(turn)[None, :] == places[:, None]) & page_first[None, :]
+        rows = jnp.sum(jnp.where(asked, local_own[None, :] + 1, 0), 1, dtype=jnp.int32) - 1
+        return rows.reshape(count, ROUND_ROWS)
+
+    def settle(chains, left):
+        for chain in chains:
+            while len(chain.joined) + len(chain.apart) > left:
+                chain.advance()
+
+    def marks_of(rows):
+        return (rows.reshape(-1)[:, None] == jnp.arange(vocab_rows)[None, :]).astype(low)
+
+
+    def held_marks(turn):
+        return (place_of(turn)[:, None] == places[None, :]).astype(low)
+
+    def fetch(turn, marks, so_far):
+        sent = jnp.dot(marks, table_low, preferred_element_type=jnp.float32).astype(low)
         came = trade(sent)
         return (
             so_far + jnp.dot(held_marks(turn), came, preferred_element_type=jnp.float32),
@@ -1240,25 +1288,54 @@
         for layer_no in range(LAYERS)
     ]
     far_steps = len(routes()[0])
-    embedded, came_first, rows_first = fetch(0, jnp.zeros((slots, WIDTH), jnp.float32))
+    told = jnp.concatenate(
+        [
+            jnp.max(rank, keepdims=True) // ROUND_ROWS + 1,
+            page_lengths,
+            own_targets,
+        ]
+    )
+    told = jnp.broadcast_to(told[None], (count, mask_slots + 2))
+    spare = jnp.zeros((count, -(ROUND_ROWS + mask_slots + 2) % 128), jnp.int32)
+    message = jnp.concatenate([requests(0), told, spare], 1)
+    mats_chains[0].advance()
+    extra_chain.advance()
+    extra_chain.advance()
+    shown = trade(tie(message, *extra_chain.sent))
+    mats_chains[0].advance()
+    extra_chain.advance()
+    shown = tie(shown, *mats_chains[0].sent, *extra_chain.sent)
+    rounds = jnp.max(shown[:, ROUND_ROWS])
+    all_lengths = shown[:, ROUND_ROWS + 1]
+    all_targets = shown[:, ROUND_ROWS + 2 : ROUND_ROWS + 2 + mask_slots].reshape(-1)
+
+    asked_first = marks_of(shown[:, :ROUND_ROWS])
+    embedded, came_first, rows_first = fetch(
+        0, asked_first, jnp.zeros((slots, WIDTH), jnp.float32)
+    )
     embedded = lax.fori_loop(
-        1, rounds, lambda turn, so_far: fetch(turn, so_far)[0], embedded
-    )
-    for number in range(far_steps + 1):
-        extra_wait = extra_chain.advance()
-        if number < far_steps:
-            mats_chains[0].advance()
-    mats_chains[0].advance()
-    extra_chain.advance(rows_first)
-    mats_chains[0].advance()
-    for number in range(far_steps):
-        for chain in unit_chains[0]:
-            chain.advance(extra_wait)
-        extra_wait = unit_chains[0][1].sent[0]
+        1,
+        rounds,
+        lambda turn, so_far: fetch(turn, marks_of(trade(requests(turn))), so_far)[0],
+        embedded,
+    )
+    settle(mats_chains[:1], 2)
+    mats_chains[0].advance(rows_first)
+    settle([extra_chain], 1)
+    extra_chain.advance(mats_chains[0].sent[0])
+    wait = extra_chain.sent[0]
+    for chain in unit_chains[0]:
+        chain.advance(wait)
     core_key = frozenset([routes()[3]])
-    extra_chain.pieces[core_key] = tie(extra_chain.pieces[core_key], came_first)
+    extra_chain.pieces[core_key] = tie(
+        extra_chain.pieces[core_key], *[chain.sent[0] for chain in unit_chains[0]]
+    )
     small_parts, lmats_all = unpack_small(*half_parts(extra_chain), lmats_half.shape[0])
     lmats_all = lmats_all.reshape(2, dp, LAYERS, -1, 2 * LAYOUT_WIDTH)
+    mats_chains[0].advance(tie(came_first, small_parts[6]))
+    for number in range(1, far_steps):
+        for chain in unit_chains[0]:
+            chain.advance(mats_chains[0].sent[0])
     tmats_first = put_in_order(*half_parts(mats_chains[0]))
     (
         text_vec,
@@ -1273,16 +1350,9 @@
         align_mat,
     ) = small_parts
 
-    quarter = LAYOUT_WIDTH // 4
-    lanes = jnp.arange(8 * quarter)
-    fold = (lanes[:, None] % quarter == jnp.arange(quarter)[None, :]).astype(low)
-    box_marks, box_masks = [], []
-    for number in range(4):
-        coords = box_coords[number, 0][:, None]
-        box_marks.append((coords // 8 == jnp.arange(BOXES // 8)[None, :]).astype(low))
-        box_masks.append(coords % 8 == lanes[None, :] // quarter)
+    coords = box_coords[:, 0].T
     text_pre, layout_pre, text, layout = embed_streams(
-        box_coords[:, 0].T, embedded, text_pos, layout_pos, box_table, text_emb, layout_emb
+        coords, embedded, text_pos, layout_pos, box_table, text_emb, layout_emb
     )
     caches = []
     layer_weights = []
@@ -1294,11 +1364,6 @@
             waits = waits + chain.sent
         return tie(value, *waits)
 
-    def settle(chains, left):
-        for chain in chains:
-            while len(chain.joined) + len(chain.apart) > left:
-                chain.advance()
-
     def after(chains, wait):
         for chain in chains:
             chain.advance(wait)
@@ -1313,24 +1378,24 @@
             if layer_no == 0:
                 value = push(value, units)
             if later:
-                value = push(value, [next_mats])
+                next_mats.advance(units[1].sent[0])
             return value
 
         def at_query(value):
-            if layer_no:
-                value = push(value, units)
-            if later:
-                value = push(value, [next_mats])
-            return value
+            return push(value, units) if layer_no else value
 
         def at_att(value):
             settle(units, 2)
-            value = push(value, units + ([next_mats] if later else []))
+            pending = [chain for chain in units if len(chain.joined) + len(chain.apart) > 1]
+            if pending or later:
+                value = push(value, pending + ([next_mats] if later else []))
             after(units, value)
+            if later:
+                after(next_units, next_mats.sent[0])
             return value
 
         def at_mid(value):
-            return push(value, next_units) if later else value
+            return push(value, [next_mats] + next_units) if later else value
 
         return {
             "low": at_low,
@@ -1437,36 +1502,23 @@
         )
         grad_text = plan.between(grad_text)
 
-    embed_grad, *text_emb_grad = norm_back(text_pre, text_emb[0], text_emb[1], grad_text)
-    looked_grad, *layout_emb_grad = norm_back(
-        layout_pre,
-        layout_emb[0],
-        layout_emb[1],
-        tie(grad_layout, plan.mats[1].advance()),
-    )
-    text_emb_grad, layout_emb_grad = jnp.stack(text_emb_grad), jnp.stack(layout_emb_grad)
-    box_parts = []
-    for number in range(4):
-        high, rest = split_high(looked_grad[:, number * quarter : (number + 1) * quarter])
-        wide = contract_cols(high, fold) + contract_cols(rest, fold)
-        box_parts.append(jnp.where(box_masks[number], wide, 0.0))
-    box_grad = jnp.stack(
-        [
-            add_rows(
-                jnp.concatenate([box_marks[side], box_marks[side + 2]], 0),
-                jnp.concatenate([box_parts[side], box_parts[side + 2]], 0),
-            )
-            for side in range(2)
-        ]
+    embed_grad, looked_grad, text_emb_grad, layout_emb_grad, box_grad = embed_back(
+        coords, text_pre, layout_pre, text_emb, layout_emb, grad_text, grad_layout
     )
     embed_low = embed_grad.astype(low)
 
-    def give(turn, so_far):
+    def give(turn, marks, so_far):
         sent = contract_rows(held_marks(turn), embed_low).astype(low)
-        return (so_far + contract_rows(asked_marks(turn), trade(sent)), sent)
-
-    table_sum, gave_rows = give(0, table_grad)
-    table_sum = lax.fori_loop(1, rounds, lambda turn, so_far: give(turn, so_far)[0], table_sum)
+        came = trade(sent)
+        return (so_far + contract_rows(marks, came), sent, came)
+
+    table_sum, gave_rows, gave_came = give(0, asked_first, table_grad)
+    table_sum = lax.fori_loop(
+        1,
+        rounds,
+        lambda turn, so_far: give(turn, marks_of(trade(requests(turn))), so_far)[0],
+        table_sum,
+    )
 
     def stacked(member):
         return jnp.stack([layer_grads[layer_no][member] for layer_no in range(LAYERS)])
@@ -1496,20 +1548,25 @@
         box_grad,
         align_grad,
     ]
-    small_items[6] = tie(
-        embed_grad, gave_rows, *[item.advance() for item in plan.units[1]]
-    )
+    plan.mats[1].advance()
+    token = plan.mats[1].sent
+    small_items[6] = tie(embed_grad, token, gave_rows)
     small_blocks = pack_small(small_items, dp).reshape(dp, 2, half_rows, 128)
     first = own_bit("mp", 0) == 0
     small_total = HalfSum(
         jnp.where(first, small_blocks[:, 1], small_blocks[:, 0]),
         jnp.where(first, small_blocks[:, 0], small_blocks[:, 1]),
     )
-    chains = [plan.mats[1], small_total] + plan.units[1] + plan.units[0] + plan.mats[:1]
-    while any(chain.left for chain in chains):
-        for chain in chains:
-            if chain.left:
-                chain.advance()
+    token = small_total.sent
+    turns = plan.units[1] + [small_total] + plan.units[1] + [plan.mats[1], small_total]
+    turns = turns + plan.units[1] + [plan.mats[1], small_total] * 4
+    for number, chain in enumerate(turns):
+        if chain.left:
+            chain.came = tie(chain.came, token)
+            chain.advance()
+            token = chain.sent
+        if number == 6:
+            token = tie(gave_came, token)
     small_sum = small_total.finish().reshape(-1)[:share]
     plan.units.reverse()
     plan.mats.reverse()

time: 1100 us -> 1030 us (0.936)
  waiting for transfers between devices: 272 us -> 238 us
  matrix products: 116 us -> 94 us
  starting transfers between devices: 114 us -> 100 us
  other arithmetic: 240 us -> 229 us
    ppermute x91, waiting for transfers between devices: 208 us -> 176 us  [hop(): return lax.ppermute(values, axis, pairs)]
    all_to_all x3 -> x2, waiting for transfers between devices: 48.4 us -> 23.5 us  [show_all(): lax.all_to_all(jnp.broadcast_to(values[None], (count,) + values.shape), e...]
    all_to_all x3 -> x4, waiting for transfers between devices: 15.7 us -> 38.7 us  [trade(): return lax.all_to_all(values, ('dp', 'mp'), 0, 0, tiled=True)]
    convert_element_type x34 -> x36, other arithmetic: 59.9 us -> 70.9 us  [add_low(): (kept.astype(jnp.float32) + came.astype(jnp.float32)).astype(jnp.bfloat16)]
    dot_general x22 -> x13, matrix products: 38.7 us -> 27.7 us  [contract_cols(): lax.dot_general(left, right, (((1,), (1,)), ((), ())), preferred_element_...]
    unnamed x978 -> x956, local copies, waits for them, and re-layouts: 91.1 us -> 94.5 us
    dot_general x17 -> x13, matrix products: 28.7 us -> 25.6 us  [contract_rows(): lax.dot_general(left, right, (((0,), (0,)), ((), ())), preferred_element_...]
  transfers between devices with their start and end apart: 97 -> 97, of which waited for: 36 -> 39; matrix products, arithmetic and copies ran while one was open for 33% -> 31% of each run, Pallas kernels for 13% -> 14%
where the time goes in v3:
time: 1030 us; the launch traced here: 1020 us
  waiting for transfers between devices  238 us (23%)
  other arithmetic  229 us (22%)
  Pallas kernels  181 us (18%)
  local copies, waits for them, and re-layouts  158 us (15%)
  starting transfers between devices  100 us (10%)
  matrix products  94 us (9%)
  between operations  18.4 us (2%)
    ppermute x91, waiting for transfers between devices, hop(): return lax.ppermute(values, axis, pairs)  176 us
    unnamed x956, local copies, waits for them, and re-layouts  94.5 us
    ppermute x91, starting transfers between devices, hop(): return lax.ppermute(values, axis, pairs)  76.6 us
    convert_element_type x36, other arithmetic, add_low(): (kept.astype(jnp.float32) + came.astype(jnp.float32)).astype(jnp.bfloat16)  70.9 us
    pallas_call x4, Pallas kernels, ffn_back(): pl.pallas_call(functools.partial(ffn_back_kernel, slot_rows[0] if slot_ro...  48.1 us
    all_to_all x4, waiting for transfers between devices, trade(): return lax.all_to_all(values, ('dp', 'mp'), 0, 0, tiled=True)  38.7 us
    pallas_call x2, Pallas kernels, attend_back(): pl.pallas_call(attend_back_kernel, grid=(HEAD_PAIRS,), in_specs=[pl.Block...  37.1 us
    pallas_call x2, Pallas kernels, attend(): pl.pallas_call(attend_kernel, grid=(HEAD_PAIRS,), in_specs=[pl.BlockSpec(...  32.9 us
  transfers between devices with their start and end apart: 97, of which 39 were waited for; matrix products, arithmetic and copies ran while one was open for 31% of the time, Pallas kernels for 14%

profile of v3, /device:TPU:0, one launch (start us, length us, event | category | flops | bytes accessed | tf_op | source)
XLA Modules:
  0.0 1020.9 jit_solution(16030078187951788465)
XLA Ops:
  2.8 3.0 collective-permute-start
  27.4 4.4 collective-permute-start.4
  31.8 4.8 all-to-all-start.4
  40.3 10.6 %all-to-all-done.4 = s32[32,1,128]{2,1,0:T(1,128)S(1)} async-done(((s32[32,1,128]{2,1,0:T(1,128)}), s32[32,1,128]{2,1,0:T(1,128)S(1)}, u32[]{:S(2)}, u32[]{:S(2)}) %all-to-all-start.4) | async-done | bytes 16416 | tf_op jit(solution)/shard_map/all_to_all | solution.py:870
  53.0 4.4 fusion.30.refs_1_
  57.4 3.7 all-to-all-start.5
  75.3 33.7 %collective-permute-done.9 = bf16[1,96,768]{2,1,0:T(8,128)(2,1)S(1)} collective-permute-done((bf16[1,96,768]{2,1,0:T(8,128)(2,1)}, bf16[1,96,768]{2,1,0:T(8,128)(2,1)S(1)}, u32[]{:S(2)}, u32[]{:S(2)}) %collective-permute-start.9) | collective-permute-done | bytes 147488 | tf_op jit(solution)/shard_map/ppermute | solution.py:193
  127.5 3.6 fusion.23
  146.1 3.7 shard_map.493
  160.2 6.9 collective-permute-done.8
  181.2 3.6 collective-permute-done.31
  187.8 16.4 %collective-permute-done.30 = bf16[2,112,768]{2,1,0:T(8,128)(2,1)} collective-permute-done((bf16[2,112,768]{2,1,0:T(8,128)(2,1)}, bf16[2,112,768]{2,1,0:T(8,128)(2,1)}, u32[]{:S(2)}, u32[]{:S(2)}) %collective-permute-start.30) | collective-permute-done | bytes 344096 | tf_op jit(solution)/shard_map/ppermute | solution.py:193
  221.2 16.5 %shard_map.500 = (bf16[512,768]{1,0:T(8,128)(2,1)S(1)}, bf16[512,192]{1,0:T(8,128)(2,1)S(1)}, f32[6,512,2]{2,1,0:T(8,128)S(1)}) custom-call(s32[1]{0:T(128)S(6)} %copy.490.length, bf16[512,768]{1,0:T(8,128)(2,1)S(1)} %fusion.32.qt, bf16[512,768]{1,0:T(8,128)(2,1)S(1)} %slice.1158.kt, bf16[512,768]{1,0:T(8,128)(2,1)S(1)} %add_convert_fusion.13.vt, ...), custom_call_target="tpu_custom_call" | custom-call | flops 4000000000 | bytes 2000000 | tf_op jit(solution)/shard_map/pallas_call | solution.py:527
  241.1 3.8 fusion.244
  252.3 4.6 collective-permute-done.32
  258.5 3.1 pad_maximum_fusion.1.refs_3_.own_ref
  272.4 4.9 collective-permute-done.34.refs_2_.refs_0_
  283.0 14.3 %shard_map.514 = (bf16[512,3072]{1,0:T(8,128)(2,1)}, bf16[512,3072]{1,0:T(8,128)(2,1)}, f32[512,768]{1,0:T(8,128)S(1)}) custom-call(bf16[512,768]{1,0:T(8,128)(2,1)S(1)} %copy-done.21, f32[1,3072]{1,0:T(1,128)S(1)} %broadcast_in_dim_reshape.15.bias_ref, bf16[4,112,768]{2,1,0:T(8,128)(2,1)} %shard_map.506.refs_0_, bf16[4,112,768]{2,1,0:T(8,128)(2,1)} %shard_map.507.refs_1_, ...), custom_call_target="tpu_custom_call" | custom-call | flops 1207959552 | bytes 3932160 | tf_op jit(solution)/shard_map/pallas_call | solution.py:664
  319.7 16.5 %shard_map.520 = (bf16[512,768]{1,0:T(8,128)(2,1)S(1)}, bf16[512,192]{1,0:T(8,128)(2,1)S(1)}, f32[6,512,2]{2,1,0:T(8,128)S(1)}) custom-call(s32[1]{0:T(128)S(6)} %copy.490.length, bf16[512,768]{1,0:T(8,128)(2,1)S(1)} %copy-done.50, bf16[512,768]{1,0:T(8,128)(2,1)S(1)} %copy-done.96, bf16[512,768]{1,0:T(8,128)(2,1)S(1)} %copy-done.156, ...), custom_call_target="tpu_custom_call" | custom-call | flops 4000000000 | bytes 2000000 | tf_op jit(solution)/shard_map/pallas_call | solution.py:527
  350.6 13.9 %shard_map.529 = (bf16[512,3072]{1,0:T(8,128)(2,1)}, bf16[512,3072]{1,0:T(8,128)(2,1)}, f32[512,768]{1,0:T(8,128)S(1)}) custom-call(bf16[512,768]{1,0:T(8,128)(2,1)S(1)} %fusion.48.rows_ref, f32[1,3072]{1,0:T(1,128)S(1)} %broadcast_in_dim_reshape.17.bias_ref, bf16[4,112,768]{2,1,0:T(8,128)(2,1)S(1)} %copy-done.10, bf16[4,112,768]{2,1,0:T(8,128)(2,1)S(1)} %copy-done.16, ...), custom_call_target="tpu_custom_call" | custom-call | flops 1207959552 | bytes 3932160 | tf_op jit(solution)/shard_map/pallas_call | solution.py:664
  367.8 3.5 all-to-all-start.6
  396.0 12.9 %all-to-all-done.6 = bf16[32,32,768]{2,1,0:T(8,128)(2,1)} async-done(((bf16[32,32,768]{2,1,0:T(8,128)(2,1)}), bf16[32,32,768]{2,1,0:T(8,128)(2,1)}, u32[]{:S(2)}, u32[]{:S(2)}) %all-to-all-start.6) | async-done | bytes 1572896 | tf_op jit(solution)/shard_map/all_to_all | solution.py:864
  408.9 4.9 fusion.247
  417.5 3.9 all-to-all-start.7
  426.4 10.6 %all-to-all-done.7 = f32[32,3,1024]{2,1,0:T(4,128)} async-done(((f32[32,3,1024]{2,1,0:T(4,128)}), f32[32,3,1024]{2,1,0:T(4,128)}, u32[]{:S(2)}, u32[]{:S(2)}) %all-to-all-start.7) | async-done | bytes 393248 | tf_op jit(solution)/shard_map/all_to_all | solution.py:864
  440.3 8.4 convolution_convert_fusion
  448.7 4.0 all-to-all-start.8
  471.1 19.1 %all-to-all-done.8 = bf16[32,32,768]{2,1,0:T(8,128)(2,1)} async-done(((bf16[32,32,768]{2,1,0:T(8,128)(2,1)}), bf16[32,32,768]{2,1,0:T(8,128)(2,1)}, u32[]{:S(2)}, u32[]{:S(2)}) %all-to-all-start.8) | async-done | bytes 1572896 | tf_op jit(solution)/shard_map/all_to_all | solution.py:870
  496.3 21.6 %shard_map.533 = (f32[512,768]{1,0:T(8,128)}, f32[1,3072]{1,0:T(1,128)S(1)}, bf16[16,112,768]{2,1,0:T(8,128)(2,1)}, bf16[16,96,768]{2,1,0:T(8,128)(2,1)}, bf16[1...) custom-call(bf16[512,768]{1,0:T(8,128)(2,1)} %copy-done.28, bf16[512,768]{1,0:T(8,128)(2,1)} %get-tuple-element.670.grad_ref, ...), custom_call_target="tpu_custom_call" | custom-call | flops 2415919104 | bytes 7864320 | tf_op jit(solution)/shard_map/pallas_call | solution.py:965
  527.0 4.2 multiply_reduce_fusion.3
  540.7 3.9 add_convert_fusion.10
  546.1 3.9 add_convert_fusion.2
  557.8 18.5 %shard_map.535 = (bf16[512,768]{1,0:T(8,128)(2,1)S(1)}, bf16[512,768]{1,0:T(8,128)(2,1)S(1)}, bf16[512,768]{1,0:T(8,128)(2,1)S(1)}, bf16[512,192]{1,0:T(8,128)(2...) custom-call(s32[1]{0:T(128)S(6)} %copy.490.length, bf16[512,768]{1,0:T(8,128)(2,1)S(1)} %copy-done.51, ...), custom_call_target="tpu_custom_call" | custom-call | flops 5000000000 | bytes 3000000 | tf_op jit(solution)/shard_map/pallas_call | solution.py:551
  599.2 5.2 shard_map.536
  610.4 4.2 add_add_fusion.5.refs_0_
  622.8 12.0 %collective-permute-done.54 = bf16[4,96,768]{2,1,0:T(8,128)(2,1)} collective-permute-done((bf16[4,96,768]{2,1,0:T(8,128)(2,1)S(1)}, bf16[4,96,768]{2,1,0:T(8,128)(2,1)}, u32[]{:S(2)}, u32[]{:S(2)}) %collective-permute-start.54) | collective-permute-done | bytes 589856 | tf_op jit(solution)/shard_map/ppermute | solution.py:193
  647.9 9.2 collective-permute-done.53
  669.3 3.1 fusion.51.refs_1_
  673.5 22.2 %shard_map.541 = (f32[512,768]{1,0:T(8,128)}, f32[1,3072]{1,0:T(1,128)S(1)}, bf16[16,112,768]{2,1,0:T(8,128)(2,1)}, bf16[16,96,768]{2,1,0:T(8,128)(2,1)}, bf16[1...) custom-call(bf16[512,768]{1,0:T(8,128)(2,1)} %shard_map.505.rows_ref, bf16[512,768]{1,0:T(8,128)(2,1)} %shard_map.539.grad_ref, ...), custom_call_target="tpu_custom_call" | custom-call | flops 2415919104 | bytes 7864320 | tf_op jit(solution)/shard_map/pallas_call | solution.py:965
  719.5 18.6 %shard_map.543 = (bf16[512,768]{1,0:T(8,128)(2,1)S(1)}, bf16[512,768]{1,0:T(8,128)(2,1)S(1)}, bf16[512,768]{1,0:T(8,128)(2,1)S(1)}, bf16[512,192]{1,0:T(8,128)(2...) custom-call(s32[1]{0:T(128)S(6)} %copy.490.length, bf16[512,768]{1,0:T(8,128)(2,1)S(1)} %copy-done.99, ...), custom_call_target="tpu_custom_call" | custom-call | flops 5000000000 | bytes 3000000 | tf_op jit(solution)/shard_map/pallas_call | solution.py:551
  744.2 3.3 fusion.80
  747.5 12.1 %collective-permute-done.81 = bf16[104,1536]{1,0:T(8,128)(2,1)S(1)} collective-permute-done((bf16[104,1536]{1,0:T(8,128)(2,1)S(1)}, bf16[104,1536]{1,0:T(8,128)(2,1)S(1)}, u32[]{:S(2)}, u32[]{:S(2)}) %collective-permute-start.81) | collective-permute-done | bytes 319520 | tf_op jit(solution)/shard_map/ppermute | solution.py:193
  763.6 4.6 add_convert_fusion.8
  771.0 4.0 add_convert_fusion
  780.1 5.1 shard_map.545
  785.2 5.2 add_add_fusion.4.refs_0_
  797.0 4.1 shard_map.548
  806.6 3.9 all-to-all-start.9
  827.6 3.1 fusion.44
  839.0 9.1 all-to-all-done.9
  848.1 4.9 fusion.18
  853.0 9.3 convolution_add_fusion
  863.1 4.2 multiply_reduce_fusion
  902.9 16.5 %collective-permute-done.70 = bf16[1,112,768]{2,1,0:T(8,128)(2,1)S(1)} collective-permute-done((bf16[1,112,768]{2,1,0:T(8,128)(2,1)S(1)}, bf16[1,112,768]{2,1,0:T(8,128)(2,1)S(1)}, u32[]{:S(2)}, u32[]{:S(2)}) %collective-permute-start.70) | collective-permute-done | bytes 172064 | tf_op jit(solution)/shard_map/ppermute | solution.py:193
  923.2 3.2 collective-permute-start.76
  931.0 10.9 %collective-permute-done.76.refs_0_ = bf16[104,1536]{1,0:T(8,128)(2,1)S(1)} collective-permute-done((bf16[104,1536]{1,0:T(8,128)(2,1)S(1)}, bf16[104,1536]{1,0:T(8,128)(2,1)S(1)}, u32[]{:S(2)}, u32[]{:S(2)}) %collective-permute-start.76) | collective-permute-done | bytes 319520 | tf_op jit(solution)/shard_map/ppermute | solution.py:193
  947.3 6.5 collective-permute-done.78.refs_0_
  968.0 3.3 collective-permute-done.87
  971.4 3.6 collective-permute-done.88
  975.0 4.5 collective-permute-done.89
  979.8 3.3 collective-permute-done.90
  992.0 4.7 add_multiply_fusion.2
  998.6 6.1 add_multiply_fusion.1
  1007.3 7.6 add_multiply_fusion
  (1574 shorter events, 489.0 us)
Async XLA Ops:
  2.8 18.9 %collective-permute-start = (bf16[1,528,128]{2,1,0:T(8,128)(2,1)S(1)}, bf16[1,528,128]{2,1,0:T(8,128)(2,1)S(1)}, u32[]{:S(2)}, u32[]{:S(2)}) collective-permute-start(bf16[1,528,128]{2,1,0:T(8,128)(2,1)S(1)} %maximum_bitcast_fusion.6), channel_id=1, source_target_pairs={{0,4},{4,0},{8,12},{12,8},{16,20},{20,16},{24,28},{28,24},{1,5},{5... | collective-permute-start | bytes 405512 | tf_op jit(solution)/shard_map/ppermute | solution.py:193
  8.5 17.6 %collective-permute-start.1 = (bf16[1,96,1536]{2,1,0:T(8,128)(2,1)S(1)}, bf16[1,96,1536]{2,1,0:T(8,128)(2,1)}, u32[]{:S(2)}, u32[]{:S(2)}) collective-permute-start(bf16[1,96,1536]{2,1,0:T(8,128)(2,1)S(1)} %get-tuple-element.708), channel_id=1, source_target_pairs={{0,16},{4,20},{8,24},{12,28},{16,0},{20,4},{24,8},{28,12},{1,17},{... | collective-permute-start | bytes 884744 | tf_op jit(solution)/shard_map/ppermute | solution.py:193
  27.4 33.7 %collective-permute-start.4 = (bf16[2,96,1536]{2,1,0:T(8,128)(2,1)S(1)}, bf16[2,96,1536]{2,1,0:T(8,128)(2,1)}, u32[]{:S(2)}, u32[]{:S(2)}) collective-permute-start(bf16[2,96,1536]{2,1,0:T(8,128)(2,1)S(1)} %pad_maximum_fusion.9.refs_1_), channel_id=1, source_target_pairs={{0,8},{4,12},{8,0},{12,4},{16,24},{20,28},{24,16},{28,20},{1,9},{5... | collective-permute-start | bytes 1769480 | tf_op jit(solution)/shard_map/ppermute | solution.py:193
  31.8 19.0 %all-to-all-start.4 = ((s32[32,1,128]{2,1,0:T(1,128)}), s32[32,1,128]{2,1,0:T(1,128)S(1)}, u32[]{:S(2)}, u32[]{:S(2)}) async-start(s32[32,1,128]{2,1,0:T(1,128)} %bitcast.501), calls=%async_computation.4 | async-start | bytes 32768 | tf_op jit(solution)/shard_map/all_to_all | solution.py:870
  39.1 24.3 %collective-permute-start.3 = (bf16[4,528,128]{2,1,0:T(8,128)(2,1)}, bf16[4,528,128]{2,1,0:T(8,128)(2,1)}, u32[]{:S(2)}, u32[]{:S(2)}) collective-permute-start(bf16[4,528,128]{2,1,0:T(8,128)(2,1)} %pad_maximum_fusion.13.refs_2_), channel_id=1, source_target_pairs={{0,8},{4,12},{8,0},{12,4},{16,24},{20,28},{24,16},{28,20},{1,9},{5... | collective-permute-start | bytes 1622024 | tf_op jit(solution)/shard_map/ppermute | solution.py:193
  57.4 70.1 %all-to-all-start.5 = ((bf16[32,32,768]{2,1,0:T(8,128)(2,1)}), bf16[32,32,768]{2,1,0:T(8,128)(2,1)}, u32[]{:S(2)}, u32[]{:S(2)}) async-start(bf16[32,32,768]{2,1,0:T(8,128)(2,1)} %bitcast.15), calls=%async_computation.5 | async-start | bytes 3145728 | tf_op jit(solution)/shard_map/all_to_all | solution.py:870
  66.5 47.4 %collective-permute-start.5 = (bf16[8,528,128]{2,1,0:T(8,128)(2,1)}, bf16[8,528,128]{2,1,0:T(8,128)(2,1)S(1)}, u32[]{:S(2)}, u32[]{:S(2)}) collective-permute-start(bf16[8,528,128]{2,1,0:T(8,128)(2,1)} %shard_map.488.refs_1_.own_ref), channel_id=1, source_target_pairs={{0,1},{1,0},{2,3},{3,2},{4,5},{5,4},{6,7},{7,6},{8,9},{9,8},{10,11... | collective-permute-start | bytes 3244040 | tf_op jit(solution)/shard_map/ppermute | solution.py:193
  69.6 39.4 %collective-permute-start.9 = (bf16[1,96,768]{2,1,0:T(8,128)(2,1)}, bf16[1,96,768]{2,1,0:T(8,128)(2,1)S(1)}, u32[]{:S(2)}, u32[]{:S(2)}) collective-permute-start(bf16[1,96,768]{2,1,0:T(8,128)(2,1)} %shard_map.490.refs_2_), channel_id=1, source_target_pairs={{0,16},{4,20},{8,24},{12,28},{16,0},{20,4},{24,8},{28,12},{1,17},{... | collective-permute-start | bytes 442376 | tf_op jit(solution)/shard_map/ppermute | solution.py:193
  72.5 39.7 %collective-permute-start.6 = (bf16[1,112,768]{2,1,0:T(8,128)(2,1)}, bf16[1,112,768]{2,1,0:T(8,128)(2,1)S(1)}, u32[]{:S(2)}, u32[]{:S(2)}) collective-permute-start(bf16[1,112,768]{2,1,0:T(8,128)(2,1)} %shard_map.489.refs_1_), channel_id=1, source_target_pairs={{0,16},{4,20},{8,24},{12,28},{16,0},{20,4},{24,8},{28,12},{1,17},{... | collective-permute-start | bytes 516104 | tf_op jit(solution)/shard_map/ppermute | solution.py:193
  73.6 51.0 %collective-permute-start.7 = (bf16[4,96,1536]{2,1,0:T(8,128)(2,1)}, bf16[4,96,1536]{2,1,0:T(8,128)(2,1)}, u32[]{:S(2)}, u32[]{:S(2)}) collective-permute-start(bf16[4,96,1536]{2,1,0:T(8,128)(2,1)} %shard_map.487.refs_1_), channel_id=1, source_target_pairs={{0,4},{4,0},{8,12},{12,8},{16,20},{20,16},{24,28},{28,24},{1,5},{5... | collective-permute-start | bytes 3538952 | tf_op jit(solution)/shard_map/ppermute | solution.py:193
  138.1 73.6 %collective-permute-start.11 = (bf16[8,96,1536]{2,1,0:T(8,128)(2,1)S(1)}, bf16[8,96,1536]{2,1,0:T(8,128)(2,1)}, u32[]{:S(2)}, u32[]{:S(2)}) collective-permute-start(bf16[8,96,1536]{2,1,0:T(8,128)(2,1)S(1)} %copy-done.7), channel_id=1, source_target_pairs={{0,1},{1,0},{2,3},{3,2},{4,5},{5,4},{6,7},{7,6},{8,9},{9,8},{10,11... | collective-permute-start | bytes 7077896 | tf_op jit(solution)/shard_map/ppermute | solution.py:193
  141.9 15.3 %collective-permute-start.14 = (bf16[1,96,1536]{2,1,0:T(8,128)(2,1)}, bf16[1,96,1536]{2,1,0:T(8,128)(2,1)}, u32[]{:S(2)}, u32[]{:S(2)}) collective-permute-start(bf16[1,96,1536]{2,1,0:T(8,128)(2,1)} %shard_map.501), channel_id=1, source_target_pairs={{0,16},{4,20},{8,24},{12,28},{16,0},{20,4},{24,8},{28,12},{1,17},{... | collective-permute-start | bytes 884744 | tf_op jit(solution)/shard_map/ppermute | solution.py:193
  169.1 38.2 %collective-permute-start.12 = (bf16[4,112,768]{2,1,0:T(8,128)(2,1)}, bf16[4,112,768]{2,1,0:T(8,128)(2,1)}, u32[]{:S(2)}, u32[]{:S(2)}) collective-permute-start(bf16[4,112,768]{2,1,0:T(8,128)(2,1)} %pad_maximum_fusion.7.refs_1_.refs_0_), channel_id=1, source_target_pairs={{0,4},{4,0},{8,12},{12,8},{16,20},{20,16},{24,28},{28,24},{1,5},{5... | collective-permute-start | bytes 2064392 | tf_op jit(solution)/shard_map/ppermute | solution.py:193
  178.4 27.5 %collective-permute-start.13 = (bf16[4,96,768]{2,1,0:T(8,128)(2,1)}, bf16[4,96,768]{2,1,0:T(8,128)(2,1)}, u32[]{:S(2)}, u32[]{:S(2)}) collective-permute-start(bf16[4,96,768]{2,1,0:T(8,128)(2,1)} %pad_maximum_fusion.10.refs_2_.refs_1_.refs_3_.refs_0_), channel_id=1, source_target_pairs={{0,2},{1,3},{2,0},{3,1},{4,6},{5,7},{6,4},{7,5},{8,10},{9,11},{10,... | collective-permute-start | bytes 1769480 | tf_op jit(solution)/shard_map/ppermute | solution.py:193
  180.4 28.5 %collective-permute-start.15 = (bf16[2,96,1536]{2,1,0:T(8,128)(2,1)}, bf16[2,96,1536]{2,1,0:T(8,128)(2,1)}, u32[]{:S(2)}, u32[]{:S(2)}) collective-permute-start(bf16[2,96,1536]{2,1,0:T(8,128)(2,1)} %pad_maximum_fusion.11.refs_5_.refs_1_), channel_id=1, source_target_pairs={{0,8},{4,12},{8,0},{12,4},{16,24},{20,28},{24,16},{28,20},{1,9},{5... | collective-permute-start | bytes 1769480 | tf_op jit(solution)/shard_map/ppermute | solution.py:193
  184.8 19.3 %collective-permute-start.30 = (bf16[2,112,768]{2,1,0:T(8,128)(2,1)}, bf16[2,112,768]{2,1,0:T(8,128)(2,1)}, u32[]{:S(2)}, u32[]{:S(2)}) collective-permute-start(bf16[2,112,768]{2,1,0:T(8,128)(2,1)} %pad_maximum_fusion.17.refs_2_), channel_id=1, source_target_pairs={{0,8},{4,12},{8,0},{12,4},{16,24},{20,28},{24,16},{28,20},{1,9},{5... | collective-permute-start | bytes 1032200 | tf_op jit(solution)/shard_map/ppermute | solution.py:193
  204.1 35.7 %collective-permute-start.24 = (bf16[4,96,768]{2,1,0:T(8,128)(2,1)}, bf16[4,96,768]{2,1,0:T(8,128)(2,1)}, u32[]{:S(2)}, u32[]{:S(2)}) collective-permute-start(bf16[4,96,768]{2,1,0:T(8,128)(2,1)} %pad_maximum_fusion.10.refs_2_.refs_1_.refs_3_.refs_0_), channel_id=1, source_target_pairs={{0,4},{4,0},{8,12},{12,8},{16,20},{20,16},{24,28},{28,24},{1,5},{5... | collective-permute-start | bytes 1769480 | tf_op jit(solution)/shard_map/ppermute | solution.py:193
  205.9 34.0 %collective-permute-start.18 = (bf16[4,112,768]{2,1,0:T(8,128)(2,1)}, bf16[4,112,768]{2,1,0:T(8,128)(2,1)}, u32[]{:S(2)}, u32[]{:S(2)}) collective-permute-start(bf16[4,112,768]{2,1,0:T(8,128)(2,1)} %pad_maximum_fusion.7.refs_1_.refs_0_), channel_id=1, source_target_pairs={{0,2},{1,3},{2,0},{3,1},{4,6},{5,7},{6,4},{7,5},{8,10},{9,11},{10,... | collective-permute-start | bytes 2064392 | tf_op jit(solution)/shard_map/ppermute | solution.py:193
  207.4 42.5 %collective-permute-start.25 = (bf16[4,96,768]{2,1,0:T(8,128)(2,1)}, bf16[4,96,768]{2,1,0:T(8,128)(2,1)}, u32[]{:S(2)}, u32[]{:S(2)}) collective-permute-start(bf16[4,96,768]{2,1,0:T(8,128)(2,1)} %collective-permute-done.13.refs_4_.refs_0_), channel_id=1, source_target_pairs={{0,4},{4,0},{8,12},{12,8},{16,20},{20,16},{24,28},{28,24},{1,5},{5... | collective-permute-start | bytes 1769480 | tf_op jit(solution)/shard_map/ppermute | solution.py:193
  208.9 36.0 %collective-permute-start.19 = (bf16[4,112,768]{2,1,0:T(8,128)(2,1)}, bf16[4,112,768]{2,1,0:T(8,128)(2,1)}, u32[]{:S(2)}, u32[]{:S(2)}) collective-permute-start(bf16[4,112,768]{2,1,0:T(8,128)(2,1)} %collective-permute-done.12.refs_2_.refs_0_), channel_id=1, source_target_pairs={{0,2},{1,3},{2,0},{3,1},{4,6},{5,7},{6,4},{7,5},{8,10},{9,11},{10,... | collective-permute-start | bytes 2064392 | tf_op jit(solution)/shard_map/ppermute | solution.py:193
  211.7 45.3 %collective-permute-start.32 = (bf16[4,96,1536]{2,1,0:T(8,128)(2,1)}, bf16[4,96,1536]{2,1,0:T(8,128)(2,1)}, u32[]{:S(2)}, u32[]{:S(2)}) collective-permute-start(bf16[4,96,1536]{2,1,0:T(8,128)(2,1)} %pad_maximum_fusion.4.refs_1_), channel_id=1, source_target_pairs={{0,4},{4,0},{8,12},{12,8},{16,20},{20,16},{24,28},{28,24},{1,5},{5... | collective-permute-start | bytes 3538952 | tf_op jit(solution)/shard_map/ppermute | solution.py:193
  239.9 21.8 %collective-permute-start.20 = (bf16[4,112,768]{2,1,0:T(8,128)(2,1)}, bf16[4,112,768]{2,1,0:T(8,128)(2,1)S(1)}, u32[]{:S(2)}, u32[]{:S(2)}) collective-permute-start(bf16[4,112,768]{2,1,0:T(8,128)(2,1)} %shard_map.506.refs_0_), channel_id=1, source_target_pairs={{0,1},{1,0},{2,3},{3,2},{4,5},{5,4},{6,7},{7,6},{8,9},{9,8},{10,11... | collective-permute-start | bytes 2064392 | tf_op jit(solution)/shard_map/ppermute | solution.py:193
  244.9 17.3 %collective-permute-start.21 = (bf16[4,112,768]{2,1,0:T(8,128)(2,1)}, bf16[4,112,768]{2,1,0:T(8,128)(2,1)}, u32[]{:S(2)}, u32[]{:S(2)}) collective-permute-start(bf16[4,112,768]{2,1,0:T(8,128)(2,1)} %shard_map.507.refs_1_), channel_id=1, source_target_pairs={{0,1},{1,0},{2,3},{3,2},{4,5},{5,4},{6,7},{7,6},{8,9},{9,8},{10,11... | collective-permute-start | bytes 2064392 | tf_op jit(solution)/shard_map/ppermute | solution.py:193
  245.0 17.2 %collective-permute-start.22 = (bf16[4,112,768]{2,1,0:T(8,128)(2,1)}, bf16[4,112,768]{2,1,0:T(8,128)(2,1)}, u32[]{:S(2)}, u32[]{:S(2)}) collective-permute-start(bf16[4,112,768]{2,1,0:T(8,128)(2,1)} %shard_map.508.refs_2_), channel_id=1, source_target_pairs={{0,1},{1,0},{2,3},{3,2},{4,5},{5,4},{6,7},{7,6},{8,9},{9,8},{10,11... | collective-permute-start | bytes 2064392 | tf_op jit(solution)/shard_map/ppermute | solution.py:193
  256.9 14.9 %collective-permute-start.35 = (bf16[4,96,768]{2,1,0:T(8,128)(2,1)S(1)}, bf16[4,96,768]{2,1,0:T(8,128)(2,1)S(1)}, u32[]{:S(2)}, u32[]{:S(2)}) collective-permute-start(bf16[4,96,768]{2,1,0:T(8,128)(2,1)S(1)} %copy-done.13), channel_id=1, source_target_pairs={{0,2},{1,3},{2,0},{3,1},{4,6},{5,7},{6,4},{7,5},{8,10},{9,11},{10,... | collective-permute-start | bytes 1769480 | tf_op jit(solution)/shard_map/ppermute | solution.py:193
  261.7 15.5 %collective-permute-start.34 = (bf16[4,112,768]{2,1,0:T(8,128)(2,1)S(1)}, bf16[4,112,768]{2,1,0:T(8,128)(2,1)S(1)}, u32[]{:S(2)}, u32[]{:S(2)}) collective-permute-start(bf16[4,112,768]{2,1,0:T(8,128)(2,1)S(1)} %pad_maximum_fusion.8.refs_1_.refs_0_), channel_id=1, source_target_pairs={{0,4},{4,0},{8,12},{12,8},{16,20},{20,16},{24,28},{28,24},{1,5},{5... | collective-permute-start | bytes 2064392 | tf_op jit(solution)/shard_map/ppermute | solution.py:193
  262.2 16.6 %collective-permute-start.26 = (bf16[4,96,768]{2,1,0:T(8,128)(2,1)}, bf16[4,96,768]{2,1,0:T(8,128)(2,1)}, u32[]{:S(2)}, u32[]{:S(2)}) collective-permute-start(bf16[4,96,768]{2,1,0:T(8,128)(2,1)} %shard_map.510.refs_8_), channel_id=1, source_target_pairs={{0,1},{1,0},{2,3},{3,2},{4,5},{5,4},{6,7},{7,6},{8,9},{9,8},{10,11... | collective-permute-start | bytes 1769480 | tf_op jit(solution)/shard_map/ppermute | solution.py:193
  262.2 17.1 %collective-permute-start.27 = (bf16[4,96,768]{2,1,0:T(8,128)(2,1)}, bf16[4,96,768]{2,1,0:T(8,128)(2,1)}, u32[]{:S(2)}, u32[]{:S(2)}) collective-permute-start(bf16[4,96,768]{2,1,0:T(8,128)(2,1)} %shard_map.511.refs_9_), channel_id=1, source_target_pairs={{0,1},{1,0},{2,3},{3,2},{4,5},{5,4},{6,7},{7,6},{8,9},{9,8},{10,11... | collective-permute-start | bytes 1769480 | tf_op jit(solution)/shard_map/ppermute | solution.py:193
  262.7 17.2 %collective-permute-start.28 = (bf16[4,96,768]{2,1,0:T(8,128)(2,1)}, bf16[4,96,768]{2,1,0:T(8,128)(2,1)}, u32[]{:S(2)}, u32[]{:S(2)}) collective-permute-start(bf16[4,96,768]{2,1,0:T(8,128)(2,1)} %shard_map.512.refs_10_), channel_id=1, source_target_pairs={{0,1},{1,0},{2,3},{3,2},{4,5},{5,4},{6,7},{7,6},{8,9},{9,8},{10,11... | collective-permute-start | bytes 1769480 | tf_op jit(solution)/shard_map/ppermute | solution.py:193
  277.2 26.8 %collective-permute-start.33 = (bf16[8,96,1536]{2,1,0:T(8,128)(2,1)}, bf16[8,96,1536]{2,1,0:T(8,128)(2,1)}, u32[]{:S(2)}, u32[]{:S(2)}) collective-permute-start(bf16[8,96,1536]{2,1,0:T(8,128)(2,1)} %pad_maximum_fusion.1.refs_3_.own_ref), channel_id=1, source_target_pairs={{0,1},{1,0},{2,3},{3,2},{4,5},{5,4},{6,7},{7,6},{8,9},{9,8},{10,11... | collective-permute-start | bytes 7077896 | tf_op jit(solution)/shard_map/ppermute | solution.py:193
  278.8 60.1 %collective-permute-start.42 = (bf16[4,96,768]{2,1,0:T(8,128)(2,1)S(1)}, bf16[4,96,768]{2,1,0:T(8,128)(2,1)}, u32[]{:S(2)}, u32[]{:S(2)}) collective-permute-start(bf16[4,96,768]{2,1,0:T(8,128)(2,1)S(1)} %copy-done.13), channel_id=1, source_target_pairs={{0,4},{4,0},{8,12},{12,8},{16,20},{20,16},{24,28},{28,24},{1,5},{5... | collective-permute-start | bytes 1769480 | tf_op jit(solution)/shard_map/ppermute | solution.py:193
  279.3 60.6 %collective-permute-start.36 = (bf16[4,112,768]{2,1,0:T(8,128)(2,1)S(1)}, bf16[4,112,768]{2,1,0:T(8,128)(2,1)S(1)}, u32[]{:S(2)}, u32[]{:S(2)}) collective-permute-start(bf16[4,112,768]{2,1,0:T(8,128)(2,1)S(1)} %pad_maximum_fusion.8.refs_1_.refs_0_), channel_id=1, source_target_pairs={{0,2},{1,3},{2,0},{3,1},{4,6},{5,7},{6,4},{7,5},{8,10},{9,11},{10,... | collective-permute-start | bytes 2064392 | tf_op jit(solution)/shard_map/ppermute | solution.py:193
  279.9 59.6 %collective-permute-start.43 = (bf16[4,96,768]{2,1,0:T(8,128)(2,1)S(1)}, bf16[4,96,768]{2,1,0:T(8,128)(2,1)}, u32[]{:S(2)}, u32[]{:S(2)}) collective-permute-start(bf16[4,96,768]{2,1,0:T(8,128)(2,1)S(1)} %collective-permute-done.35.refs_4_.refs_0_), channel_id=1, source_target_pairs={{0,4},{4,0},{8,12},{12,8},{16,20},{20,16},{24,28},{28,24},{1,5},{5... | collective-permute-start | bytes 1769480 | tf_op jit(solution)/shard_map/ppermute | solution.py:193
  281.3 59.8 %collective-permute-start.37 = (bf16[4,112,768]{2,1,0:T(8,128)(2,1)S(1)}, bf16[4,112,768]{2,1,0:T(8,128)(2,1)}, u32[]{:S(2)}, u32[]{:S(2)}) collective-permute-start(bf16[4,112,768]{2,1,0:T(8,128)(2,1)S(1)} %collective-permute-done.34.refs_2_.refs_0_), channel_id=1, source_target_pairs={{0,2},{1,3},{2,0},{3,1},{4,6},{5,7},{6,4},{7,5},{8,10},{9,11},{10,... | collective-permute-start | bytes 2064392 | tf_op jit(solution)/shard_map/ppermute | solution.py:193
  367.8 41.0 %all-to-all-start.6 = ((bf16[32,32,768]{2,1,0:T(8,128)(2,1)}), bf16[32,32,768]{2,1,0:T(8,128)(2,1)}, u32[]{:S(2)}, u32[]{:S(2)}) async-start(bf16[32,32,768]{2,1,0:T(8,128)(2,1)} %broadcast_in_dim.303), calls=%async_computation.6 | async-start | bytes 3145728 | tf_op jit(solution)/shard_map/all_to_all | solution.py:864
  417.5 19.5 %all-to-all-start.7 = ((f32[32,3,1024]{2,1,0:T(4,128)}), f32[32,3,1024]{2,1,0:T(4,128)}, u32[]{:S(2)}, u32[]{:S(2)}) async-start(f32[32,3,1024]{2,1,0:T(4,128)} %broadcast_in_dim.305), calls=%async_computation.7 | async-start | bytes 1048576 | tf_op jit(solution)/shard_map/all_to_all | solution.py:864
  448.7 41.5 %all-to-all-start.8 = ((bf16[32,32,768]{2,1,0:T(8,128)(2,1)}), bf16[32,32,768]{2,1,0:T(8,128)(2,1)}, u32[]{:S(2)}, u32[]{:S(2)}) async-start(bf16[32,32,768]{2,1,0:T(8,128)(2,1)} %bitcast.494), calls=%async_computation.8 | async-start | bytes 3145728 | tf_op jit(solution)/shard_map/all_to_all | solution.py:870
  517.8 22.8 %collective-permute-start.49 = (bf16[16,96,768]{2,1,0:T(8,128)(2,1)}, bf16[16,96,768]{2,1,0:T(8,128)(2,1)}, u32[]{:S(2)}, u32[]{:S(2)}) collective-permute-start(bf16[16,96,768]{2,1,0:T(8,128)(2,1)} %get-tuple-element.378), channel_id=1, source_target_pairs={{0,1},{1,0},{2,3},{3,2},{4,5},{5,4},{6,7},{7,6},{8,9},{9,8},{10,11... | collective-permute-start | bytes 7077896 | tf_op jit(solution)/shard_map/ppermute | solution.py:193
  517.9 28.1 %collective-permute-start.48 = (bf16[16,112,768]{2,1,0:T(8,128)(2,1)}, bf16[16,112,768]{2,1,0:T(8,128)(2,1)}, u32[]{:S(2)}, u32[]{:S(2)}) collective-permute-start(bf16[16,112,768]{2,1,0:T(8,128)(2,1)} %get-tuple-element.376), channel_id=1, source_target_pairs={{0,1},{1,0},{2,3},{3,2},{4,5},{5,4},{6,7},{7,6},{8,9},{9,8},{10,11... | collective-permute-start | bytes 8257544 | tf_op jit(solution)/shard_map/ppermute | solution.py:193
  544.6 71.9 %collective-permute-start.51 = (bf16[2,4,96,768]{3,2,1,0:T(8,128)(2,1)}, bf16[2,4,96,768]{3,2,1,0:T(8,128)(2,1)}, u32[]{:S(2)}, u32[]{:S(2)}) collective-permute-start(bf16[2,4,96,768]{3,2,1,0:T(8,128)(2,1)} %get-tuple-element.654.refs_2_), channel_id=1, source_target_pairs={{0,4},{4,0},{8,12},{12,8},{16,20},{20,16},{24,28},{28,24},{1,5},{5... | collective-permute-start | bytes 3538952 | tf_op jit(solution)/shard_map/ppermute | solution.py:193
  550.0 86.9 %collective-permute-start.50 = (bf16[2,4,112,768]{3,2,1,0:T(8,128)(2,1)}, bf16[2,4,112,768]{3,2,1,0:T(8,128)(2,1)}, u32[]{:S(2)}, u32[]{:S(2)}) collective-permute-start(bf16[2,4,112,768]{3,2,1,0:T(8,128)(2,1)} %bitcast.57.refs_1_), channel_id=1, source_target_pairs={{0,2},{1,3},{2,0},{3,1},{4,6},{5,7},{6,4},{7,5},{8,10},{9,11},{10,... | collective-permute-start | bytes 4128776 | tf_op jit(solution)/shard_map/ppermute | solution.py:193
  608.1 61.2 %collective-permute-start.52 = (bf16[8,104,1536]{2,1,0:T(8,128)(2,1)}, bf16[8,104,1536]{2,1,0:T(8,128)(2,1)}, u32[]{:S(2)}, u32[]{:S(2)}) collective-permute-start(bf16[8,104,1536]{2,1,0:T(8,128)(2,1)} %pad_dynamic-update-slice_fusion.3.refs_1_), channel_id=1, source_target_pairs={{0,1},{1,0},{2,3},{3,2},{4,5},{5,4},{6,7},{7,6},{8,9},{9,8},{10,11... | collective-permute-start | bytes 7667720 | tf_op jit(solution)/shard_map/ppermute | solution.py:193
  619.1 15.7 %collective-permute-start.54 = (bf16[4,96,768]{2,1,0:T(8,128)(2,1)S(1)}, bf16[4,96,768]{2,1,0:T(8,128)(2,1)}, u32[]{:S(2)}, u32[]{:S(2)}) collective-permute-start(bf16[4,96,768]{2,1,0:T(8,128)(2,1)S(1)} %get-tuple-element.664.refs_2_), channel_id=1, source_target_pairs={{0,2},{1,3},{2,0},{3,1},{4,6},{5,7},{6,4},{7,5},{8,10},{9,11},{10,... | collective-permute-start | bytes 1769480 | tf_op jit(solution)/shard_map/ppermute | solution.py:193
  639.8 17.3 %collective-permute-start.53 = (bf16[4,112,768]{2,1,0:T(8,128)(2,1)}, bf16[4,112,768]{2,1,0:T(8,128)(2,1)}, u32[]{:S(2)}, u32[]{:S(2)}) collective-permute-start(bf16[4,112,768]{2,1,0:T(8,128)(2,1)} %get-tuple-element.658.refs_1_), channel_id=1, source_target_pairs={{0,4},{4,0},{8,12},{12,8},{16,20},{20,16},{24,28},{28,24},{1,5},{5... | collective-permute-start | bytes 2064392 | tf_op jit(solution)/shard_map/ppermute | solution.py:193
  646.6 16.3 %collective-permute-start.74 = (bf16[1,96,768]{2,1,0:T(8,128)(2,1)S(1)}, bf16[1,96,768]{2,1,0:T(8,128)(2,1)S(1)}, u32[]{:S(2)}, u32[]{:S(2)}) collective-permute-start(bf16[1,96,768]{2,1,0:T(8,128)(2,1)S(1)} %add_convert_fusion.33.refs_2_), channel_id=1, source_target_pairs={{0,16},{4,20},{8,24},{12,28},{16,0},{20,4},{24,8},{28,12},{1,17},{... | collective-permute-start | bytes 442376 | tf_op jit(solution)/shard_map/ppermute | solution.py:193
  667.9 39.7 %collective-permute-start.73 = (bf16[1,112,768]{2,1,0:T(8,128)(2,1)}, bf16[1,112,768]{2,1,0:T(8,128)(2,1)}, u32[]{:S(2)}, u32[]{:S(2)}) collective-permute-start(bf16[1,112,768]{2,1,0:T(8,128)(2,1)} %add_convert_fusion.29.refs_1_), channel_id=1, source_target_pairs={{0,16},{4,20},{8,24},{12,28},{16,0},{20,4},{24,8},{28,12},{1,17},{... | collective-permute-start | bytes 516104 | tf_op jit(solution)/shard_map/ppermute | solution.py:193
  672.4 37.8 %collective-permute-start.55 = (bf16[2,2,104,1536]{3,2,1,0:T(8,128)(2,1)}, bf16[2,2,104,1536]{3,2,1,0:T(8,128)(2,1)}, u32[]{:S(2)}, u32[]{:S(2)}) collective-permute-start(bf16[2,2,104,1536]{3,2,1,0:T(8,128)(2,1)} %fusion.51.refs_1_), channel_id=1, source_target_pairs={{0,4},{4,0},{8,12},{12,8},{16,20},{20,16},{24,28},{28,24},{1,5},{5... | collective-permute-start | bytes 3833864 | tf_op jit(solution)/shard_map/ppermute | solution.py:193
  702.0 61.7 %collective-permute-start.57 = (bf16[16,96,768]{2,1,0:T(8,128)(2,1)}, bf16[16,96,768]{2,1,0:T(8,128)(2,1)}, u32[]{:S(2)}, u32[]{:S(2)}) collective-permute-start(bf16[16,96,768]{2,1,0:T(8,128)(2,1)} %get-tuple-element.404), channel_id=1, source_target_pairs={{0,1},{1,0},{2,3},{3,2},{4,5},{5,4},{6,7},{7,6},{8,9},{9,8},{10,11... | collective-permute-start | bytes 7077896 | tf_op jit(solution)/shard_map/ppermute | solution.py:193
  702.0 69.0 %collective-permute-start.56 = (bf16[16,112,768]{2,1,0:T(8,128)(2,1)}, bf16[16,112,768]{2,1,0:T(8,128)(2,1)}, u32[]{:S(2)}, u32[]{:S(2)}) collective-permute-start(bf16[16,112,768]{2,1,0:T(8,128)(2,1)} %get-tuple-element.402), channel_id=1, source_target_pairs={{0,1},{1,0},{2,3},{3,2},{4,5},{5,4},{6,7},{7,6},{8,9},{9,8},{10,11... | collective-permute-start | bytes 8257544 | tf_op jit(solution)/shard_map/ppermute | solution.py:193
  713.0 28.3 %collective-permute-start.60 = (bf16[2,104,1536]{2,1,0:T(8,128)(2,1)}, bf16[2,104,1536]{2,1,0:T(8,128)(2,1)}, u32[]{:S(2)}, u32[]{:S(2)}) collective-permute-start(bf16[2,104,1536]{2,1,0:T(8,128)(2,1)} %get-tuple-element.660.refs_3_), channel_id=1, source_target_pairs={{0,8},{4,12},{8,0},{12,4},{16,24},{20,28},{24,16},{28,20},{1,9},{5... | collective-permute-start | bytes 1916936 | tf_op jit(solution)/shard_map/ppermute | solution.py:193
  742.4 17.3 %collective-permute-start.81 = (bf16[104,1536]{1,0:T(8,128)(2,1)S(1)}, bf16[104,1536]{1,0:T(8,128)(2,1)S(1)}, u32[]{:S(2)}, u32[]{:S(2)}) collective-permute-start(bf16[104,1536]{1,0:T(8,128)(2,1)S(1)} %fusion.127.refs_3_), channel_id=1, source_target_pairs={{0,16},{4,20},{8,24},{12,28},{16,0},{20,4},{24,8},{28,12},{1,17},{... | collective-permute-start | bytes 958472 | tf_op jit(solution)/shard_map/ppermute | solution.py:193
  768.2 63.7 %collective-permute-start.65 = (bf16[2,4,96,768]{3,2,1,0:T(8,128)(2,1)}, bf16[2,4,96,768]{3,2,1,0:T(8,128)(2,1)}, u32[]{:S(2)}, u32[]{:S(2)}) collective-permute-start(bf16[2,4,96,768]{3,2,1,0:T(8,128)(2,1)} %get-tuple-element.652.refs_2_), channel_id=1, source_target_pairs={{0,4},{4,0},{8,12},{12,8},{16,20},{20,16},{24,28},{28,24},{1,5},{5... | collective-permute-start | bytes 3538952 | tf_op jit(solution)/shard_map/ppermute | solution.py:193
  771.0 39.6 %collective-permute-start.83 = (bf16[104,1536]{1,0:T(8,128)(2,1)}, bf16[104,1536]{1,0:T(8,128)(2,1)}, u32[]{:S(2)}, u32[]{:S(2)}) collective-permute-start(bf16[104,1536]{1,0:T(8,128)(2,1)} %add_convert_fusion.20), channel_id=1, source_target_pairs={{0,1},{1,0},{2,3},{3,2},{4,5},{5,4},{6,7},{7,6},{8,9},{9,8},{10,11... | collective-permute-start | bytes 958472 | tf_op jit(solution)/shard_map/ppermute | solution.py:193
  775.0 52.6 %collective-permute-start.61 = (bf16[2,4,112,768]{3,2,1,0:T(8,128)(2,1)}, bf16[2,4,112,768]{3,2,1,0:T(8,128)(2,1)}, u32[]{:S(2)}, u32[]{:S(2)}) collective-permute-start(bf16[2,4,112,768]{3,2,1,0:T(8,128)(2,1)} %bitcast.76.refs_1_), channel_id=1, source_target_pairs={{0,2},{1,3},{2,0},{3,1},{4,6},{5,7},{6,4},{7,5},{8,10},{9,11},{10,... | collective-permute-start | bytes 4128776 | tf_op jit(solution)/shard_map/ppermute | solution.py:193
  791.2 24.3 %collective-permute-start.62 = (bf16[8,104,1536]{2,1,0:T(8,128)(2,1)}, bf16[8,104,1536]{2,1,0:T(8,128)(2,1)}, u32[]{:S(2)}, u32[]{:S(2)}) collective-permute-start(bf16[8,104,1536]{2,1,0:T(8,128)(2,1)} %pad_dynamic-update-slice_fusion.1.refs_1_), channel_id=1, source_target_pairs={{0,1},{1,0},{2,3},{3,2},{4,5},{5,4},{6,7},{7,6},{8,9},{9,8},{10,11... | collective-permute-start | bytes 7667720 | tf_op jit(solution)/shard_map/ppermute | solution.py:193
  806.6 41.4 %all-to-all-start.9 = ((bf16[32,32,768]{2,1,0:T(8,128)(2,1)}), bf16[32,32,768]{2,1,0:T(8,128)(2,1)}, u32[]{:S(2)}, u32[]{:S(2)}) async-start(bf16[32,32,768]{2,1,0:T(8,128)(2,1)} %bitcast.476), calls=%async_computation.9 | async-start | bytes 3145728 | tf_op jit(solution)/shard_map/all_to_all | solution.py:870
  818.2 61.4 %collective-permute-start.68 = (bf16[2,2,104,1536]{3,2,1,0:T(8,128)(2,1)}, bf16[2,2,104,1536]{3,2,1,0:T(8,128)(2,1)}, u32[]{:S(2)}, u32[]{:S(2)}) collective-permute-start(bf16[2,2,104,1536]{3,2,1,0:T(8,128)(2,1)} %fusion.52.refs_1_), channel_id=1, source_target_pairs={{0,4},{4,0},{8,12},{12,8},{16,20},{20,16},{24,28},{28,24},{1,5},{5... | collective-permute-start | bytes 3833864 | tf_op jit(solution)/shard_map/ppermute | solution.py:193
  827.6 39.8 %collective-permute-start.64 = (bf16[8,384,128]{2,1,0:T(8,128)(2,1)}, bf16[8,384,128]{2,1,0:T(8,128)(2,1)S(1)}, u32[]{:S(2)}, u32[]{:S(2)}) collective-permute-start(bf16[8,384,128]{2,1,0:T(8,128)(2,1)} %get-tuple-element.674.refs_1_), channel_id=1, source_target_pairs={{0,1},{1,0},{2,3},{3,2},{4,5},{5,4},{6,7},{7,6},{8,9},{9,8},{10,11... | collective-permute-start | bytes 2359304 | tf_op jit(solution)/shard_map/ppermute | solution.py:193
  830.7 42.5 %collective-permute-start.63 = (bf16[4,112,768]{2,1,0:T(8,128)(2,1)}, bf16[4,112,768]{2,1,0:T(8,128)(2,1)}, u32[]{:S(2)}, u32[]{:S(2)}) collective-permute-start(bf16[4,112,768]{2,1,0:T(8,128)(2,1)} %get-tuple-element.656.refs_1_), channel_id=1, source_target_pairs={{0,4},{4,0},{8,12},{12,8},{16,20},{20,16},{24,28},{28,24},{1,5},{5... | collective-permute-start | bytes 2064392 | tf_op jit(solution)/shard_map/ppermute | solution.py:193
  834.8 42.3 %collective-permute-start.69 = (bf16[4,96,768]{2,1,0:T(8,128)(2,1)}, bf16[4,96,768]{2,1,0:T(8,128)(2,1)}, u32[]{:S(2)}, u32[]{:S(2)}) collective-permute-start(bf16[4,96,768]{2,1,0:T(8,128)(2,1)} %get-tuple-element.662.refs_1_), channel_id=1, source_target_pairs={{0,2},{1,3},{2,0},{3,1},{4,6},{5,7},{6,4},{7,5},{8,10},{9,11},{10,... | collective-permute-start | bytes 1769480 | tf_op jit(solution)/shard_map/ppermute | solution.py:193
  896.4 33.4 %collective-permute-start.77 = (bf16[2,384,128]{2,1,0:T(8,128)(2,1)}, bf16[2,384,128]{2,1,0:T(8,128)(2,1)}, u32[]{:S(2)}, u32[]{:S(2)}) collective-permute-start(bf16[2,384,128]{2,1,0:T(8,128)(2,1)} %fusion.135.refs_1_), channel_id=1, source_target_pairs={{0,8},{4,12},{8,0},{12,4},{16,24},{20,28},{24,16},{28,20},{1,9},{5... | collective-permute-start | bytes 589832 | tf_op jit(solution)/shard_map/ppermute | solution.py:193
  898.0 23.3 %collective-permute-start.75 = (bf16[2,104,1536]{2,1,0:T(8,128)(2,1)}, bf16[2,104,1536]{2,1,0:T(8,128)(2,1)S(1)}, u32[]{:S(2)}, u32[]{:S(2)}) collective-permute-start(bf16[2,104,1536]{2,1,0:T(8,128)(2,1)} %fusion.99.refs_1_), channel_id=1, source_target_pairs={{0,8},{4,12},{8,0},{12,4},{16,24},{20,28},{24,16},{28,20},{1,9},{5... | collective-permute-start | bytes 1916936 | tf_op jit(solution)/shard_map/ppermute | solution.py:193
  898.5 20.9 %collective-permute-start.70 = (bf16[1,112,768]{2,1,0:T(8,128)(2,1)S(1)}, bf16[1,112,768]{2,1,0:T(8,128)(2,1)S(1)}, u32[]{:S(2)}, u32[]{:S(2)}) collective-permute-start(bf16[1,112,768]{2,1,0:T(8,128)(2,1)S(1)} %copy-done.283), channel_id=1, source_target_pairs={{0,16},{4,20},{8,24},{12,28},{16,0},{20,4},{24,8},{28,12},{1,17},{... | collective-permute-start | bytes 516104 | tf_op jit(solution)/shard_map/ppermute | solution.py:193
  923.2 18.7 %collective-permute-start.76 = (bf16[104,1536]{1,0:T(8,128)(2,1)S(1)}, bf16[104,1536]{1,0:T(8,128)(2,1)S(1)}, u32[]{:S(2)}, u32[]{:S(2)}) collective-permute-start(bf16[104,1536]{1,0:T(8,128)(2,1)S(1)} %fusion.129.refs_1_), channel_id=1, source_target_pairs={{0,16},{4,20},{8,24},{12,28},{16,0},{20,4},{24,8},{28,12},{1,17},{... | collective-permute-start | bytes 958472 | tf_op jit(solution)/shard_map/ppermute | solution.py:193
  (510 other events, 3422.5 us)

commit v4 on v3

--- a/solution.py
+++ b/solution.py
@@ -694,19 +694,29 @@
     def __init__(self, block, joined, apart):
         self.joined, self.apart = list(joined), list(apart)
         self.masks = [frozenset()]
-        self.pieces = {frozenset(): block[None]}
+        self.held, self.came = block[None], None
+        self.pieces = None
+
+    def join(self, wait):
+        if self.came is None:
+            self.held = self.held if wait is None else tie(self.held, wait)
+        else:
+            came = self.came if wait is None else tie(self.came, wait)
+            self.held = jnp.concatenate([self.held, came], 0)
+        return self.held
 
     def advance(self, wait=None):
         if self.joined:
             step = self.joined.pop(0)
-            (held,) = self.pieces.values()
-            held = held if wait is None else tie(held, wait)
+            held = self.join(wait)
             self.sent = [held]
-            came = hop(held, *step)
-            self.pieces = {frozenset(): jnp.concatenate([held, came], 0)}
+            self.came = hop(held, *step)
             self.masks = self.masks + [mask | {step} for mask in self.masks]
-            return came
+            return self.came
         step = self.apart.pop(0)
+        if self.pieces is None:
+            self.pieces = {frozenset(): self.join(wait)}
+            wait = None
         self.sent = []
         for key, piece in list(self.pieces.items()):
             piece = piece if wait is None else tie(piece, wait)
@@ -1100,6 +1110,8 @@
         self.mats = []
 
     def step(self, value, items):
+        for item in items:
+            item.came = tie(item.came, value)
         return tie(value, *[item.advance() for item in items])
 
     def before_units(self, value):
@@ -1360,7 +1372,7 @@
     def push(value, chains):
         waits = []
         for chain in chains:
-            chain.advance()
+            chain.advance(value)
             waits = waits + chain.sent
         return tie(value, *waits)
 
@@ -1558,14 +1570,15 @@
         jnp.where(first, small_blocks[:, 0], small_blocks[:, 1]),
     )
     token = small_total.sent
-    turns = plan.units[1] + [small_total] + plan.units[1] + [plan.mats[1], small_total]
-    turns = turns + plan.units[1] + [plan.mats[1], small_total] * 4
+    outer = plan.units[1]
+    turns = outer + [plan.mats[1]] + outer + [small_total, plan.mats[1]] + outer
+    turns = turns + [small_total, plan.mats[1]] * 5
     for number, chain in enumerate(turns):
         if chain.left:
             chain.came = tie(chain.came, token)
             chain.advance()
             token = chain.sent
-        if number == 6:
+        if number == 2:
             token = tie(gave_came, token)
     small_sum = small_total.finish().reshape(-1)[:share]
     plan.units.reverse()

time: 1030 us -> 1010 us (0.981)
  waiting for transfers between devices: 238 us -> 210 us
    ppermute x91, waiting for transfers between devices: 176 us -> 118 us  [hop(): return lax.ppermute(values, axis, pairs)]
    all_to_all x4, waiting for transfers between devices: 38.7 us -> 58.9 us  [trade(): return lax.all_to_all(values, ('dp', 'mp'), 0, 0, tiled=True)]
    unnamed x956 -> x932, local copies, waits for them, and re-layouts: 94.5 us -> 103 us
    convert_element_type x36 -> x37, other arithmetic: 70.9 us -> 75.7 us  [add_low(): (kept.astype(jnp.float32) + came.astype(jnp.float32)).astype(jnp.bfloat16)]
  transfers between devices with their start and end apart: 97 -> 97, of which waited for: 39 -> 32; matrix products, arithmetic and copies ran while one was open for 31% -> 32% of each run, Pallas kernels for 14% -> 15%
where the time goes in v4:
time: 1010 us; the launch traced here: 1000 us
  other arithmetic  226 us (22%)
  waiting for transfers between devices  210 us (21%)
  Pallas kernels  181 us (18%)
  local copies, waits for them, and re-layouts  168 us (17%)
  matrix products  102 us (10%)
  starting transfers between devices  92.9 us (9%)
  between operations  18.6 us (2%)
    ppermute x91, waiting for transfers between devices, hop(): return lax.ppermute(values, axis, pairs)  118 us
    unnamed x932, local copies, waits for them, and re-layouts  103 us
    convert_element_type x37, other arithmetic, add_low(): (kept.astype(jnp.float32) + came.astype(jnp.float32)).astype(jnp.bfloat16)  75.7 us
    ppermute x91, starting transfers between devices, hop(): return lax.ppermute(values, axis, pairs)  68.4 us
    all_to_all x4, waiting for transfers between devices, trade(): return lax.all_to_all(values, ('dp', 'mp'), 0, 0, tiled=True)  58.9 us
    pallas_call x4, Pallas kernels, ffn_back(): pl.pallas_call(functools.partial(ffn_back_kernel, slot_rows[0] if slot_ro...  47.6 us
    pallas_call x2, Pallas kernels, attend_back(): pl.pallas_call(attend_back_kernel, grid=(HEAD_PAIRS,), in_specs=[pl.Block...  37.4 us
    pallas_call x2, Pallas kernels, attend(): pl.pallas_call(attend_kernel, grid=(HEAD_PAIRS,), in_specs=[pl.BlockSpec(...  33.4 us
  transfers between devices with their start and end apart: 97, of which 32 were waited for; matrix products, arithmetic and copies ran while one was open for 32% of the time, Pallas kernels for 15%

profile of v4, /device:TPU:0, one launch (start us, length us, event | category | flops | bytes accessed | tf_op | source)
XLA Modules:
  0.0 999.9 jit_solution(12938095284547640648)
XLA Ops:
  21.3 4.0 convert_element_type.1022
  25.4 5.5 collective-permute-start.4
  30.9 4.7 all-to-all-start.4
  37.5 12.1 %all-to-all-done.4 = s32[32,1,128]{2,1,0:T(1,128)S(1)} async-done(((s32[32,1,128]{2,1,0:T(1,128)}), s32[32,1,128]{2,1,0:T(1,128)S(1)}, u32[]{:S(2)}, u32[]{:S(2)}) %all-to-all-start.4) | async-done | bytes 16416 | tf_op jit(solution)/shard_map/all_to_all | solution.py:880
  51.2 6.1 fusion.34.refs_1_
  63.2 5.0 all-to-all-start.5
  92.1 21.0 %all-to-all-done.5 = bf16[32,32,768]{2,1,0:T(8,128)(2,1)} async-done(((bf16[32,32,768]{2,1,0:T(8,128)(2,1)}), bf16[32,32,768]{2,1,0:T(8,128)(2,1)}, u32[]{:S(2)}, u32[]{:S(2)}) %all-to-all-start.5) | async-done | bytes 1572896 | tf_op jit(solution)/shard_map/all_to_all | solution.py:880
  113.1 3.6 fusion.27
  122.2 3.6 shard_map.493
  137.2 3.6 collective-permute-done.10.refs_0_
  144.2 4.4 collective-permute-done.8.refs_0_
  161.8 16.9 %shard_map.502 = (bf16[512,768]{1,0:T(8,128)(2,1)S(1)}, bf16[512,192]{1,0:T(8,128)(2,1)S(1)}, f32[6,512,2]{2,1,0:T(8,128)S(1)}) custom-call(s32[1]{0:T(128)S(6)} %copy.553.length, bf16[512,768]{1,0:T(8,128)(2,1)S(1)} %fusion.36.qt, bf16[512,768]{1,0:T(8,128)(2,1)S(1)} %slice.1146.kt, bf16[512,768]{1,0:T(8,128)(2,1)S(1)} %add_convert_fusion.9.vt, ...), custom_call_target="tpu_custom_call" | custom-call | flops 4000000000 | bytes 2000000 | tf_op jit(solution)/shard_map/pallas_call | solution.py:527
  188.6 4.0 fusion.246
  196.5 3.7 collective-permute-done.24.refs_0_
  200.4 10.7 %collective-permute-done.25.refs_0_ = bf16[4,96,768]{2,1,0:T(8,128)(2,1)S(1)} collective-permute-done((bf16[4,96,768]{2,1,0:T(8,128)(2,1)}, bf16[4,96,768]{2,1,0:T(8,128)(2,1)S(1)}, u32[]{:S(2)}, u32[]{:S(2)}) %collective-permute-start.25) | collective-permute-done | bytes 589856 | tf_op jit(solution)/shard_map/ppermute | solution.py:193
  218.3 8.2 collective-permute-done.16.refs_0_
  237.7 13.5 %shard_map.524 = (bf16[512,3072]{1,0:T(8,128)(2,1)}, bf16[512,3072]{1,0:T(8,128)(2,1)}, f32[512,768]{1,0:T(8,128)S(1)}) custom-call(bf16[512,768]{1,0:T(8,128)(2,1)S(1)} %copy-done.16, f32[1,3072]{1,0:T(1,128)S(1)} %broadcast_in_dim_reshape.15.bias_ref, bf16[4,112,768]{2,1,0:T(8,128)(2,1)S(1)} %copy-done.14, bf16[4,112,768]{2,1,0:T(8,128)(2,1)S(1)} %copy-done.25, ...), custom_call_target="tpu_custom_call" | custom-call | flops 1207959552 | bytes 3932160 | tf_op jit(solution)/shard_map/pallas_call | solution.py:664
  254.1 8.0 collective-permute-done.32.refs_0_
  279.1 3.3 collective-permute-done.30.refs_0_
  309.9 16.5 %shard_map.537 = (bf16[512,768]{1,0:T(8,128)(2,1)S(1)}, bf16[512,192]{1,0:T(8,128)(2,1)S(1)}, f32[6,512,2]{2,1,0:T(8,128)S(1)}) custom-call(s32[1]{0:T(128)S(6)} %copy.553.length, bf16[512,768]{1,0:T(8,128)(2,1)S(1)} %copy-done.23, bf16[512,768]{1,0:T(8,128)(2,1)S(1)} %copy-done.96, bf16[512,768]{1,0:T(8,128)(2,1)S(1)} %add_convert_fusion.8.vt, ...), custom_call_target="tpu_custom_call" | custom-call | flops 4000000000 | bytes 2000000 | tf_op jit(solution)/shard_map/pallas_call | solution.py:527
  336.2 3.7 fusion.248
  348.2 13.8 %shard_map.546 = (bf16[512,3072]{1,0:T(8,128)(2,1)}, bf16[512,3072]{1,0:T(8,128)(2,1)}, f32[512,768]{1,0:T(8,128)S(1)}) custom-call(bf16[512,768]{1,0:T(8,128)(2,1)S(1)} %fusion.48.rows_ref, f32[1,3072]{1,0:T(1,128)S(1)} %broadcast_in_dim_reshape.17.bias_ref, bf16[4,112,768]{2,1,0:T(8,128)(2,1)S(1)} %copy-done.10, bf16[4,112,768]{2,1,0:T(8,128)(2,1)S(1)} %copy-done.29, ...), custom_call_target="tpu_custom_call" | custom-call | flops 1207959552 | bytes 3932160 | tf_op jit(solution)/shard_map/pallas_call | solution.py:664
  365.6 3.8 all-to-all-start.6
  384.4 22.6 %all-to-all-done.6 = bf16[32,32,768]{2,1,0:T(8,128)(2,1)} async-done(((bf16[32,32,768]{2,1,0:T(8,128)(2,1)}), bf16[32,32,768]{2,1,0:T(8,128)(2,1)}, u32[]{:S(2)}, u32[]{:S(2)}) %all-to-all-start.6) | async-done | bytes 1572896 | tf_op jit(solution)/shard_map/all_to_all | solution.py:874
  406.9 4.9 fusion.249
  415.5 4.0 all-to-all-start.7
  424.9 10.1 %all-to-all-done.7 = f32[32,3,1024]{2,1,0:T(4,128)} async-done(((f32[32,3,1024]{2,1,0:T(4,128)}), f32[32,3,1024]{2,1,0:T(4,128)}, u32[]{:S(2)}, u32[]{:S(2)}) %all-to-all-start.7) | async-done | bytes 393248 | tf_op jit(solution)/shard_map/all_to_all | solution.py:874
  438.3 8.4 convolution_convert_fusion
  446.8 3.4 all-to-all-start.8
  472.1 15.6 %all-to-all-done.8 = bf16[32,32,768]{2,1,0:T(8,128)(2,1)} async-done(((bf16[32,32,768]{2,1,0:T(8,128)(2,1)}), bf16[32,32,768]{2,1,0:T(8,128)(2,1)}, u32[]{:S(2)}, u32[]{:S(2)}) %all-to-all-start.8) | async-done | bytes 1572896 | tf_op jit(solution)/shard_map/all_to_all | solution.py:880
  494.5 21.7 %shard_map.550 = (f32[512,768]{1,0:T(8,128)}, f32[1,3072]{1,0:T(1,128)S(1)}, bf16[16,112,768]{2,1,0:T(8,128)(2,1)}, bf16[16,96,768]{2,1,0:T(8,128)(2,1)}, bf16[1...) custom-call(bf16[512,768]{1,0:T(8,128)(2,1)} %copy-done.49, bf16[512,768]{1,0:T(8,128)(2,1)} %get-tuple-element.672.grad_ref, ...), custom_call_target="tpu_custom_call" | custom-call | flops 2415919104 | bytes 7864320 | tf_op jit(solution)/shard_map/pallas_call | solution.py:975
  524.3 4.3 multiply_reduce_fusion.3
  539.1 4.4 add_convert_fusion.6
  545.0 4.5 fusion.24
  556.4 18.5 %shard_map.554 = (bf16[512,768]{1,0:T(8,128)(2,1)S(1)}, bf16[512,768]{1,0:T(8,128)(2,1)S(1)}, bf16[512,768]{1,0:T(8,128)(2,1)S(1)}, bf16[512,192]{1,0:T(8,128)(2...) custom-call(s32[1]{0:T(128)S(6)} %copy.553.length, bf16[512,768]{1,0:T(8,128)(2,1)S(1)} %copy-done.23, ...), custom_call_target="tpu_custom_call" | custom-call | flops 5000000000 | bytes 3000000 | tf_op jit(solution)/shard_map/pallas_call | solution.py:551
  594.2 5.2 shard_map.555
  601.8 4.3 add_add_fusion.5.refs_0_
  632.2 21.6 %shard_map.563 = (f32[512,768]{1,0:T(8,128)}, f32[1,3072]{1,0:T(1,128)S(1)}, bf16[16,112,768]{2,1,0:T(8,128)(2,1)}, bf16[16,96,768]{2,1,0:T(8,128)(2,1)}, bf16[1...) custom-call(bf16[512,768]{1,0:T(8,128)(2,1)} %shard_map.515.rows_ref, bf16[512,768]{1,0:T(8,128)(2,1)} %shard_map.561.grad_ref, ...), custom_call_target="tpu_custom_call" | custom-call | flops 2415919104 | bytes 7864320 | tf_op jit(solution)/shard_map/pallas_call | solution.py:975
  674.3 3.6 fusion.234
  690.7 18.9 %shard_map.568 = (bf16[512,768]{1,0:T(8,128)(2,1)S(1)}, bf16[512,768]{1,0:T(8,128)(2,1)S(1)}, bf16[512,768]{1,0:T(8,128)(2,1)S(1)}, bf16[512,192]{1,0:T(8,128)(2...) custom-call(s32[1]{0:T(128)S(6)} %copy.553.length, bf16[512,768]{1,0:T(8,128)(2,1)S(1)} %copy-done.99, ...), custom_call_target="tpu_custom_call" | custom-call | flops 5000000000 | bytes 3000000 | tf_op jit(solution)/shard_map/pallas_call | solution.py:551
  724.4 4.4 add_convert_fusion.4
  731.4 4.5 fusion.22
  739.6 5.2 shard_map.572
  744.8 5.2 add_add_fusion.4.refs_0_
  766.0 4.1 shard_map.578
  775.7 8.7 collective-permute-done.80
  788.7 6.9 collective-permute-done.81
  797.3 3.6 all-to-all-start.9
  828.3 10.2 %all-to-all-done.9 = bf16[32,32,768]{2,1,0:T(8,128)(2,1)} async-done(((bf16[32,32,768]{2,1,0:T(8,128)(2,1)}), bf16[32,32,768]{2,1,0:T(8,128)(2,1)}, u32[]{:S(2)}, u32[]{:S(2)}) %all-to-all-start.9) | async-done | bytes 1572896 | tf_op jit(solution)/shard_map/all_to_all | solution.py:880
  838.5 4.9 fusion.18
  843.5 9.3 convolution_add_fusion
  853.6 4.2 multiply_reduce_fusion
  873.8 5.1 collective-permute-done.67.refs_0_
  880.7 12.4 %collective-permute-done.66.refs_0_ = bf16[2,112,768]{2,1,0:T(8,128)(2,1)} collective-permute-done((bf16[2,112,768]{2,1,0:T(8,128)(2,1)}, bf16[2,112,768]{2,1,0:T(8,128)(2,1)}, u32[]{:S(2)}, u32[]{:S(2)}) %collective-permute-start.66) | collective-permute-done | bytes 344096 | tf_op jit(solution)/shard_map/ppermute | solution.py:193
  894.1 4.0 collective-permute-done.71.refs_0_
  905.5 7.3 collective-permute-done.72
  920.5 5.9 collective-permute-done.77.refs_0_
  931.0 4.3 collective-permute-done.84.refs_0_
  946.8 3.3 collective-permute-done.87
  953.8 4.5 collective-permute-done.89
  958.3 3.6 collective-permute-done.90
  970.7 4.7 add_multiply_fusion.2
  977.4 6.1 add_multiply_fusion.1
  986.0 7.6 add_multiply_fusion
  (1585 shorter events, 485.8 us)
Async XLA Ops:
  2.8 18.0 %collective-permute-start = (bf16[1,528,128]{2,1,0:T(8,128)(2,1)S(1)}, bf16[1,528,128]{2,1,0:T(8,128)(2,1)S(1)}, u32[]{:S(2)}, u32[]{:S(2)}) collective-permute-start(bf16[1,528,128]{2,1,0:T(8,128)(2,1)S(1)} %maximum_bitcast_fusion.6), channel_id=1, source_target_pairs={{0,4},{4,0},{8,12},{12,8},{16,20},{20,16},{24,28},{28,24},{1,5},{5... | collective-permute-start | bytes 405512 | tf_op jit(solution)/shard_map/ppermute | solution.py:193
  8.5 16.8 %collective-permute-start.1 = (bf16[1,96,1536]{2,1,0:T(8,128)(2,1)S(1)}, bf16[1,96,1536]{2,1,0:T(8,128)(2,1)S(1)}, u32[]{:S(2)}, u32[]{:S(2)}) collective-permute-start(bf16[1,96,1536]{2,1,0:T(8,128)(2,1)S(1)} %get-tuple-element.710), channel_id=1, source_target_pairs={{0,16},{4,20},{8,24},{12,28},{16,0},{20,4},{24,8},{28,12},{1,17},{... | collective-permute-start | bytes 884744 | tf_op jit(solution)/shard_map/ppermute | solution.py:193
  25.4 31.8 %collective-permute-start.4 = (bf16[2,96,1536]{2,1,0:T(8,128)(2,1)S(1)}, bf16[2,96,1536]{2,1,0:T(8,128)(2,1)S(1)}, u32[]{:S(2)}, u32[]{:S(2)}) collective-permute-start(bf16[2,96,1536]{2,1,0:T(8,128)(2,1)S(1)} %pad_maximum_fusion.9.refs_1_), channel_id=1, source_target_pairs={{0,8},{4,12},{8,0},{12,4},{16,24},{20,28},{24,16},{28,20},{1,9},{5... | collective-permute-start | bytes 1769480 | tf_op jit(solution)/shard_map/ppermute | solution.py:193
  30.9 18.7 %all-to-all-start.4 = ((s32[32,1,128]{2,1,0:T(1,128)}), s32[32,1,128]{2,1,0:T(1,128)S(1)}, u32[]{:S(2)}, u32[]{:S(2)}) async-start(s32[32,1,128]{2,1,0:T(1,128)} %bitcast.511), calls=%async_computation.4 | async-start | bytes 32768 | tf_op jit(solution)/shard_map/all_to_all | solution.py:880
  35.9 24.3 %collective-permute-start.3 = (bf16[4,528,128]{2,1,0:T(8,128)(2,1)S(1)}, bf16[4,528,128]{2,1,0:T(8,128)(2,1)S(1)}, u32[]{:S(2)}, u32[]{:S(2)}) collective-permute-start(bf16[4,528,128]{2,1,0:T(8,128)(2,1)S(1)} %pad_maximum_fusion.13.refs_2_), channel_id=1, source_target_pairs={{0,8},{4,12},{8,0},{12,4},{16,24},{20,28},{24,16},{28,20},{1,9},{5... | collective-permute-start | bytes 1622024 | tf_op jit(solution)/shard_map/ppermute | solution.py:193
  63.2 16.5 %collective-permute-start.5 = (bf16[8,528,128]{2,1,0:T(8,128)(2,1)}, bf16[8,528,128]{2,1,0:T(8,128)(2,1)S(1)}, u32[]{:S(2)}, u32[]{:S(2)}) collective-permute-start(bf16[8,528,128]{2,1,0:T(8,128)(2,1)} %pad_maximum_fusion.6.refs_1_.own_ref), channel_id=1, source_target_pairs={{0,1},{1,0},{2,3},{3,2},{4,5},{5,4},{6,7},{7,6},{8,9},{9,8},{10,11... | collective-permute-start | bytes 3244040 | tf_op jit(solution)/shard_map/ppermute | solution.py:193
  63.2 49.9 %all-to-all-start.5 = ((bf16[32,32,768]{2,1,0:T(8,128)(2,1)}), bf16[32,32,768]{2,1,0:T(8,128)(2,1)}, u32[]{:S(2)}, u32[]{:S(2)}) async-start(bf16[32,32,768]{2,1,0:T(8,128)(2,1)} %bitcast.15), calls=%async_computation.5 | async-start | bytes 3145728 | tf_op jit(solution)/shard_map/all_to_all | solution.py:880
  75.1 41.6 %collective-permute-start.7 = (bf16[4,96,1536]{2,1,0:T(8,128)(2,1)}, bf16[4,96,1536]{2,1,0:T(8,128)(2,1)}, u32[]{:S(2)}, u32[]{:S(2)}) collective-permute-start(bf16[4,96,1536]{2,1,0:T(8,128)(2,1)} %pad_maximum_fusion.3.refs_1_), channel_id=1, source_target_pairs={{0,4},{4,0},{8,12},{12,8},{16,20},{20,16},{24,28},{28,24},{1,5},{5... | collective-permute-start | bytes 3538952 | tf_op jit(solution)/shard_map/ppermute | solution.py:193
  76.8 52.3 %collective-permute-start.9 = (bf16[1,96,768]{2,1,0:T(8,128)(2,1)}, bf16[1,96,768]{2,1,0:T(8,128)(2,1)}, u32[]{:S(2)}, u32[]{:S(2)}) collective-permute-start(bf16[1,96,768]{2,1,0:T(8,128)(2,1)} %shard_map.490.refs_2_), channel_id=1, source_target_pairs={{0,16},{4,20},{8,24},{12,28},{16,0},{20,4},{24,8},{28,12},{1,17},{... | collective-permute-start | bytes 442376 | tf_op jit(solution)/shard_map/ppermute | solution.py:193
  79.2 51.9 %collective-permute-start.6 = (bf16[1,112,768]{2,1,0:T(8,128)(2,1)}, bf16[1,112,768]{2,1,0:T(8,128)(2,1)}, u32[]{:S(2)}, u32[]{:S(2)}) collective-permute-start(bf16[1,112,768]{2,1,0:T(8,128)(2,1)} %shard_map.489.refs_1_), channel_id=1, source_target_pairs={{0,16},{4,20},{8,24},{12,28},{16,0},{20,4},{24,8},{28,12},{1,17},{... | collective-permute-start | bytes 516104 | tf_op jit(solution)/shard_map/ppermute | solution.py:193
  120.8 32.4 %collective-permute-start.11 = (bf16[8,96,1536]{2,1,0:T(8,128)(2,1)}, bf16[8,96,1536]{2,1,0:T(8,128)(2,1)}, u32[]{:S(2)}, u32[]{:S(2)}) collective-permute-start(bf16[8,96,1536]{2,1,0:T(8,128)(2,1)} %pad_maximum_fusion.refs_1_.own_ref), channel_id=1, source_target_pairs={{0,1},{1,0},{2,3},{3,2},{4,5},{5,4},{6,7},{7,6},{8,9},{9,8},{10,11... | collective-permute-start | bytes 7077896 | tf_op jit(solution)/shard_map/ppermute | solution.py:193
  142.5 38.2 %collective-permute-start.13 = (bf16[4,96,768]{2,1,0:T(8,128)(2,1)S(1)}, bf16[4,96,768]{2,1,0:T(8,128)(2,1)S(1)}, u32[]{:S(2)}, u32[]{:S(2)}) collective-permute-start(bf16[4,96,768]{2,1,0:T(8,128)(2,1)S(1)} %pad_maximum_fusion.10.refs_2_.refs_0_.refs_1_), channel_id=1, source_target_pairs={{0,2},{1,3},{2,0},{3,1},{4,6},{5,7},{6,4},{7,5},{8,10},{9,11},{10,... | collective-permute-start | bytes 1769480 | tf_op jit(solution)/shard_map/ppermute | solution.py:193
  144.0 37.6 %collective-permute-start.14 = (bf16[1,96,1536]{2,1,0:T(8,128)(2,1)}, bf16[1,96,1536]{2,1,0:T(8,128)(2,1)}, u32[]{:S(2)}, u32[]{:S(2)}) collective-permute-start(bf16[1,96,1536]{2,1,0:T(8,128)(2,1)} %shard_map.507), channel_id=1, source_target_pairs={{0,16},{4,20},{8,24},{12,28},{16,0},{20,4},{24,8},{28,12},{1,17},{... | collective-permute-start | bytes 884744 | tf_op jit(solution)/shard_map/ppermute | solution.py:193
  152.4 28.3 %collective-permute-start.12 = (bf16[4,112,768]{2,1,0:T(8,128)(2,1)S(1)}, bf16[4,112,768]{2,1,0:T(8,128)(2,1)S(1)}, u32[]{:S(2)}, u32[]{:S(2)}) collective-permute-start(bf16[4,112,768]{2,1,0:T(8,128)(2,1)S(1)} %copy-done.12), channel_id=1, source_target_pairs={{0,4},{4,0},{8,12},{12,8},{16,20},{20,16},{24,28},{28,24},{1,5},{5... | collective-permute-start | bytes 2064392 | tf_op jit(solution)/shard_map/ppermute | solution.py:193
  183.8 16.4 %collective-permute-start.24 = (bf16[4,96,768]{2,1,0:T(8,128)(2,1)S(1)}, bf16[4,96,768]{2,1,0:T(8,128)(2,1)}, u32[]{:S(2)}, u32[]{:S(2)}) collective-permute-start(bf16[4,96,768]{2,1,0:T(8,128)(2,1)S(1)} %copy-done.18), channel_id=1, source_target_pairs={{0,4},{4,0},{8,12},{12,8},{16,20},{20,16},{24,28},{28,24},{1,5},{5... | collective-permute-start | bytes 1769480 | tf_op jit(solution)/shard_map/ppermute | solution.py:193
  185.1 26.0 %collective-permute-start.25 = (bf16[4,96,768]{2,1,0:T(8,128)(2,1)}, bf16[4,96,768]{2,1,0:T(8,128)(2,1)S(1)}, u32[]{:S(2)}, u32[]{:S(2)}) collective-permute-start(bf16[4,96,768]{2,1,0:T(8,128)(2,1)} %shard_map.506.refs_4_.refs_0_), channel_id=1, source_target_pairs={{0,4},{4,0},{8,12},{12,8},{16,20},{20,16},{24,28},{28,24},{1,5},{5... | collective-permute-start | bytes 1769480 | tf_op jit(solution)/shard_map/ppermute | solution.py:193
  185.8 26.1 %collective-permute-start.18 = (bf16[4,112,768]{2,1,0:T(8,128)(2,1)S(1)}, bf16[4,112,768]{2,1,0:T(8,128)(2,1)S(1)}, u32[]{:S(2)}, u32[]{:S(2)}) collective-permute-start(bf16[4,112,768]{2,1,0:T(8,128)(2,1)S(1)} %copy-done.13), channel_id=1, source_target_pairs={{0,2},{1,3},{2,0},{3,1},{4,6},{5,7},{6,4},{7,5},{8,10},{9,11},{10,... | collective-permute-start | bytes 2064392 | tf_op jit(solution)/shard_map/ppermute | solution.py:193
  188.0 29.2 %collective-permute-start.19 = (bf16[4,112,768]{2,1,0:T(8,128)(2,1)}, bf16[4,112,768]{2,1,0:T(8,128)(2,1)S(1)}, u32[]{:S(2)}, u32[]{:S(2)}) collective-permute-start(bf16[4,112,768]{2,1,0:T(8,128)(2,1)} %shard_map.504.refs_2_.refs_0_), channel_id=1, source_target_pairs={{0,2},{1,3},{2,0},{3,1},{4,6},{5,7},{6,4},{7,5},{8,10},{9,11},{10,... | collective-permute-start | bytes 2064392 | tf_op jit(solution)/shard_map/ppermute | solution.py:193
  192.7 19.3 %collective-permute-start.17 = (bf16[1,96,768]{2,1,0:T(8,128)(2,1)}, bf16[1,96,768]{2,1,0:T(8,128)(2,1)}, u32[]{:S(2)}, u32[]{:S(2)}) collective-permute-start(bf16[1,96,768]{2,1,0:T(8,128)(2,1)} %shard_map.513), channel_id=1, source_target_pairs={{0,16},{4,20},{8,24},{12,28},{16,0},{20,4},{24,8},{28,12},{1,17},{... | collective-permute-start | bytes 442376 | tf_op jit(solution)/shard_map/ppermute | solution.py:193
  200.2 26.3 %collective-permute-start.15 = (bf16[2,96,1536]{2,1,0:T(8,128)(2,1)}, bf16[2,96,1536]{2,1,0:T(8,128)(2,1)}, u32[]{:S(2)}, u32[]{:S(2)}) collective-permute-start(bf16[2,96,1536]{2,1,0:T(8,128)(2,1)} %pad_maximum_fusion.11.refs_5_.refs_1_), channel_id=1, source_target_pairs={{0,8},{4,12},{8,0},{12,4},{16,24},{20,28},{24,16},{28,20},{1,9},{5... | collective-permute-start | bytes 1769480 | tf_op jit(solution)/shard_map/ppermute | solution.py:193
  211.1 15.9 %collective-permute-start.27 = (bf16[4,96,768]{2,1,0:T(8,128)(2,1)}, bf16[4,96,768]{2,1,0:T(8,128)(2,1)}, u32[]{:S(2)}, u32[]{:S(2)}) collective-permute-start(bf16[4,96,768]{2,1,0:T(8,128)(2,1)} %shard_map.521.refs_9_), channel_id=1, source_target_pairs={{0,1},{1,0},{2,3},{3,2},{4,5},{5,4},{6,7},{7,6},{8,9},{9,8},{10,11... | collective-permute-start | bytes 1769480 | tf_op jit(solution)/shard_map/ppermute | solution.py:193
  233.3 28.7 %collective-permute-start.32 = (bf16[4,96,1536]{2,1,0:T(8,128)(2,1)}, bf16[4,96,1536]{2,1,0:T(8,128)(2,1)}, u32[]{:S(2)}, u32[]{:S(2)}) collective-permute-start(bf16[4,96,1536]{2,1,0:T(8,128)(2,1)} %pad_maximum_fusion.4.refs_1_), channel_id=1, source_target_pairs={{0,4},{4,0},{8,12},{12,8},{16,20},{20,16},{24,28},{28,24},{1,5},{5... | collective-permute-start | bytes 3538952 | tf_op jit(solution)/shard_map/ppermute | solution.py:193
  265.3 24.6 %collective-permute-start.33 = (bf16[8,96,1536]{2,1,0:T(8,128)(2,1)}, bf16[8,96,1536]{2,1,0:T(8,128)(2,1)}, u32[]{:S(2)}, u32[]{:S(2)}) collective-permute-start(bf16[8,96,1536]{2,1,0:T(8,128)(2,1)} %pad_maximum_fusion.1.refs_3_.own_ref), channel_id=1, source_target_pairs={{0,1},{1,0},{2,3},{3,2},{4,5},{5,4},{6,7},{7,6},{8,9},{9,8},{10,11... | collective-permute-start | bytes 7077896 | tf_op jit(solution)/shard_map/ppermute | solution.py:193
  265.6 16.8 %collective-permute-start.30 = (bf16[2,112,768]{2,1,0:T(8,128)(2,1)}, bf16[2,112,768]{2,1,0:T(8,128)(2,1)S(1)}, u32[]{:S(2)}, u32[]{:S(2)}) collective-permute-start(bf16[2,112,768]{2,1,0:T(8,128)(2,1)} %pad_maximum_fusion.17.refs_2_), channel_id=1, source_target_pairs={{0,8},{4,12},{8,0},{12,4},{16,24},{20,28},{24,16},{28,20},{1,9},{5... | collective-permute-start | bytes 1032200 | tf_op jit(solution)/shard_map/ppermute | solution.py:193
  277.6 19.5 %collective-permute-start.35 = (bf16[4,96,768]{2,1,0:T(8,128)(2,1)S(1)}, bf16[4,96,768]{2,1,0:T(8,128)(2,1)S(1)}, u32[]{:S(2)}, u32[]{:S(2)}) collective-permute-start(bf16[4,96,768]{2,1,0:T(8,128)(2,1)S(1)} %pad_maximum_fusion.12.refs_2_.refs_0_), channel_id=1, source_target_pairs={{0,2},{1,3},{2,0},{3,1},{4,6},{5,7},{6,4},{7,5},{8,10},{9,11},{10,... | collective-permute-start | bytes 1769480 | tf_op jit(solution)/shard_map/ppermute | solution.py:193
  284.2 17.1 %collective-permute-start.34 = (bf16[4,112,768]{2,1,0:T(8,128)(2,1)S(1)}, bf16[4,112,768]{2,1,0:T(8,128)(2,1)S(1)}, u32[]{:S(2)}, u32[]{:S(2)}) collective-permute-start(bf16[4,112,768]{2,1,0:T(8,128)(2,1)S(1)} %pad_maximum_fusion.8.refs_1_.refs_0_), channel_id=1, source_target_pairs={{0,4},{4,0},{8,12},{12,8},{16,20},{20,16},{24,28},{28,24},{1,5},{5... | collective-permute-start | bytes 2064392 | tf_op jit(solution)/shard_map/ppermute | solution.py:193
  302.2 27.7 %collective-permute-start.42 = (bf16[4,96,768]{2,1,0:T(8,128)(2,1)S(1)}, bf16[4,96,768]{2,1,0:T(8,128)(2,1)}, u32[]{:S(2)}, u32[]{:S(2)}) collective-permute-start(bf16[4,96,768]{2,1,0:T(8,128)(2,1)S(1)} %copy-done.21), channel_id=1, source_target_pairs={{0,4},{4,0},{8,12},{12,8},{16,20},{20,16},{24,28},{28,24},{1,5},{5... | collective-permute-start | bytes 1769480 | tf_op jit(solution)/shard_map/ppermute | solution.py:193
  304.0 25.9 %collective-permute-start.43 = (bf16[4,96,768]{2,1,0:T(8,128)(2,1)}, bf16[4,96,768]{2,1,0:T(8,128)(2,1)}, u32[]{:S(2)}, u32[]{:S(2)}) collective-permute-start(bf16[4,96,768]{2,1,0:T(8,128)(2,1)} %shard_map.533.refs_4_.refs_0_), channel_id=1, source_target_pairs={{0,4},{4,0},{8,12},{12,8},{16,20},{20,16},{24,28},{28,24},{1,5},{5... | collective-permute-start | bytes 1769480 | tf_op jit(solution)/shard_map/ppermute | solution.py:193
  304.3 36.2 %collective-permute-start.36 = (bf16[4,112,768]{2,1,0:T(8,128)(2,1)S(1)}, bf16[4,112,768]{2,1,0:T(8,128)(2,1)}, u32[]{:S(2)}, u32[]{:S(2)}) collective-permute-start(bf16[4,112,768]{2,1,0:T(8,128)(2,1)S(1)} %copy-done.9), channel_id=1, source_target_pairs={{0,2},{1,3},{2,0},{3,1},{4,6},{5,7},{6,4},{7,5},{8,10},{9,11},{10,... | collective-permute-start | bytes 2064392 | tf_op jit(solution)/shard_map/ppermute | solution.py:193
  307.3 32.6 %collective-permute-start.37 = (bf16[4,112,768]{2,1,0:T(8,128)(2,1)S(1)}, bf16[4,112,768]{2,1,0:T(8,128)(2,1)}, u32[]{:S(2)}, u32[]{:S(2)}) collective-permute-start(bf16[4,112,768]{2,1,0:T(8,128)(2,1)S(1)} %copy-done.28), channel_id=1, source_target_pairs={{0,2},{1,3},{2,0},{3,1},{4,6},{5,7},{6,4},{7,5},{8,10},{9,11},{10,... | collective-permute-start | bytes 2064392 | tf_op jit(solution)/shard_map/ppermute | solution.py:193
  365.6 41.3 %all-to-all-start.6 = ((bf16[32,32,768]{2,1,0:T(8,128)(2,1)}), bf16[32,32,768]{2,1,0:T(8,128)(2,1)}, u32[]{:S(2)}, u32[]{:S(2)}) async-start(bf16[32,32,768]{2,1,0:T(8,128)(2,1)} %broadcast_in_dim.303), calls=%async_computation.6 | async-start | bytes 3145728 | tf_op jit(solution)/shard_map/all_to_all | solution.py:874
  415.5 19.5 %all-to-all-start.7 = ((f32[32,3,1024]{2,1,0:T(4,128)}), f32[32,3,1024]{2,1,0:T(4,128)}, u32[]{:S(2)}, u32[]{:S(2)}) async-start(f32[32,3,1024]{2,1,0:T(4,128)} %broadcast_in_dim.305), calls=%async_computation.7 | async-start | bytes 1048576 | tf_op jit(solution)/shard_map/all_to_all | solution.py:874
  446.8 40.9 %all-to-all-start.8 = ((bf16[32,32,768]{2,1,0:T(8,128)(2,1)}), bf16[32,32,768]{2,1,0:T(8,128)(2,1)}, u32[]{:S(2)}, u32[]{:S(2)}) async-start(bf16[32,32,768]{2,1,0:T(8,128)(2,1)} %bitcast.504), calls=%async_computation.8 | async-start | bytes 3145728 | tf_op jit(solution)/shard_map/all_to_all | solution.py:880
  516.2 22.9 %collective-permute-start.49 = (bf16[16,96,768]{2,1,0:T(8,128)(2,1)}, bf16[16,96,768]{2,1,0:T(8,128)(2,1)}, u32[]{:S(2)}, u32[]{:S(2)}) collective-permute-start(bf16[16,96,768]{2,1,0:T(8,128)(2,1)} %get-tuple-element.378), channel_id=1, source_target_pairs={{0,1},{1,0},{2,3},{3,2},{4,5},{5,4},{6,7},{7,6},{8,9},{9,8},{10,11... | collective-permute-start | bytes 7077896 | tf_op jit(solution)/shard_map/ppermute | solution.py:193
  516.3 28.7 %collective-permute-start.48 = (bf16[16,112,768]{2,1,0:T(8,128)(2,1)}, bf16[16,112,768]{2,1,0:T(8,128)(2,1)}, u32[]{:S(2)}, u32[]{:S(2)}) collective-permute-start(bf16[16,112,768]{2,1,0:T(8,128)(2,1)} %get-tuple-element.376), channel_id=1, source_target_pairs={{0,1},{1,0},{2,3},{3,2},{4,5},{5,4},{6,7},{7,6},{8,9},{9,8},{10,11... | collective-permute-start | bytes 8257544 | tf_op jit(solution)/shard_map/ppermute | solution.py:193
  543.6 67.8 %collective-permute-start.51 = (bf16[2,4,96,768]{3,2,1,0:T(8,128)(2,1)}, bf16[2,4,96,768]{3,2,1,0:T(8,128)(2,1)}, u32[]{:S(2)}, u32[]{:S(2)}) collective-permute-start(bf16[2,4,96,768]{3,2,1,0:T(8,128)(2,1)} %get-tuple-element.650.refs_2_), channel_id=1, source_target_pairs={{0,4},{4,0},{8,12},{12,8},{16,20},{20,16},{24,28},{28,24},{1,5},{5... | collective-permute-start | bytes 3538952 | tf_op jit(solution)/shard_map/ppermute | solution.py:193
  549.5 66.6 %collective-permute-start.50 = (bf16[2,4,112,768]{3,2,1,0:T(8,128)(2,1)}, bf16[2,4,112,768]{3,2,1,0:T(8,128)(2,1)}, u32[]{:S(2)}, u32[]{:S(2)}) collective-permute-start(bf16[2,4,112,768]{3,2,1,0:T(8,128)(2,1)} %get-tuple-element.660.refs_1_), channel_id=1, source_target_pairs={{0,2},{1,3},{2,0},{3,1},{4,6},{5,7},{6,4},{7,5},{8,10},{9,11},{10,... | collective-permute-start | bytes 4128776 | tf_op jit(solution)/shard_map/ppermute | solution.py:193
  600.1 27.4 %collective-permute-start.52 = (bf16[8,104,1536]{2,1,0:T(8,128)(2,1)}, bf16[8,104,1536]{2,1,0:T(8,128)(2,1)}, u32[]{:S(2)}, u32[]{:S(2)}) collective-permute-start(bf16[8,104,1536]{2,1,0:T(8,128)(2,1)} %pad_dynamic-update-slice_fusion.3.refs_1_), channel_id=1, source_target_pairs={{0,1},{1,0},{2,3},{3,2},{4,5},{5,4},{6,7},{7,6},{8,9},{9,8},{10,11... | collective-permute-start | bytes 7667720 | tf_op jit(solution)/shard_map/ppermute | solution.py:193
  615.2 48.3 %collective-permute-start.54 = (bf16[4,96,768]{2,1,0:T(8,128)(2,1)}, bf16[4,96,768]{2,1,0:T(8,128)(2,1)}, u32[]{:S(2)}, u32[]{:S(2)}) collective-permute-start(bf16[4,96,768]{2,1,0:T(8,128)(2,1)} %get-tuple-element.666.refs_2_), channel_id=1, source_target_pairs={{0,2},{1,3},{2,0},{3,1},{4,6},{5,7},{6,4},{7,5},{8,10},{9,11},{10,... | collective-permute-start | bytes 1769480 | tf_op jit(solution)/shard_map/ppermute | solution.py:193
  619.4 49.2 %collective-permute-start.53 = (bf16[4,112,768]{2,1,0:T(8,128)(2,1)}, bf16[4,112,768]{2,1,0:T(8,128)(2,1)}, u32[]{:S(2)}, u32[]{:S(2)}) collective-permute-start(bf16[4,112,768]{2,1,0:T(8,128)(2,1)} %get-tuple-element.658.refs_1_), channel_id=1, source_target_pairs={{0,4},{4,0},{8,12},{12,8},{16,20},{20,16},{24,28},{28,24},{1,5},{5... | collective-permute-start | bytes 2064392 | tf_op jit(solution)/shard_map/ppermute | solution.py:193
  630.6 49.3 %collective-permute-start.55 = (bf16[2,2,104,1536]{3,2,1,0:T(8,128)(2,1)}, bf16[2,2,104,1536]{3,2,1,0:T(8,128)(2,1)}, u32[]{:S(2)}, u32[]{:S(2)}) collective-permute-start(bf16[2,2,104,1536]{3,2,1,0:T(8,128)(2,1)} %fusion.51.refs_1_), channel_id=1, source_target_pairs={{0,4},{4,0},{8,12},{12,8},{16,20},{20,16},{24,28},{28,24},{1,5},{5... | collective-permute-start | bytes 3833864 | tf_op jit(solution)/shard_map/ppermute | solution.py:193
  665.6 85.3 %collective-permute-start.59 = (bf16[2,96,768]{2,1,0:T(8,128)(2,1)}, bf16[2,96,768]{2,1,0:T(8,128)(2,1)}, u32[]{:S(2)}, u32[]{:S(2)}) collective-permute-start(bf16[2,96,768]{2,1,0:T(8,128)(2,1)} %get-tuple-element.688.refs_2_), channel_id=1, source_target_pairs={{0,8},{4,12},{8,0},{12,4},{16,24},{20,28},{24,16},{28,20},{1,9},{5... | collective-permute-start | bytes 884744 | tf_op jit(solution)/shard_map/ppermute | solution.py:193
  671.8 82.7 %collective-permute-start.58 = (bf16[2,112,768]{2,1,0:T(8,128)(2,1)}, bf16[2,112,768]{2,1,0:T(8,128)(2,1)}, u32[]{:S(2)}, u32[]{:S(2)}) collective-permute-start(bf16[2,112,768]{2,1,0:T(8,128)(2,1)} %get-tuple-element.680.refs_1_), channel_id=1, source_target_pairs={{0,8},{4,12},{8,0},{12,4},{16,24},{20,28},{24,16},{28,20},{1,9},{5... | collective-permute-start | bytes 1032200 | tf_op jit(solution)/shard_map/ppermute | solution.py:193
  673.8 50.6 %collective-permute-start.57 = (bf16[16,96,768]{2,1,0:T(8,128)(2,1)}, bf16[16,96,768]{2,1,0:T(8,128)(2,1)}, u32[]{:S(2)}, u32[]{:S(2)}) collective-permute-start(bf16[16,96,768]{2,1,0:T(8,128)(2,1)} %get-tuple-element.404), channel_id=1, source_target_pairs={{0,1},{1,0},{2,3},{3,2},{4,5},{5,4},{6,7},{7,6},{8,9},{9,8},{10,11... | collective-permute-start | bytes 7077896 | tf_op jit(solution)/shard_map/ppermute | solution.py:193
  673.8 56.2 %collective-permute-start.56 = (bf16[16,112,768]{2,1,0:T(8,128)(2,1)}, bf16[16,112,768]{2,1,0:T(8,128)(2,1)}, u32[]{:S(2)}, u32[]{:S(2)}) collective-permute-start(bf16[16,112,768]{2,1,0:T(8,128)(2,1)} %get-tuple-element.402), channel_id=1, source_target_pairs={{0,1},{1,0},{2,3},{3,2},{4,5},{5,4},{6,7},{7,6},{8,9},{9,8},{10,11... | collective-permute-start | bytes 8257544 | tf_op jit(solution)/shard_map/ppermute | solution.py:193
  683.3 74.3 %collective-permute-start.60 = (bf16[2,104,1536]{2,1,0:T(8,128)(2,1)}, bf16[2,104,1536]{2,1,0:T(8,128)(2,1)}, u32[]{:S(2)}, u32[]{:S(2)}) collective-permute-start(bf16[2,104,1536]{2,1,0:T(8,128)(2,1)} %fusion.98.refs_3_), channel_id=1, source_target_pairs={{0,8},{4,12},{8,0},{12,4},{16,24},{20,28},{24,16},{28,20},{1,9},{5... | collective-permute-start | bytes 1916936 | tf_op jit(solution)/shard_map/ppermute | solution.py:193
  728.9 92.3 %collective-permute-start.65 = (bf16[2,4,96,768]{3,2,1,0:T(8,128)(2,1)}, bf16[2,4,96,768]{3,2,1,0:T(8,128)(2,1)}, u32[]{:S(2)}, u32[]{:S(2)}) collective-permute-start(bf16[2,4,96,768]{3,2,1,0:T(8,128)(2,1)} %get-tuple-element.648.refs_2_), channel_id=1, source_target_pairs={{0,4},{4,0},{8,12},{12,8},{16,20},{20,16},{24,28},{28,24},{1,5},{5... | collective-permute-start | bytes 3538952 | tf_op jit(solution)/shard_map/ppermute | solution.py:193
  735.9 80.9 %collective-permute-start.61 = (bf16[2,4,112,768]{3,2,1,0:T(8,128)(2,1)}, bf16[2,4,112,768]{3,2,1,0:T(8,128)(2,1)}, u32[]{:S(2)}, u32[]{:S(2)}) collective-permute-start(bf16[2,4,112,768]{3,2,1,0:T(8,128)(2,1)} %get-tuple-element.654.refs_1_), channel_id=1, source_target_pairs={{0,2},{1,3},{2,0},{3,1},{4,6},{5,7},{6,4},{7,5},{8,10},{9,11},{10,... | collective-permute-start | bytes 4128776 | tf_op jit(solution)/shard_map/ppermute | solution.py:193
  753.5 32.1 %collective-permute-start.74 = (bf16[1,96,768]{2,1,0:T(8,128)(2,1)}, bf16[1,96,768]{2,1,0:T(8,128)(2,1)}, u32[]{:S(2)}, u32[]{:S(2)}) collective-permute-start(bf16[1,96,768]{2,1,0:T(8,128)(2,1)} %add_convert_fusion.33.refs_2_), channel_id=1, source_target_pairs={{0,16},{4,20},{8,24},{12,28},{16,0},{20,4},{24,8},{28,12},{1,17},{... | collective-permute-start | bytes 442376 | tf_op jit(solution)/shard_map/ppermute | solution.py:193
  755.6 32.0 %collective-permute-start.73 = (bf16[1,112,768]{2,1,0:T(8,128)(2,1)S(1)}, bf16[1,112,768]{2,1,0:T(8,128)(2,1)}, u32[]{:S(2)}, u32[]{:S(2)}) collective-permute-start(bf16[1,112,768]{2,1,0:T(8,128)(2,1)S(1)} %add_convert_fusion.29.refs_1_), channel_id=1, source_target_pairs={{0,16},{4,20},{8,24},{12,28},{16,0},{20,4},{24,8},{28,12},{1,17},{... | collective-permute-start | bytes 516104 | tf_op jit(solution)/shard_map/ppermute | solution.py:193
  759.4 25.0 %collective-permute-start.80 = (bf16[104,1536]{1,0:T(8,128)(2,1)}, bf16[104,1536]{1,0:T(8,128)(2,1)}, u32[]{:S(2)}, u32[]{:S(2)}) collective-permute-start(bf16[104,1536]{1,0:T(8,128)(2,1)} %fusion.127.refs_3_), channel_id=1, source_target_pairs={{0,16},{4,20},{8,24},{12,28},{16,0},{20,4},{24,8},{28,12},{1,17},{... | collective-permute-start | bytes 958472 | tf_op jit(solution)/shard_map/ppermute | solution.py:193
  784.4 20.4 %collective-permute-start.62 = (bf16[8,104,1536]{2,1,0:T(8,128)(2,1)}, bf16[8,104,1536]{2,1,0:T(8,128)(2,1)}, u32[]{:S(2)}, u32[]{:S(2)}) collective-permute-start(bf16[8,104,1536]{2,1,0:T(8,128)(2,1)} %pad_dynamic-update-slice_fusion.1.refs_1_), channel_id=1, source_target_pairs={{0,1},{1,0},{2,3},{3,2},{4,5},{5,4},{6,7},{7,6},{8,9},{9,8},{10,11... | collective-permute-start | bytes 7667720 | tf_op jit(solution)/shard_map/ppermute | solution.py:193
  797.3 41.1 %all-to-all-start.9 = ((bf16[32,32,768]{2,1,0:T(8,128)(2,1)}), bf16[32,32,768]{2,1,0:T(8,128)(2,1)}, u32[]{:S(2)}, u32[]{:S(2)}) async-start(bf16[32,32,768]{2,1,0:T(8,128)(2,1)} %bitcast.89), calls=%async_computation.9 | async-start | bytes 3145728 | tf_op jit(solution)/shard_map/all_to_all | solution.py:880
  807.6 50.2 %collective-permute-start.64 = (bf16[2,2,104,1536]{3,2,1,0:T(8,128)(2,1)}, bf16[2,2,104,1536]{3,2,1,0:T(8,128)(2,1)}, u32[]{:S(2)}, u32[]{:S(2)}) collective-permute-start(bf16[2,2,104,1536]{3,2,1,0:T(8,128)(2,1)} %fusion.52.refs_1_), channel_id=1, source_target_pairs={{0,4},{4,0},{8,12},{12,8},{16,20},{20,16},{24,28},{28,24},{1,5},{5... | collective-permute-start | bytes 3833864 | tf_op jit(solution)/shard_map/ppermute | solution.py:193
  816.8 52.5 %collective-permute-start.68 = (bf16[8,384,128]{2,1,0:T(8,128)(2,1)}, bf16[8,384,128]{2,1,0:T(8,128)(2,1)S(1)}, u32[]{:S(2)}, u32[]{:S(2)}) collective-permute-start(bf16[8,384,128]{2,1,0:T(8,128)(2,1)} %get-tuple-element.676.refs_1_), channel_id=1, source_target_pairs={{0,1},{1,0},{2,3},{3,2},{4,5},{5,4},{6,7},{7,6},{8,9},{9,8},{10,11... | collective-permute-start | bytes 2359304 | tf_op jit(solution)/shard_map/ppermute | solution.py:193
  819.9 42.9 %collective-permute-start.63 = (bf16[4,112,768]{2,1,0:T(8,128)(2,1)}, bf16[4,112,768]{2,1,0:T(8,128)(2,1)}, u32[]{:S(2)}, u32[]{:S(2)}) collective-permute-start(bf16[4,112,768]{2,1,0:T(8,128)(2,1)} %get-tuple-element.652.refs_1_), channel_id=1, source_target_pairs={{0,4},{4,0},{8,12},{12,8},{16,20},{20,16},{24,28},{28,24},{1,5},{5... | collective-permute-start | bytes 2064392 | tf_op jit(solution)/shard_map/ppermute | solution.py:193
  824.1 42.4 %collective-permute-start.69 = (bf16[4,96,768]{2,1,0:T(8,128)(2,1)}, bf16[4,96,768]{2,1,0:T(8,128)(2,1)}, u32[]{:S(2)}, u32[]{:S(2)}) collective-permute-start(bf16[4,96,768]{2,1,0:T(8,128)(2,1)} %get-tuple-element.664.refs_1_), channel_id=1, source_target_pairs={{0,2},{1,3},{2,0},{3,1},{4,6},{5,7},{6,4},{7,5},{8,10},{9,11},{10,... | collective-permute-start | bytes 1769480 | tf_op jit(solution)/shard_map/ppermute | solution.py:193
  861.2 17.6 %collective-permute-start.67 = (bf16[2,104,1536]{2,1,0:T(8,128)(2,1)}, bf16[2,104,1536]{2,1,0:T(8,128)(2,1)}, u32[]{:S(2)}, u32[]{:S(2)}) collective-permute-start(bf16[2,104,1536]{2,1,0:T(8,128)(2,1)} %fusion.99.refs_1_), channel_id=1, source_target_pairs={{0,8},{4,12},{8,0},{12,4},{16,24},{20,28},{24,16},{28,20},{1,9},{5... | collective-permute-start | bytes 1916936 | tf_op jit(solution)/shard_map/ppermute | solution.py:193
  865.0 28.0 %collective-permute-start.66 = (bf16[2,112,768]{2,1,0:T(8,128)(2,1)}, bf16[2,112,768]{2,1,0:T(8,128)(2,1)}, u32[]{:S(2)}, u32[]{:S(2)}) collective-permute-start(bf16[2,112,768]{2,1,0:T(8,128)(2,1)} %get-tuple-element.678.refs_1_), channel_id=1, source_target_pairs={{0,8},{4,12},{8,0},{12,4},{16,24},{20,28},{24,16},{28,20},{1,9},{5... | collective-permute-start | bytes 1032200 | tf_op jit(solution)/shard_map/ppermute | solution.py:193
  868.7 29.4 %collective-permute-start.71 = (bf16[2,96,768]{2,1,0:T(8,128)(2,1)}, bf16[2,96,768]{2,1,0:T(8,128)(2,1)}, u32[]{:S(2)}, u32[]{:S(2)}) collective-permute-start(bf16[2,96,768]{2,1,0:T(8,128)(2,1)} %get-tuple-element.686.refs_1_), channel_id=1, source_target_pairs={{0,8},{4,12},{8,0},{12,4},{16,24},{20,28},{24,16},{28,20},{1,9},{5... | collective-permute-start | bytes 884744 | tf_op jit(solution)/shard_map/ppermute | solution.py:193
  871.4 27.7 %collective-permute-start.76 = (bf16[2,2,384,128]{3,2,1,0:T(8,128)(2,1)S(1)}, bf16[2,2,384,128]{3,2,1,0:T(8,128)(2,1)S(1)}, u32[]{:S(2)}, u32[]{:S(2)}) collective-permute-start(bf16[2,2,384,128]{3,2,1,0:T(8,128)(2,1)S(1)} %fusion.122.refs_1_), channel_id=1, source_target_pairs={{0,4},{4,0},{8,12},{12,8},{16,20},{20,16},{24,28},{28,24},{1,5},{5... | collective-permute-start | bytes 1179656 | tf_op jit(solution)/shard_map/ppermute | solution.py:193
  880.6 34.3 %collective-permute-start.75 = (bf16[104,1536]{1,0:T(8,128)(2,1)}, bf16[104,1536]{1,0:T(8,128)(2,1)S(1)}, u32[]{:S(2)}, u32[]{:S(2)}) collective-permute-start(bf16[104,1536]{1,0:T(8,128)(2,1)} %fusion.128.refs_1_), channel_id=1, source_target_pairs={{0,16},{4,20},{8,24},{12,28},{16,0},{20,4},{24,8},{28,12},{1,17},{... | collective-permute-start | bytes 958472 | tf_op jit(solution)/shard_map/ppermute | solution.py:193
  894.0 19.8 %collective-permute-start.70 = (bf16[1,112,768]{2,1,0:T(8,128)(2,1)S(1)}, bf16[1,112,768]{2,1,0:T(8,128)(2,1)}, u32[]{:S(2)}, u32[]{:S(2)}) collective-permute-start(bf16[1,112,768]{2,1,0:T(8,128)(2,1)S(1)} %add_convert_fusion.27.refs_1_), channel_id=1, source_target_pairs={{0,16},{4,20},{8,24},{12,28},{16,0},{20,4},{24,8},{28,12},{1,17},{... | collective-permute-start | bytes 516104 | tf_op jit(solution)/shard_map/ppermute | solution.py:193
  902.1 17.3 %collective-permute-start.78 = (bf16[2,384,128]{2,1,0:T(8,128)(2,1)}, bf16[2,384,128]{2,1,0:T(8,128)(2,1)}, u32[]{:S(2)}, u32[]{:S(2)}) collective-permute-start(bf16[2,384,128]{2,1,0:T(8,128)(2,1)} %fusion.135.refs_1_), channel_id=1, source_target_pairs={{0,8},{4,12},{8,0},{12,4},{16,24},{20,28},{24,16},{28,20},{1,9},{5... | collective-permute-start | bytes 589832 | tf_op jit(solution)/shard_map/ppermute | solution.py:193
  (498 other events, 3227.9 us)

commit v5 on v4

--- a/solution.py
+++ b/solution.py
@@ -862,9 +862,21 @@
 
 
 def sum_everywhere(values):
-    far, near, high, core = routes()
-    for step in [core] + high + [near] + far:
-        values = values + hop(values, *step)
+    for axis in ("mp", "dp"):
+        size = lax.axis_size(axis)
+
+        def jump(mask):
+            pairs = [(spot, spot ^ mask) for spot in range(size)]
+            return lax.ppermute(values, axis, pairs)
+
+        steps = [1 << bit for bit in bits_of(size)]
+        for number in range(0, len(steps), 2):
+            pair = steps[number : number + 2]
+            if len(pair) == 2:
+                near, far, both = jump(pair[0]), jump(pair[1]), jump(pair[0] | pair[1])
+                values = (values + near) + (far + both)
+            else:
+                values = values + jump(pair[0])
     return values
 
 
@@ -1126,7 +1138,7 @@
 
     def after_attend(self, value):
         if self.mats:
-            return self.step(value, self.units[1])
+            return self.step(value, self.units[1] + self.mats[:1])
         return value
 
     def after_mats(self, text, layout):

time: 1010 us -> 995 us (0.985)
  waiting for transfers between devices: 210 us -> 192 us
    ppermute x91 -> x86, waiting for transfers between devices: 118 us -> 101 us  [hop(): return lax.ppermute(values, axis, pairs)]
    ppermute x91 -> x86, starting transfers between devices: 68.4 us -> 62.1 us  [hop(): return lax.ppermute(values, axis, pairs)]
    unnamed x932 -> x916, local copies, waits for them, and re-layouts: 103 us -> 100 us
  transfers between devices with their start and end apart: 97 -> 99, of which waited for: 32 -> 33; matrix products, arithmetic and copies ran while one was open for 32% -> 33% of each run, Pallas kernels for 15% -> 15%
where the time goes in v5:
time: 995 us; the launch traced here: 982 us
  other arithmetic  228 us (23%)
  waiting for transfers between devices  192 us (19%)
  Pallas kernels  180 us (18%)
  local copies, waits for them, and re-layouts  162 us (16%)
  matrix products  104 us (10%)
  starting transfers between devices  94.4 us (9%)
  between operations  18.3 us (2%)
    ppermute x86, waiting for transfers between devices, hop(): return lax.ppermute(values, axis, pairs)  101 us
    unnamed x916, local copies, waits for them, and re-layouts  100 us
    convert_element_type x37, other arithmetic, add_low(): (kept.astype(jnp.float32) + came.astype(jnp.float32)).astype(jnp.bfloat16)  78.3 us
    ppermute x86, starting transfers between devices, hop(): return lax.ppermute(values, axis, pairs)  62.1 us
    all_to_all x4, waiting for transfers between devices, trade(): return lax.all_to_all(values, ('dp', 'mp'), 0, 0, tiled=True)  50.4 us
    pallas_call x4, Pallas kernels, ffn_back(): pl.pallas_call(functools.partial(ffn_back_kernel, slot_rows[0] if slot_ro...  47.8 us
    pallas_call x2, Pallas kernels, attend_back(): pl.pallas_call(attend_back_kernel, grid=(HEAD_PAIRS,), in_specs=[pl.Block...  37.1 us
    pallas_call x2, Pallas kernels, attend(): pl.pallas_call(attend_kernel, grid=(HEAD_PAIRS,), in_specs=[pl.BlockSpec(...  33.1 us
  transfers between devices with their start and end apart: 99, of which 33 were waited for; matrix products, arithmetic and copies ran while one was open for 33% of the time, Pallas kernels for 15%

profile of v5, /device:TPU:0, one launch (start us, length us, event | category | flops | bytes accessed | tf_op | source)
XLA Modules:
  0.0 982.0 jit_solution(1670169154394698419)
XLA Ops:
  21.2 4.0 convert_element_type.1022
  25.2 5.3 collective-permute-done.1
  30.9 4.7 all-to-all-start.4
  37.5 12.1 %all-to-all-done.4 = s32[32,1,128]{2,1,0:T(1,128)S(1)} async-done(((s32[32,1,128]{2,1,0:T(1,128)}), s32[32,1,128]{2,1,0:T(1,128)S(1)}, u32[]{:S(2)}, u32[]{:S(2)}) %all-to-all-start.4) | async-done | bytes 16416 | tf_op jit(solution)/shard_map/all_to_all | solution.py:892
  51.2 6.1 fusion.34.refs_1_
  63.2 5.0 all-to-all-start.5
  92.2 20.9 %all-to-all-done.5 = bf16[32,32,768]{2,1,0:T(8,128)(2,1)} async-done(((bf16[32,32,768]{2,1,0:T(8,128)(2,1)}), bf16[32,32,768]{2,1,0:T(8,128)(2,1)}, u32[]{:S(2)}, u32[]{:S(2)}) %all-to-all-start.5) | async-done | bytes 1572896 | tf_op jit(solution)/shard_map/all_to_all | solution.py:892
  113.1 3.6 fusion.27
  122.2 3.6 shard_map.493
  137.2 3.6 collective-permute-done.10.refs_0_
  144.2 4.5 collective-permute-done.8.refs_0_
  161.8 16.6 %shard_map.502 = (bf16[512,768]{1,0:T(8,128)(2,1)S(1)}, bf16[512,192]{1,0:T(8,128)(2,1)S(1)}, f32[6,512,2]{2,1,0:T(8,128)S(1)}) custom-call(s32[1]{0:T(128)S(6)} %copy.555.length, bf16[512,768]{1,0:T(8,128)(2,1)S(1)} %fusion.36.qt, bf16[512,768]{1,0:T(8,128)(2,1)S(1)} %slice.1146.kt, bf16[512,768]{1,0:T(8,128)(2,1)S(1)} %add_convert_fusion.9.vt, ...), custom_call_target="tpu_custom_call" | custom-call | flops 4000000000 | bytes 2000000 | tf_op jit(solution)/shard_map/pallas_call | solution.py:527
  188.4 4.0 fusion.246
  196.3 3.7 collective-permute-done.24.refs_0_
  200.2 10.7 %collective-permute-done.25.refs_0_ = bf16[4,96,768]{2,1,0:T(8,128)(2,1)S(1)} collective-permute-done((bf16[4,96,768]{2,1,0:T(8,128)(2,1)}, bf16[4,96,768]{2,1,0:T(8,128)(2,1)S(1)}, u32[]{:S(2)}, u32[]{:S(2)}) %collective-permute-start.25) | collective-permute-done | bytes 589856 | tf_op jit(solution)/shard_map/ppermute | solution.py:193
  213.8 3.2 collective-permute-done.19.refs_0_
  218.0 8.2 collective-permute-done.16.refs_0_
  237.5 13.5 %shard_map.524 = (bf16[512,3072]{1,0:T(8,128)(2,1)}, bf16[512,3072]{1,0:T(8,128)(2,1)}, f32[512,768]{1,0:T(8,128)S(1)}) custom-call(bf16[512,768]{1,0:T(8,128)(2,1)S(1)} %copy-done.16, f32[1,3072]{1,0:T(1,128)S(1)} %broadcast_in_dim_reshape.15.bias_ref, bf16[4,112,768]{2,1,0:T(8,128)(2,1)S(1)} %copy-done.14, bf16[4,112,768]{2,1,0:T(8,128)(2,1)S(1)} %copy-done.27, ...), custom_call_target="tpu_custom_call" | custom-call | flops 1207959552 | bytes 3932160 | tf_op jit(solution)/shard_map/pallas_call | solution.py:664
  253.8 8.0 collective-permute-done.32.refs_0_
  261.8 3.2 pad_maximum_fusion.1.refs_3_.own_ref
  297.7 3.2 slice_bitcast_fusion
  309.7 16.5 %shard_map.537 = (bf16[512,768]{1,0:T(8,128)(2,1)S(1)}, bf16[512,192]{1,0:T(8,128)(2,1)S(1)}, f32[6,512,2]{2,1,0:T(8,128)S(1)}) custom-call(s32[1]{0:T(128)S(6)} %copy.555.length, bf16[512,768]{1,0:T(8,128)(2,1)S(1)} %copy-done.25, bf16[512,768]{1,0:T(8,128)(2,1)S(1)} %copy-done.95, bf16[512,768]{1,0:T(8,128)(2,1)S(1)} %add_convert_fusion.8.vt, ...), custom_call_target="tpu_custom_call" | custom-call | flops 4000000000 | bytes 2000000 | tf_op jit(solution)/shard_map/pallas_call | solution.py:527
  336.0 3.7 fusion.248
  348.0 13.8 %shard_map.546 = (bf16[512,3072]{1,0:T(8,128)(2,1)}, bf16[512,3072]{1,0:T(8,128)(2,1)}, f32[512,768]{1,0:T(8,128)S(1)}) custom-call(bf16[512,768]{1,0:T(8,128)(2,1)S(1)} %fusion.48.rows_ref, f32[1,3072]{1,0:T(1,128)S(1)} %broadcast_in_dim_reshape.17.bias_ref, bf16[4,112,768]{2,1,0:T(8,128)(2,1)S(1)} %copy-done.10, bf16[4,112,768]{2,1,0:T(8,128)(2,1)S(1)} %copy-done.31, ...), custom_call_target="tpu_custom_call" | custom-call | flops 1207959552 | bytes 3932160 | tf_op jit(solution)/shard_map/pallas_call | solution.py:664
  365.4 3.8 all-to-all-start.6
  384.1 22.7 %all-to-all-done.6 = bf16[32,32,768]{2,1,0:T(8,128)(2,1)} async-done(((bf16[32,32,768]{2,1,0:T(8,128)(2,1)}), bf16[32,32,768]{2,1,0:T(8,128)(2,1)}, u32[]{:S(2)}, u32[]{:S(2)}) %all-to-all-start.6) | async-done | bytes 1572896 | tf_op jit(solution)/shard_map/all_to_all | solution.py:886
  406.8 4.9 fusion.249
  415.4 4.2 all-to-all-start.7
  424.9 10.2 %all-to-all-done.7 = f32[32,3,1024]{2,1,0:T(4,128)} async-done(((f32[32,3,1024]{2,1,0:T(4,128)}), f32[32,3,1024]{2,1,0:T(4,128)}, u32[]{:S(2)}, u32[]{:S(2)}) %all-to-all-start.7) | async-done | bytes 393248 | tf_op jit(solution)/shard_map/all_to_all | solution.py:886
  438.5 8.4 convolution_convert_fusion
  447.0 3.4 all-to-all-start.8
  472.4 15.5 %all-to-all-done.8 = bf16[32,32,768]{2,1,0:T(8,128)(2,1)} async-done(((bf16[32,32,768]{2,1,0:T(8,128)(2,1)}), bf16[32,32,768]{2,1,0:T(8,128)(2,1)}, u32[]{:S(2)}, u32[]{:S(2)}) %all-to-all-start.8) | async-done | bytes 1572896 | tf_op jit(solution)/shard_map/all_to_all | solution.py:892
  494.7 21.4 %shard_map.550 = (f32[512,768]{1,0:T(8,128)}, f32[1,3072]{1,0:T(1,128)S(1)}, bf16[16,112,768]{2,1,0:T(8,128)(2,1)}, bf16[16,96,768]{2,1,0:T(8,128)(2,1)}, bf16[1...) custom-call(bf16[512,768]{1,0:T(8,128)(2,1)} %copy-done.49, bf16[512,768]{1,0:T(8,128)(2,1)} %get-tuple-element.672.grad_ref, ...), custom_call_target="tpu_custom_call" | custom-call | flops 2415919104 | bytes 7864320 | tf_op jit(solution)/shard_map/pallas_call | solution.py:987
  524.3 4.3 multiply_reduce_fusion.3
  538.5 4.4 add_convert_fusion.6
  544.4 4.5 fusion.24
  555.8 18.5 %shard_map.554 = (bf16[512,768]{1,0:T(8,128)(2,1)S(1)}, bf16[512,768]{1,0:T(8,128)(2,1)S(1)}, bf16[512,768]{1,0:T(8,128)(2,1)S(1)}, bf16[512,192]{1,0:T(8,128)(2...) custom-call(s32[1]{0:T(128)S(6)} %copy.555.length, bf16[512,768]{1,0:T(8,128)(2,1)S(1)} %copy-done.25, ...), custom_call_target="tpu_custom_call" | custom-call | flops 5000000000 | bytes 3000000 | tf_op jit(solution)/shard_map/pallas_call | solution.py:551
  593.0 5.2 shard_map.555
  600.6 4.3 add_add_fusion.5.refs_0_
  626.5 3.1 fusion.51.refs_1_
  631.2 22.0 %shard_map.563 = (f32[512,768]{1,0:T(8,128)}, f32[1,3072]{1,0:T(1,128)S(1)}, bf16[16,112,768]{2,1,0:T(8,128)(2,1)}, bf16[16,96,768]{2,1,0:T(8,128)(2,1)}, bf16[1...) custom-call(bf16[512,768]{1,0:T(8,128)(2,1)} %shard_map.515.rows_ref, bf16[512,768]{1,0:T(8,128)(2,1)} %shard_map.561.grad_ref, ...), custom_call_target="tpu_custom_call" | custom-call | flops 2415919104 | bytes 7864320 | tf_op jit(solution)/shard_map/pallas_call | solution.py:987
  674.4 3.6 fusion.234
  689.9 18.6 %shard_map.568 = (bf16[512,768]{1,0:T(8,128)(2,1)S(1)}, bf16[512,768]{1,0:T(8,128)(2,1)S(1)}, bf16[512,768]{1,0:T(8,128)(2,1)S(1)}, bf16[512,192]{1,0:T(8,128)(2...) custom-call(s32[1]{0:T(128)S(6)} %copy.555.length, bf16[512,768]{1,0:T(8,128)(2,1)S(1)} %copy-done.98, ...), custom_call_target="tpu_custom_call" | custom-call | flops 5000000000 | bytes 3000000 | tf_op jit(solution)/shard_map/pallas_call | solution.py:551
  719.3 3.2 fusion.80
  726.2 4.4 add_convert_fusion.4
  731.8 4.8 fusion.22
  736.7 5.8 add_add_fusion.4.refs_0_
  742.4 5.1 shard_map.573
  764.8 4.1 shard_map.579
  780.7 4.0 all-to-all-start.9
  800.7 9.2 collective-permute-done.62.refs_0_
  810.0 3.1 add_convert_fusion.15
  822.3 4.9 fusion.18
  827.3 9.3 convolution_add_fusion
  837.4 4.2 multiply_reduce_fusion
  857.6 5.0 collective-permute-done.68.refs_0_
  864.6 12.2 %collective-permute-done.67.refs_0_ = bf16[2,112,768]{2,1,0:T(8,128)(2,1)} collective-permute-done((bf16[2,112,768]{2,1,0:T(8,128)(2,1)}, bf16[2,112,768]{2,1,0:T(8,128)(2,1)}, u32[]{:S(2)}, u32[]{:S(2)}) %collective-permute-start.67) | collective-permute-done | bytes 344096 | tf_op jit(solution)/shard_map/ppermute | solution.py:193
  877.9 4.0 collective-permute-done.72.refs_0_
  889.5 7.2 collective-permute-done.73
  904.4 5.9 collective-permute-done.78.refs_0_
  914.9 4.3 collective-permute-done.84.refs_0_
  953.1 4.7 add_multiply_fusion.2
  959.7 6.1 add_multiply_fusion.1
  968.4 7.6 add_multiply_fusion
  (1572 shorter events, 479.6 us)
Async XLA Ops:
  2.8 17.9 %collective-permute-start = (bf16[1,528,128]{2,1,0:T(8,128)(2,1)S(1)}, bf16[1,528,128]{2,1,0:T(8,128)(2,1)S(1)}, u32[]{:S(2)}, u32[]{:S(2)}) collective-permute-start(bf16[1,528,128]{2,1,0:T(8,128)(2,1)S(1)} %maximum_bitcast_fusion.6), channel_id=1, source_target_pairs={{0,4},{4,0},{8,12},{12,8},{16,20},{20,16},{24,28},{28,24},{1,5},{5... | collective-permute-start | bytes 405512 | tf_op jit(solution)/shard_map/ppermute | solution.py:193
  8.5 22.0 %collective-permute-start.1 = (bf16[1,96,1536]{2,1,0:T(8,128)(2,1)S(1)}, bf16[1,96,1536]{2,1,0:T(8,128)(2,1)S(1)}, u32[]{:S(2)}, u32[]{:S(2)}) collective-permute-start(bf16[1,96,1536]{2,1,0:T(8,128)(2,1)S(1)} %get-tuple-element.710), channel_id=1, source_target_pairs={{0,16},{4,20},{8,24},{12,28},{16,0},{20,4},{24,8},{28,12},{1,17},{... | collective-permute-start | bytes 884744 | tf_op jit(solution)/shard_map/ppermute | solution.py:193
  30.6 26.7 %collective-permute-start.4 = (bf16[2,96,1536]{2,1,0:T(8,128)(2,1)S(1)}, bf16[2,96,1536]{2,1,0:T(8,128)(2,1)S(1)}, u32[]{:S(2)}, u32[]{:S(2)}) collective-permute-start(bf16[2,96,1536]{2,1,0:T(8,128)(2,1)S(1)} %pad_maximum_fusion.9.refs_1_), channel_id=1, source_target_pairs={{0,8},{4,12},{8,0},{12,4},{16,24},{20,28},{24,16},{28,20},{1,9},{5... | collective-permute-start | bytes 1769480 | tf_op jit(solution)/shard_map/ppermute | solution.py:193
  30.9 18.8 %all-to-all-start.4 = ((s32[32,1,128]{2,1,0:T(1,128)}), s32[32,1,128]{2,1,0:T(1,128)S(1)}, u32[]{:S(2)}, u32[]{:S(2)}) async-start(s32[32,1,128]{2,1,0:T(1,128)} %bitcast.511), calls=%async_computation.4 | async-start | bytes 32768 | tf_op jit(solution)/shard_map/all_to_all | solution.py:892
  35.9 24.3 %collective-permute-start.3 = (bf16[4,528,128]{2,1,0:T(8,128)(2,1)S(1)}, bf16[4,528,128]{2,1,0:T(8,128)(2,1)S(1)}, u32[]{:S(2)}, u32[]{:S(2)}) collective-permute-start(bf16[4,528,128]{2,1,0:T(8,128)(2,1)S(1)} %pad_maximum_fusion.13.refs_2_), channel_id=1, source_target_pairs={{0,8},{4,12},{8,0},{12,4},{16,24},{20,28},{24,16},{28,20},{1,9},{5... | collective-permute-start | bytes 1622024 | tf_op jit(solution)/shard_map/ppermute | solution.py:193
  63.2 16.6 %collective-permute-start.5 = (bf16[8,528,128]{2,1,0:T(8,128)(2,1)}, bf16[8,528,128]{2,1,0:T(8,128)(2,1)S(1)}, u32[]{:S(2)}, u32[]{:S(2)}) collective-permute-start(bf16[8,528,128]{2,1,0:T(8,128)(2,1)} %pad_maximum_fusion.6.refs_1_.own_ref), channel_id=1, source_target_pairs={{0,1},{1,0},{2,3},{3,2},{4,5},{5,4},{6,7},{7,6},{8,9},{9,8},{10,11... | collective-permute-start | bytes 3244040 | tf_op jit(solution)/shard_map/ppermute | solution.py:193
  63.2 49.9 %all-to-all-start.5 = ((bf16[32,32,768]{2,1,0:T(8,128)(2,1)}), bf16[32,32,768]{2,1,0:T(8,128)(2,1)}, u32[]{:S(2)}, u32[]{:S(2)}) async-start(bf16[32,32,768]{2,1,0:T(8,128)(2,1)} %bitcast.15), calls=%async_computation.5 | async-start | bytes 3145728 | tf_op jit(solution)/shard_map/all_to_all | solution.py:892
  75.1 41.6 %collective-permute-start.7 = (bf16[4,96,1536]{2,1,0:T(8,128)(2,1)}, bf16[4,96,1536]{2,1,0:T(8,128)(2,1)}, u32[]{:S(2)}, u32[]{:S(2)}) collective-permute-start(bf16[4,96,1536]{2,1,0:T(8,128)(2,1)} %pad_maximum_fusion.3.refs_1_), channel_id=1, source_target_pairs={{0,4},{4,0},{8,12},{12,8},{16,20},{20,16},{24,28},{28,24},{1,5},{5... | collective-permute-start | bytes 3538952 | tf_op jit(solution)/shard_map/ppermute | solution.py:193
  76.8 52.3 %collective-permute-start.9 = (bf16[1,96,768]{2,1,0:T(8,128)(2,1)}, bf16[1,96,768]{2,1,0:T(8,128)(2,1)}, u32[]{:S(2)}, u32[]{:S(2)}) collective-permute-start(bf16[1,96,768]{2,1,0:T(8,128)(2,1)} %shard_map.490.refs_2_), channel_id=1, source_target_pairs={{0,16},{4,20},{8,24},{12,28},{16,0},{20,4},{24,8},{28,12},{1,17},{... | collective-permute-start | bytes 442376 | tf_op jit(solution)/shard_map/ppermute | solution.py:193
  79.2 51.9 %collective-permute-start.6 = (bf16[1,112,768]{2,1,0:T(8,128)(2,1)}, bf16[1,112,768]{2,1,0:T(8,128)(2,1)}, u32[]{:S(2)}, u32[]{:S(2)}) collective-permute-start(bf16[1,112,768]{2,1,0:T(8,128)(2,1)} %shard_map.489.refs_1_), channel_id=1, source_target_pairs={{0,16},{4,20},{8,24},{12,28},{16,0},{20,4},{24,8},{28,12},{1,17},{... | collective-permute-start | bytes 516104 | tf_op jit(solution)/shard_map/ppermute | solution.py:193
  120.8 32.4 %collective-permute-start.11 = (bf16[8,96,1536]{2,1,0:T(8,128)(2,1)}, bf16[8,96,1536]{2,1,0:T(8,128)(2,1)}, u32[]{:S(2)}, u32[]{:S(2)}) collective-permute-start(bf16[8,96,1536]{2,1,0:T(8,128)(2,1)} %pad_maximum_fusion.refs_1_.own_ref), channel_id=1, source_target_pairs={{0,1},{1,0},{2,3},{3,2},{4,5},{5,4},{6,7},{7,6},{8,9},{9,8},{10,11... | collective-permute-start | bytes 7077896 | tf_op jit(solution)/shard_map/ppermute | solution.py:193
  142.5 38.0 %collective-permute-start.13 = (bf16[4,96,768]{2,1,0:T(8,128)(2,1)S(1)}, bf16[4,96,768]{2,1,0:T(8,128)(2,1)S(1)}, u32[]{:S(2)}, u32[]{:S(2)}) collective-permute-start(bf16[4,96,768]{2,1,0:T(8,128)(2,1)S(1)} %pad_maximum_fusion.10.refs_2_.refs_0_.refs_1_), channel_id=1, source_target_pairs={{0,2},{1,3},{2,0},{3,1},{4,6},{5,7},{6,4},{7,5},{8,10},{9,11},{10,... | collective-permute-start | bytes 1769480 | tf_op jit(solution)/shard_map/ppermute | solution.py:193
  144.0 37.3 %collective-permute-start.14 = (bf16[1,96,1536]{2,1,0:T(8,128)(2,1)}, bf16[1,96,1536]{2,1,0:T(8,128)(2,1)}, u32[]{:S(2)}, u32[]{:S(2)}) collective-permute-start(bf16[1,96,1536]{2,1,0:T(8,128)(2,1)} %shard_map.507), channel_id=1, source_target_pairs={{0,16},{4,20},{8,24},{12,28},{16,0},{20,4},{24,8},{28,12},{1,17},{... | collective-permute-start | bytes 884744 | tf_op jit(solution)/shard_map/ppermute | solution.py:193
  152.4 28.1 %collective-permute-start.12 = (bf16[4,112,768]{2,1,0:T(8,128)(2,1)S(1)}, bf16[4,112,768]{2,1,0:T(8,128)(2,1)S(1)}, u32[]{:S(2)}, u32[]{:S(2)}) collective-permute-start(bf16[4,112,768]{2,1,0:T(8,128)(2,1)S(1)} %copy-done.12), channel_id=1, source_target_pairs={{0,4},{4,0},{8,12},{12,8},{16,20},{20,16},{24,28},{28,24},{1,5},{5... | collective-permute-start | bytes 2064392 | tf_op jit(solution)/shard_map/ppermute | solution.py:193
  183.6 16.4 %collective-permute-start.24 = (bf16[4,96,768]{2,1,0:T(8,128)(2,1)S(1)}, bf16[4,96,768]{2,1,0:T(8,128)(2,1)}, u32[]{:S(2)}, u32[]{:S(2)}) collective-permute-start(bf16[4,96,768]{2,1,0:T(8,128)(2,1)S(1)} %copy-done.18), channel_id=1, source_target_pairs={{0,4},{4,0},{8,12},{12,8},{16,20},{20,16},{24,28},{28,24},{1,5},{5... | collective-permute-start | bytes 1769480 | tf_op jit(solution)/shard_map/ppermute | solution.py:193
  184.9 26.0 %collective-permute-start.25 = (bf16[4,96,768]{2,1,0:T(8,128)(2,1)}, bf16[4,96,768]{2,1,0:T(8,128)(2,1)S(1)}, u32[]{:S(2)}, u32[]{:S(2)}) collective-permute-start(bf16[4,96,768]{2,1,0:T(8,128)(2,1)} %shard_map.506.refs_4_.refs_0_), channel_id=1, source_target_pairs={{0,4},{4,0},{8,12},{12,8},{16,20},{20,16},{24,28},{28,24},{1,5},{5... | collective-permute-start | bytes 1769480 | tf_op jit(solution)/shard_map/ppermute | solution.py:193
  185.6 26.1 %collective-permute-start.18 = (bf16[4,112,768]{2,1,0:T(8,128)(2,1)S(1)}, bf16[4,112,768]{2,1,0:T(8,128)(2,1)S(1)}, u32[]{:S(2)}, u32[]{:S(2)}) collective-permute-start(bf16[4,112,768]{2,1,0:T(8,128)(2,1)S(1)} %copy-done.13), channel_id=1, source_target_pairs={{0,2},{1,3},{2,0},{3,1},{4,6},{5,7},{6,4},{7,5},{8,10},{9,11},{10,... | collective-permute-start | bytes 2064392 | tf_op jit(solution)/shard_map/ppermute | solution.py:193
  187.7 29.2 %collective-permute-start.19 = (bf16[4,112,768]{2,1,0:T(8,128)(2,1)}, bf16[4,112,768]{2,1,0:T(8,128)(2,1)S(1)}, u32[]{:S(2)}, u32[]{:S(2)}) collective-permute-start(bf16[4,112,768]{2,1,0:T(8,128)(2,1)} %shard_map.504.refs_2_.refs_0_), channel_id=1, source_target_pairs={{0,2},{1,3},{2,0},{3,1},{4,6},{5,7},{6,4},{7,5},{8,10},{9,11},{10,... | collective-permute-start | bytes 2064392 | tf_op jit(solution)/shard_map/ppermute | solution.py:193
  192.4 19.3 %collective-permute-start.17 = (bf16[1,96,768]{2,1,0:T(8,128)(2,1)}, bf16[1,96,768]{2,1,0:T(8,128)(2,1)}, u32[]{:S(2)}, u32[]{:S(2)}) collective-permute-start(bf16[1,96,768]{2,1,0:T(8,128)(2,1)} %shard_map.513), channel_id=1, source_target_pairs={{0,16},{4,20},{8,24},{12,28},{16,0},{20,4},{24,8},{28,12},{1,17},{... | collective-permute-start | bytes 442376 | tf_op jit(solution)/shard_map/ppermute | solution.py:193
  199.9 26.3 %collective-permute-start.15 = (bf16[2,96,1536]{2,1,0:T(8,128)(2,1)}, bf16[2,96,1536]{2,1,0:T(8,128)(2,1)}, u32[]{:S(2)}, u32[]{:S(2)}) collective-permute-start(bf16[2,96,1536]{2,1,0:T(8,128)(2,1)} %pad_maximum_fusion.11.refs_5_.refs_1_), channel_id=1, source_target_pairs={{0,8},{4,12},{8,0},{12,4},{16,24},{20,28},{24,16},{28,20},{1,9},{5... | collective-permute-start | bytes 1769480 | tf_op jit(solution)/shard_map/ppermute | solution.py:193
  210.9 15.9 %collective-permute-start.27 = (bf16[4,96,768]{2,1,0:T(8,128)(2,1)}, bf16[4,96,768]{2,1,0:T(8,128)(2,1)}, u32[]{:S(2)}, u32[]{:S(2)}) collective-permute-start(bf16[4,96,768]{2,1,0:T(8,128)(2,1)} %shard_map.521.refs_9_), channel_id=1, source_target_pairs={{0,1},{1,0},{2,3},{3,2},{4,5},{5,4},{6,7},{7,6},{8,9},{9,8},{10,11... | collective-permute-start | bytes 1769480 | tf_op jit(solution)/shard_map/ppermute | solution.py:193
  233.1 28.7 %collective-permute-start.32 = (bf16[4,96,1536]{2,1,0:T(8,128)(2,1)}, bf16[4,96,1536]{2,1,0:T(8,128)(2,1)}, u32[]{:S(2)}, u32[]{:S(2)}) collective-permute-start(bf16[4,96,1536]{2,1,0:T(8,128)(2,1)} %pad_maximum_fusion.4.refs_1_), channel_id=1, source_target_pairs={{0,4},{4,0},{8,12},{12,8},{16,20},{20,16},{24,28},{28,24},{1,5},{5... | collective-permute-start | bytes 3538952 | tf_op jit(solution)/shard_map/ppermute | solution.py:193
  265.0 24.6 %collective-permute-start.33 = (bf16[8,96,1536]{2,1,0:T(8,128)(2,1)}, bf16[8,96,1536]{2,1,0:T(8,128)(2,1)}, u32[]{:S(2)}, u32[]{:S(2)}) collective-permute-start(bf16[8,96,1536]{2,1,0:T(8,128)(2,1)} %pad_maximum_fusion.1.refs_3_.own_ref), channel_id=1, source_target_pairs={{0,1},{1,0},{2,3},{3,2},{4,5},{5,4},{6,7},{7,6},{8,9},{9,8},{10,11... | collective-permute-start | bytes 7077896 | tf_op jit(solution)/shard_map/ppermute | solution.py:193
  265.4 16.8 %collective-permute-start.30 = (bf16[2,112,768]{2,1,0:T(8,128)(2,1)}, bf16[2,112,768]{2,1,0:T(8,128)(2,1)S(1)}, u32[]{:S(2)}, u32[]{:S(2)}) collective-permute-start(bf16[2,112,768]{2,1,0:T(8,128)(2,1)} %pad_maximum_fusion.17.refs_2_), channel_id=1, source_target_pairs={{0,8},{4,12},{8,0},{12,4},{16,24},{20,28},{24,16},{28,20},{1,9},{5... | collective-permute-start | bytes 1032200 | tf_op jit(solution)/shard_map/ppermute | solution.py:193
  277.6 19.3 %collective-permute-start.35 = (bf16[4,96,768]{2,1,0:T(8,128)(2,1)S(1)}, bf16[4,96,768]{2,1,0:T(8,128)(2,1)S(1)}, u32[]{:S(2)}, u32[]{:S(2)}) collective-permute-start(bf16[4,96,768]{2,1,0:T(8,128)(2,1)S(1)} %pad_maximum_fusion.12.refs_2_.refs_0_), channel_id=1, source_target_pairs={{0,2},{1,3},{2,0},{3,1},{4,6},{5,7},{6,4},{7,5},{8,10},{9,11},{10,... | collective-permute-start | bytes 1769480 | tf_op jit(solution)/shard_map/ppermute | solution.py:193
  284.0 17.1 %collective-permute-start.34 = (bf16[4,112,768]{2,1,0:T(8,128)(2,1)S(1)}, bf16[4,112,768]{2,1,0:T(8,128)(2,1)S(1)}, u32[]{:S(2)}, u32[]{:S(2)}) collective-permute-start(bf16[4,112,768]{2,1,0:T(8,128)(2,1)S(1)} %pad_maximum_fusion.8.refs_1_.refs_0_), channel_id=1, source_target_pairs={{0,4},{4,0},{8,12},{12,8},{16,20},{20,16},{24,28},{28,24},{1,5},{5... | collective-permute-start | bytes 2064392 | tf_op jit(solution)/shard_map/ppermute | solution.py:193
  302.0 27.7 %collective-permute-start.42 = (bf16[4,96,768]{2,1,0:T(8,128)(2,1)S(1)}, bf16[4,96,768]{2,1,0:T(8,128)(2,1)}, u32[]{:S(2)}, u32[]{:S(2)}) collective-permute-start(bf16[4,96,768]{2,1,0:T(8,128)(2,1)S(1)} %copy-done.21), channel_id=1, source_target_pairs={{0,4},{4,0},{8,12},{12,8},{16,20},{20,16},{24,28},{28,24},{1,5},{5... | collective-permute-start | bytes 1769480 | tf_op jit(solution)/shard_map/ppermute | solution.py:193
  303.8 25.9 %collective-permute-start.43 = (bf16[4,96,768]{2,1,0:T(8,128)(2,1)}, bf16[4,96,768]{2,1,0:T(8,128)(2,1)}, u32[]{:S(2)}, u32[]{:S(2)}) collective-permute-start(bf16[4,96,768]{2,1,0:T(8,128)(2,1)} %shard_map.533.refs_4_.refs_0_), channel_id=1, source_target_pairs={{0,4},{4,0},{8,12},{12,8},{16,20},{20,16},{24,28},{28,24},{1,5},{5... | collective-permute-start | bytes 1769480 | tf_op jit(solution)/shard_map/ppermute | solution.py:193
  304.0 36.2 %collective-permute-start.36 = (bf16[4,112,768]{2,1,0:T(8,128)(2,1)S(1)}, bf16[4,112,768]{2,1,0:T(8,128)(2,1)}, u32[]{:S(2)}, u32[]{:S(2)}) collective-permute-start(bf16[4,112,768]{2,1,0:T(8,128)(2,1)S(1)} %copy-done.9), channel_id=1, source_target_pairs={{0,2},{1,3},{2,0},{3,1},{4,6},{5,7},{6,4},{7,5},{8,10},{9,11},{10,... | collective-permute-start | bytes 2064392 | tf_op jit(solution)/shard_map/ppermute | solution.py:193
  307.1 32.6 %collective-permute-start.37 = (bf16[4,112,768]{2,1,0:T(8,128)(2,1)S(1)}, bf16[4,112,768]{2,1,0:T(8,128)(2,1)}, u32[]{:S(2)}, u32[]{:S(2)}) collective-permute-start(bf16[4,112,768]{2,1,0:T(8,128)(2,1)S(1)} %copy-done.30), channel_id=1, source_target_pairs={{0,2},{1,3},{2,0},{3,1},{4,6},{5,7},{6,4},{7,5},{8,10},{9,11},{10,... | collective-permute-start | bytes 2064392 | tf_op jit(solution)/shard_map/ppermute | solution.py:193
  365.4 41.3 %all-to-all-start.6 = ((bf16[32,32,768]{2,1,0:T(8,128)(2,1)}), bf16[32,32,768]{2,1,0:T(8,128)(2,1)}, u32[]{:S(2)}, u32[]{:S(2)}) async-start(bf16[32,32,768]{2,1,0:T(8,128)(2,1)} %broadcast_in_dim.303), calls=%async_computation.6 | async-start | bytes 3145728 | tf_op jit(solution)/shard_map/all_to_all | solution.py:886
  415.4 19.7 %all-to-all-start.7 = ((f32[32,3,1024]{2,1,0:T(4,128)}), f32[32,3,1024]{2,1,0:T(4,128)}, u32[]{:S(2)}, u32[]{:S(2)}) async-start(f32[32,3,1024]{2,1,0:T(4,128)} %broadcast_in_dim.305), calls=%async_computation.7 | async-start | bytes 1048576 | tf_op jit(solution)/shard_map/all_to_all | solution.py:886
  447.0 40.9 %all-to-all-start.8 = ((bf16[32,32,768]{2,1,0:T(8,128)(2,1)}), bf16[32,32,768]{2,1,0:T(8,128)(2,1)}, u32[]{:S(2)}, u32[]{:S(2)}) async-start(bf16[32,32,768]{2,1,0:T(8,128)(2,1)} %bitcast.504), calls=%async_computation.8 | async-start | bytes 3145728 | tf_op jit(solution)/shard_map/all_to_all | solution.py:892
  516.2 22.4 %collective-permute-start.49 = (bf16[16,96,768]{2,1,0:T(8,128)(2,1)}, bf16[16,96,768]{2,1,0:T(8,128)(2,1)}, u32[]{:S(2)}, u32[]{:S(2)}) collective-permute-start(bf16[16,96,768]{2,1,0:T(8,128)(2,1)} %get-tuple-element.378), channel_id=1, source_target_pairs={{0,1},{1,0},{2,3},{3,2},{4,5},{5,4},{6,7},{7,6},{8,9},{9,8},{10,11... | collective-permute-start | bytes 7077896 | tf_op jit(solution)/shard_map/ppermute | solution.py:193
  516.3 28.2 %collective-permute-start.48 = (bf16[16,112,768]{2,1,0:T(8,128)(2,1)}, bf16[16,112,768]{2,1,0:T(8,128)(2,1)}, u32[]{:S(2)}, u32[]{:S(2)}) collective-permute-start(bf16[16,112,768]{2,1,0:T(8,128)(2,1)} %get-tuple-element.376), channel_id=1, source_target_pairs={{0,1},{1,0},{2,3},{3,2},{4,5},{5,4},{6,7},{7,6},{8,9},{9,8},{10,11... | collective-permute-start | bytes 8257544 | tf_op jit(solution)/shard_map/ppermute | solution.py:193
  543.0 67.3 %collective-permute-start.51 = (bf16[2,4,96,768]{3,2,1,0:T(8,128)(2,1)}, bf16[2,4,96,768]{3,2,1,0:T(8,128)(2,1)}, u32[]{:S(2)}, u32[]{:S(2)}) collective-permute-start(bf16[2,4,96,768]{3,2,1,0:T(8,128)(2,1)} %get-tuple-element.650.refs_2_), channel_id=1, source_target_pairs={{0,4},{4,0},{8,12},{12,8},{16,20},{20,16},{24,28},{28,24},{1,5},{5... | collective-permute-start | bytes 3538952 | tf_op jit(solution)/shard_map/ppermute | solution.py:193
  548.9 66.1 %collective-permute-start.50 = (bf16[2,4,112,768]{3,2,1,0:T(8,128)(2,1)}, bf16[2,4,112,768]{3,2,1,0:T(8,128)(2,1)}, u32[]{:S(2)}, u32[]{:S(2)}) collective-permute-start(bf16[2,4,112,768]{3,2,1,0:T(8,128)(2,1)} %get-tuple-element.660.refs_1_), channel_id=1, source_target_pairs={{0,2},{1,3},{2,0},{3,1},{4,6},{5,7},{6,4},{7,5},{8,10},{9,11},{10,... | collective-permute-start | bytes 4128776 | tf_op jit(solution)/shard_map/ppermute | solution.py:193
  599.0 27.5 %collective-permute-start.52 = (bf16[8,104,1536]{2,1,0:T(8,128)(2,1)}, bf16[8,104,1536]{2,1,0:T(8,128)(2,1)}, u32[]{:S(2)}, u32[]{:S(2)}) collective-permute-start(bf16[8,104,1536]{2,1,0:T(8,128)(2,1)} %pad_dynamic-update-slice_fusion.3.refs_1_), channel_id=1, source_target_pairs={{0,1},{1,0},{2,3},{3,2},{4,5},{5,4},{6,7},{7,6},{8,9},{9,8},{10,11... | collective-permute-start | bytes 7667720 | tf_op jit(solution)/shard_map/ppermute | solution.py:193
  614.1 49.4 %collective-permute-start.54 = (bf16[4,96,768]{2,1,0:T(8,128)(2,1)}, bf16[4,96,768]{2,1,0:T(8,128)(2,1)}, u32[]{:S(2)}, u32[]{:S(2)}) collective-permute-start(bf16[4,96,768]{2,1,0:T(8,128)(2,1)} %get-tuple-element.666.refs_2_), channel_id=1, source_target_pairs={{0,2},{1,3},{2,0},{3,1},{4,6},{5,7},{6,4},{7,5},{8,10},{9,11},{10,... | collective-permute-start | bytes 1769480 | tf_op jit(solution)/shard_map/ppermute | solution.py:193
  618.4 50.3 %collective-permute-start.53 = (bf16[4,112,768]{2,1,0:T(8,128)(2,1)}, bf16[4,112,768]{2,1,0:T(8,128)(2,1)}, u32[]{:S(2)}, u32[]{:S(2)}) collective-permute-start(bf16[4,112,768]{2,1,0:T(8,128)(2,1)} %get-tuple-element.658.refs_1_), channel_id=1, source_target_pairs={{0,4},{4,0},{8,12},{12,8},{16,20},{20,16},{24,28},{28,24},{1,5},{5... | collective-permute-start | bytes 2064392 | tf_op jit(solution)/shard_map/ppermute | solution.py:193
  629.6 50.4 %collective-permute-start.55 = (bf16[2,2,104,1536]{3,2,1,0:T(8,128)(2,1)}, bf16[2,2,104,1536]{3,2,1,0:T(8,128)(2,1)}, u32[]{:S(2)}, u32[]{:S(2)}) collective-permute-start(bf16[2,2,104,1536]{3,2,1,0:T(8,128)(2,1)} %fusion.51.refs_1_), channel_id=1, source_target_pairs={{0,4},{4,0},{8,12},{12,8},{16,20},{20,16},{24,28},{28,24},{1,5},{5... | collective-permute-start | bytes 3833864 | tf_op jit(solution)/shard_map/ppermute | solution.py:193
  665.6 84.1 %collective-permute-start.60 = (bf16[2,96,768]{2,1,0:T(8,128)(2,1)}, bf16[2,96,768]{2,1,0:T(8,128)(2,1)}, u32[]{:S(2)}, u32[]{:S(2)}) collective-permute-start(bf16[2,96,768]{2,1,0:T(8,128)(2,1)} %get-tuple-element.688.refs_2_), channel_id=1, source_target_pairs={{0,8},{4,12},{8,0},{12,4},{16,24},{20,28},{24,16},{28,20},{1,9},{5... | collective-permute-start | bytes 884744 | tf_op jit(solution)/shard_map/ppermute | solution.py:193
  671.8 82.6 %collective-permute-start.59 = (bf16[2,112,768]{2,1,0:T(8,128)(2,1)}, bf16[2,112,768]{2,1,0:T(8,128)(2,1)}, u32[]{:S(2)}, u32[]{:S(2)}) collective-permute-start(bf16[2,112,768]{2,1,0:T(8,128)(2,1)} %get-tuple-element.680.refs_1_), channel_id=1, source_target_pairs={{0,8},{4,12},{8,0},{12,4},{16,24},{20,28},{24,16},{28,20},{1,9},{5... | collective-permute-start | bytes 1032200 | tf_op jit(solution)/shard_map/ppermute | solution.py:193
  673.9 52.4 %collective-permute-start.57 = (bf16[16,96,768]{2,1,0:T(8,128)(2,1)}, bf16[16,96,768]{2,1,0:T(8,128)(2,1)}, u32[]{:S(2)}, u32[]{:S(2)}) collective-permute-start(bf16[16,96,768]{2,1,0:T(8,128)(2,1)} %get-tuple-element.404), channel_id=1, source_target_pairs={{0,1},{1,0},{2,3},{3,2},{4,5},{5,4},{6,7},{7,6},{8,9},{9,8},{10,11... | collective-permute-start | bytes 7077896 | tf_op jit(solution)/shard_map/ppermute | solution.py:193
  673.9 58.0 %collective-permute-start.56 = (bf16[16,112,768]{2,1,0:T(8,128)(2,1)}, bf16[16,112,768]{2,1,0:T(8,128)(2,1)}, u32[]{:S(2)}, u32[]{:S(2)}) collective-permute-start(bf16[16,112,768]{2,1,0:T(8,128)(2,1)} %get-tuple-element.402), channel_id=1, source_target_pairs={{0,1},{1,0},{2,3},{3,2},{4,5},{5,4},{6,7},{7,6},{8,9},{9,8},{10,11... | collective-permute-start | bytes 8257544 | tf_op jit(solution)/shard_map/ppermute | solution.py:193
  683.4 39.1 %collective-permute-start.58 = (bf16[2,104,1536]{2,1,0:T(8,128)(2,1)}, bf16[2,104,1536]{2,1,0:T(8,128)(2,1)}, u32[]{:S(2)}, u32[]{:S(2)}) collective-permute-start(bf16[2,104,1536]{2,1,0:T(8,128)(2,1)} %fusion.98.refs_3_), channel_id=1, source_target_pairs={{0,8},{4,12},{8,0},{12,4},{16,24},{20,28},{24,16},{28,20},{1,9},{5... | collective-permute-start | bytes 1916936 | tf_op jit(solution)/shard_map/ppermute | solution.py:193
  725.4 31.6 %collective-permute-start.61 = (bf16[104,1536]{1,0:T(8,128)(2,1)}, bf16[104,1536]{1,0:T(8,128)(2,1)}, u32[]{:S(2)}, u32[]{:S(2)}) collective-permute-start(bf16[104,1536]{1,0:T(8,128)(2,1)} %fusion.127.refs_3_), channel_id=1, source_target_pairs={{0,16},{4,20},{8,24},{12,28},{16,0},{20,4},{24,8},{28,12},{1,17},{... | collective-permute-start | bytes 958472 | tf_op jit(solution)/shard_map/ppermute | solution.py:193
  730.7 83.8 %collective-permute-start.66 = (bf16[2,4,96,768]{3,2,1,0:T(8,128)(2,1)}, bf16[2,4,96,768]{3,2,1,0:T(8,128)(2,1)}, u32[]{:S(2)}, u32[]{:S(2)}) collective-permute-start(bf16[2,4,96,768]{3,2,1,0:T(8,128)(2,1)} %get-tuple-element.648.refs_2_), channel_id=1, source_target_pairs={{0,4},{4,0},{8,12},{12,8},{16,20},{20,16},{24,28},{28,24},{1,5},{5... | collective-permute-start | bytes 3538952 | tf_op jit(solution)/shard_map/ppermute | solution.py:193
  752.3 23.0 %collective-permute-start.75 = (bf16[1,96,768]{2,1,0:T(8,128)(2,1)}, bf16[1,96,768]{2,1,0:T(8,128)(2,1)}, u32[]{:S(2)}, u32[]{:S(2)}) collective-permute-start(bf16[1,96,768]{2,1,0:T(8,128)(2,1)} %add_convert_fusion.33.refs_2_), channel_id=1, source_target_pairs={{0,16},{4,20},{8,24},{12,28},{16,0},{20,4},{24,8},{28,12},{1,17},{... | collective-permute-start | bytes 442376 | tf_op jit(solution)/shard_map/ppermute | solution.py:193
  756.1 20.3 %collective-permute-start.74 = (bf16[1,112,768]{2,1,0:T(8,128)(2,1)}, bf16[1,112,768]{2,1,0:T(8,128)(2,1)}, u32[]{:S(2)}, u32[]{:S(2)}) collective-permute-start(bf16[1,112,768]{2,1,0:T(8,128)(2,1)} %add_convert_fusion.29.refs_1_), channel_id=1, source_target_pairs={{0,16},{4,20},{8,24},{12,28},{16,0},{20,4},{24,8},{28,12},{1,17},{... | collective-permute-start | bytes 516104 | tf_op jit(solution)/shard_map/ppermute | solution.py:193
  758.9 18.6 %collective-permute-start.81 = (bf16[104,1536]{1,0:T(8,128)(2,1)}, bf16[104,1536]{1,0:T(8,128)(2,1)}, u32[]{:S(2)}, u32[]{:S(2)}) collective-permute-start(bf16[104,1536]{1,0:T(8,128)(2,1)} %fusion.103.refs_3_), channel_id=1, source_target_pairs={{0,2},{1,3},{2,0},{3,1},{4,6},{5,7},{6,4},{7,5},{8,10},{9,11},{10,... | collective-permute-start | bytes 958472 | tf_op jit(solution)/shard_map/ppermute | solution.py:193
  759.9 50.1 %collective-permute-start.62 = (bf16[2,4,112,768]{3,2,1,0:T(8,128)(2,1)}, bf16[2,4,112,768]{3,2,1,0:T(8,128)(2,1)}, u32[]{:S(2)}, u32[]{:S(2)}) collective-permute-start(bf16[2,4,112,768]{3,2,1,0:T(8,128)(2,1)} %get-tuple-element.654.refs_1_), channel_id=1, source_target_pairs={{0,2},{1,3},{2,0},{3,1},{4,6},{5,7},{6,4},{7,5},{8,10},{9,11},{10,... | collective-permute-start | bytes 4128776 | tf_op jit(solution)/shard_map/ppermute | solution.py:193
  780.7 41.6 %all-to-all-start.9 = ((bf16[32,32,768]{2,1,0:T(8,128)(2,1)}), bf16[32,32,768]{2,1,0:T(8,128)(2,1)}, u32[]{:S(2)}, u32[]{:S(2)}) async-start(bf16[32,32,768]{2,1,0:T(8,128)(2,1)} %bitcast.91), calls=%async_computation.9 | async-start | bytes 3145728 | tf_op jit(solution)/shard_map/all_to_all | solution.py:892
  791.4 50.2 %collective-permute-start.65 = (bf16[2,2,104,1536]{3,2,1,0:T(8,128)(2,1)}, bf16[2,2,104,1536]{3,2,1,0:T(8,128)(2,1)}, u32[]{:S(2)}, u32[]{:S(2)}) collective-permute-start(bf16[2,2,104,1536]{3,2,1,0:T(8,128)(2,1)} %fusion.52.refs_1_), channel_id=1, source_target_pairs={{0,4},{4,0},{8,12},{12,8},{16,20},{20,16},{24,28},{28,24},{1,5},{5... | collective-permute-start | bytes 3833864 | tf_op jit(solution)/shard_map/ppermute | solution.py:193
  800.7 52.5 %collective-permute-start.69 = (bf16[8,384,128]{2,1,0:T(8,128)(2,1)}, bf16[8,384,128]{2,1,0:T(8,128)(2,1)S(1)}, u32[]{:S(2)}, u32[]{:S(2)}) collective-permute-start(bf16[8,384,128]{2,1,0:T(8,128)(2,1)} %get-tuple-element.676.refs_1_), channel_id=1, source_target_pairs={{0,1},{1,0},{2,3},{3,2},{4,5},{5,4},{6,7},{7,6},{8,9},{9,8},{10,11... | collective-permute-start | bytes 2359304 | tf_op jit(solution)/shard_map/ppermute | solution.py:193
  813.1 33.7 %collective-permute-start.64 = (bf16[4,112,768]{2,1,0:T(8,128)(2,1)}, bf16[4,112,768]{2,1,0:T(8,128)(2,1)}, u32[]{:S(2)}, u32[]{:S(2)}) collective-permute-start(bf16[4,112,768]{2,1,0:T(8,128)(2,1)} %get-tuple-element.652.refs_1_), channel_id=1, source_target_pairs={{0,4},{4,0},{8,12},{12,8},{16,20},{20,16},{24,28},{28,24},{1,5},{5... | collective-permute-start | bytes 2064392 | tf_op jit(solution)/shard_map/ppermute | solution.py:193
  817.4 32.9 %collective-permute-start.70 = (bf16[4,96,768]{2,1,0:T(8,128)(2,1)}, bf16[4,96,768]{2,1,0:T(8,128)(2,1)}, u32[]{:S(2)}, u32[]{:S(2)}) collective-permute-start(bf16[4,96,768]{2,1,0:T(8,128)(2,1)} %get-tuple-element.664.refs_1_), channel_id=1, source_target_pairs={{0,2},{1,3},{2,0},{3,1},{4,6},{5,7},{6,4},{7,5},{8,10},{9,11},{10,... | collective-permute-start | bytes 1769480 | tf_op jit(solution)/shard_map/ppermute | solution.py:193
  845.0 17.6 %collective-permute-start.68 = (bf16[2,104,1536]{2,1,0:T(8,128)(2,1)}, bf16[2,104,1536]{2,1,0:T(8,128)(2,1)}, u32[]{:S(2)}, u32[]{:S(2)}) collective-permute-start(bf16[2,104,1536]{2,1,0:T(8,128)(2,1)} %fusion.99.refs_1_), channel_id=1, source_target_pairs={{0,8},{4,12},{8,0},{12,4},{16,24},{20,28},{24,16},{28,20},{1,9},{5... | collective-permute-start | bytes 1916936 | tf_op jit(solution)/shard_map/ppermute | solution.py:193
  849.0 27.9 %collective-permute-start.67 = (bf16[2,112,768]{2,1,0:T(8,128)(2,1)}, bf16[2,112,768]{2,1,0:T(8,128)(2,1)}, u32[]{:S(2)}, u32[]{:S(2)}) collective-permute-start(bf16[2,112,768]{2,1,0:T(8,128)(2,1)} %get-tuple-element.678.refs_1_), channel_id=1, source_target_pairs={{0,8},{4,12},{8,0},{12,4},{16,24},{20,28},{24,16},{28,20},{1,9},{5... | collective-permute-start | bytes 1032200 | tf_op jit(solution)/shard_map/ppermute | solution.py:193
  852.5 29.4 %collective-permute-start.72 = (bf16[2,96,768]{2,1,0:T(8,128)(2,1)}, bf16[2,96,768]{2,1,0:T(8,128)(2,1)}, u32[]{:S(2)}, u32[]{:S(2)}) collective-permute-start(bf16[2,96,768]{2,1,0:T(8,128)(2,1)} %get-tuple-element.686.refs_1_), channel_id=1, source_target_pairs={{0,8},{4,12},{8,0},{12,4},{16,24},{20,28},{24,16},{28,20},{1,9},{5... | collective-permute-start | bytes 884744 | tf_op jit(solution)/shard_map/ppermute | solution.py:193
  855.3 27.6 %collective-permute-start.77 = (bf16[2,2,384,128]{3,2,1,0:T(8,128)(2,1)S(1)}, bf16[2,2,384,128]{3,2,1,0:T(8,128)(2,1)S(1)}, u32[]{:S(2)}, u32[]{:S(2)}) collective-permute-start(bf16[2,2,384,128]{3,2,1,0:T(8,128)(2,1)S(1)} %fusion.122.refs_1_), channel_id=1, source_target_pairs={{0,4},{4,0},{8,12},{12,8},{16,20},{20,16},{24,28},{28,24},{1,5},{5... | collective-permute-start | bytes 1179656 | tf_op jit(solution)/shard_map/ppermute | solution.py:193
  864.5 34.4 %collective-permute-start.76 = (bf16[104,1536]{1,0:T(8,128)(2,1)}, bf16[104,1536]{1,0:T(8,128)(2,1)S(1)}, u32[]{:S(2)}, u32[]{:S(2)}) collective-permute-start(bf16[104,1536]{1,0:T(8,128)(2,1)} %fusion.129.refs_1_), channel_id=1, source_target_pairs={{0,16},{4,20},{8,24},{12,28},{16,0},{20,4},{24,8},{28,12},{1,17},{... | collective-permute-start | bytes 958472 | tf_op jit(solution)/shard_map/ppermute | solution.py:193
  877.8 19.9 %collective-permute-start.71 = (bf16[1,112,768]{2,1,0:T(8,128)(2,1)S(1)}, bf16[1,112,768]{2,1,0:T(8,128)(2,1)}, u32[]{:S(2)}, u32[]{:S(2)}) collective-permute-start(bf16[1,112,768]{2,1,0:T(8,128)(2,1)S(1)} %add_convert_fusion.27.refs_1_), channel_id=1, source_target_pairs={{0,16},{4,20},{8,24},{12,28},{16,0},{20,4},{24,8},{28,12},{1,17},{... | collective-permute-start | bytes 516104 | tf_op jit(solution)/shard_map/ppermute | solution.py:193
  885.9 17.4 %collective-permute-start.79 = (bf16[2,384,128]{2,1,0:T(8,128)(2,1)}, bf16[2,384,128]{2,1,0:T(8,128)(2,1)}, u32[]{:S(2)}, u32[]{:S(2)}) collective-permute-start(bf16[2,384,128]{2,1,0:T(8,128)(2,1)} %fusion.135.refs_1_), channel_id=1, source_target_pairs={{0,8},{4,12},{8,0},{12,4},{16,24},{20,28},{24,16},{28,20},{1,9},{5... | collective-permute-start | bytes 589832 | tf_op jit(solution)/shard_map/ppermute | solution.py:193
  (492 other events, 3087.7 us)

commit v6 on v5

--- a/solution.py
+++ b/solution.py
@@ -1013,7 +1013,7 @@
     )
     mid = norm_apply(first, vec[3], vec[4])
     mid_low = hook(mid.astype(jnp.bfloat16))
-    chunks = 4 if width == WIDTH else 1
+    chunks = 2 if width == WIDTH else 1
     hidden, slope, part = ffn_front(mid_low, units, bias_in, chunks, unit_rows)
     last = mid + part + vec[5]
     return (norm_apply(last, vec[6], vec[7]), (first, mid_low, slope, hidden, last))

time: 995 us -> 996 us (level)
  no operation moved by 1% of the time
where the time goes in v6:
time: 996 us; the launch traced here: 982 us
  other arithmetic  228 us (23%)
  waiting for transfers between devices  193 us (19%)
  Pallas kernels  181 us (18%)
  local copies, waits for them, and re-layouts  162 us (16%)
  matrix products  104 us (10%)
  starting transfers between devices  94.4 us (9%)
  between operations  18.3 us (2%)
    ppermute x86, waiting for transfers between devices, hop(): return lax.ppermute(values, axis, pairs)  102 us
    unnamed x916, local copies, waits for them, and re-layouts  100 us
    convert_element_type x37, other arithmetic, add_low(): (kept.astype(jnp.float32) + came.astype(jnp.float32)).astype(jnp.bfloat16)  78.3 us
    ppermute x86, starting transfers between devices, hop(): return lax.ppermute(values, axis, pairs)  62 us
    all_to_all x4, waiting for transfers between devices, trade(): return lax.all_to_all(values, ('dp', 'mp'), 0, 0, tiled=True)  50.4 us
    pallas_call x4, Pallas kernels, ffn_back(): pl.pallas_call(functools.partial(ffn_back_kernel, slot_rows[0] if slot_ro...  47.9 us
    pallas_call x2, Pallas kernels, attend_back(): pl.pallas_call(attend_back_kernel, grid=(HEAD_PAIRS,), in_specs=[pl.Block...  37.1 us
    pallas_call x2, Pallas kernels, attend(): pl.pallas_call(attend_kernel, grid=(HEAD_PAIRS,), in_specs=[pl.BlockSpec(...  33.5 us
  transfers between devices with their start and end apart: 99, of which 33 were waited for; matrix products, arithmetic and copies ran while one was open for 33% of the time, Pallas kernels for 15%

profile of v6, /device:TPU:0, one launch (start us, length us, event | category | flops | bytes accessed | tf_op | source)
XLA Modules:
  0.0 982.3 jit_solution(14005865538277522074)
XLA Ops:
  21.2 4.0 convert_element_type.1022
  25.2 5.3 collective-permute-done.1
  30.9 4.7 all-to-all-start.4
  37.5 12.1 %all-to-all-done.4 = s32[32,1,128]{2,1,0:T(1,128)S(1)} async-done(((s32[32,1,128]{2,1,0:T(1,128)}), s32[32,1,128]{2,1,0:T(1,128)S(1)}, u32[]{:S(2)}, u32[]{:S(2)}) %all-to-all-start.4) | async-done | bytes 16416 | tf_op jit(solution)/shard_map/all_to_all | solution.py:892
  51.2 6.1 fusion.34.refs_1_
  63.2 5.0 all-to-all-start.5
  92.2 20.9 %all-to-all-done.5 = bf16[32,32,768]{2,1,0:T(8,128)(2,1)} async-done(((bf16[32,32,768]{2,1,0:T(8,128)(2,1)}), bf16[32,32,768]{2,1,0:T(8,128)(2,1)}, u32[]{:S(2)}, u32[]{:S(2)}) %all-to-all-start.5) | async-done | bytes 1572896 | tf_op jit(solution)/shard_map/all_to_all | solution.py:892
  113.1 3.6 fusion.27
  122.2 3.6 shard_map.493
  137.2 3.6 collective-permute-done.10.refs_0_
  144.2 4.5 collective-permute-done.8.refs_0_
  161.8 16.6 %shard_map.502 = (bf16[512,768]{1,0:T(8,128)(2,1)S(1)}, bf16[512,192]{1,0:T(8,128)(2,1)S(1)}, f32[6,512,2]{2,1,0:T(8,128)S(1)}) custom-call(s32[1]{0:T(128)S(6)} %copy.555.length, bf16[512,768]{1,0:T(8,128)(2,1)S(1)} %fusion.36.qt, bf16[512,768]{1,0:T(8,128)(2,1)S(1)} %slice.1146.kt, bf16[512,768]{1,0:T(8,128)(2,1)S(1)} %add_convert_fusion.9.vt, ...), custom_call_target="tpu_custom_call" | custom-call | flops 4000000000 | bytes 2000000 | tf_op jit(solution)/shard_map/pallas_call | solution.py:527
  188.4 4.0 fusion.246
  196.3 3.7 collective-permute-done.24.refs_0_
  200.2 10.7 %collective-permute-done.25.refs_0_ = bf16[4,96,768]{2,1,0:T(8,128)(2,1)S(1)} collective-permute-done((bf16[4,96,768]{2,1,0:T(8,128)(2,1)}, bf16[4,96,768]{2,1,0:T(8,128)(2,1)S(1)}, u32[]{:S(2)}, u32[]{:S(2)}) %collective-permute-start.25) | collective-permute-done | bytes 589856 | tf_op jit(solution)/shard_map/ppermute | solution.py:193
  213.8 3.2 collective-permute-done.19.refs_0_
  218.0 8.2 collective-permute-done.16.refs_0_
  237.5 13.2 %shard_map.524 = (bf16[512,3072]{1,0:T(8,128)(2,1)}, bf16[512,3072]{1,0:T(8,128)(2,1)}, f32[512,768]{1,0:T(8,128)S(1)}) custom-call(bf16[512,768]{1,0:T(8,128)(2,1)S(1)} %copy-done.16, f32[1,3072]{1,0:T(1,128)S(1)} %broadcast_in_dim_reshape.15.bias_ref, bf16[4,112,768]{2,1,0:T(8,128)(2,1)S(1)} %copy-done.14, bf16[4,112,768]{2,1,0:T(8,128)(2,1)S(1)} %copy-done.27, ...), custom_call_target="tpu_custom_call" | custom-call | flops 1207959552 | bytes 3932160 | tf_op jit(solution)/shard_map/pallas_call | solution.py:664
  253.5 8.3 collective-permute-done.32.refs_0_
  261.8 3.2 pad_maximum_fusion.1.refs_3_.own_ref
  278.7 3.4 collective-permute-done.30.refs_0_
  297.7 3.2 slice_bitcast_fusion
  309.7 16.9 %shard_map.537 = (bf16[512,768]{1,0:T(8,128)(2,1)S(1)}, bf16[512,192]{1,0:T(8,128)(2,1)S(1)}, f32[6,512,2]{2,1,0:T(8,128)S(1)}) custom-call(s32[1]{0:T(128)S(6)} %copy.555.length, bf16[512,768]{1,0:T(8,128)(2,1)S(1)} %copy-done.25, bf16[512,768]{1,0:T(8,128)(2,1)S(1)} %copy-done.95, bf16[512,768]{1,0:T(8,128)(2,1)S(1)} %add_convert_fusion.8.vt, ...), custom_call_target="tpu_custom_call" | custom-call | flops 4000000000 | bytes 2000000 | tf_op jit(solution)/shard_map/pallas_call | solution.py:527
  336.0 3.7 fusion.248
  348.0 13.8 %shard_map.546 = (bf16[512,3072]{1,0:T(8,128)(2,1)}, bf16[512,3072]{1,0:T(8,128)(2,1)}, f32[512,768]{1,0:T(8,128)S(1)}) custom-call(bf16[512,768]{1,0:T(8,128)(2,1)S(1)} %fusion.48.rows_ref, f32[1,3072]{1,0:T(1,128)S(1)} %broadcast_in_dim_reshape.17.bias_ref, bf16[4,112,768]{2,1,0:T(8,128)(2,1)S(1)} %copy-done.10, bf16[4,112,768]{2,1,0:T(8,128)(2,1)S(1)} %copy-done.31, ...), custom_call_target="tpu_custom_call" | custom-call | flops 1207959552 | bytes 3932160 | tf_op jit(solution)/shard_map/pallas_call | solution.py:664
  365.5 4.0 all-to-all-start.6
  384.4 22.6 %all-to-all-done.6 = bf16[32,32,768]{2,1,0:T(8,128)(2,1)} async-done(((bf16[32,32,768]{2,1,0:T(8,128)(2,1)}), bf16[32,32,768]{2,1,0:T(8,128)(2,1)}, u32[]{:S(2)}, u32[]{:S(2)}) %all-to-all-start.6) | async-done | bytes 1572896 | tf_op jit(solution)/shard_map/all_to_all | solution.py:886
  407.0 4.9 fusion.249
  415.6 4.0 all-to-all-start.7
  424.9 10.2 %all-to-all-done.7 = f32[32,3,1024]{2,1,0:T(4,128)} async-done(((f32[32,3,1024]{2,1,0:T(4,128)}), f32[32,3,1024]{2,1,0:T(4,128)}, u32[]{:S(2)}, u32[]{:S(2)}) %all-to-all-start.7) | async-done | bytes 393248 | tf_op jit(solution)/shard_map/all_to_all | solution.py:886
  438.6 8.4 convolution_convert_fusion
  447.0 3.4 all-to-all-start.8
  472.4 15.5 %all-to-all-done.8 = bf16[32,32,768]{2,1,0:T(8,128)(2,1)} async-done(((bf16[32,32,768]{2,1,0:T(8,128)(2,1)}), bf16[32,32,768]{2,1,0:T(8,128)(2,1)}, u32[]{:S(2)}, u32[]{:S(2)}) %all-to-all-start.8) | async-done | bytes 1572896 | tf_op jit(solution)/shard_map/all_to_all | solution.py:892
  494.8 21.7 %shard_map.550 = (f32[512,768]{1,0:T(8,128)}, f32[1,3072]{1,0:T(1,128)S(1)}, bf16[16,112,768]{2,1,0:T(8,128)(2,1)}, bf16[16,96,768]{2,1,0:T(8,128)(2,1)}, bf16[1...) custom-call(bf16[512,768]{1,0:T(8,128)(2,1)} %copy-done.49, bf16[512,768]{1,0:T(8,128)(2,1)} %get-tuple-element.672.grad_ref, ...), custom_call_target="tpu_custom_call" | custom-call | flops 2415919104 | bytes 7864320 | tf_op jit(solution)/shard_map/pallas_call | solution.py:987
  524.7 4.3 multiply_reduce_fusion.3
  538.9 4.4 add_convert_fusion.6
  544.8 4.5 fusion.24
  556.1 18.5 %shard_map.554 = (bf16[512,768]{1,0:T(8,128)(2,1)S(1)}, bf16[512,768]{1,0:T(8,128)(2,1)S(1)}, bf16[512,768]{1,0:T(8,128)(2,1)S(1)}, bf16[512,192]{1,0:T(8,128)(2...) custom-call(s32[1]{0:T(128)S(6)} %copy.555.length, bf16[512,768]{1,0:T(8,128)(2,1)S(1)} %copy-done.25, ...), custom_call_target="tpu_custom_call" | custom-call | flops 5000000000 | bytes 3000000 | tf_op jit(solution)/shard_map/pallas_call | solution.py:551
  593.4 5.2 shard_map.555
  601.0 4.3 add_add_fusion.5.refs_0_
  631.6 21.9 %shard_map.563 = (f32[512,768]{1,0:T(8,128)}, f32[1,3072]{1,0:T(1,128)S(1)}, bf16[16,112,768]{2,1,0:T(8,128)(2,1)}, bf16[16,96,768]{2,1,0:T(8,128)(2,1)}, bf16[1...) custom-call(bf16[512,768]{1,0:T(8,128)(2,1)} %shard_map.515.rows_ref, bf16[512,768]{1,0:T(8,128)(2,1)} %shard_map.561.grad_ref, ...), custom_call_target="tpu_custom_call" | custom-call | flops 2415919104 | bytes 7864320 | tf_op jit(solution)/shard_map/pallas_call | solution.py:987
  674.6 3.6 fusion.234
  690.1 18.7 %shard_map.568 = (bf16[512,768]{1,0:T(8,128)(2,1)S(1)}, bf16[512,768]{1,0:T(8,128)(2,1)S(1)}, bf16[512,768]{1,0:T(8,128)(2,1)S(1)}, bf16[512,192]{1,0:T(8,128)(2...) custom-call(s32[1]{0:T(128)S(6)} %copy.555.length, bf16[512,768]{1,0:T(8,128)(2,1)S(1)} %copy-done.98, ...), custom_call_target="tpu_custom_call" | custom-call | flops 5000000000 | bytes 3000000 | tf_op jit(solution)/shard_map/pallas_call | solution.py:551
  719.5 3.2 fusion.80
  726.4 4.4 add_convert_fusion.4
  732.1 4.8 fusion.22
  736.9 5.8 add_add_fusion.4.refs_0_
  742.7 5.1 shard_map.573
  765.1 4.1 shard_map.579
  781.0 4.0 all-to-all-start.9
  801.0 9.2 collective-permute-done.62.refs_0_
  810.2 3.1 add_convert_fusion.15
  822.5 4.9 fusion.18
  827.5 9.3 convolution_add_fusion
  837.6 4.2 multiply_reduce_fusion
  857.8 5.0 collective-permute-done.68.refs_0_
  864.8 12.2 %collective-permute-done.67.refs_0_ = bf16[2,112,768]{2,1,0:T(8,128)(2,1)} collective-permute-done((bf16[2,112,768]{2,1,0:T(8,128)(2,1)}, bf16[2,112,768]{2,1,0:T(8,128)(2,1)}, u32[]{:S(2)}, u32[]{:S(2)}) %collective-permute-start.67) | collective-permute-done | bytes 344096 | tf_op jit(solution)/shard_map/ppermute | solution.py:193
  878.1 4.0 collective-permute-done.72.refs_0_
  889.7 7.2 collective-permute-done.73
  904.6 5.9 collective-permute-done.78.refs_0_
  915.1 4.3 collective-permute-done.84.refs_0_
  953.3 4.7 add_multiply_fusion.2
  960.0 6.1 add_multiply_fusion.1
  968.6 7.6 add_multiply_fusion
  (1572 shorter events, 478.8 us)
Async XLA Ops:
  2.8 17.9 %collective-permute-start = (bf16[1,528,128]{2,1,0:T(8,128)(2,1)S(1)}, bf16[1,528,128]{2,1,0:T(8,128)(2,1)S(1)}, u32[]{:S(2)}, u32[]{:S(2)}) collective-permute-start(bf16[1,528,128]{2,1,0:T(8,128)(2,1)S(1)} %maximum_bitcast_fusion.6), channel_id=1, source_target_pairs={{0,4},{4,0},{8,12},{12,8},{16,20},{20,16},{24,28},{28,24},{1,5},{5... | collective-permute-start | bytes 405512 | tf_op jit(solution)/shard_map/ppermute | solution.py:193
  8.5 22.0 %collective-permute-start.1 = (bf16[1,96,1536]{2,1,0:T(8,128)(2,1)S(1)}, bf16[1,96,1536]{2,1,0:T(8,128)(2,1)S(1)}, u32[]{:S(2)}, u32[]{:S(2)}) collective-permute-start(bf16[1,96,1536]{2,1,0:T(8,128)(2,1)S(1)} %get-tuple-element.710), channel_id=1, source_target_pairs={{0,16},{4,20},{8,24},{12,28},{16,0},{20,4},{24,8},{28,12},{1,17},{... | collective-permute-start | bytes 884744 | tf_op jit(solution)/shard_map/ppermute | solution.py:193
  30.6 26.7 %collective-permute-start.4 = (bf16[2,96,1536]{2,1,0:T(8,128)(2,1)S(1)}, bf16[2,96,1536]{2,1,0:T(8,128)(2,1)S(1)}, u32[]{:S(2)}, u32[]{:S(2)}) collective-permute-start(bf16[2,96,1536]{2,1,0:T(8,128)(2,1)S(1)} %pad_maximum_fusion.9.refs_1_), channel_id=1, source_target_pairs={{0,8},{4,12},{8,0},{12,4},{16,24},{20,28},{24,16},{28,20},{1,9},{5... | collective-permute-start | bytes 1769480 | tf_op jit(solution)/shard_map/ppermute | solution.py:193
  30.9 18.8 %all-to-all-start.4 = ((s32[32,1,128]{2,1,0:T(1,128)}), s32[32,1,128]{2,1,0:T(1,128)S(1)}, u32[]{:S(2)}, u32[]{:S(2)}) async-start(s32[32,1,128]{2,1,0:T(1,128)} %bitcast.511), calls=%async_computation.4 | async-start | bytes 32768 | tf_op jit(solution)/shard_map/all_to_all | solution.py:892
  35.9 24.3 %collective-permute-start.3 = (bf16[4,528,128]{2,1,0:T(8,128)(2,1)S(1)}, bf16[4,528,128]{2,1,0:T(8,128)(2,1)S(1)}, u32[]{:S(2)}, u32[]{:S(2)}) collective-permute-start(bf16[4,528,128]{2,1,0:T(8,128)(2,1)S(1)} %pad_maximum_fusion.13.refs_2_), channel_id=1, source_target_pairs={{0,8},{4,12},{8,0},{12,4},{16,24},{20,28},{24,16},{28,20},{1,9},{5... | collective-permute-start | bytes 1622024 | tf_op jit(solution)/shard_map/ppermute | solution.py:193
  63.2 16.6 %collective-permute-start.5 = (bf16[8,528,128]{2,1,0:T(8,128)(2,1)}, bf16[8,528,128]{2,1,0:T(8,128)(2,1)S(1)}, u32[]{:S(2)}, u32[]{:S(2)}) collective-permute-start(bf16[8,528,128]{2,1,0:T(8,128)(2,1)} %pad_maximum_fusion.6.refs_1_.own_ref), channel_id=1, source_target_pairs={{0,1},{1,0},{2,3},{3,2},{4,5},{5,4},{6,7},{7,6},{8,9},{9,8},{10,11... | collective-permute-start | bytes 3244040 | tf_op jit(solution)/shard_map/ppermute | solution.py:193
  63.2 49.9 %all-to-all-start.5 = ((bf16[32,32,768]{2,1,0:T(8,128)(2,1)}), bf16[32,32,768]{2,1,0:T(8,128)(2,1)}, u32[]{:S(2)}, u32[]{:S(2)}) async-start(bf16[32,32,768]{2,1,0:T(8,128)(2,1)} %bitcast.15), calls=%async_computation.5 | async-start | bytes 3145728 | tf_op jit(solution)/shard_map/all_to_all | solution.py:892
  75.1 41.6 %collective-permute-start.7 = (bf16[4,96,1536]{2,1,0:T(8,128)(2,1)}, bf16[4,96,1536]{2,1,0:T(8,128)(2,1)}, u32[]{:S(2)}, u32[]{:S(2)}) collective-permute-start(bf16[4,96,1536]{2,1,0:T(8,128)(2,1)} %pad_maximum_fusion.3.refs_1_), channel_id=1, source_target_pairs={{0,4},{4,0},{8,12},{12,8},{16,20},{20,16},{24,28},{28,24},{1,5},{5... | collective-permute-start | bytes 3538952 | tf_op jit(solution)/shard_map/ppermute | solution.py:193
  76.8 52.3 %collective-permute-start.9 = (bf16[1,96,768]{2,1,0:T(8,128)(2,1)}, bf16[1,96,768]{2,1,0:T(8,128)(2,1)}, u32[]{:S(2)}, u32[]{:S(2)}) collective-permute-start(bf16[1,96,768]{2,1,0:T(8,128)(2,1)} %shard_map.490.refs_2_), channel_id=1, source_target_pairs={{0,16},{4,20},{8,24},{12,28},{16,0},{20,4},{24,8},{28,12},{1,17},{... | collective-permute-start | bytes 442376 | tf_op jit(solution)/shard_map/ppermute | solution.py:193
  79.2 51.9 %collective-permute-start.6 = (bf16[1,112,768]{2,1,0:T(8,128)(2,1)}, bf16[1,112,768]{2,1,0:T(8,128)(2,1)}, u32[]{:S(2)}, u32[]{:S(2)}) collective-permute-start(bf16[1,112,768]{2,1,0:T(8,128)(2,1)} %shard_map.489.refs_1_), channel_id=1, source_target_pairs={{0,16},{4,20},{8,24},{12,28},{16,0},{20,4},{24,8},{28,12},{1,17},{... | collective-permute-start | bytes 516104 | tf_op jit(solution)/shard_map/ppermute | solution.py:193
  120.8 32.4 %collective-permute-start.11 = (bf16[8,96,1536]{2,1,0:T(8,128)(2,1)}, bf16[8,96,1536]{2,1,0:T(8,128)(2,1)}, u32[]{:S(2)}, u32[]{:S(2)}) collective-permute-start(bf16[8,96,1536]{2,1,0:T(8,128)(2,1)} %pad_maximum_fusion.refs_1_.own_ref), channel_id=1, source_target_pairs={{0,1},{1,0},{2,3},{3,2},{4,5},{5,4},{6,7},{7,6},{8,9},{9,8},{10,11... | collective-permute-start | bytes 7077896 | tf_op jit(solution)/shard_map/ppermute | solution.py:193
  142.5 38.0 %collective-permute-start.13 = (bf16[4,96,768]{2,1,0:T(8,128)(2,1)S(1)}, bf16[4,96,768]{2,1,0:T(8,128)(2,1)S(1)}, u32[]{:S(2)}, u32[]{:S(2)}) collective-permute-start(bf16[4,96,768]{2,1,0:T(8,128)(2,1)S(1)} %pad_maximum_fusion.10.refs_2_.refs_0_.refs_1_), channel_id=1, source_target_pairs={{0,2},{1,3},{2,0},{3,1},{4,6},{5,7},{6,4},{7,5},{8,10},{9,11},{10,... | collective-permute-start | bytes 1769480 | tf_op jit(solution)/shard_map/ppermute | solution.py:193
  144.0 37.3 %collective-permute-start.14 = (bf16[1,96,1536]{2,1,0:T(8,128)(2,1)}, bf16[1,96,1536]{2,1,0:T(8,128)(2,1)}, u32[]{:S(2)}, u32[]{:S(2)}) collective-permute-start(bf16[1,96,1536]{2,1,0:T(8,128)(2,1)} %shard_map.507), channel_id=1, source_target_pairs={{0,16},{4,20},{8,24},{12,28},{16,0},{20,4},{24,8},{28,12},{1,17},{... | collective-permute-start | bytes 884744 | tf_op jit(solution)/shard_map/ppermute | solution.py:193
  152.4 28.1 %collective-permute-start.12 = (bf16[4,112,768]{2,1,0:T(8,128)(2,1)S(1)}, bf16[4,112,768]{2,1,0:T(8,128)(2,1)S(1)}, u32[]{:S(2)}, u32[]{:S(2)}) collective-permute-start(bf16[4,112,768]{2,1,0:T(8,128)(2,1)S(1)} %copy-done.12), channel_id=1, source_target_pairs={{0,4},{4,0},{8,12},{12,8},{16,20},{20,16},{24,28},{28,24},{1,5},{5... | collective-permute-start | bytes 2064392 | tf_op jit(solution)/shard_map/ppermute | solution.py:193
  183.6 16.4 %collective-permute-start.24 = (bf16[4,96,768]{2,1,0:T(8,128)(2,1)S(1)}, bf16[4,96,768]{2,1,0:T(8,128)(2,1)}, u32[]{:S(2)}, u32[]{:S(2)}) collective-permute-start(bf16[4,96,768]{2,1,0:T(8,128)(2,1)S(1)} %copy-done.18), channel_id=1, source_target_pairs={{0,4},{4,0},{8,12},{12,8},{16,20},{20,16},{24,28},{28,24},{1,5},{5... | collective-permute-start | bytes 1769480 | tf_op jit(solution)/shard_map/ppermute | solution.py:193
  184.9 26.0 %collective-permute-start.25 = (bf16[4,96,768]{2,1,0:T(8,128)(2,1)}, bf16[4,96,768]{2,1,0:T(8,128)(2,1)S(1)}, u32[]{:S(2)}, u32[]{:S(2)}) collective-permute-start(bf16[4,96,768]{2,1,0:T(8,128)(2,1)} %shard_map.506.refs_4_.refs_0_), channel_id=1, source_target_pairs={{0,4},{4,0},{8,12},{12,8},{16,20},{20,16},{24,28},{28,24},{1,5},{5... | collective-permute-start | bytes 1769480 | tf_op jit(solution)/shard_map/ppermute | solution.py:193
  185.6 26.1 %collective-permute-start.18 = (bf16[4,112,768]{2,1,0:T(8,128)(2,1)S(1)}, bf16[4,112,768]{2,1,0:T(8,128)(2,1)S(1)}, u32[]{:S(2)}, u32[]{:S(2)}) collective-permute-start(bf16[4,112,768]{2,1,0:T(8,128)(2,1)S(1)} %copy-done.13), channel_id=1, source_target_pairs={{0,2},{1,3},{2,0},{3,1},{4,6},{5,7},{6,4},{7,5},{8,10},{9,11},{10,... | collective-permute-start | bytes 2064392 | tf_op jit(solution)/shard_map/ppermute | solution.py:193
  187.7 29.2 %collective-permute-start.19 = (bf16[4,112,768]{2,1,0:T(8,128)(2,1)}, bf16[4,112,768]{2,1,0:T(8,128)(2,1)S(1)}, u32[]{:S(2)}, u32[]{:S(2)}) collective-permute-start(bf16[4,112,768]{2,1,0:T(8,128)(2,1)} %shard_map.504.refs_2_.refs_0_), channel_id=1, source_target_pairs={{0,2},{1,3},{2,0},{3,1},{4,6},{5,7},{6,4},{7,5},{8,10},{9,11},{10,... | collective-permute-start | bytes 2064392 | tf_op jit(solution)/shard_map/ppermute | solution.py:193
  192.4 19.3 %collective-permute-start.17 = (bf16[1,96,768]{2,1,0:T(8,128)(2,1)}, bf16[1,96,768]{2,1,0:T(8,128)(2,1)}, u32[]{:S(2)}, u32[]{:S(2)}) collective-permute-start(bf16[1,96,768]{2,1,0:T(8,128)(2,1)} %shard_map.513), channel_id=1, source_target_pairs={{0,16},{4,20},{8,24},{12,28},{16,0},{20,4},{24,8},{28,12},{1,17},{... | collective-permute-start | bytes 442376 | tf_op jit(solution)/shard_map/ppermute | solution.py:193
  199.9 26.3 %collective-permute-start.15 = (bf16[2,96,1536]{2,1,0:T(8,128)(2,1)}, bf16[2,96,1536]{2,1,0:T(8,128)(2,1)}, u32[]{:S(2)}, u32[]{:S(2)}) collective-permute-start(bf16[2,96,1536]{2,1,0:T(8,128)(2,1)} %pad_maximum_fusion.11.refs_5_.refs_1_), channel_id=1, source_target_pairs={{0,8},{4,12},{8,0},{12,4},{16,24},{20,28},{24,16},{28,20},{1,9},{5... | collective-permute-start | bytes 1769480 | tf_op jit(solution)/shard_map/ppermute | solution.py:193
  210.9 15.9 %collective-permute-start.27 = (bf16[4,96,768]{2,1,0:T(8,128)(2,1)}, bf16[4,96,768]{2,1,0:T(8,128)(2,1)}, u32[]{:S(2)}, u32[]{:S(2)}) collective-permute-start(bf16[4,96,768]{2,1,0:T(8,128)(2,1)} %shard_map.521.refs_9_), channel_id=1, source_target_pairs={{0,1},{1,0},{2,3},{3,2},{4,5},{5,4},{6,7},{7,6},{8,9},{9,8},{10,11... | collective-permute-start | bytes 1769480 | tf_op jit(solution)/shard_map/ppermute | solution.py:193
  233.1 28.7 %collective-permute-start.32 = (bf16[4,96,1536]{2,1,0:T(8,128)(2,1)}, bf16[4,96,1536]{2,1,0:T(8,128)(2,1)}, u32[]{:S(2)}, u32[]{:S(2)}) collective-permute-start(bf16[4,96,1536]{2,1,0:T(8,128)(2,1)} %pad_maximum_fusion.4.refs_1_), channel_id=1, source_target_pairs={{0,4},{4,0},{8,12},{12,8},{16,20},{20,16},{24,28},{28,24},{1,5},{5... | collective-permute-start | bytes 3538952 | tf_op jit(solution)/shard_map/ppermute | solution.py:193
  265.0 24.6 %collective-permute-start.33 = (bf16[8,96,1536]{2,1,0:T(8,128)(2,1)}, bf16[8,96,1536]{2,1,0:T(8,128)(2,1)}, u32[]{:S(2)}, u32[]{:S(2)}) collective-permute-start(bf16[8,96,1536]{2,1,0:T(8,128)(2,1)} %pad_maximum_fusion.1.refs_3_.own_ref), channel_id=1, source_target_pairs={{0,1},{1,0},{2,3},{3,2},{4,5},{5,4},{6,7},{7,6},{8,9},{9,8},{10,11... | collective-permute-start | bytes 7077896 | tf_op jit(solution)/shard_map/ppermute | solution.py:193
  265.4 16.8 %collective-permute-start.30 = (bf16[2,112,768]{2,1,0:T(8,128)(2,1)}, bf16[2,112,768]{2,1,0:T(8,128)(2,1)S(1)}, u32[]{:S(2)}, u32[]{:S(2)}) collective-permute-start(bf16[2,112,768]{2,1,0:T(8,128)(2,1)} %pad_maximum_fusion.17.refs_2_), channel_id=1, source_target_pairs={{0,8},{4,12},{8,0},{12,4},{16,24},{20,28},{24,16},{28,20},{1,9},{5... | collective-permute-start | bytes 1032200 | tf_op jit(solution)/shard_map/ppermute | solution.py:193
  277.2 19.7 %collective-permute-start.35 = (bf16[4,96,768]{2,1,0:T(8,128)(2,1)S(1)}, bf16[4,96,768]{2,1,0:T(8,128)(2,1)S(1)}, u32[]{:S(2)}, u32[]{:S(2)}) collective-permute-start(bf16[4,96,768]{2,1,0:T(8,128)(2,1)S(1)} %pad_maximum_fusion.12.refs_2_.refs_0_), channel_id=1, source_target_pairs={{0,2},{1,3},{2,0},{3,1},{4,6},{5,7},{6,4},{7,5},{8,10},{9,11},{10,... | collective-permute-start | bytes 1769480 | tf_op jit(solution)/shard_map/ppermute | solution.py:193
  284.0 17.1 %collective-permute-start.34 = (bf16[4,112,768]{2,1,0:T(8,128)(2,1)S(1)}, bf16[4,112,768]{2,1,0:T(8,128)(2,1)S(1)}, u32[]{:S(2)}, u32[]{:S(2)}) collective-permute-start(bf16[4,112,768]{2,1,0:T(8,128)(2,1)S(1)} %pad_maximum_fusion.8.refs_1_.refs_0_), channel_id=1, source_target_pairs={{0,4},{4,0},{8,12},{12,8},{16,20},{20,16},{24,28},{28,24},{1,5},{5... | collective-permute-start | bytes 2064392 | tf_op jit(solution)/shard_map/ppermute | solution.py:193
  302.0 27.7 %collective-permute-start.42 = (bf16[4,96,768]{2,1,0:T(8,128)(2,1)S(1)}, bf16[4,96,768]{2,1,0:T(8,128)(2,1)}, u32[]{:S(2)}, u32[]{:S(2)}) collective-permute-start(bf16[4,96,768]{2,1,0:T(8,128)(2,1)S(1)} %copy-done.21), channel_id=1, source_target_pairs={{0,4},{4,0},{8,12},{12,8},{16,20},{20,16},{24,28},{28,24},{1,5},{5... | collective-permute-start | bytes 1769480 | tf_op jit(solution)/shard_map/ppermute | solution.py:193
  303.8 25.9 %collective-permute-start.43 = (bf16[4,96,768]{2,1,0:T(8,128)(2,1)}, bf16[4,96,768]{2,1,0:T(8,128)(2,1)}, u32[]{:S(2)}, u32[]{:S(2)}) collective-permute-start(bf16[4,96,768]{2,1,0:T(8,128)(2,1)} %shard_map.533.refs_4_.refs_0_), channel_id=1, source_target_pairs={{0,4},{4,0},{8,12},{12,8},{16,20},{20,16},{24,28},{28,24},{1,5},{5... | collective-permute-start | bytes 1769480 | tf_op jit(solution)/shard_map/ppermute | solution.py:193
  304.0 36.2 %collective-permute-start.36 = (bf16[4,112,768]{2,1,0:T(8,128)(2,1)S(1)}, bf16[4,112,768]{2,1,0:T(8,128)(2,1)}, u32[]{:S(2)}, u32[]{:S(2)}) collective-permute-start(bf16[4,112,768]{2,1,0:T(8,128)(2,1)S(1)} %copy-done.9), channel_id=1, source_target_pairs={{0,2},{1,3},{2,0},{3,1},{4,6},{5,7},{6,4},{7,5},{8,10},{9,11},{10,... | collective-permute-start | bytes 2064392 | tf_op jit(solution)/shard_map/ppermute | solution.py:193
  307.1 32.7 %collective-permute-start.37 = (bf16[4,112,768]{2,1,0:T(8,128)(2,1)S(1)}, bf16[4,112,768]{2,1,0:T(8,128)(2,1)}, u32[]{:S(2)}, u32[]{:S(2)}) collective-permute-start(bf16[4,112,768]{2,1,0:T(8,128)(2,1)S(1)} %copy-done.30), channel_id=1, source_target_pairs={{0,2},{1,3},{2,0},{3,1},{4,6},{5,7},{6,4},{7,5},{8,10},{9,11},{10,... | collective-permute-start | bytes 2064392 | tf_op jit(solution)/shard_map/ppermute | solution.py:193
  365.5 41.5 %all-to-all-start.6 = ((bf16[32,32,768]{2,1,0:T(8,128)(2,1)}), bf16[32,32,768]{2,1,0:T(8,128)(2,1)}, u32[]{:S(2)}, u32[]{:S(2)}) async-start(bf16[32,32,768]{2,1,0:T(8,128)(2,1)} %broadcast_in_dim.303), calls=%async_computation.6 | async-start | bytes 3145728 | tf_op jit(solution)/shard_map/all_to_all | solution.py:886
  415.6 19.6 %all-to-all-start.7 = ((f32[32,3,1024]{2,1,0:T(4,128)}), f32[32,3,1024]{2,1,0:T(4,128)}, u32[]{:S(2)}, u32[]{:S(2)}) async-start(f32[32,3,1024]{2,1,0:T(4,128)} %broadcast_in_dim.305), calls=%async_computation.7 | async-start | bytes 1048576 | tf_op jit(solution)/shard_map/all_to_all | solution.py:886
  447.0 40.9 %all-to-all-start.8 = ((bf16[32,32,768]{2,1,0:T(8,128)(2,1)}), bf16[32,32,768]{2,1,0:T(8,128)(2,1)}, u32[]{:S(2)}, u32[]{:S(2)}) async-start(bf16[32,32,768]{2,1,0:T(8,128)(2,1)} %bitcast.504), calls=%async_computation.8 | async-start | bytes 3145728 | tf_op jit(solution)/shard_map/all_to_all | solution.py:892
  516.5 22.4 %collective-permute-start.49 = (bf16[16,96,768]{2,1,0:T(8,128)(2,1)}, bf16[16,96,768]{2,1,0:T(8,128)(2,1)}, u32[]{:S(2)}, u32[]{:S(2)}) collective-permute-start(bf16[16,96,768]{2,1,0:T(8,128)(2,1)} %get-tuple-element.378), channel_id=1, source_target_pairs={{0,1},{1,0},{2,3},{3,2},{4,5},{5,4},{6,7},{7,6},{8,9},{9,8},{10,11... | collective-permute-start | bytes 7077896 | tf_op jit(solution)/shard_map/ppermute | solution.py:193
  516.6 28.2 %collective-permute-start.48 = (bf16[16,112,768]{2,1,0:T(8,128)(2,1)}, bf16[16,112,768]{2,1,0:T(8,128)(2,1)}, u32[]{:S(2)}, u32[]{:S(2)}) collective-permute-start(bf16[16,112,768]{2,1,0:T(8,128)(2,1)} %get-tuple-element.376), channel_id=1, source_target_pairs={{0,1},{1,0},{2,3},{3,2},{4,5},{5,4},{6,7},{7,6},{8,9},{9,8},{10,11... | collective-permute-start | bytes 8257544 | tf_op jit(solution)/shard_map/ppermute | solution.py:193
  543.3 67.3 %collective-permute-start.51 = (bf16[2,4,96,768]{3,2,1,0:T(8,128)(2,1)}, bf16[2,4,96,768]{3,2,1,0:T(8,128)(2,1)}, u32[]{:S(2)}, u32[]{:S(2)}) collective-permute-start(bf16[2,4,96,768]{3,2,1,0:T(8,128)(2,1)} %get-tuple-element.650.refs_2_), channel_id=1, source_target_pairs={{0,4},{4,0},{8,12},{12,8},{16,20},{20,16},{24,28},{28,24},{1,5},{5... | collective-permute-start | bytes 3538952 | tf_op jit(solution)/shard_map/ppermute | solution.py:193
  549.3 66.1 %collective-permute-start.50 = (bf16[2,4,112,768]{3,2,1,0:T(8,128)(2,1)}, bf16[2,4,112,768]{3,2,1,0:T(8,128)(2,1)}, u32[]{:S(2)}, u32[]{:S(2)}) collective-permute-start(bf16[2,4,112,768]{3,2,1,0:T(8,128)(2,1)} %get-tuple-element.660.refs_1_), channel_id=1, source_target_pairs={{0,2},{1,3},{2,0},{3,1},{4,6},{5,7},{6,4},{7,5},{8,10},{9,11},{10,... | collective-permute-start | bytes 4128776 | tf_op jit(solution)/shard_map/ppermute | solution.py:193
  599.3 27.5 %collective-permute-start.52 = (bf16[8,104,1536]{2,1,0:T(8,128)(2,1)}, bf16[8,104,1536]{2,1,0:T(8,128)(2,1)}, u32[]{:S(2)}, u32[]{:S(2)}) collective-permute-start(bf16[8,104,1536]{2,1,0:T(8,128)(2,1)} %pad_dynamic-update-slice_fusion.3.refs_1_), channel_id=1, source_target_pairs={{0,1},{1,0},{2,3},{3,2},{4,5},{5,4},{6,7},{7,6},{8,9},{9,8},{10,11... | collective-permute-start | bytes 7667720 | tf_op jit(solution)/shard_map/ppermute | solution.py:193
  614.4 49.3 %collective-permute-start.54 = (bf16[4,96,768]{2,1,0:T(8,128)(2,1)}, bf16[4,96,768]{2,1,0:T(8,128)(2,1)}, u32[]{:S(2)}, u32[]{:S(2)}) collective-permute-start(bf16[4,96,768]{2,1,0:T(8,128)(2,1)} %get-tuple-element.666.refs_2_), channel_id=1, source_target_pairs={{0,2},{1,3},{2,0},{3,1},{4,6},{5,7},{6,4},{7,5},{8,10},{9,11},{10,... | collective-permute-start | bytes 1769480 | tf_op jit(solution)/shard_map/ppermute | solution.py:193
  618.7 50.2 %collective-permute-start.53 = (bf16[4,112,768]{2,1,0:T(8,128)(2,1)}, bf16[4,112,768]{2,1,0:T(8,128)(2,1)}, u32[]{:S(2)}, u32[]{:S(2)}) collective-permute-start(bf16[4,112,768]{2,1,0:T(8,128)(2,1)} %get-tuple-element.658.refs_1_), channel_id=1, source_target_pairs={{0,4},{4,0},{8,12},{12,8},{16,20},{20,16},{24,28},{28,24},{1,5},{5... | collective-permute-start | bytes 2064392 | tf_op jit(solution)/shard_map/ppermute | solution.py:193
  629.9 50.3 %collective-permute-start.55 = (bf16[2,2,104,1536]{3,2,1,0:T(8,128)(2,1)}, bf16[2,2,104,1536]{3,2,1,0:T(8,128)(2,1)}, u32[]{:S(2)}, u32[]{:S(2)}) collective-permute-start(bf16[2,2,104,1536]{3,2,1,0:T(8,128)(2,1)} %fusion.51.refs_1_), channel_id=1, source_target_pairs={{0,4},{4,0},{8,12},{12,8},{16,20},{20,16},{24,28},{28,24},{1,5},{5... | collective-permute-start | bytes 3833864 | tf_op jit(solution)/shard_map/ppermute | solution.py:193
  665.9 84.1 %collective-permute-start.60 = (bf16[2,96,768]{2,1,0:T(8,128)(2,1)}, bf16[2,96,768]{2,1,0:T(8,128)(2,1)}, u32[]{:S(2)}, u32[]{:S(2)}) collective-permute-start(bf16[2,96,768]{2,1,0:T(8,128)(2,1)} %get-tuple-element.688.refs_2_), channel_id=1, source_target_pairs={{0,8},{4,12},{8,0},{12,4},{16,24},{20,28},{24,16},{28,20},{1,9},{5... | collective-permute-start | bytes 884744 | tf_op jit(solution)/shard_map/ppermute | solution.py:193
  672.1 82.6 %collective-permute-start.59 = (bf16[2,112,768]{2,1,0:T(8,128)(2,1)}, bf16[2,112,768]{2,1,0:T(8,128)(2,1)}, u32[]{:S(2)}, u32[]{:S(2)}) collective-permute-start(bf16[2,112,768]{2,1,0:T(8,128)(2,1)} %get-tuple-element.680.refs_1_), channel_id=1, source_target_pairs={{0,8},{4,12},{8,0},{12,4},{16,24},{20,28},{24,16},{28,20},{1,9},{5... | collective-permute-start | bytes 1032200 | tf_op jit(solution)/shard_map/ppermute | solution.py:193
  674.1 52.4 %collective-permute-start.57 = (bf16[16,96,768]{2,1,0:T(8,128)(2,1)}, bf16[16,96,768]{2,1,0:T(8,128)(2,1)}, u32[]{:S(2)}, u32[]{:S(2)}) collective-permute-start(bf16[16,96,768]{2,1,0:T(8,128)(2,1)} %get-tuple-element.404), channel_id=1, source_target_pairs={{0,1},{1,0},{2,3},{3,2},{4,5},{5,4},{6,7},{7,6},{8,9},{9,8},{10,11... | collective-permute-start | bytes 7077896 | tf_op jit(solution)/shard_map/ppermute | solution.py:193
  674.1 58.0 %collective-permute-start.56 = (bf16[16,112,768]{2,1,0:T(8,128)(2,1)}, bf16[16,112,768]{2,1,0:T(8,128)(2,1)}, u32[]{:S(2)}, u32[]{:S(2)}) collective-permute-start(bf16[16,112,768]{2,1,0:T(8,128)(2,1)} %get-tuple-element.402), channel_id=1, source_target_pairs={{0,1},{1,0},{2,3},{3,2},{4,5},{5,4},{6,7},{7,6},{8,9},{9,8},{10,11... | collective-permute-start | bytes 8257544 | tf_op jit(solution)/shard_map/ppermute | solution.py:193
  683.6 39.2 %collective-permute-start.58 = (bf16[2,104,1536]{2,1,0:T(8,128)(2,1)}, bf16[2,104,1536]{2,1,0:T(8,128)(2,1)}, u32[]{:S(2)}, u32[]{:S(2)}) collective-permute-start(bf16[2,104,1536]{2,1,0:T(8,128)(2,1)} %fusion.98.refs_3_), channel_id=1, source_target_pairs={{0,8},{4,12},{8,0},{12,4},{16,24},{20,28},{24,16},{28,20},{1,9},{5... | collective-permute-start | bytes 1916936 | tf_op jit(solution)/shard_map/ppermute | solution.py:193
  725.6 31.6 %collective-permute-start.61 = (bf16[104,1536]{1,0:T(8,128)(2,1)}, bf16[104,1536]{1,0:T(8,128)(2,1)}, u32[]{:S(2)}, u32[]{:S(2)}) collective-permute-start(bf16[104,1536]{1,0:T(8,128)(2,1)} %fusion.127.refs_3_), channel_id=1, source_target_pairs={{0,16},{4,20},{8,24},{12,28},{16,0},{20,4},{24,8},{28,12},{1,17},{... | collective-permute-start | bytes 958472 | tf_op jit(solution)/shard_map/ppermute | solution.py:193
  730.9 83.8 %collective-permute-start.66 = (bf16[2,4,96,768]{3,2,1,0:T(8,128)(2,1)}, bf16[2,4,96,768]{3,2,1,0:T(8,128)(2,1)}, u32[]{:S(2)}, u32[]{:S(2)}) collective-permute-start(bf16[2,4,96,768]{3,2,1,0:T(8,128)(2,1)} %get-tuple-element.648.refs_2_), channel_id=1, source_target_pairs={{0,4},{4,0},{8,12},{12,8},{16,20},{20,16},{24,28},{28,24},{1,5},{5... | collective-permute-start | bytes 3538952 | tf_op jit(solution)/shard_map/ppermute | solution.py:193
  752.5 23.0 %collective-permute-start.75 = (bf16[1,96,768]{2,1,0:T(8,128)(2,1)}, bf16[1,96,768]{2,1,0:T(8,128)(2,1)}, u32[]{:S(2)}, u32[]{:S(2)}) collective-permute-start(bf16[1,96,768]{2,1,0:T(8,128)(2,1)} %add_convert_fusion.33.refs_2_), channel_id=1, source_target_pairs={{0,16},{4,20},{8,24},{12,28},{16,0},{20,4},{24,8},{28,12},{1,17},{... | collective-permute-start | bytes 442376 | tf_op jit(solution)/shard_map/ppermute | solution.py:193
  756.4 20.3 %collective-permute-start.74 = (bf16[1,112,768]{2,1,0:T(8,128)(2,1)}, bf16[1,112,768]{2,1,0:T(8,128)(2,1)}, u32[]{:S(2)}, u32[]{:S(2)}) collective-permute-start(bf16[1,112,768]{2,1,0:T(8,128)(2,1)} %add_convert_fusion.29.refs_1_), channel_id=1, source_target_pairs={{0,16},{4,20},{8,24},{12,28},{16,0},{20,4},{24,8},{28,12},{1,17},{... | collective-permute-start | bytes 516104 | tf_op jit(solution)/shard_map/ppermute | solution.py:193
  759.1 18.6 %collective-permute-start.81 = (bf16[104,1536]{1,0:T(8,128)(2,1)}, bf16[104,1536]{1,0:T(8,128)(2,1)}, u32[]{:S(2)}, u32[]{:S(2)}) collective-permute-start(bf16[104,1536]{1,0:T(8,128)(2,1)} %fusion.103.refs_3_), channel_id=1, source_target_pairs={{0,2},{1,3},{2,0},{3,1},{4,6},{5,7},{6,4},{7,5},{8,10},{9,11},{10,... | collective-permute-start | bytes 958472 | tf_op jit(solution)/shard_map/ppermute | solution.py:193
  760.1 50.1 %collective-permute-start.62 = (bf16[2,4,112,768]{3,2,1,0:T(8,128)(2,1)}, bf16[2,4,112,768]{3,2,1,0:T(8,128)(2,1)}, u32[]{:S(2)}, u32[]{:S(2)}) collective-permute-start(bf16[2,4,112,768]{3,2,1,0:T(8,128)(2,1)} %get-tuple-element.654.refs_1_), channel_id=1, source_target_pairs={{0,2},{1,3},{2,0},{3,1},{4,6},{5,7},{6,4},{7,5},{8,10},{9,11},{10,... | collective-permute-start | bytes 4128776 | tf_op jit(solution)/shard_map/ppermute | solution.py:193
  781.0 41.5 %all-to-all-start.9 = ((bf16[32,32,768]{2,1,0:T(8,128)(2,1)}), bf16[32,32,768]{2,1,0:T(8,128)(2,1)}, u32[]{:S(2)}, u32[]{:S(2)}) async-start(bf16[32,32,768]{2,1,0:T(8,128)(2,1)} %bitcast.91), calls=%async_computation.9 | async-start | bytes 3145728 | tf_op jit(solution)/shard_map/all_to_all | solution.py:892
  791.6 50.2 %collective-permute-start.65 = (bf16[2,2,104,1536]{3,2,1,0:T(8,128)(2,1)}, bf16[2,2,104,1536]{3,2,1,0:T(8,128)(2,1)}, u32[]{:S(2)}, u32[]{:S(2)}) collective-permute-start(bf16[2,2,104,1536]{3,2,1,0:T(8,128)(2,1)} %fusion.52.refs_1_), channel_id=1, source_target_pairs={{0,4},{4,0},{8,12},{12,8},{16,20},{20,16},{24,28},{28,24},{1,5},{5... | collective-permute-start | bytes 3833864 | tf_op jit(solution)/shard_map/ppermute | solution.py:193
  801.0 52.5 %collective-permute-start.69 = (bf16[8,384,128]{2,1,0:T(8,128)(2,1)}, bf16[8,384,128]{2,1,0:T(8,128)(2,1)S(1)}, u32[]{:S(2)}, u32[]{:S(2)}) collective-permute-start(bf16[8,384,128]{2,1,0:T(8,128)(2,1)} %get-tuple-element.676.refs_1_), channel_id=1, source_target_pairs={{0,1},{1,0},{2,3},{3,2},{4,5},{5,4},{6,7},{7,6},{8,9},{9,8},{10,11... | collective-permute-start | bytes 2359304 | tf_op jit(solution)/shard_map/ppermute | solution.py:193
  813.3 33.7 %collective-permute-start.64 = (bf16[4,112,768]{2,1,0:T(8,128)(2,1)}, bf16[4,112,768]{2,1,0:T(8,128)(2,1)}, u32[]{:S(2)}, u32[]{:S(2)}) collective-permute-start(bf16[4,112,768]{2,1,0:T(8,128)(2,1)} %get-tuple-element.652.refs_1_), channel_id=1, source_target_pairs={{0,4},{4,0},{8,12},{12,8},{16,20},{20,16},{24,28},{28,24},{1,5},{5... | collective-permute-start | bytes 2064392 | tf_op jit(solution)/shard_map/ppermute | solution.py:193
  817.6 32.9 %collective-permute-start.70 = (bf16[4,96,768]{2,1,0:T(8,128)(2,1)}, bf16[4,96,768]{2,1,0:T(8,128)(2,1)}, u32[]{:S(2)}, u32[]{:S(2)}) collective-permute-start(bf16[4,96,768]{2,1,0:T(8,128)(2,1)} %get-tuple-element.664.refs_1_), channel_id=1, source_target_pairs={{0,2},{1,3},{2,0},{3,1},{4,6},{5,7},{6,4},{7,5},{8,10},{9,11},{10,... | collective-permute-start | bytes 1769480 | tf_op jit(solution)/shard_map/ppermute | solution.py:193
  845.2 17.6 %collective-permute-start.68 = (bf16[2,104,1536]{2,1,0:T(8,128)(2,1)}, bf16[2,104,1536]{2,1,0:T(8,128)(2,1)}, u32[]{:S(2)}, u32[]{:S(2)}) collective-permute-start(bf16[2,104,1536]{2,1,0:T(8,128)(2,1)} %fusion.99.refs_1_), channel_id=1, source_target_pairs={{0,8},{4,12},{8,0},{12,4},{16,24},{20,28},{24,16},{28,20},{1,9},{5... | collective-permute-start | bytes 1916936 | tf_op jit(solution)/shard_map/ppermute | solution.py:193
  849.2 27.9 %collective-permute-start.67 = (bf16[2,112,768]{2,1,0:T(8,128)(2,1)}, bf16[2,112,768]{2,1,0:T(8,128)(2,1)}, u32[]{:S(2)}, u32[]{:S(2)}) collective-permute-start(bf16[2,112,768]{2,1,0:T(8,128)(2,1)} %get-tuple-element.678.refs_1_), channel_id=1, source_target_pairs={{0,8},{4,12},{8,0},{12,4},{16,24},{20,28},{24,16},{28,20},{1,9},{5... | collective-permute-start | bytes 1032200 | tf_op jit(solution)/shard_map/ppermute | solution.py:193
  852.8 29.4 %collective-permute-start.72 = (bf16[2,96,768]{2,1,0:T(8,128)(2,1)}, bf16[2,96,768]{2,1,0:T(8,128)(2,1)}, u32[]{:S(2)}, u32[]{:S(2)}) collective-permute-start(bf16[2,96,768]{2,1,0:T(8,128)(2,1)} %get-tuple-element.686.refs_1_), channel_id=1, source_target_pairs={{0,8},{4,12},{8,0},{12,4},{16,24},{20,28},{24,16},{28,20},{1,9},{5... | collective-permute-start | bytes 884744 | tf_op jit(solution)/shard_map/ppermute | solution.py:193
  855.6 27.6 %collective-permute-start.77 = (bf16[2,2,384,128]{3,2,1,0:T(8,128)(2,1)S(1)}, bf16[2,2,384,128]{3,2,1,0:T(8,128)(2,1)S(1)}, u32[]{:S(2)}, u32[]{:S(2)}) collective-permute-start(bf16[2,2,384,128]{3,2,1,0:T(8,128)(2,1)S(1)} %fusion.122.refs_1_), channel_id=1, source_target_pairs={{0,4},{4,0},{8,12},{12,8},{16,20},{20,16},{24,28},{28,24},{1,5},{5... | collective-permute-start | bytes 1179656 | tf_op jit(solution)/shard_map/ppermute | solution.py:193
  864.7 34.4 %collective-permute-start.76 = (bf16[104,1536]{1,0:T(8,128)(2,1)}, bf16[104,1536]{1,0:T(8,128)(2,1)S(1)}, u32[]{:S(2)}, u32[]{:S(2)}) collective-permute-start(bf16[104,1536]{1,0:T(8,128)(2,1)} %fusion.129.refs_1_), channel_id=1, source_target_pairs={{0,16},{4,20},{8,24},{12,28},{16,0},{20,4},{24,8},{28,12},{1,17},{... | collective-permute-start | bytes 958472 | tf_op jit(solution)/shard_map/ppermute | solution.py:193
  878.1 19.9 %collective-permute-start.71 = (bf16[1,112,768]{2,1,0:T(8,128)(2,1)S(1)}, bf16[1,112,768]{2,1,0:T(8,128)(2,1)}, u32[]{:S(2)}, u32[]{:S(2)}) collective-permute-start(bf16[1,112,768]{2,1,0:T(8,128)(2,1)S(1)} %add_convert_fusion.27.refs_1_), channel_id=1, source_target_pairs={{0,16},{4,20},{8,24},{12,28},{16,0},{20,4},{24,8},{28,12},{1,17},{... | collective-permute-start | bytes 516104 | tf_op jit(solution)/shard_map/ppermute | solution.py:193
  886.2 17.4 %collective-permute-start.79 = (bf16[2,384,128]{2,1,0:T(8,128)(2,1)}, bf16[2,384,128]{2,1,0:T(8,128)(2,1)}, u32[]{:S(2)}, u32[]{:S(2)}) collective-permute-start(bf16[2,384,128]{2,1,0:T(8,128)(2,1)} %fusion.135.refs_1_), channel_id=1, source_target_pairs={{0,8},{4,12},{8,0},{12,4},{16,24},{20,28},{24,16},{28,20},{1,9},{5... | collective-permute-start | bytes 589832 | tf_op jit(solution)/shard_map/ppermute | solution.py:193
  (492 other events, 3089.7 us)
